TPU v7x, 32 devices: a whole 2x2x4 slice. The times are simulated.
32 devices in a mesh: wide: 8 (over y, x, core), tensor: 4 (over z).
Axes of the slice: x: 2, y: 2, z: 4, core: 2. Of those that a mesh axis runs over, the one named last changes fastest.
Arguments:
- pixels: bfloat16 [1, 16, 128, 1024], P(None, 'wide', None, 'tensor'), may hold values from -25 to 25
- text_states: bfloat16 [1, 128, 4096], replicated, may hold values from -6 to 6
- text_length: int32 [1], replicated, may hold values from 17 to 128
- timestep: int32 [1], replicated, may hold values from 0 to 999
- conv_weights: bfloat16 [2, 9, 1024, 1024], P(None, None, 'wide', 'tensor'), may hold values from -0.0625 to 0.0625
- film_time: bfloat16 [1024, 2, 1024], P('wide', None, 'tensor'), may hold values from -0.1875 to 0.1875
- film_text: bfloat16 [4096, 2, 1024], P('wide', None, 'tensor'), may hold values from -0.375 to 0.375
- group_gain: float32 [2, 1024], P(None, 'tensor'), may hold values from 0.25 to 1.75
- group_bias: float32 [2, 1024], P(None, 'tensor'), may hold values from -3 to 3
- layer_gain: float32 [1024], P('tensor'), may hold values from 0.25 to 1.75
- layer_bias: float32 [1024], P('tensor'), may hold values from -3 to 3
- attn_in: bfloat16 [4, 1024, 1024], P(None, 'wide', 'tensor'), may hold values from -0.25 to 0.25
- text_kv: bfloat16 [2, 4096, 1024], P(None, 'wide', 'tensor'), may hold values from -0.125 to 0.125
- out_self: bfloat16 [1024, 1024], P('tensor', 'wide'), may hold values from -3 to 3
- out_cross: bfloat16 [1024, 1024], P('tensor', 'wide'), may hold values from -0.25 to 0.25
- cotangent: float32 [1, 16, 128, 1024], P(None, 'wide', None, 'tensor'), may hold values from -6 to 6
Outputs:
- result: float32 [1, 16, 128, 1024], P(None, 'wide', None, 'tensor')
- pixels_grad: float32 [1, 16, 128, 1024], P(None, 'wide', None, 'tensor')
- conv_grad: float32 [2, 9, 1024, 1024], P(None, None, 'wide', 'tensor')
- film_time_grad: float32 [1024, 2, 1024], P('wide', None, 'tensor')
- film_text_grad: float32 [4096, 2, 1024], P('wide', None, 'tensor')
- group_gain_grad: float32 [2, 1024], P(None, 'tensor')
- group_bias_grad: float32 [2, 1024], P(None, 'tensor')
- layer_gain_grad: float32 [1024], P('tensor')
- layer_bias_grad: float32 [1024], P('tensor')
- attn_in_grad: float32 [4, 1024, 1024], P(None, 'wide', 'tensor')
- text_kv_grad: float32 [2, 4096, 1024], P(None, 'wide', 'tensor')
- out_self_grad: float32 [1024, 1024], P('tensor', 'wide')
- out_cross_grad: float32 [1024, 1024], P('tensor', 'wide')
All inputs are finite; a program needn't handle non-finite values.
Results may differ from a plain program's by a relative error of at most 0.02.
Values may be sent and summed in bfloat16 or wider, within the bound.
No kernel may reach another device: no remote copies, remote signals or barrier semaphores. Data moves between devices by JAX's collectives and lax.ppermute only.
A program may use at most 192 MiB of HBM per device.

v0:
```python
import functools
import math

import jax
import jax.numpy as jnp
from jax import lax
from jax.experimental import pallas as pl
from jax.experimental.pallas import tpu as pltpu
from jax.sharding import PartitionSpec as P

C = 1024
GROUPS = 32
HEAD_DIM = 128
TEXT = 128
TEMB = 1024
MIB = 1 << 20
in_vmem = pl.BlockSpec(memory_space=pltpu.VMEM)
in_smem = pl.BlockSpec(memory_space=pltpu.SMEM)


def local_kernel(body, outs, operands, scratch, limit, flops, aliases=None, out_specs=None):
    size = sum(a.size * a.dtype.itemsize for a in operands)
    size += sum(math.prod(o.shape) * o.dtype.itemsize for o in outs)
    return pl.pallas_call(
        body,
        grid=(1,),
        out_shape=outs,
        in_specs=[in_smem] + [in_vmem] * (len(operands) - 1),
        out_specs=[in_vmem] * len(outs) if out_specs is None else out_specs,
        scratch_shapes=scratch,
        input_output_aliases={} if aliases is None else aliases,
        compiler_params=pltpu.CompilerParams(vmem_limit_bytes=limit * MIB),
        cost_estimate=pl.CostEstimate(flops=flops, bytes_accessed=size, transcendentals=0),
    )(*operands)


def turned(values, width):
    rows = values.shape[0]
    wide = values.astype(jnp.float32)
    column = lax.rem(lax.broadcasted_iota(jnp.int32, values.shape, 0), width)
    before = jnp.where(column == 0, 0.0, pltpu.roll(wide, 1, 0))
    after = jnp.where(column == width - 1, 0.0, pltpu.roll(wide, rows - 1, 0))
    return before.astype(jnp.bfloat16), values, after.astype(jnp.bfloat16)


def halves_swapped(values, odd):
    half = values.shape[1] // 2
    other = jnp.concatenate([values[:, half:], values[:, :half]], axis=1)
    return jnp.where(odd, other, values)


class Weights:
    def __init__(self, refs, spot, axis=0):
        self.refs = refs
        self.axis = axis
        self.paired = len(refs) > 1
        self.wide = spot[0]
        self.odd = lax.rem(spot[0], 2) == 1

    def block(self, chunk):
        return lax.bitwise_xor(lax.div(self.wide, 2), chunk) if self.paired else chunk

    def tap(self, chunk, position):
        if not self.paired:
            span = self.refs[0].shape[1 + self.axis] // 4
            part = slice(chunk * span, (chunk + 1) * span)
            return self.refs[0][(position, slice(None), part) if self.axis else (position, part)]
        parts = []
        for refs in (self.refs[:5], self.refs[5:]):
            if chunk < 3:
                parts.append(refs[chunk][position])
            else:
                first = refs[3].shape[0]
                parts.append(refs[3][position] if position < first else refs[4][position - first])
        return jnp.concatenate(parts, axis=self.axis)

    def ordered(self, values):
        return halves_swapped(values, self.odd) if self.paired else values


def conv_body(groups, parts, rows, width, spot, *refs):
    pieces = refs[:groups]
    top, bottom = refs[groups : groups + 2]
    weights = Weights(refs[groups + 2 : groups + 2 + parts], spot)
    source, first_out, second_out, *sends, frame = refs[groups + 2 + parts :]
    span = pieces[0].shape[1]
    for mask in range(groups):
        block = lax.bitwise_xor(spot[1], mask)
        own = pieces[mask][...]
        lanes = slice(mask * span, (mask + 1) * span)
        framed = jnp.concatenate([top[:, lanes], own, bottom[:, lanes]], axis=0)
        for column, values in enumerate(turned(weights.ordered(framed), width)):
            frame[block, column] = values
    total_sum = jnp.zeros(first_out.shape, jnp.float32)
    for chunk in range(groups):
        block = weights.block(chunk)
        for position in range(9):
            start = (position // 3) * width
            window = frame[block, position % 3, start : start + rows * width, :]
            total_sum += jnp.dot(
                window, weights.tap(chunk, position), preferred_element_type=jnp.float32
            )
        center = frame[block, 1, width : (rows + 1) * width, :]
        if weights.paired:
            sends[2 * chunk][...] = center[:, : span // 2]
            sends[2 * chunk + 1][...] = center[:, span // 2 :]
        else:
            sends[0][:, chunk * span : (chunk + 1) * span] = center
    if second_out.shape[0] == 2:
        first_out[...] = total_sum
        second_out[...] = channel_sums(total_sum)
    else:
        middle = (source[...].astype(jnp.float32) + total_sum) * root_half
        first_out[...] = middle
        second_out[...] = middle.astype(jnp.bfloat16)


def back_body(groups, rows, width, spot, grad, top, bottom, *refs):
    frame, held = refs[-2:]
    outs = refs[-2 - groups : -2]
    weights = Weights(refs[: -2 - groups], spot)
    framed = jnp.concatenate([top[...], grad[...], bottom[...]], axis=0)
    for column, values in enumerate(turned(framed, width)):
        frame[column] = values
    for chunk in range(groups):
        total_sum = jnp.zeros(held.shape[1:], jnp.float32)
        for position in range(9):
            start = (2 - position // 3) * width
            total_sum += lax.dot_general(
                frame[2 - position % 3, start : start + rows * width, :],
                weights.tap(chunk, position),
                (((1,), (1,)), ((), ())),
                preferred_element_type=jnp.float32,
            )
        held[weights.block(chunk)] = weights.ordered(total_sum).astype(jnp.bfloat16)
    for mask in range(groups):
        outs[mask][...] = held[lax.bitwise_xor(spot[1], mask)]


def bf16_like(*shape):
    return jax.ShapeDtypeStruct(shape, jnp.bfloat16)


def f32_like(*shape):
    return jax.ShapeDtypeStruct(shape, jnp.float32)


def flipped(values, axis, mask):
    count = lax.axis_size(axis)
    return lax.ppermute(values, axis, [(i, i ^ mask) for i in range(count)])


def spread_slots(values, first):
    over_x, over_y = flipped(values, "wide", 2), flipped(values, "wide", 4)
    low, high = flipped(over_x[:first], "wide", 4), flipped(over_y[first:], "wide", 2)
    mine = [values, over_x, over_y, low, high]
    return mine + [flipped(part, "wide", 1) for part in mine]


def has_slots():
    return lax.axis_size("wide") == 8


def after(value, *others):
    return lax.optimization_barrier((value, others))[0]


def gathered_grads(grad, first):
    return spread_slots(grad, first) if has_slots() else [grad]


def gathered_blocks(blocks, first, axis=1):
    if has_slots():
        return spread_slots(blocks, first)
    return [lax.all_gather(blocks, "wide", axis=axis, tiled=True)]


def spread_chips(values, first):
    if has_slots():
        over_x, over_y = flipped(values, "wide", 2), flipped(values, "wide", 4)
        low, high = flipped(over_x[:first], "wide", 4), flipped(over_y[first:], "wide", 2)
        return [values, over_x, over_y, low, high]
    mask = 2
    while mask < lax.axis_size("wide"):
        values = jnp.concatenate([values, flipped(values, "wide", mask)])
        mask *= 2
    return [values]


def spread_stats(values):
    if has_slots():
        over_x, over_y = flipped(values, "wide", 2), flipped(values, "wide", 4)
        return [values, over_x, over_y, flipped(over_x, "wide", 4)]
    mask = 2
    while mask < lax.axis_size("wide"):
        values = jnp.concatenate([values, flipped(values, "wide", mask)], axis=1)
        mask *= 2
    return [values]


def channel_pieces(values):
    count = lax.axis_size("tensor")
    return [values] + [flipped(values, "tensor", mask) for mask in range(1, count)]


def edge_rows(last, first):
    count = lax.axis_size("wide")
    above = lax.ppermute(last, "wide", [(i, i + 1) for i in range(count - 1)])
    below = lax.ppermute(first, "wide", [(i + 1, i) for i in range(count - 1)])
    return above, below


def convolve(spot, pieces, edges, kernel, source, second_shape, rows, width):
    groups, (area, span) = len(pieces), pieces[0].shape
    sends = [bf16_like(area, span // 2)] * (2 * groups) if has_slots() else [bf16_like(area, C)]
    return local_kernel(
        functools.partial(conv_body, groups, len(kernel), rows, width),
        [f32_like(area, span), second_shape] + sends,
        [spot, *pieces, *edges, *kernel, source],
        [pltpu.VMEM((groups, 3, (rows + 2) * width, span), jnp.bfloat16)],
        32,
        2 * 9 * area * C * span,
    )


def piece_edges(pieces, width):
    return edge_rows(
        jnp.concatenate([piece[-width:] for piece in pieces], axis=1),
        jnp.concatenate([piece[:width] for piece in pieces], axis=1),
    )


def convolve_back(spot, grad, edges, kernel, rows, width):
    groups, (area, span) = lax.axis_size("tensor"), grad.shape
    return local_kernel(
        functools.partial(back_body, groups, rows, width),
        [bf16_like(area, span)] * groups,
        [spot, grad, *edges, *kernel],
        [
            pltpu.VMEM((3, (rows + 2) * width, span), jnp.bfloat16),
            pltpu.VMEM((groups, area, span), jnp.bfloat16),
        ],
        32,
        2 * 9 * area * C * span,
    )


def sent_parts(parts):
    return [parts[0]] + [flipped(parts[mask], "tensor", mask) for mask in range(1, len(parts))]


def kernel_grad_body(count, width, spot, *refs):
    pieces = refs[:count]
    grads = refs[count : count + 10]
    out, turned_all, grad_all = refs[-3:]
    wide = spot[0]
    area, span = pieces[0].shape
    depth = count * area
    turned_all[:, :width] = jnp.zeros((3 * span, width), jnp.bfloat16)
    turned_all[:, depth + width :] = jnp.zeros((3 * span, width), jnp.bfloat16)
    for mask in range(count):
        start = pl.multiple_of(lax.bitwise_xor(wide, mask) * area, area)
        for column, values in enumerate(turned(pieces[mask][...], width)):
            flat = jnp.transpose(values.astype(jnp.float32)).astype(jnp.bfloat16)
            turned_all[column * span : (column + 1) * span, pl.ds(start + width, area)] = flat
        half = grads[5 * (mask % 2) : 5 * (mask % 2) + 5]
        if mask < 6:
            grad_all[pl.ds(start, area), :] = half[mask // 2][...]
        else:
            grad_all[pl.ds(start, width), :] = half[3][...]
            grad_all[pl.ds(start + width, area - width), :] = half[4][...]
    for row in range(3):
        product = jnp.dot(
            turned_all[:, row * width : row * width + depth],
            grad_all[...],
            preferred_element_type=jnp.float32,
        )
        for column in range(3):
            out[0, 3 * row + column] = product[column * span : (column + 1) * span, :]


def swapped_blocks(sends):
    if not has_slots():
        return sends
    return [sends[0]] + [flipped(sends[mask], "wide", mask) for mask in range(1, len(sends))]


def kernel_grad(spot, pieces, grads, rows, width, layer, earlier):
    count, area = len(pieces), rows * width
    span, columns = pieces[0].shape[1], grads[0].shape[1]
    operands = [spot, *pieces, *grads]
    specs = [in_smem] + [in_vmem] * (len(operands) - 1)
    shape = f32_like(2, 9, span, columns)
    if earlier is not None:
        operands.append(earlier)
        specs.append(pl.BlockSpec(memory_space=pl.ANY))
    return pl.pallas_call(
        functools.partial(kernel_grad_body, count, width),
        out_shape=shape,
        in_specs=specs,
        grid=(1,),
        out_specs=pl.BlockSpec((1, 9, span, columns), lambda i: (layer, 0, 0, 0)),
        scratch_shapes=[
            pltpu.VMEM((3 * span, count * area + 2 * width), jnp.bfloat16),
            pltpu.VMEM((count * area, columns), jnp.bfloat16),
        ],
        input_output_aliases={} if earlier is None else {len(operands) - 1: 0},
        compiler_params=pltpu.CompilerParams(vmem_limit_bytes=24 * MIB),
        cost_estimate=pl.CostEstimate(
            flops=2 * 9 * count * area * span * columns, bytes_accessed=4 * MIB, transcendentals=0
        ),
    )(*operands)


def kernel_grad_whole(sends, grad, rows, width):
    natural = sends[0].reshape(1, rows, width, C)
    swapped = lax.all_to_all(natural, "wide", split_axis=3, concat_axis=1, tiled=True)
    framed = jnp.pad(swapped, ((0, 0), (1, 1), (1, 1), (0, 0)))
    low = lax.all_gather(
        grad.reshape(1, rows, width, grad.shape[1]), "wide", axis=1, tiled=True
    )
    return jnp.stack(
        [
            jnp.einsum(
                "mrwc,mrwd->cd",
                framed[:, tap // 3 : tap // 3 + low.shape[1], tap % 3 : tap % 3 + width, :],
                low,
                preferred_element_type=jnp.float32,
            )
            for tap in range(9)
        ]
    )


root_half = 1.0 / math.sqrt(2.0)
highest = lax.Precision.HIGHEST


def sinusoid(steps):
    half_width = TEMB // 2
    frequency = jnp.exp(-math.log(10000.0) * jnp.arange(half_width, dtype=jnp.float32) / half_width)
    angles = steps.astype(jnp.float32)[:, None] * frequency[None, :]
    return jnp.concatenate([jnp.cos(angles), jnp.sin(angles)], axis=1)


def total(values, axis):
    mask = 1
    while mask < lax.axis_size(axis):
        values = values + flipped(values, axis, mask)
        mask *= 2
    return values


def silu_slope(values):
    logistic = lax.logistic(values)
    return logistic * (1.0 + values * (1.0 - logistic))


def channel_sums(values):
    return jnp.concatenate(
        [
            jnp.sum(values, axis=0, keepdims=True),
            jnp.sum(values * values, axis=0, keepdims=True),
        ],
        axis=0,
    )


def group_means(first, second, pixel_count):
    channels = first.shape[1]
    per_group = C // GROUPS
    row = lax.div(lax.broadcasted_iota(jnp.int32, (channels, channels), 0), per_group)
    column = lax.div(lax.broadcasted_iota(jnp.int32, (channels, channels), 1), per_group)
    same = jnp.where(row == column, 1.0, 0.0)
    rows = jnp.concatenate([first, second, jnp.zeros((6, channels), jnp.float32)], axis=0)
    means = jnp.dot(rows, same, precision=highest, preferred_element_type=jnp.float32)
    means = means / (pixel_count * per_group)
    return means[0:1], means[1:2]


def group_scale(first, second, pixel_count):
    center, square = group_means(first, second, pixel_count)
    return center, lax.rsqrt(square - center * center + 1e-05)


def lifted_sums(sums, film, pixel_count):
    slope, shift = 1.0 + film[0:1], film[1:2]
    plain, square = sums[0:1], sums[1:2]
    return (
        slope * plain + pixel_count * shift,
        slope * slope * square + 2.0 * slope * shift * plain + pixel_count * shift * shift,
    )


def silu_low(values):
    return (values * lax.logistic(values)).astype(jnp.bfloat16)


def first_norm_body(pixel_count, spot, pixels, sums, affine, out):
    center, inverse = group_scale(sums[0:1], sums[1:2], pixel_count)
    scaled = (pixels[...].astype(jnp.float32) - center) * inverse
    out[...] = silu_low(scaled * affine[0:1] + affine[1:2])


def second_norm_body(pixel_count, spot, inner, sums, film, affine, out):
    center, inverse = group_scale(*lifted_sums(sums[...], film[...], pixel_count), pixel_count)
    lifted = inner[...] * (1.0 + film[0:1]) + film[1:2]
    out[...] = silu_low((lifted - center) * inverse * affine[0:1] + affine[1:2])


def parts_sum(refs):
    summed = refs[0][...].astype(jnp.float32)
    for ref in refs[1:]:
        summed += ref[...].astype(jnp.float32)
    return summed


def stacked_rows(rows):
    return jnp.concatenate([jnp.sum(row, axis=0, keepdims=True) for row in rows], axis=0)


def second_back_body(groups, pixel_count, spot, *refs):
    inner, sums, film, affine, terms, out, rows = refs[groups:]
    center, inverse = group_scale(*lifted_sums(sums[...], film[...], pixel_count), pixel_count)
    own = inner[...]
    scaled = (own * (1.0 + film[0:1]) + film[1:2] - center) * inverse
    back = parts_sum(refs[:groups]) * silu_slope(scaled * affine[0:1] + affine[1:2])
    out[...] = back
    rows[0:3, :] = stacked_rows([back * scaled, back, back * own])
    rows[3:5, :] = terms[...]
    rows[5:8, :] = jnp.zeros((3, own.shape[1]), jnp.float32)


def second_input_body(pixel_count, width, spot, back, inner, sums, film, affine, rows, *outs):
    low, last, first, film_rows = outs
    slope, shift, gain = 1.0 + film[0:1], film[1:2], affine[0:1]
    plain_sum, square_sum = sums[0:1], sums[1:2]
    lifted_sum, lifted_square = lifted_sums(sums[...], film[...], pixel_count)
    center, inverse = group_scale(lifted_sum, lifted_square, pixel_count)
    dotted, plain = group_means(gain * rows[0:1], gain * rows[1:2], pixel_count)
    scaled = (inner[...] * slope + shift - center) * inverse
    grad = inverse * (back[...] * gain - plain - scaled * dotted)
    grad_low = (grad * slope).astype(jnp.bfloat16)
    low[...] = grad_low
    last[...] = grad_low[-width:]
    first[...] = grad_low[:width]
    scaled_sum = inverse * (lifted_sum - pixel_count * center)
    scaled_inner = inverse * (slope * square_sum + (shift - center) * plain_sum)
    film_rows[0:1, :] = inverse * (
        gain * rows[2:3] - plain * plain_sum - dotted * scaled_inner
    )
    film_rows[1:2, :] = inverse * (
        gain * rows[1:2] - pixel_count * plain - dotted * scaled_sum
    )


def first_back_body(groups, pixel_count, spot, *refs):
    pixels, sums, affine, out, rows = refs[groups:]
    center, inverse = group_scale(sums[0:1], sums[1:2], pixel_count)
    scaled = (pixels[...].astype(jnp.float32) - center) * inverse
    back = parts_sum(refs[:groups]) * silu_slope(scaled * affine[0:1] + affine[1:2])
    out[...] = back
    rows[...] = stacked_rows([back * scaled, back])


def first_input_body(pixel_count, spot, back, pixels, sums, affine, rows, middle, out):
    gain = affine[0:1]
    center, inverse = group_scale(sums[0:1], sums[1:2], pixel_count)
    dotted, plain = group_means(gain * rows[0:1], gain * rows[1:2], pixel_count)
    scaled = (pixels[...].astype(jnp.float32) - center) * inverse
    out[...] = inverse * (back[...] * gain - plain - scaled * dotted) + middle[...] * root_half


def dot(left, right):
    return jnp.dot(left, right, preferred_element_type=jnp.float32)


def dot_last(left, right):
    return lax.dot_general(
        left, right, (((1,), (1,)), ((), ())), preferred_element_type=jnp.float32
    )


def flat_turn(values):
    return jnp.transpose(values.astype(jnp.float32)).astype(jnp.bfloat16)


def dot_first(left, right):
    return dot(flat_turn(left), right)


def head_choice(values, odd):
    first, second = values[:, :HEAD_DIM], values[:, HEAD_DIM:]
    return jnp.where(odd, second, first), jnp.where(odd, first, second)


def heads_joined(kept, received, odd):
    return jnp.where(
        odd,
        jnp.concatenate([received, kept], axis=1),
        jnp.concatenate([kept, received], axis=1),
    )


def project_body(groups, parts, spot, *refs):
    pieces, gains = refs[:groups], refs[groups : 2 * groups]
    own = refs[2 * groups]
    weights = Weights(refs[2 * groups + 1 : 2 * groups + 1 + parts], spot)
    keep_q, keep_kv, send, cross, normed, scaled, center, inverse = refs[2 * groups + 1 + parts :]
    odd = lax.rem(spot[0], 2) == 1
    token_sum = token_square = 0.0
    for piece in pieces:
        values = piece[...].astype(jnp.float32)
        token_sum += jnp.sum(values, axis=1, keepdims=True)
        token_square += jnp.sum(values * values, axis=1, keepdims=True)
    mean = token_sum / C
    scale = lax.rsqrt(token_square / C - mean * mean + 1e-05)
    for mask in range(groups):
        values = (pieces[mask][...].astype(jnp.float32) - mean) * scale
        values = (values * gains[mask][0:1] + gains[mask][1:2]).astype(jnp.bfloat16)
        normed[lax.bitwise_xor(spot[1], mask)] = weights.ordered(values)
    center[...] = mean
    inverse[...] = scale
    scaled[...] = (own[...] - mean) * scale
    projected = []
    for position in range(4):
        total_sum = 0.0
        for chunk in range(groups):
            total_sum += dot(normed[weights.block(chunk)], weights.tap(chunk, position))
        projected.append(total_sum.astype(jnp.bfloat16))
    cross[...] = projected[3]
    chosen = [head_choice(values, odd) for values in projected[:3]]
    keep_q[...] = chosen[0][0]
    keep_kv[...] = jnp.concatenate([chosen[1][0], chosen[2][0]], axis=1)
    send[...] = jnp.concatenate([pair[1] for pair in chosen], axis=1)


def out_grad_body(groups, parts, spot, *refs):
    pieces = refs[:groups]
    weights = Weights(refs[groups : groups + parts], spot, 1)
    keep, send, cross, frame = refs[groups + parts :]
    for mask in range(groups):
        frame[lax.bitwise_xor(spot[1], mask)] = weights.ordered(pieces[mask][...])
    sums = []
    for position in range(2):
        total_sum = 0.0
        for chunk in range(groups):
            total_sum += dot_last(frame[weights.block(chunk)], weights.tap(chunk, position))
        sums.append(total_sum.astype(jnp.bfloat16))
    kept, sent = head_choice(sums[0], lax.rem(spot[0], 2) == 1)
    keep[...] = kept
    send[...] = sent
    cross[...] = sums[1]


def mix_body(groups, parts, spot, kept, received, crossed, *refs):
    weights = Weights(refs[:parts], spot, 1)
    outs, held = refs[parts:-1], refs[-1]
    attended = heads_joined(kept[...], received[...], lax.rem(spot[0], 2) == 1)
    for chunk in range(groups):
        total_sum = dot(attended, weights.tap(chunk, 0)) + dot(crossed[...], weights.tap(chunk, 1))
        held[weights.block(chunk)] = weights.ordered(total_sum).astype(jnp.bfloat16)
    for mask in range(groups):
        outs[mask][...] = held[lax.bitwise_xor(spot[1], mask)]


def over_rows(refs, step, state):
    for index, ref in enumerate(refs):
        rows = ref.shape[0]
        if rows <= 512:
            state = step(state, ref[...], index, 0)
        else:
            state = lax.fori_loop(
                0,
                rows // 512,
                lambda i, held: step(
                    held, ref[pl.ds(pl.multiple_of(i * 512, 512), 512), :], index, i * 512
                ),
                state,
            )
    return state


score_scale = HEAD_DIM ** (-0.5)


def attend_body(count, spot, query_grad, *refs):
    pairs = refs[:count]
    keep, send, stats = refs[count:]
    query, grad = query_grad[:, :HEAD_DIM], query_grad[:, HEAD_DIM:]
    queries = query.shape[0]

    def step(state, pair, index, start):
        top, weight_sum, weighted = state
        scores = dot_last(pair[:, :HEAD_DIM], query) * score_scale
        raised = jnp.maximum(top, jnp.max(scores, axis=0, keepdims=True))
        rescale = jnp.exp(top - raised)
        weights = jnp.exp(scores - raised)
        weight_sum = weight_sum * rescale + jnp.sum(weights, axis=0, keepdims=True)
        weighted = weighted * rescale + dot_first(pair[:, HEAD_DIM:], weights.astype(jnp.bfloat16))
        return raised, weight_sum, weighted

    top, weight_sum, weighted = over_rows(
        pairs,
        step,
        (
            jnp.full((1, queries), -1e30, jnp.float32),
            jnp.zeros((1, queries), jnp.float32),
            jnp.zeros((HEAD_DIM, queries), jnp.float32),
        ),
    )
    attended = weighted / weight_sum
    delta = jnp.sum(attended * jnp.transpose(grad.astype(jnp.float32)), axis=0, keepdims=True)
    stats[...] = jnp.concatenate([top + jnp.log(weight_sum), delta], axis=0)
    turned_back = jnp.transpose(attended).astype(jnp.bfloat16)
    keep[...] = turned_back[: queries // 2]
    send[...] = turned_back[queries // 2 :]


def query_grad_body(count, spot, query_grad, stats, *refs):
    pairs = refs[:count]
    keep, send = refs[count:]
    query, grad = query_grad[:, :HEAD_DIM], query_grad[:, HEAD_DIM:]
    queries = query.shape[0]
    log_sum, delta = stats[0:1, :], stats[1:2, :]

    def step(state, pair, index, start):
        scores = dot_last(pair[:, :HEAD_DIM], query) * score_scale
        probs = jnp.exp(scores - log_sum)
        grad_probs = dot_last(pair[:, HEAD_DIM:], grad)
        grad_scores = (probs * (grad_probs - delta)).astype(jnp.bfloat16)
        return state + dot_first(pair[:, :HEAD_DIM], grad_scores)

    flat = over_rows(pairs, step, jnp.zeros((HEAD_DIM, queries), jnp.float32))
    result = jnp.transpose(flat * score_scale).astype(jnp.bfloat16)
    keep[...] = result[: queries // 2]
    send[...] = result[queries // 2 :]


def key_grad_body(count, spot, pair, *refs):
    queries, stats = refs[:count], refs[count:-2]
    keep, send = refs[-2:]
    keys, values = pair[:, :HEAD_DIM], pair[:, HEAD_DIM:]
    depth = keys.shape[0]

    def step(state, block, index, start):
        grad_keys, grad_values = state
        rows = block.shape[0]
        if index < len(stats):
            lanes = pl.ds(start if isinstance(start, int) else pl.multiple_of(start, 512), rows)
            log_sum, delta = stats[index][0:1, lanes], stats[index][1:2, lanes]
        else:
            log_sum, delta = stats[-1][0:1, rows:], stats[-1][1:2, rows:]
        query, grad = block[:, :HEAD_DIM], block[:, HEAD_DIM:]
        probs = jnp.exp(dot_last(keys, query) * score_scale - log_sum)
        grad_values += dot(probs.astype(jnp.bfloat16), grad)
        grad_scores = probs * (dot_last(values, grad) - delta)
        grad_keys += dot(grad_scores.astype(jnp.bfloat16), query)
        return grad_keys, grad_values

    zero = jnp.zeros((depth, HEAD_DIM), jnp.float32)
    grad_keys, grad_values = over_rows(queries, step, (zero, zero))
    both = jnp.concatenate([grad_keys * score_scale, grad_values], axis=1).astype(jnp.bfloat16)
    keep[...] = both[: depth // 2]
    send[...] = both[depth // 2 :]


def cross_body(spot, query, text, grad, crossed, grad_query, text_grad):
    live = lax.broadcasted_iota(jnp.int32, (query.shape[0], text.shape[1]), 1) < spot[2]
    for head in range(query.shape[1] // HEAD_DIM):
        lanes = slice(head * HEAD_DIM, (head + 1) * HEAD_DIM)
        own, keys, values, back = query[:, lanes], text[0, :, lanes], text[1, :, lanes], grad[:, lanes]
        scores = jnp.where(live, dot_last(own, keys) * score_scale, -1e30)
        weights = jnp.exp(scores - jnp.max(scores, axis=1, keepdims=True))
        probs = weights / jnp.sum(weights, axis=1, keepdims=True)
        low = probs.astype(jnp.bfloat16)
        crossed[:, lanes] = dot(low, values).astype(jnp.bfloat16)
        grad_probs = dot_last(back, values)
        grad_scores = probs * (grad_probs - jnp.sum(probs * grad_probs, axis=1, keepdims=True))
        grad_low = grad_scores.astype(jnp.bfloat16)
        grad_query[:, lanes] = (dot(grad_low, keys) * score_scale).astype(jnp.bfloat16)
        text_grad[0, :, lanes] = (dot_first(grad_low, own) * score_scale).astype(jnp.bfloat16)
        text_grad[1, :, lanes] = dot_first(low, back).astype(jnp.bfloat16)


def joined_grads(spot, kept_query, got_query, kept_pair, got_pair, cross):
    odd = lax.rem(spot[0], 2) == 1
    return [
        heads_joined(kept_query[...], got_query[...], odd),
        heads_joined(kept_pair[:, :HEAD_DIM], got_pair[:, :HEAD_DIM], odd),
        heads_joined(kept_pair[:, HEAD_DIM:], got_pair[:, HEAD_DIM:], odd),
        cross[...],
    ]


def project_back_body(groups, parts, spot, kq, gq, kp, gp, cross, center, inverse, *refs):
    pieces, gains = refs[:groups], refs[groups : 2 * groups]
    weights = Weights(refs[2 * groups : 2 * groups + parts], spot)
    *outs, sums, held = refs[2 * groups + parts :]
    grads = joined_grads(spot, kq, gq, kp, gp, cross)
    for chunk in range(groups):
        total_sum = 0.0
        for position in range(4):
            total_sum += dot_last(grads[position], weights.tap(chunk, position))
        held[weights.block(chunk)] = weights.ordered(total_sum)
    plain = dotted = 0.0
    ones = jnp.ones((8, held.shape[2]), jnp.float32)
    for mask in range(groups):
        part = held[lax.bitwise_xor(spot[1], mask)]
        outs[mask][...] = part.astype(jnp.bfloat16)
        eased = part * gains[mask][0:1]
        unit = (pieces[mask][...].astype(jnp.float32) - center[...]) * inverse[...]
        plain += eased
        dotted += eased * unit
    for row, values in enumerate((plain, dotted)):
        sums[row : row + 1, :] = lax.dot_general(
            ones,
            values,
            (((1,), (1,)), ((), ())),
            precision=highest,
            preferred_element_type=jnp.float32,
        )[0:1]


def weight_grad_body(groups, paired, spot, kq, gq, kp, gp, cross, kept, received, crossed, normed, *refs):
    cotangents, out = refs[:groups], refs[groups]
    odd = lax.rem(spot[0], 2) == 1
    area, span = cross.shape
    right = jnp.concatenate(joined_grads(spot, kq, gq, kp, gp, cross), axis=1)
    columns = right.shape[1]
    out_right = jnp.concatenate(
        [heads_joined(kept[...], received[...], odd), crossed[...]], axis=1
    )
    for chunk in range(groups):
        rows = slice(chunk * span, (chunk + 1) * span)
        values = normed[chunk]
        left = halves_swapped(values, odd) if paired else values
        out[rows, :columns] = dot_first(left, right).astype(jnp.bfloat16)
    for mask in range(groups):
        start = pl.multiple_of(lax.bitwise_xor(spot[1], mask) * span, span)
        out[pl.ds(start, span), columns:] = dot_first(cotangents[mask][...], out_right).astype(
            jnp.bfloat16
        )


def norm_back_body(groups, width, spot, *refs):
    sums, scaled, inverse, cotangent, gain, middle, low, last, first, terms = refs[groups:]
    grad = parts_sum(refs[:groups])
    area = grad.shape[0]
    same = lax.broadcasted_iota(jnp.int32, (area, area), 0) == lax.broadcasted_iota(
        jnp.int32, (area, area), 1
    )
    plain = jnp.sum(jnp.where(same, sums[0:1, :], 0.0), axis=1, keepdims=True) / C
    dotted = jnp.sum(jnp.where(same, sums[1:2, :], 0.0), axis=1, keepdims=True) / C
    unit = scaled[...]
    terms[0:1, :] = jnp.sum(grad * unit, axis=0, keepdims=True)
    terms[1:2, :] = jnp.sum(grad, axis=0, keepdims=True)
    back = inverse[...] * (grad * gain[...] - plain - unit * dotted) + cotangent[...]
    middle[...] = back
    grad_low = (back * root_half).astype(jnp.bfloat16)
    low[...] = grad_low
    last[...] = grad_low[-width:]
    first[...] = grad_low[:width]


def shards(
    pixels,
    text_states,
    text_length,
    timestep,
    conv_weights,
    film_time,
    film_text,
    group_gain,
    group_bias,
    layer_gain,
    layer_bias,
    attn_in,
    text_kv,
    out_self,
    out_cross,
    cotangent,
):
    map_count, row_count, col_count, width_own = pixels.shape
    token_count = row_count * col_count
    groups = lax.axis_size("tensor")
    pixel_count = token_count * lax.axis_size("wide")
    own_shape = (map_count, row_count, col_count, width_own)
    flat = (token_count, width_own)
    half = (token_count, HEAD_DIM)
    edge = (col_count, width_own)
    spot = jnp.stack([lax.axis_index("wide"), lax.axis_index("tensor"), text_length[0]])
    spot = spot.astype(jnp.int32)
    own_pixels = pixels.reshape(flat)
    flat_cotangent = cotangent.reshape(flat)
    affine = [jnp.stack([group_gain[layer], group_bias[layer]]) for layer in range(2)]

    first_sums = total(channel_sums(own_pixels.astype(jnp.float32)), "wide")
    norm_gains = channel_pieces(jnp.stack([layer_gain, layer_bias]))
    grad_pieces = channel_pieces(flat_cotangent.astype(jnp.bfloat16))
    kernel_one = gathered_blocks(after(conv_weights[0], first_sums), 5)

    features = sinusoid(timestep).astype(jnp.bfloat16)
    present = jnp.arange(TEXT)[None, :] < text_length[:, None]
    pooled = jnp.einsum(
        "mtx,mt->mx", text_states, present.astype(jnp.bfloat16), preferred_element_type=jnp.float32
    )
    pooled = (pooled / text_length.astype(jnp.float32)[:, None]).astype(jnp.bfloat16)
    wide_index = lax.axis_index("wide")
    time_rows = film_time.shape[0]
    text_rows = film_text.shape[0]
    own_features = lax.dynamic_slice_in_dim(features, wide_index * time_rows, time_rows, 1)
    own_pooled = lax.dynamic_slice_in_dim(pooled, wide_index * text_rows, text_rows, 1)
    own_text = lax.dynamic_slice_in_dim(text_states, wide_index * text_rows, text_rows, 2)
    film_term = jnp.einsum(
        "mk,ksc->msc", own_features, film_time, preferred_element_type=jnp.float32
    ) + jnp.einsum("mk,ksc->msc", own_pooled, film_text, preferred_element_type=jnp.float32)
    film = total(film_term[0], "wide")
    text_term = jnp.einsum("mtx,pxd->pmtd", own_text, text_kv, preferred_element_type=jnp.float32)
    text_term = text_term.astype(jnp.bfloat16).reshape(2, TEXT, width_own)

    (first,) = local_kernel(
        functools.partial(first_norm_body, pixel_count),
        [bf16_like(*flat)],
        [spot, own_pixels, first_sums, affine[0]],
        [],
        8,
        0,
    )
    pieces = channel_pieces(first)
    edges = piece_edges(pieces, col_count)
    inner, sums, *first_sends = convolve(
        spot, pieces, edges, kernel_one, own_pixels, f32_like(2, width_own), row_count, col_count
    )
    inner_sums = total(sums, "wide")
    kernel_two = gathered_blocks(after(conv_weights[1], inner_sums), 5)
    (second,) = local_kernel(
        functools.partial(second_norm_body, pixel_count),
        [bf16_like(*flat)],
        [spot, inner, inner_sums, film, affine[1]],
        [],
        8,
        0,
    )
    pieces = channel_pieces(second)
    edges = piece_edges(pieces, col_count)
    in_maps = gathered_blocks(after(attn_in, *kernel_two[:5], *edges), 2)
    text_proj = total(after(text_term, *in_maps[:5]), "wide")
    out_maps = gathered_blocks(after(jnp.stack([out_self, out_cross]), *in_maps[:5]), 1, 2)
    middle, middle_low, *second_sends = convolve(
        spot, pieces, edges, kernel_two, own_pixels, bf16_like(*flat), row_count, col_count
    )

    middle_pieces = channel_pieces(middle_low)
    parts = len(in_maps)
    column = f32_like(token_count, 1)
    square = 2 * token_count * C * width_own
    kept_query, kept_pair, sent, cross_query, normed, scaled, center, inverse = local_kernel(
        functools.partial(project_body, groups, parts),
        [
            bf16_like(*half),
            bf16_like(*flat),
            bf16_like(token_count, 3 * HEAD_DIM),
            bf16_like(*flat),
            bf16_like(groups, *flat),
            f32_like(*flat),
            column,
            column,
        ],
        [spot, *middle_pieces, *norm_gains, middle, *in_maps],
        [],
        24,
        4 * square,
    )
    got = flipped(sent, "wide", 1)
    kept_grad, sent_grad, grad_crossed = local_kernel(
        functools.partial(out_grad_body, groups, len(out_maps)),
        [bf16_like(*half), bf16_like(*half), bf16_like(*flat)],
        [spot, *grad_pieces, *out_maps],
        [pltpu.VMEM((groups, *flat), jnp.bfloat16)],
        16,
        2 * square,
    )
    got_grad = flipped(sent_grad, "wide", 1)
    pair = jnp.concatenate([kept_pair, got[:, HEAD_DIM:]])
    pairs = spread_chips(pair, token_count)
    query_grad = jnp.concatenate(
        [
            jnp.concatenate([kept_query, got[:, :HEAD_DIM]]),
            jnp.concatenate([kept_grad, got_grad]),
        ],
        axis=1,
    )
    query_grads = spread_chips(after(query_grad, *pairs), token_count)
    scores = 2 * (2 * token_count) * HEAD_DIM * pixel_count
    kept_out, sent_out, stats = local_kernel(
        functools.partial(attend_body, len(pairs)),
        [bf16_like(*half), bf16_like(*half), f32_like(2, 2 * token_count)],
        [spot, query_grad, *pairs],
        [],
        24,
        2 * scores,
    )
    all_stats = spread_stats(stats)
    got_out = flipped(sent_out, "wide", 1)
    crossed, grad_cross_query, text_grads = local_kernel(
        cross_body,
        [bf16_like(*flat), bf16_like(*flat), bf16_like(2, TEXT, width_own)],
        [spot, cross_query, text_proj, grad_crossed],
        [],
        8,
        12 * token_count * TEXT * width_own,
    )
    kept_dq, sent_dq = local_kernel(
        functools.partial(query_grad_body, len(pairs)),
        [bf16_like(*half), bf16_like(*half)],
        [spot, query_grad, stats, *pairs],
        [],
        24,
        3 * scores,
    )
    got_dq = flipped(sent_dq, "wide", 1)
    kept_dk, sent_dk = local_kernel(
        functools.partial(key_grad_body, len(query_grads)),
        [bf16_like(*flat), bf16_like(*flat)],
        [spot, pair, *query_grads, *all_stats],
        [],
        24,
        4 * scores,
    )
    got_dk = flipped(sent_dk, "wide", 1)
    text_all = total(after(text_grads, *all_stats), "wide").astype(jnp.float32)
    first_blocks = swapped_blocks([after(send, text_all) for send in first_sends])
    second_blocks = swapped_blocks([after(send, text_all) for send in second_sends])
    mixed = local_kernel(
        functools.partial(mix_body, groups, len(out_maps)),
        [bf16_like(*flat)] * groups,
        [spot, kept_out, got_out, crossed, *out_maps],
        [pltpu.VMEM((groups, *flat), jnp.bfloat16)],
        16,
        2 * square,
    )
    mixed = sent_parts(mixed)
    result = middle
    for part in mixed:
        result = result + part.astype(jnp.float32)
    projected_grads = [after(kept_dq, *mixed), got_dq, kept_dk, got_dk, grad_cross_query]
    *norm_parts, sums = local_kernel(
        functools.partial(project_back_body, groups, parts),
        [bf16_like(*flat)] * groups + [f32_like(2, token_count)],
        [spot, *projected_grads, center, inverse, *middle_pieces, *norm_gains, *in_maps],
        [pltpu.VMEM((groups, *flat), jnp.float32)],
        24,
        4 * square,
    )
    norm_parts = sent_parts(norm_parts)
    sums = total(sums, "tensor")
    (weight_parts,) = local_kernel(
        functools.partial(weight_grad_body, groups, has_slots()),
        [bf16_like(C, 6 * width_own)],
        [spot, *projected_grads, kept_out, got_out, crossed, normed, *grad_pieces],
        [],
        24,
        6 * square,
    )
    weight_sums = lax.psum_scatter(weight_parts, "wide", scatter_dimension=0, tiled=True)
    grad_middle, grad_two, last, head, terms = local_kernel(
        functools.partial(norm_back_body, groups, col_count),
        [
            f32_like(*flat),
            bf16_like(*flat),
            bf16_like(*edge),
            bf16_like(*edge),
            f32_like(2, width_own),
        ],
        [
            spot,
            *norm_parts,
            after(sums, weight_parts, first_blocks, second_blocks),
            scaled,
            inverse,
            flat_cotangent,
            layer_gain[None],
        ],
        [],
        16,
        0,
    )

    edges = edge_rows(last, head)
    grads_two = gathered_grads(after(grad_two, *edges), col_count)
    back_parts = sent_parts(
        convolve_back(spot, grad_two, edges, kernel_two, row_count, col_count)
    )
    back, rows = local_kernel(
        functools.partial(second_back_body, groups, pixel_count),
        [f32_like(*flat), f32_like(8, width_own)],
        [spot, *back_parts, inner, inner_sums, film, affine[1], terms],
        [],
        16,
        0,
    )
    second_rows = total(after(rows, *grads_two), "wide")
    grad_one, last, head, film_rows = local_kernel(
        functools.partial(second_input_body, pixel_count, col_count),
        [bf16_like(*flat), bf16_like(*edge), bf16_like(*edge), f32_like(2, width_own)],
        [spot, back, inner, inner_sums, film, affine[1], second_rows],
        [],
        16,
        0,
    )
    edges = edge_rows(last, head)
    grads_one = gathered_grads(after(grad_one, *edges), col_count)
    conv_grad = None
    if has_slots():
        conv_grad = kernel_grad(
            spot, second_blocks, grads_two, row_count, col_count, 1, conv_grad
        )
        second_rows = after(second_rows, conv_grad)
    time_grad = own_features.astype(jnp.float32)[0][:, None, None] * film_rows[None]
    text_grad = own_pooled.astype(jnp.float32)[0][:, None, None] * film_rows[None]
    kv_grad = jnp.einsum(
        "tx,ptd->pxd", own_text[0].astype(jnp.float32), text_all, precision=highest
    )
    back_parts = sent_parts(
        convolve_back(spot, grad_one, edges, kernel_one, row_count, col_count)
    )
    back, rows = local_kernel(
        functools.partial(first_back_body, groups, pixel_count),
        [f32_like(*flat), f32_like(2, width_own)],
        [spot, *back_parts, own_pixels, first_sums, affine[0]],
        [],
        16,
        0,
    )
    first_rows = total(rows, "wide")
    if has_slots():
        conv_grad = kernel_grad(
            spot, first_blocks, grads_one, row_count, col_count, 0, conv_grad
        )
    else:
        conv_grad = jnp.stack(
            [
                kernel_grad_whole(first_sends, grad_one, row_count, col_count),
                kernel_grad_whole(second_sends, grad_two, row_count, col_count),
            ]
        )
    (pixels_grad,) = local_kernel(
        functools.partial(first_input_body, pixel_count),
        [f32_like(*flat)],
        [spot, back, own_pixels, first_sums, affine[0], first_rows, grad_middle],
        [],
        16,
        0,
    )
    weight_sums = weight_sums.astype(jnp.float32)
    in_count = 4 * width_own
    attn_in_grad = jnp.moveaxis(weight_sums[:, :in_count].reshape(-1, 4, width_own), 1, 0)
    return (
        result.reshape(own_shape),
        pixels_grad.reshape(own_shape),
        conv_grad,
        time_grad,
        text_grad,
        jnp.stack([first_rows[0], second_rows[0]]),
        jnp.stack([first_rows[1], second_rows[1]]),
        second_rows[3],
        second_rows[4],
        attn_in_grad,
        kv_grad,
        weight_sums[:, in_count : in_count + width_own].T,
        weight_sums[:, in_count + width_own :].T,
    )


def solution(mesh):
    placed = (
        P(None, "wide", None, "tensor"),
        P(),
        P(),
        P(),
        P(None, None, "wide", "tensor"),
        P("wide", None, "tensor"),
        P("wide", None, "tensor"),
        P(None, "tensor"),
        P(None, "tensor"),
        P("tensor"),
        P("tensor"),
        P(None, "wide", "tensor"),
        P(None, "wide", "tensor"),
        P("tensor", "wide"),
        P("tensor", "wide"),
        P(None, "wide", None, "tensor"),
    )
    return jax.shard_map(
        shards,
        mesh=mesh,
        in_specs=placed,
        out_specs=(
            P(None, "wide", None, "tensor"),
            P(None, "wide", None, "tensor"),
            P(None, None, "wide", "tensor"),
            P("wide", None, "tensor"),
            P("wide", None, "tensor"),
            P(None, "tensor"),
            P(None, "tensor"),
            P("tensor"),
            P("tensor"),
            P(None, "wide", "tensor"),
            P(None, "wide", "tensor"),
            P("tensor", "wide"),
            P("tensor", "wide"),
        ),
        check_vma=False,
    )
```

profile of v0, /device:TPU:0, one launch (start us, length us, event | category | flops | bytes accessed | tf_op | source)
XLA Modules:
  0.0 394.0 jit_solution(9712736755034519563)
XLA Ops:
  21.0 4.2 %collective-permute-start.5 = (bf16[256,256]{1,0:T(8,128)(2,1)S(1)}, bf16[256,256]{1,0:T(8,128)(2,1)S(1)}, u32[]{:S(2)}, u32[]{:S(2)}) collective-permute-start(bf16[256,256]{1,0:T(8,128)(2,1)S(1)} %shard_map.255.refs_0_), channel_id=1, source_target_pairs={{0,3},{1,2},{2,1},{3,0},{4,7},{5,6},{6,5},{7,4},{8,11},{9,10},{10,... | collective-permute-start | bytes 393224 | tf_op jit(solution)/shard_map/ppermute | solution.py:150
  29.6 5.0 %collective-permute-done.4.refs_2_ = bf16[256,256]{1,0:T(8,128)(2,1)S(1)} collective-permute-done((bf16[256,256]{1,0:T(8,128)(2,1)S(1)}, bf16[256,256]{1,0:T(8,128)(2,1)S(1)}, u32[]{:S(2)}, u32[]{:S(2)}) %collective-permute-start.4) | collective-permute-done | bytes 131104 | tf_op jit(solution)/shard_map/ppermute | solution.py:150
  40.1 4.5 %collective-permute-start.11 = (bf16[4,128,256]{2,1,0:T(8,128)(2,1)}, bf16[4,128,256]{2,1,0:T(8,128)(2,1)}, u32[]{:S(2)}, u32[]{:S(2)}) collective-permute-start(bf16[4,128,256]{2,1,0:T(8,128)(2,1)} %slice.205), channel_id=1, source_target_pairs={{0,8},{4,12},{8,0},{12,4},{16,24},{20,28},{24,16},{28,20},{1,9},{5... | collective-permute-start | bytes 786440 | tf_op jit(solution)/shard_map/ppermute | solution.py:150
  62.9 4.0 %shard_map.256 = (f32[256,256]{1,0:T(8,128)S(1)}, f32[2,256]{1,0:T(2,128)S(1)}, bf16[256,128]{1,0:T(8,128)(2,1)S(1)}, bf16[256,128]{1,0:T(8,128)(2,1)S(1)}, bf16...) custom-call(s32[3]{0:T(128)S(1)} %pad_add_fusion.spot, ...), custom_call_target="tpu_custom_call" | custom-call | flops 1207959552 | bytes 6686732 | tf_op jit(solution)/shard_map/pallas_call | solution.py:24
  82.0 2.8 collective-permute-done.25.refs_3_
  86.0 2.8 collective-permute-done.24.refs_2_
  91.7 5.7 %collective-permute-done.29.refs_8_.refs_2_ = bf16[9,128,256]{2,1,0:T(8,128)(2,1)S(1)} collective-permute-done((bf16[9,128,256]{2,1,0:T(8,128)(2,1)S(1)}, bf16[9,128,256]{2,1,0:T(8,128)(2,1)S(1)}, u32[]{:S(2)}, u32[]{:S(2)}) %collective-permute-start.29) | collective-permute-done | bytes 589856 | tf_op jit(solution)/shard_map/ppermute | solution.py:150
  98.0 3.0 collective-permute-done.28.refs_7_.refs_1_
  101.3 4.8 %collective-permute-start.33 = (bf16[9,128,256]{2,1,0:T(8,128)(2,1)S(1)}, bf16[9,128,256]{2,1,0:T(8,128)(2,1)S(1)}, u32[]{:S(2)}, u32[]{:S(2)}) collective-permute-start(bf16[9,128,256]{2,1,0:T(8,128)(2,1)S(1)} %collective-permute-done.28.refs_7_.refs_1_), channel_id=1, source_target_pairs={{0,4},{4,0},{8,12},{12,8},{16,20},{20,16},{24,28},{28,24},{1,5},{5... | collective-permute-start | bytes 1769480 | tf_op jit(solution)/shard_map/ppermute | solution.py:150
  109.2 2.9 collective-permute-start.43
  112.0 5.5 %collective-permute-done.44.refs_11_.refs_10_ = bf16[4,128,256]{2,1,0:T(8,128)(2,1)S(1)} collective-permute-done((bf16[4,128,256]{2,1,0:T(8,128)(2,1)S(1)}, bf16[4,128,256]{2,1,0:T(8,128)(2,1)S(1)}, u32[]{:S(2)}, u32[]{:S(2)}) %collective-permute-start.44) | collective-permute-done | bytes 262176 | tf_op jit(solution)/shard_map/ppermute | solution.py:150
  132.9 3.9 collective-permute-done.39.refs_3_
  136.8 5.3 %collective-permute-done.38.refs_2_ = bf16[256,256]{1,0:T(8,128)(2,1)S(1)} collective-permute-done((bf16[256,256]{1,0:T(8,128)(2,1)S(1)}, bf16[256,256]{1,0:T(8,128)(2,1)S(1)}, u32[]{:S(2)}, u32[]{:S(2)}) %collective-permute-start.38) | collective-permute-done | bytes 131104 | tf_op jit(solution)/shard_map/ppermute | solution.py:150
  156.1 3.4 collective-permute-done.54.refs_2_
  161.0 4.6 %collective-permute-done.59.refs_8_.refs_4_ = bf16[1,256,128]{2,1,0:T(8,128)(2,1)S(1)} collective-permute-done((bf16[1,256,128]{2,1,0:T(8,128)(2,1)S(1)}, bf16[1,256,128]{2,1,0:T(8,128)(2,1)S(1)}, u32[]{:S(2)}, u32[]{:S(2)}) %collective-permute-start.59) | collective-permute-done | bytes 65568 | tf_op jit(solution)/shard_map/ppermute | solution.py:150
  172.0 3.5 collective-permute-done.69.refs_4_
  179.2 7.8 %collective-permute-done.72 = bf16[2,128,256]{2,1,0:T(8,128)(2,1)S(1)} collective-permute-done((bf16[2,128,256]{2,1,0:T(8,128)(2,1)S(1)}, bf16[2,128,256]{2,1,0:T(8,128)(2,1)S(1)}, u32[]{:S(2)}, u32[]{:S(2)}) %collective-permute-start.72) | collective-permute-done | bytes 131104 | tf_op jit(solution)/shard_map/ppermute | solution.py:150
  190.4 3.1 shard_map.261
  200.9 2.9 collective-permute-start.75
  205.3 3.3 shard_map.265
  223.6 4.5 %collective-permute-done.92 = bf16[2,128,256]{2,1,0:T(8,128)(2,1)S(1)} collective-permute-done((bf16[2,128,256]{2,1,0:T(8,128)(2,1)S(1)}, bf16[2,128,256]{2,1,0:T(8,128)(2,1)S(1)}, u32[]{:S(2)}, u32[]{:S(2)}) %collective-permute-start.92) | collective-permute-done | bytes 131104 | tf_op jit(solution)/shard_map/ppermute | solution.py:150
  229.0 4.2 %collective-permute-done.93 = bf16[2,128,256]{2,1,0:T(8,128)(2,1)S(1)} collective-permute-done((bf16[2,128,256]{2,1,0:T(8,128)(2,1)S(1)}, bf16[2,128,256]{2,1,0:T(8,128)(2,1)S(1)}, u32[]{:S(2)}, u32[]{:S(2)}) %collective-permute-start.93) | collective-permute-done | bytes 131104 | tf_op jit(solution)/shard_map/ppermute | solution.py:150
  279.5 8.8 %collective-permute-done.90 = f32[2,256]{1,0:T(2,128)S(1)} collective-permute-done((f32[2,256]{1,0:T(2,128)S(1)}, f32[2,256]{1,0:T(2,128)S(1)}, u32[]{:S(2)}, u32[]{:S(2)}) %collective-permute-start.90) | collective-permute-done | bytes 2080 | tf_op jit(solution)/shard_map/ppermute | solution.py:150
  288.8 4.3 %collective-permute-done.107.refs_7_ = bf16[256,128]{1,0:T(8,128)(2,1)S(1)} collective-permute-done((bf16[256,128]{1,0:T(8,128)(2,1)S(1)}, bf16[256,128]{1,0:T(8,128)(2,1)S(1)}, u32[]{:S(2)}, u32[]{:S(2)}) %collective-permute-start.107) | collective-permute-done | bytes 65568 | tf_op jit(solution)/shard_map/ppermute | solution.py:150
  300.3 3.5 collective-permute-start.114
  306.6 2.8 collective-permute-start.111
  315.1 4.5 %collective-permute-done.111.refs_2_ = bf16[256,256]{1,0:T(8,128)(2,1)S(1)} collective-permute-done((bf16[256,256]{1,0:T(8,128)(2,1)S(1)}, bf16[256,256]{1,0:T(8,128)(2,1)S(1)}, u32[]{:S(2)}, u32[]{:S(2)}) %collective-permute-start.111) | collective-permute-done | bytes 131104 | tf_op jit(solution)/shard_map/ppermute | solution.py:150
  337.3 2.8 collective-permute-done.126.bottom
  340.0 3.8 shard_map.272
  353.7 3.5 shard_map.275.refs_18_
  358.8 2.8 collective-permute-start.130
  379.6 3.5 shard_map.276
  (765 shorter events, 243.8 us)
Async XLA Ops:
  7.2 375.9 %reduce-scatter.2.cloned.1.call-start = ((), (), s32[]{:S(2)}) async-start(), calls=%async_computation.1 | async-start | bytes 3538944 | tf_op jit(solution)/shard_map/reduce_scatter | solution.py:966
  25.8 13.5 %collective-permute-start.9 = (bf16[9,128,256]{2,1,0:T(8,128)(2,1)S(1)}, bf16[9,128,256]{2,1,0:T(8,128)(2,1)S(1)}, u32[]{:S(2)}, u32[]{:S(2)}) collective-permute-start(bf16[9,128,256]{2,1,0:T(8,128)(2,1)S(1)} %get-tuple-element.113.refs_6_.refs_0_), channel_id=1, source_target_pairs={{0,16},{4,20},{8,24},{12,28},{16,0},{20,4},{24,8},{28,12},{1,17},{... | collective-permute-start | bytes 1769480 | tf_op jit(solution)/shard_map/ppermute | solution.py:150
  27.4 17.1 %collective-permute-start.8 = (bf16[9,128,256]{2,1,0:T(8,128)(2,1)S(1)}, bf16[9,128,256]{2,1,0:T(8,128)(2,1)S(1)}, u32[]{:S(2)}, u32[]{:S(2)}) collective-permute-start(bf16[9,128,256]{2,1,0:T(8,128)(2,1)S(1)} %get-tuple-element.113.refs_6_.refs_0_), channel_id=1, source_target_pairs={{0,8},{4,12},{8,0},{12,4},{16,24},{20,28},{24,16},{28,20},{1,9},{5... | collective-permute-start | bytes 1769480 | tf_op jit(solution)/shard_map/ppermute | solution.py:150
  35.3 13.5 %collective-permute-start.6 = (bf16[128,1024]{1,0:T(8,128)(2,1)S(1)}, bf16[128,1024]{1,0:T(8,128)(2,1)S(1)}, u32[]{:S(2)}, u32[]{:S(2)}) collective-permute-start(bf16[128,1024]{1,0:T(8,128)(2,1)S(1)} %pad_maximum_fusion), channel_id=1, source_target_pairs={{0,4},{4,8},{8,12},{12,16},{16,20},{20,24},{24,28},{1,5},{5,9},{9,... | collective-permute-start | bytes 786440 | tf_op jit(solution)/shard_map/ppermute | solution.py:208
  36.6 13.3 %collective-permute-start.7 = (bf16[128,1024]{1,0:T(8,128)(2,1)S(1)}, bf16[128,1024]{1,0:T(8,128)(2,1)S(1)}, u32[]{:S(2)}, u32[]{:S(2)}) collective-permute-start(bf16[128,1024]{1,0:T(8,128)(2,1)S(1)} %pad_maximum_fusion.1), channel_id=1, source_target_pairs={{4,0},{8,4},{12,8},{16,12},{20,16},{24,20},{28,24},{5,1},{9,5},{13... | collective-permute-start | bytes 786440 | tf_op jit(solution)/shard_map/ppermute | solution.py:209
  40.1 15.0 %collective-permute-start.11 = (bf16[4,128,256]{2,1,0:T(8,128)(2,1)}, bf16[4,128,256]{2,1,0:T(8,128)(2,1)}, u32[]{:S(2)}, u32[]{:S(2)}) collective-permute-start(bf16[4,128,256]{2,1,0:T(8,128)(2,1)} %slice.205), channel_id=1, source_target_pairs={{0,8},{4,12},{8,0},{12,4},{16,24},{20,28},{24,16},{28,20},{1,9},{5... | collective-permute-start | bytes 786440 | tf_op jit(solution)/shard_map/ppermute | solution.py:150
  81.4 27.8 %collective-permute-start.32 = (bf16[9,128,256]{2,1,0:T(8,128)(2,1)S(1)}, bf16[9,128,256]{2,1,0:T(8,128)(2,1)S(1)}, u32[]{:S(2)}, u32[]{:S(2)}) collective-permute-start(bf16[9,128,256]{2,1,0:T(8,128)(2,1)S(1)} %get-tuple-element.116.refs_6_.refs_0_), channel_id=1, source_target_pairs={{0,4},{4,0},{8,12},{12,8},{16,20},{20,16},{24,28},{28,24},{1,5},{5... | collective-permute-start | bytes 1769480 | tf_op jit(solution)/shard_map/ppermute | solution.py:150
  81.4 15.9 %collective-permute-start.29 = (bf16[9,128,256]{2,1,0:T(8,128)(2,1)S(1)}, bf16[9,128,256]{2,1,0:T(8,128)(2,1)S(1)}, u32[]{:S(2)}, u32[]{:S(2)}) collective-permute-start(bf16[9,128,256]{2,1,0:T(8,128)(2,1)S(1)} %get-tuple-element.116.refs_6_.refs_0_), channel_id=1, source_target_pairs={{0,16},{4,20},{8,24},{12,28},{16,0},{20,4},{24,8},{28,12},{1,17},{... | collective-permute-start | bytes 1769480 | tf_op jit(solution)/shard_map/ppermute | solution.py:150
  84.8 16.3 %collective-permute-start.28 = (bf16[9,128,256]{2,1,0:T(8,128)(2,1)S(1)}, bf16[9,128,256]{2,1,0:T(8,128)(2,1)S(1)}, u32[]{:S(2)}, u32[]{:S(2)}) collective-permute-start(bf16[9,128,256]{2,1,0:T(8,128)(2,1)S(1)} %get-tuple-element.116.refs_6_.refs_0_), channel_id=1, source_target_pairs={{0,8},{4,12},{8,0},{12,4},{16,24},{20,28},{24,16},{28,20},{1,9},{5... | collective-permute-start | bytes 1769480 | tf_op jit(solution)/shard_map/ppermute | solution.py:150
  88.9 12.4 %collective-permute-start.26 = (bf16[128,1024]{1,0:T(8,128)(2,1)S(1)}, bf16[128,1024]{1,0:T(8,128)(2,1)S(1)}, u32[]{:S(2)}, u32[]{:S(2)}) collective-permute-start(bf16[128,1024]{1,0:T(8,128)(2,1)S(1)} %pad_maximum_fusion.2), channel_id=1, source_target_pairs={{0,4},{4,8},{8,12},{12,16},{16,20},{20,24},{24,28},{1,5},{5,9},{9,... | collective-permute-start | bytes 786440 | tf_op jit(solution)/shard_map/ppermute | solution.py:208
  101.2 18.4 %collective-permute-start.34 = (bf16[9,128,256]{2,1,0:T(8,128)(2,1)S(1)}, bf16[9,128,256]{2,1,0:T(8,128)(2,1)S(1)}, u32[]{:S(2)}, u32[]{:S(2)}) collective-permute-start(bf16[9,128,256]{2,1,0:T(8,128)(2,1)S(1)} %collective-permute-done.29.refs_8_.refs_2_), channel_id=1, source_target_pairs={{0,4},{4,0},{8,12},{12,8},{16,20},{20,16},{24,28},{28,24},{1,5},{5... | collective-permute-start | bytes 1769480 | tf_op jit(solution)/shard_map/ppermute | solution.py:150
  101.3 20.8 %collective-permute-start.33 = (bf16[9,128,256]{2,1,0:T(8,128)(2,1)S(1)}, bf16[9,128,256]{2,1,0:T(8,128)(2,1)S(1)}, u32[]{:S(2)}, u32[]{:S(2)}) collective-permute-start(bf16[9,128,256]{2,1,0:T(8,128)(2,1)S(1)} %collective-permute-done.28.refs_7_.refs_1_), channel_id=1, source_target_pairs={{0,4},{4,0},{8,12},{12,8},{16,20},{20,16},{24,28},{28,24},{1,5},{5... | collective-permute-start | bytes 1769480 | tf_op jit(solution)/shard_map/ppermute | solution.py:150
  117.8 13.2 %collective-permute-start.46 = (bf16[2,128,256]{2,1,0:T(8,128)(2,1)S(1)}, bf16[2,128,256]{2,1,0:T(8,128)(2,1)S(1)}, u32[]{:S(2)}, u32[]{:S(2)}) collective-permute-start(bf16[2,128,256]{2,1,0:T(8,128)(2,1)S(1)} %slice.217), channel_id=1, source_target_pairs={{0,8},{4,12},{8,0},{12,4},{16,24},{20,28},{24,16},{28,20},{1,9},{5... | collective-permute-start | bytes 393224 | tf_op jit(solution)/shard_map/ppermute | solution.py:150
  128.0 14.1 %collective-permute-start.49 = (bf16[4,128,256]{2,1,0:T(8,128)(2,1)S(1)}, bf16[4,128,256]{2,1,0:T(8,128)(2,1)S(1)}, u32[]{:S(2)}, u32[]{:S(2)}) collective-permute-start(bf16[4,128,256]{2,1,0:T(8,128)(2,1)S(1)} %collective-permute-done.44.refs_11_.refs_10_), channel_id=1, source_target_pairs={{0,4},{4,0},{8,12},{12,8},{16,20},{20,16},{24,28},{28,24},{1,5},{5... | collective-permute-start | bytes 786440 | tf_op jit(solution)/shard_map/ppermute | solution.py:150
  128.0 14.1 %collective-permute-start.48 = (bf16[4,128,256]{2,1,0:T(8,128)(2,1)S(1)}, bf16[4,128,256]{2,1,0:T(8,128)(2,1)S(1)}, u32[]{:S(2)}, u32[]{:S(2)}) collective-permute-start(bf16[4,128,256]{2,1,0:T(8,128)(2,1)S(1)} %collective-permute-done.43.refs_10_.refs_9_), channel_id=1, source_target_pairs={{0,4},{4,0},{8,12},{12,8},{16,20},{20,16},{24,28},{28,24},{1,5},{5... | collective-permute-start | bytes 786440 | tf_op jit(solution)/shard_map/ppermute | solution.py:150
  154.5 15.1 %collective-permute-start.67 = (bf16[512,256]{1,0:T(8,128)(2,1)S(1)}, bf16[512,256]{1,0:T(8,128)(2,1)S(1)}, u32[]{:S(2)}, u32[]{:S(2)}) collective-permute-start(bf16[512,256]{1,0:T(8,128)(2,1)S(1)} %pad_maximum_fusion.4.refs_0_.pair), channel_id=1, source_target_pairs={{0,16},{4,20},{8,24},{12,28},{16,0},{20,4},{24,8},{28,12},{1,17},{... | collective-permute-start | bytes 786440 | tf_op jit(solution)/shard_map/ppermute | solution.py:150
  155.8 14.2 %collective-permute-start.66 = (bf16[512,256]{1,0:T(8,128)(2,1)S(1)}, bf16[512,256]{1,0:T(8,128)(2,1)S(1)}, u32[]{:S(2)}, u32[]{:S(2)}) collective-permute-start(bf16[512,256]{1,0:T(8,128)(2,1)S(1)} %pad_maximum_fusion.4.refs_0_.pair), channel_id=1, source_target_pairs={{0,8},{4,12},{8,0},{12,4},{16,24},{20,28},{24,16},{28,20},{1,9},{5... | collective-permute-start | bytes 786440 | tf_op jit(solution)/shard_map/ppermute | solution.py:150
  175.6 12.3 %collective-permute-start.79 = (bf16[512,256]{1,0:T(8,128)(2,1)S(1)}, bf16[512,256]{1,0:T(8,128)(2,1)S(1)}, u32[]{:S(2)}, u32[]{:S(2)}) collective-permute-start(bf16[512,256]{1,0:T(8,128)(2,1)S(1)} %maximum_maximum_fusion.query_grad.refs_0_), channel_id=1, source_target_pairs={{0,16},{4,20},{8,24},{12,28},{16,0},{20,4},{24,8},{28,12},{1,17},{... | collective-permute-start | bytes 786440 | tf_op jit(solution)/shard_map/ppermute | solution.py:150
  177.0 12.4 %collective-permute-start.78 = (bf16[512,256]{1,0:T(8,128)(2,1)S(1)}, bf16[512,256]{1,0:T(8,128)(2,1)S(1)}, u32[]{:S(2)}, u32[]{:S(2)}) collective-permute-start(bf16[512,256]{1,0:T(8,128)(2,1)S(1)} %maximum_maximum_fusion.query_grad.refs_0_), channel_id=1, source_target_pairs={{0,8},{4,12},{8,0},{12,4},{16,24},{20,28},{24,16},{28,20},{1,9},{5... | collective-permute-start | bytes 786440 | tf_op jit(solution)/shard_map/ppermute | solution.py:150
  187.9 17.4 %collective-permute-start.81 = (bf16[256,256]{1,0:T(8,128)(2,1)S(1)}, bf16[256,256]{1,0:T(8,128)(2,1)S(1)}, u32[]{:S(2)}, u32[]{:S(2)}) collective-permute-start(bf16[256,256]{1,0:T(8,128)(2,1)S(1)} %slice.225), channel_id=1, source_target_pairs={{0,8},{4,12},{8,0},{12,4},{16,24},{20,28},{24,16},{28,20},{1,9},{5... | collective-permute-start | bytes 393224 | tf_op jit(solution)/shard_map/ppermute | solution.py:150
  189.5 15.8 %collective-permute-start.80 = (bf16[256,256]{1,0:T(8,128)(2,1)S(1)}, bf16[256,256]{1,0:T(8,128)(2,1)S(1)}, u32[]{:S(2)}, u32[]{:S(2)}) collective-permute-start(bf16[256,256]{1,0:T(8,128)(2,1)S(1)} %slice.224), channel_id=1, source_target_pairs={{0,16},{4,20},{8,24},{12,28},{16,0},{20,4},{24,8},{28,12},{1,17},{... | collective-permute-start | bytes 393224 | tf_op jit(solution)/shard_map/ppermute | solution.py:150
  200.9 12.9 %collective-permute-start.75 = (bf16[256,256]{1,0:T(8,128)(2,1)S(1)}, bf16[256,256]{1,0:T(8,128)(2,1)S(1)}, u32[]{:S(2)}, u32[]{:S(2)}) collective-permute-start(bf16[256,256]{1,0:T(8,128)(2,1)S(1)} %get-tuple-element.134), channel_id=1, source_target_pairs={{0,2},{1,3},{2,0},{3,1},{4,6},{5,7},{6,4},{7,5},{8,10},{9,11},{10,... | collective-permute-start | bytes 393224 | tf_op jit(solution)/shard_map/ppermute | solution.py:150
  239.7 30.3 %collective-permute-start.100 = (bf16[256,128]{1,0:T(8,128)(2,1)}, bf16[256,128]{1,0:T(8,128)(2,1)S(1)}, u32[]{:S(2)}, u32[]{:S(2)}) collective-permute-start(bf16[256,128]{1,0:T(8,128)(2,1)} %copy-done.144), channel_id=1, source_target_pairs={{0,28},{4,24},{8,20},{12,16},{16,12},{20,8},{24,4},{28,0},{1,29},{... | collective-permute-start | bytes 196616 | tf_op jit(solution)/shard_map/ppermute | solution.py:150
  241.3 30.8 %collective-permute-start.101 = (bf16[256,128]{1,0:T(8,128)(2,1)}, bf16[256,128]{1,0:T(8,128)(2,1)S(1)}, u32[]{:S(2)}, u32[]{:S(2)}) collective-permute-start(bf16[256,128]{1,0:T(8,128)(2,1)} %copy-done.159), channel_id=1, source_target_pairs={{0,4},{4,0},{8,12},{12,8},{16,20},{20,16},{24,28},{28,24},{1,5},{5... | collective-permute-start | bytes 196616 | tf_op jit(solution)/shard_map/ppermute | solution.py:150
  242.2 30.7 %collective-permute-start.102 = (bf16[256,128]{1,0:T(8,128)(2,1)}, bf16[256,128]{1,0:T(8,128)(2,1)S(1)}, u32[]{:S(2)}, u32[]{:S(2)}) collective-permute-start(bf16[256,128]{1,0:T(8,128)(2,1)} %copy-done.158), channel_id=1, source_target_pairs={{0,8},{4,12},{8,0},{12,4},{16,24},{20,28},{24,16},{28,20},{1,9},{5... | collective-permute-start | bytes 196616 | tf_op jit(solution)/shard_map/ppermute | solution.py:150
  243.9 29.4 %collective-permute-start.103 = (bf16[256,128]{1,0:T(8,128)(2,1)}, bf16[256,128]{1,0:T(8,128)(2,1)S(1)}, u32[]{:S(2)}, u32[]{:S(2)}) collective-permute-start(bf16[256,128]{1,0:T(8,128)(2,1)} %copy-done.157), channel_id=1, source_target_pairs={{0,12},{4,8},{8,4},{12,0},{16,28},{20,24},{24,20},{28,16},{1,13},{... | collective-permute-start | bytes 196616 | tf_op jit(solution)/shard_map/ppermute | solution.py:150
  245.1 32.2 %collective-permute-start.104 = (bf16[256,128]{1,0:T(8,128)(2,1)}, bf16[256,128]{1,0:T(8,128)(2,1)S(1)}, u32[]{:S(2)}, u32[]{:S(2)}) collective-permute-start(bf16[256,128]{1,0:T(8,128)(2,1)} %copy-done.156), channel_id=1, source_target_pairs={{0,16},{4,20},{8,24},{12,28},{16,0},{20,4},{24,8},{28,12},{1,17},{... | collective-permute-start | bytes 196616 | tf_op jit(solution)/shard_map/ppermute | solution.py:150
  272.9 20.8 %collective-permute-start.86 = (bf16[256,256]{1,0:T(8,128)(2,1)S(1)}, bf16[256,256]{1,0:T(8,128)(2,1)S(1)}, u32[]{:S(2)}, u32[]{:S(2)}) collective-permute-start(bf16[256,256]{1,0:T(8,128)(2,1)S(1)} %get-tuple-element.147), channel_id=1, source_target_pairs={{0,1},{1,0},{2,3},{3,2},{4,5},{5,4},{6,7},{7,6},{8,9},{9,8},{10,11... | collective-permute-start | bytes 393224 | tf_op jit(solution)/shard_map/ppermute | solution.py:150
  273.3 20.4 %collective-permute-start.87 = (bf16[256,256]{1,0:T(8,128)(2,1)S(1)}, bf16[256,256]{1,0:T(8,128)(2,1)S(1)}, u32[]{:S(2)}, u32[]{:S(2)}) collective-permute-start(bf16[256,256]{1,0:T(8,128)(2,1)S(1)} %get-tuple-element.148), channel_id=1, source_target_pairs={{0,2},{1,3},{2,0},{3,1},{4,6},{5,7},{6,4},{7,5},{8,10},{9,11},{10,... | collective-permute-start | bytes 393224 | tf_op jit(solution)/shard_map/ppermute | solution.py:150
  275.8 17.9 %collective-permute-start.88 = (bf16[256,256]{1,0:T(8,128)(2,1)S(1)}, bf16[256,256]{1,0:T(8,128)(2,1)S(1)}, u32[]{:S(2)}, u32[]{:S(2)}) collective-permute-start(bf16[256,256]{1,0:T(8,128)(2,1)S(1)} %get-tuple-element.149), channel_id=1, source_target_pairs={{0,3},{1,2},{2,1},{3,0},{4,7},{5,6},{6,5},{7,4},{8,11},{9,10},{10,... | collective-permute-start | bytes 393224 | tf_op jit(solution)/shard_map/ppermute | solution.py:150
  306.6 13.0 %collective-permute-start.111 = (bf16[256,256]{1,0:T(8,128)(2,1)S(1)}, bf16[256,256]{1,0:T(8,128)(2,1)S(1)}, u32[]{:S(2)}, u32[]{:S(2)}) collective-permute-start(bf16[256,256]{1,0:T(8,128)(2,1)S(1)} %get-tuple-element.193), channel_id=1, source_target_pairs={{0,2},{1,3},{2,0},{3,1},{4,6},{5,7},{6,4},{7,5},{8,10},{9,11},{10,... | collective-permute-start | bytes 393224 | tf_op jit(solution)/shard_map/ppermute | solution.py:150
  344.1 13.2 %collective-permute-start.127 = (bf16[256,256]{1,0:T(8,128)(2,1)}, bf16[256,256]{1,0:T(8,128)(2,1)S(1)}, u32[]{:S(2)}, u32[]{:S(2)}) collective-permute-start(bf16[256,256]{1,0:T(8,128)(2,1)} %get-tuple-element.204), channel_id=1, source_target_pairs={{0,1},{1,0},{2,3},{3,2},{4,5},{5,4},{6,7},{7,6},{8,9},{9,8},{10,11... | collective-permute-start | bytes 393224 | tf_op jit(solution)/shard_map/ppermute | solution.py:150
  (310 other events, 4568.3 us)
Sparse Core Ops, SparseCore 0:
  219.9 49.0 reduce-scatter.1
where the time goes:
time: 400 us; the launch traced here: 394 us
  starting transfers between devices  140 us (35%)
  waiting for transfers between devices  117 us (29%)
  local copies, waits for them, and re-layouts  57.4 us (14%)
  Pallas kernels  46 us (12%)
  between operations  18.3 us (5%)
  other arithmetic  10.9 us (3%)
  matrix products  4.64 us (1%)
    ppermute x134, starting transfers between devices, flipped(): return lax.ppermute(values, axis, [(i, i ^ mask) for i in range(count)])  129 us
    ppermute x134, waiting for transfers between devices, flipped(): return lax.ppermute(values, axis, [(i, i ^ mask) for i in range(count)])  111 us
    unnamed x401, local copies, waits for them, and re-layouts  48.7 us
    pallas_call x20, Pallas kernels, local_kernel(): pl.pallas_call(body, grid=(1,), out_shape=outs, in_specs=[in_smem] + [in_...  38.9 us
  transfers between devices with their start and end apart: 143, of which 43 were waited for; matrix products, arithmetic and copies ran while one was open for 6% of the time, Pallas kernels for 10%

commit v1 on v0

--- a/solution.py
+++ b/solution.py
@@ -34,6 +34,10 @@
     )(*operands)
 
 
+def far(arrays):
+    return [pltpu.with_memory_space_constraint(array, pltpu.HBM) for array in arrays]
+
+
 def turned(values, width):
     rows = values.shape[0]
     wide = values.astype(jnp.float32)
@@ -50,39 +54,40 @@
 
 
 class Weights:
-    def __init__(self, refs, spot, axis=0):
+    def __init__(self, refs, spot, groups):
         self.refs = refs
-        self.axis = axis
         self.paired = len(refs) > 1
-        self.wide = spot[0]
+        self.groups = groups
+        self.spot = spot
         self.odd = lax.rem(spot[0], 2) == 1
 
     def block(self, chunk):
-        return lax.bitwise_xor(lax.div(self.wide, 2), chunk) if self.paired else chunk
+        return lax.bitwise_xor(lax.div(self.spot[0], 2) if self.paired else self.spot[1], chunk)
 
     def tap(self, chunk, position):
         if not self.paired:
-            span = self.refs[0].shape[1 + self.axis] // 4
-            part = slice(chunk * span, (chunk + 1) * span)
-            return self.refs[0][(position, slice(None), part) if self.axis else (position, part)]
-        parts = []
-        for refs in (self.refs[:5], self.refs[5:]):
-            if chunk < 3:
-                parts.append(refs[chunk][position])
-            else:
-                first = refs[3].shape[0]
-                parts.append(refs[3][position] if position < first else refs[4][position - first])
-        return jnp.concatenate(parts, axis=self.axis)
+            each = self.refs[0].shape[0] // self.groups
+            start = self.block(chunk) * each
+            parts = [self.refs[0][start + i, position] for i in range(each)]
+            return jnp.concatenate(parts, axis=0)
+        parts = [self.refs[chunk][position], self.refs[4 + chunk][position]]
+        return jnp.concatenate(parts, axis=0)
 
     def ordered(self, values):
         return halves_swapped(values, self.odd) if self.paired else values
 
 
-def conv_body(groups, parts, rows, width, spot, *refs):
+def conv_body(groups, parts, count, rows, width, spot, *refs):
     pieces = refs[:groups]
     top, bottom = refs[groups : groups + 2]
-    weights = Weights(refs[groups + 2 : groups + 2 + parts], spot)
-    source, first_out, second_out, *sends, frame = refs[groups + 2 + parts :]
+    weights = Weights(refs[groups + 2 : groups + 2 + parts], spot, groups)
+    source, *rest = refs[groups + 2 + parts :]
+    earlier, rest = rest[:count], rest[count:]
+    first_out, second_out, *sends, frame = rest
+    for send, held in zip(sends, earlier):
+        send[:, 0] = held[...]
+    if earlier:
+        sends = [send.at[:, 1] for send in sends]
     span = pieces[0].shape[1]
     for mask in range(groups):
         block = lax.bitwise_xor(spot[1], mask)
@@ -100,12 +105,14 @@
             total_sum += jnp.dot(
                 window, weights.tap(chunk, position), preferred_element_type=jnp.float32
             )
-        center = frame[block, 1, width : (rows + 1) * width, :]
-        if weights.paired:
-            sends[2 * chunk][...] = center[:, : span // 2]
-            sends[2 * chunk + 1][...] = center[:, span // 2 :]
+        if len(sends) == 1:
+            sends[0][chunk] = frame[chunk, 1, width : (rows + 1) * width, :]
         else:
-            sends[0][:, chunk * span : (chunk + 1) * span] = center
+            near = lax.bitwise_xor(lax.div(spot[0], 2), chunk)
+            center = frame[near, 1, width : (rows + 1) * width, :]
+            center = center if weights.paired else halves_swapped(center, weights.odd)
+            sends[0][chunk] = center[:, : span // 2]
+            sends[1][chunk] = center[:, span // 2 :]
     if second_out.shape[0] == 2:
         first_out[...] = total_sum
         second_out[...] = channel_sums(total_sum)
@@ -118,7 +125,7 @@
 def back_body(groups, rows, width, spot, grad, top, bottom, *refs):
     frame, held = refs[-2:]
     outs = refs[-2 - groups : -2]
-    weights = Weights(refs[: -2 - groups], spot)
+    weights = Weights(refs[: -2 - groups], spot, groups)
     framed = jnp.concatenate([top[...], grad[...], bottom[...]], axis=0)
     for column, values in enumerate(turned(framed, width)):
         frame[column] = values
@@ -150,10 +157,16 @@
     return lax.ppermute(values, axis, [(i, i ^ mask) for i in range(count)])
 
 
-def spread_slots(values, first):
+def over_chips(values):
     over_x, over_y = flipped(values, "wide", 2), flipped(values, "wide", 4)
-    low, high = flipped(over_x[:first], "wide", 4), flipped(over_y[first:], "wide", 2)
-    mine = [values, over_x, over_y, low, high]
+    odd = lax.rem(lax.axis_index("wide"), 2) == 1
+    relayed = jnp.where(odd, over_y, over_x)
+    far_pairs = [(i, i ^ (2 if i % 2 else 4)) for i in range(8)]
+    return [values, over_x, over_y, lax.ppermute(relayed, "wide", far_pairs)]
+
+
+def spread_slots(values):
+    mine = over_chips(values)
     return mine + [flipped(part, "wide", 1) for part in mine]
 
 
@@ -165,21 +178,17 @@
     return lax.optimization_barrier((value, others))[0]
 
 
-def gathered_grads(grad, first):
-    return spread_slots(grad, first) if has_slots() else [grad]
-
-
-def gathered_blocks(blocks, first, axis=1):
+def gathered_grads(grad):
+    return lax.all_gather(grad, "wide", tiled=True)
+
+
+def gathered_blocks(blocks):
+    return [lax.all_gather(blocks, "wide")]
+
+
+def spread_chips(values):
     if has_slots():
-        return spread_slots(blocks, first)
-    return [lax.all_gather(blocks, "wide", axis=axis, tiled=True)]
-
-
-def spread_chips(values, first):
-    if has_slots():
-        over_x, over_y = flipped(values, "wide", 2), flipped(values, "wide", 4)
-        low, high = flipped(over_x[:first], "wide", 4), flipped(over_y[first:], "wide", 2)
-        return [values, over_x, over_y, low, high]
+        return over_chips(values)
     mask = 2
     while mask < lax.axis_size("wide"):
         values = jnp.concatenate([values, flipped(values, "wide", mask)])
@@ -210,13 +219,15 @@
     return above, below
 
 
-def convolve(spot, pieces, edges, kernel, source, second_shape, rows, width):
+def convolve(spot, pieces, edges, kernel, source, second_shape, earlier, rows, width):
     groups, (area, span) = len(pieces), pieces[0].shape
-    sends = [bf16_like(area, span // 2)] * (2 * groups) if has_slots() else [bf16_like(area, C)]
+    count, block = (2, span // 2) if has_slots() else (1, span)
+    layers = (2,) if earlier else ()
+    sends = [bf16_like(groups, *layers, area, block)] * count
     return local_kernel(
-        functools.partial(conv_body, groups, len(kernel), rows, width),
+        functools.partial(conv_body, groups, len(kernel), len(earlier), rows, width),
         [f32_like(area, span), second_shape] + sends,
-        [spot, *pieces, *edges, *kernel, source],
+        [spot, *pieces, *edges, *far(kernel), source, *far(earlier)],
         [pltpu.VMEM((groups, 3, (rows + 2) * width, span), jnp.bfloat16)],
         32,
         2 * 9 * area * C * span,
@@ -235,7 +246,7 @@
     return local_kernel(
         functools.partial(back_body, groups, rows, width),
         [bf16_like(area, span)] * groups,
-        [spot, grad, *edges, *kernel],
+        [spot, grad, *edges, *far(kernel)],
         [
             pltpu.VMEM((3, (rows + 2) * width, span), jnp.bfloat16),
             pltpu.VMEM((groups, area, span), jnp.bfloat16),
@@ -249,76 +260,80 @@
     return [parts[0]] + [flipped(parts[mask], "tensor", mask) for mask in range(1, len(parts))]
 
 
-def kernel_grad_body(count, width, spot, *refs):
-    pieces = refs[:count]
-    grads = refs[count : count + 10]
-    out, turned_all, grad_all = refs[-3:]
-    wide = spot[0]
-    area, span = pieces[0].shape
-    depth = count * area
+def pair_blocks_body(spot, kept, got, *outs):
+    for index, out in enumerate(outs):
+        out[0] = kept[index + 1]
+        out[1] = got[index + 1]
+
+
+def kernel_grad_body(width, layer, spot, kept, got, *refs):
+    *pairs, grads = refs[:4]
+    out, turned_all = refs[-2:]
+    area, span = kept.shape[2:]
+    depth = 8 * area
     turned_all[:, :width] = jnp.zeros((3 * span, width), jnp.bfloat16)
     turned_all[:, depth + width :] = jnp.zeros((3 * span, width), jnp.bfloat16)
-    for mask in range(count):
-        start = pl.multiple_of(lax.bitwise_xor(wide, mask) * area, area)
-        for column, values in enumerate(turned(pieces[mask][...], width)):
-            flat = jnp.transpose(values.astype(jnp.float32)).astype(jnp.bfloat16)
-            turned_all[column * span : (column + 1) * span, pl.ds(start + width, area)] = flat
-        half = grads[5 * (mask % 2) : 5 * (mask % 2) + 5]
-        if mask < 6:
-            grad_all[pl.ds(start, area), :] = half[mask // 2][...]
-        else:
-            grad_all[pl.ds(start, width), :] = half[3][...]
-            grad_all[pl.ds(start + width, area - width), :] = half[4][...]
+    pieces = [kept[0, layer], got[0, layer]]
+    pieces += [pair[core, layer] for pair in pairs for core in range(2)]
+    for mask, piece in enumerate(pieces):
+        start = pl.multiple_of(lax.bitwise_xor(spot[0], mask) * area, area)
+        for column, values in enumerate(turned(piece, width)):
+            turned_all[column * span : (column + 1) * span, pl.ds(start + width, area)] = flat_turn(
+                values
+            )
     for row in range(3):
         product = jnp.dot(
             turned_all[:, row * width : row * width + depth],
-            grad_all[...],
+            grads[...],
             preferred_element_type=jnp.float32,
         )
         for column in range(3):
             out[0, 3 * row + column] = product[column * span : (column + 1) * span, :]
 
 
-def swapped_blocks(sends):
-    if not has_slots():
-        return sends
-    return [sends[0]] + [flipped(sends[mask], "wide", mask) for mask in range(1, len(sends))]
+def swapped_blocks(spot, kept, sent):
+    got = flipped(sent, "wide", 1)
+    pairs = local_kernel(
+        pair_blocks_body, [bf16_like(2, *kept.shape[1:])] * 3, [spot, *far([kept, got])], [], 16, 0
+    )
+    return [kept, got, *pairs]
+
+
+def traded_blocks(blocks):
+    return blocks[:2] + [flipped(blocks[2 + k], "wide", 2 * k + 2) for k in range(3)]
 
 
 def kernel_grad(spot, pieces, grads, rows, width, layer, earlier):
-    count, area = len(pieces), rows * width
-    span, columns = pieces[0].shape[1], grads[0].shape[1]
-    operands = [spot, *pieces, *grads]
+    area, span = pieces[0].shape[2:]
+    columns, depth = grads.shape[1], grads.shape[0]
+    operands = [spot, *far(pieces), *far([grads])]
     specs = [in_smem] + [in_vmem] * (len(operands) - 1)
     shape = f32_like(2, 9, span, columns)
     if earlier is not None:
         operands.append(earlier)
         specs.append(pl.BlockSpec(memory_space=pl.ANY))
     return pl.pallas_call(
-        functools.partial(kernel_grad_body, count, width),
+        functools.partial(kernel_grad_body, width, layer),
         out_shape=shape,
         in_specs=specs,
         grid=(1,),
         out_specs=pl.BlockSpec((1, 9, span, columns), lambda i: (layer, 0, 0, 0)),
         scratch_shapes=[
-            pltpu.VMEM((3 * span, count * area + 2 * width), jnp.bfloat16),
-            pltpu.VMEM((count * area, columns), jnp.bfloat16),
+            pltpu.VMEM((3 * span, depth + 2 * width), jnp.bfloat16),
         ],
         input_output_aliases={} if earlier is None else {len(operands) - 1: 0},
         compiler_params=pltpu.CompilerParams(vmem_limit_bytes=24 * MIB),
         cost_estimate=pl.CostEstimate(
-            flops=2 * 9 * count * area * span * columns, bytes_accessed=4 * MIB, transcendentals=0
+            flops=2 * 9 * depth * span * columns, bytes_accessed=4 * MIB, transcendentals=0
         ),
     )(*operands)
 
 
-def kernel_grad_whole(sends, grad, rows, width):
-    natural = sends[0].reshape(1, rows, width, C)
+def kernel_grad_whole(send, grads, rows, width):
+    natural = jnp.moveaxis(send, 0, 1).reshape(1, rows, width, C)
     swapped = lax.all_to_all(natural, "wide", split_axis=3, concat_axis=1, tiled=True)
     framed = jnp.pad(swapped, ((0, 0), (1, 1), (1, 1), (0, 0)))
-    low = lax.all_gather(
-        grad.reshape(1, rows, width, grad.shape[1]), "wide", axis=1, tiled=True
-    )
+    low = grads.reshape(1, -1, width, grads.shape[1])
     return jnp.stack(
         [
             jnp.einsum(
@@ -343,6 +358,19 @@
     return jnp.concatenate([jnp.cos(angles), jnp.sin(angles)], axis=1)
 
 
+def part_totals(rows):
+    if not has_slots():
+        return [total(rows, "wide")]
+    rows = rows + flipped(rows, "wide", 1)
+    return [rows] + [flipped(rows, "wide", mask) for mask in (2, 4, 6)]
+
+
+def sum_of_parts(refs):
+    if len(refs) == 1:
+        return refs[0][...]
+    return (refs[0][...] + refs[1][...]) + (refs[2][...] + refs[3][...])
+
+
 def total(values, axis):
     mask = 1
     while mask < lax.axis_size(axis):
@@ -396,13 +424,18 @@
     return (values * lax.logistic(values)).astype(jnp.bfloat16)
 
 
-def first_norm_body(pixel_count, spot, pixels, sums, affine, out):
+def first_norm_body(pixel_count, spot, pixels, affine, *refs):
+    *parts, out, sums = refs
+    sums[...] = sum_of_parts(parts)
     center, inverse = group_scale(sums[0:1], sums[1:2], pixel_count)
     scaled = (pixels[...].astype(jnp.float32) - center) * inverse
     out[...] = silu_low(scaled * affine[0:1] + affine[1:2])
 
 
-def second_norm_body(pixel_count, spot, inner, sums, film, affine, out):
+def second_norm_body(pixel_count, spot, inner, affine, *refs):
+    *parts, out, film, sums = refs
+    summed = sum_of_parts(parts)
+    film[...], sums[...] = summed[:2], summed[2:]
     center, inverse = group_scale(*lifted_sums(sums[...], film[...], pixel_count), pixel_count)
     lifted = inner[...] * (1.0 + film[0:1]) + film[1:2]
     out[...] = silu_low((lifted - center) * inverse * affine[0:1] + affine[1:2])
@@ -431,8 +464,9 @@
     rows[5:8, :] = jnp.zeros((3, own.shape[1]), jnp.float32)
 
 
-def second_input_body(pixel_count, width, spot, back, inner, sums, film, affine, rows, *outs):
-    low, last, first, film_rows = outs
+def second_input_body(pixel_count, width, spot, back, inner, sums, film, affine, *refs):
+    *parts, low, last, first, film_rows, rows = refs
+    rows[...] = sum_of_parts(parts)
     slope, shift, gain = 1.0 + film[0:1], film[1:2], affine[0:1]
     plain_sum, square_sum = sums[0:1], sums[1:2]
     lifted_sum, lifted_square = lifted_sums(sums[...], film[...], pixel_count)
@@ -463,7 +497,9 @@
     rows[...] = stacked_rows([back * scaled, back])
 
 
-def first_input_body(pixel_count, spot, back, pixels, sums, affine, rows, middle, out):
+def first_input_body(pixel_count, spot, back, pixels, sums, affine, middle, *refs):
+    *parts, out, rows = refs
+    rows[...] = sum_of_parts(parts)
     gain = affine[0:1]
     center, inverse = group_scale(sums[0:1], sums[1:2], pixel_count)
     dotted, plain = group_means(gain * rows[0:1], gain * rows[1:2], pixel_count)
@@ -502,12 +538,33 @@
     )
 
 
-def project_body(groups, parts, spot, *refs):
-    pieces, gains = refs[:groups], refs[groups : 2 * groups]
-    own = refs[2 * groups]
-    weights = Weights(refs[2 * groups + 1 : 2 * groups + 1 + parts], spot)
-    keep_q, keep_kv, send, cross, normed, scaled, center, inverse = refs[2 * groups + 1 + parts :]
+def packed_rows(values):
+    rows = []
+    for _ in range(3):
+        rows.append(values.astype(jnp.bfloat16).astype(jnp.float32))
+        values = values - rows[-1]
+    rows.append(jnp.zeros((10, values.shape[1]), jnp.float32))
+    return jnp.concatenate(rows, axis=0).astype(jnp.bfloat16)
+
+
+def unpacked_rows(packed, area):
+    rows = packed[area:, :].astype(jnp.float32)
+    return rows[0:1] + rows[2:3] + rows[4:5], rows[1:2] + rows[3:4] + rows[5:6]
+
+
+def prepare_body(spot, pixels, cotangent, terms, pack, sums):
+    area = cotangent.shape[0]
+    pack[:area] = cotangent[...].astype(jnp.bfloat16)
+    pack[area:] = packed_rows(terms[...])
+    sums[...] = channel_sums(pixels[...].astype(jnp.float32))
+
+
+def project_body(groups, spot, *refs):
+    pieces, packs = refs[:groups], refs[groups : 2 * groups]
+    own, maps, keep_q, keep_kv, send, cross, normed, scaled, center, inverse = refs[2 * groups :]
+    weights = Weights([maps], spot, groups)
     odd = lax.rem(spot[0], 2) == 1
+    area = own.shape[0]
     token_sum = token_square = 0.0
     for piece in pieces:
         values = piece[...].astype(jnp.float32)
@@ -515,18 +572,20 @@
         token_square += jnp.sum(values * values, axis=1, keepdims=True)
     mean = token_sum / C
     scale = lax.rsqrt(token_square / C - mean * mean + 1e-05)
+    lows = []
     for mask in range(groups):
+        gain, bias = unpacked_rows(packs[mask], area)
         values = (pieces[mask][...].astype(jnp.float32) - mean) * scale
-        values = (values * gains[mask][0:1] + gains[mask][1:2]).astype(jnp.bfloat16)
-        normed[lax.bitwise_xor(spot[1], mask)] = weights.ordered(values)
+        lows.append((values * gain + bias).astype(jnp.bfloat16))
+        normed[lax.bitwise_xor(spot[1], mask)] = lows[-1]
     center[...] = mean
     inverse[...] = scale
     scaled[...] = (own[...] - mean) * scale
     projected = []
     for position in range(4):
         total_sum = 0.0
-        for chunk in range(groups):
-            total_sum += dot(normed[weights.block(chunk)], weights.tap(chunk, position))
+        for mask in range(groups):
+            total_sum += dot(lows[mask], weights.tap(mask, position))
         projected.append(total_sum.astype(jnp.bfloat16))
     cross[...] = projected[3]
     chosen = [head_choice(values, odd) for values in projected[:3]]
@@ -535,17 +594,15 @@
     send[...] = jnp.concatenate([pair[1] for pair in chosen], axis=1)
 
 
-def out_grad_body(groups, parts, spot, *refs):
-    pieces = refs[:groups]
-    weights = Weights(refs[groups : groups + parts], spot, 1)
-    keep, send, cross, frame = refs[groups + parts :]
-    for mask in range(groups):
-        frame[lax.bitwise_xor(spot[1], mask)] = weights.ordered(pieces[mask][...])
+def out_grad_body(groups, spot, *refs):
+    packs = refs[:groups]
+    maps, keep, send, cross = refs[groups:]
+    weights = Weights([maps], spot, groups)
     sums = []
-    for position in range(2):
+    for position in (4, 5):
         total_sum = 0.0
-        for chunk in range(groups):
-            total_sum += dot_last(frame[weights.block(chunk)], weights.tap(chunk, position))
+        for mask in range(groups):
+            total_sum += dot(packs[mask][: cross.shape[0]], weights.tap(mask, position))
         sums.append(total_sum.astype(jnp.bfloat16))
     kept, sent = head_choice(sums[0], lax.rem(spot[0], 2) == 1)
     keep[...] = kept
@@ -553,15 +610,17 @@
     cross[...] = sums[1]
 
 
-def mix_body(groups, parts, spot, kept, received, crossed, *refs):
-    weights = Weights(refs[:parts], spot, 1)
-    outs, held = refs[parts:-1], refs[-1]
-    attended = heads_joined(kept[...], received[...], lax.rem(spot[0], 2) == 1)
-    for chunk in range(groups):
-        total_sum = dot(attended, weights.tap(chunk, 0)) + dot(crossed[...], weights.tap(chunk, 1))
-        held[weights.block(chunk)] = weights.ordered(total_sum).astype(jnp.bfloat16)
+def mix_body(groups, spot, kept, received, crossed, maps, out):
+    weights = Weights([maps], spot, groups)
+    area = kept.shape[0]
+    attended = heads_joined(
+        kept[...], received[:, 3 * HEAD_DIM :], lax.rem(spot[0], 2) == 1
+    )
     for mask in range(groups):
-        outs[mask][...] = held[lax.bitwise_xor(spot[1], mask)]
+        total_sum = dot_last(attended, weights.tap(mask, 4))
+        total_sum += dot_last(crossed[...], weights.tap(mask, 5))
+        start = pl.multiple_of(weights.block(mask) * area, area)
+        out[pl.ds(start, area), :] = total_sum.astype(jnp.bfloat16)
 
 
 def over_rows(refs, step, state):
@@ -637,7 +696,7 @@
     send[...] = result[queries // 2 :]
 
 
-def key_grad_body(count, spot, pair, *refs):
+def key_grad_body(count, spot, pair, sent_query, sent_out, *refs):
     queries, stats = refs[:count], refs[count:-2]
     keep, send = refs[-2:]
     keys, values = pair[:, :HEAD_DIM], pair[:, HEAD_DIM:]
@@ -646,11 +705,8 @@
     def step(state, block, index, start):
         grad_keys, grad_values = state
         rows = block.shape[0]
-        if index < len(stats):
-            lanes = pl.ds(start if isinstance(start, int) else pl.multiple_of(start, 512), rows)
-            log_sum, delta = stats[index][0:1, lanes], stats[index][1:2, lanes]
-        else:
-            log_sum, delta = stats[-1][0:1, rows:], stats[-1][1:2, rows:]
+        lanes = pl.ds(start if isinstance(start, int) else pl.multiple_of(start, 512), rows)
+        log_sum, delta = stats[index][0:1, lanes], stats[index][1:2, lanes]
         query, grad = block[:, :HEAD_DIM], block[:, HEAD_DIM:]
         probs = jnp.exp(dot_last(keys, query) * score_scale - log_sum)
         grad_values += dot(probs.astype(jnp.bfloat16), grad)
@@ -662,7 +718,9 @@
     grad_keys, grad_values = over_rows(queries, step, (zero, zero))
     both = jnp.concatenate([grad_keys * score_scale, grad_values], axis=1).astype(jnp.bfloat16)
     keep[...] = both[: depth // 2]
-    send[...] = both[depth // 2 :]
+    send[:, : 2 * HEAD_DIM] = both[depth // 2 :]
+    send[:, 2 * HEAD_DIM : 3 * HEAD_DIM] = sent_query[...]
+    send[:, 3 * HEAD_DIM :] = sent_out[...]
 
 
 def cross_body(spot, query, text, grad, crossed, grad_query, text_grad):
@@ -683,75 +741,101 @@
         text_grad[1, :, lanes] = dot_first(low, back).astype(jnp.bfloat16)
 
 
-def joined_grads(spot, kept_query, got_query, kept_pair, got_pair, cross):
+def joined_grads(spot, kept_query, kept_pair, got, cross):
     odd = lax.rem(spot[0], 2) == 1
+    parts = [got[:, i * HEAD_DIM : (i + 1) * HEAD_DIM] for i in range(3)]
     return [
-        heads_joined(kept_query[...], got_query[...], odd),
-        heads_joined(kept_pair[:, :HEAD_DIM], got_pair[:, :HEAD_DIM], odd),
-        heads_joined(kept_pair[:, HEAD_DIM:], got_pair[:, HEAD_DIM:], odd),
+        heads_joined(kept_query[...], parts[2], odd),
+        heads_joined(kept_pair[:, :HEAD_DIM], parts[0], odd),
+        heads_joined(kept_pair[:, HEAD_DIM:], parts[1], odd),
         cross[...],
     ]
 
 
-def project_back_body(groups, parts, spot, kq, gq, kp, gp, cross, center, inverse, *refs):
-    pieces, gains = refs[:groups], refs[groups : 2 * groups]
-    weights = Weights(refs[2 * groups : 2 * groups + parts], spot)
-    *outs, sums, held = refs[2 * groups + parts :]
-    grads = joined_grads(spot, kq, gq, kp, gp, cross)
-    for chunk in range(groups):
-        total_sum = 0.0
+def project_back_body(groups, spot, kq, kp, got, cross, center, inverse, maps, *refs):
+    pieces, packs = refs[:groups], refs[groups : 2 * groups]
+    outs = refs[2 * groups :]
+    weights = Weights([maps], spot, groups)
+    grads = joined_grads(spot, kq, kp, got, cross)
+    area = cross.shape[0]
+    plain = dotted = 0.0
+    for mask in range(groups):
+        part = 0.0
         for position in range(4):
-            total_sum += dot_last(grads[position], weights.tap(chunk, position))
-        held[weights.block(chunk)] = weights.ordered(total_sum)
-    plain = dotted = 0.0
-    ones = jnp.ones((8, held.shape[2]), jnp.float32)
-    for mask in range(groups):
-        part = held[lax.bitwise_xor(spot[1], mask)]
-        outs[mask][...] = part.astype(jnp.bfloat16)
-        eased = part * gains[mask][0:1]
+            part += dot_last(grads[position], weights.tap(mask, position))
+        outs[mask][:area] = part.astype(jnp.bfloat16)
+        eased = part * unpacked_rows(packs[mask], part.shape[0])[0]
         unit = (pieces[mask][...].astype(jnp.float32) - center[...]) * inverse[...]
         plain += eased
         dotted += eased * unit
-    for row, values in enumerate((plain, dotted)):
-        sums[row : row + 1, :] = lax.dot_general(
+    ones = jnp.ones((8, plain.shape[1]), jnp.float32)
+    sums = [
+        lax.dot_general(
             ones,
             values,
             (((1,), (1,)), ((), ())),
             precision=highest,
             preferred_element_type=jnp.float32,
         )[0:1]
-
-
-def weight_grad_body(groups, paired, spot, kq, gq, kp, gp, cross, kept, received, crossed, normed, *refs):
-    cotangents, out = refs[:groups], refs[groups]
+        for values in (plain, dotted)
+    ]
+    packed = packed_rows(jnp.concatenate(sums, axis=0))
+    for out in outs:
+        out[area:] = packed
+
+
+def weight_grad_body(groups, spot, kq, kp, got, cross, kept, crossed, normed, *refs):
+    packs, outs, frame = refs[:groups], refs[groups:-1], refs[-1]
     odd = lax.rem(spot[0], 2) == 1
     area, span = cross.shape
-    right = jnp.concatenate(joined_grads(spot, kq, gq, kp, gp, cross), axis=1)
-    columns = right.shape[1]
+    right = jnp.concatenate(joined_grads(spot, kq, kp, got, cross), axis=1)
     out_right = jnp.concatenate(
-        [heads_joined(kept[...], received[...], odd), crossed[...]], axis=1
-    )
+        [heads_joined(kept[...], got[:, 3 * HEAD_DIM :], odd), crossed[...]], axis=1
+    )
+    for mask in range(groups):
+        frame[lax.bitwise_xor(spot[1], mask)] = packs[mask][:area]
     for chunk in range(groups):
-        rows = slice(chunk * span, (chunk + 1) * span)
-        values = normed[chunk]
-        left = halves_swapped(values, odd) if paired else values
-        out[rows, :columns] = dot_first(left, right).astype(jnp.bfloat16)
-    for mask in range(groups):
-        start = pl.multiple_of(lax.bitwise_xor(spot[1], mask) * span, span)
-        out[pl.ds(start, span), columns:] = dot_first(cotangents[mask][...], out_right).astype(
-            jnp.bfloat16
-        )
+        near = lax.bitwise_xor(lax.div(spot[0], 2), chunk) if len(outs) == 2 else chunk
+        product = jnp.concatenate(
+            [dot_first(normed[near], right), dot_first(frame[near], out_right)], axis=1
+        ).astype(jnp.bfloat16)
+        if len(outs) == 2:
+            low, high = product[: span // 2], product[span // 2 :]
+            outs[0][chunk] = jnp.where(odd, high, low)
+            outs[1][chunk] = jnp.where(odd, low, high)
+        else:
+            outs[0][chunk * span : (chunk + 1) * span, :] = product
+
+
+def weight_sum_body(spot, kept, got, own, *outs):
+    for index, out in enumerate((own,) + outs):
+        both = kept[index].astype(jnp.float32) + got[index].astype(jnp.float32)
+        out[...] = both.astype(out.dtype)
+
+
+def weight_out_body(spot, own, *refs):
+    *parts, in_grad, self_grad, cross_grad = refs
+    summed = own[...] + parts_sum(parts)
+    span = in_grad.shape[2]
+    for position in range(4):
+        in_grad[position] = summed[:, position * span : (position + 1) * span]
+    self_grad[...] = jnp.transpose(summed[:, 4 * span : 5 * span])
+    cross_grad[...] = jnp.transpose(summed[:, 5 * span :])
 
 
 def norm_back_body(groups, width, spot, *refs):
-    sums, scaled, inverse, cotangent, gain, middle, low, last, first, terms = refs[groups:]
-    grad = parts_sum(refs[:groups])
-    area = grad.shape[0]
+    scaled, inverse, cotangent, gain, middle, low, last, first, terms = refs[groups:]
+    area = scaled.shape[0]
+    grad = plain = dotted = 0.0
+    for ref in refs[:groups]:
+        grad += ref[:area].astype(jnp.float32)
+        sums = unpacked_rows(ref, area)
+        plain, dotted = plain + sums[0], dotted + sums[1]
     same = lax.broadcasted_iota(jnp.int32, (area, area), 0) == lax.broadcasted_iota(
         jnp.int32, (area, area), 1
     )
-    plain = jnp.sum(jnp.where(same, sums[0:1, :], 0.0), axis=1, keepdims=True) / C
-    dotted = jnp.sum(jnp.where(same, sums[1:2, :], 0.0), axis=1, keepdims=True) / C
+    plain = jnp.sum(jnp.where(same, plain, 0.0), axis=1, keepdims=True) / C
+    dotted = jnp.sum(jnp.where(same, dotted, 0.0), axis=1, keepdims=True) / C
     unit = scaled[...]
     terms[0:1, :] = jnp.sum(grad * unit, axis=0, keepdims=True)
     terms[1:2, :] = jnp.sum(grad, axis=0, keepdims=True)
@@ -795,10 +879,24 @@
     flat_cotangent = cotangent.reshape(flat)
     affine = [jnp.stack([group_gain[layer], group_bias[layer]]) for layer in range(2)]
 
-    first_sums = total(channel_sums(own_pixels.astype(jnp.float32)), "wide")
-    norm_gains = channel_pieces(jnp.stack([layer_gain, layer_bias]))
-    grad_pieces = channel_pieces(flat_cotangent.astype(jnp.bfloat16))
-    kernel_one = gathered_blocks(after(conv_weights[0], first_sums), 5)
+    pack, sums = local_kernel(
+        prepare_body,
+        [bf16_like(token_count + 16, width_own), f32_like(2, width_own)],
+        [spot, own_pixels, flat_cotangent, jnp.stack([layer_gain, layer_bias])],
+        [],
+        8,
+        0,
+    )
+    first_parts = part_totals(sums)
+    if has_slots():
+        kernel_one = spread_slots(after(conv_weights[0], first_parts))
+    else:
+        kernel_one = gathered_blocks(conv_weights[0])
+    kernel_two = gathered_blocks(conv_weights[1])
+    maps = jnp.concatenate(
+        [attn_in, jnp.transpose(jnp.stack([out_self, out_cross]), (0, 2, 1))], axis=0
+    )
+    maps = gathered_blocks(maps)[0]
 
     features = sinusoid(timestep).astype(jnp.bfloat16)
     present = jnp.arange(TEXT)[None, :] < text_length[:, None]
@@ -815,48 +913,63 @@
     film_term = jnp.einsum(
         "mk,ksc->msc", own_features, film_time, preferred_element_type=jnp.float32
     ) + jnp.einsum("mk,ksc->msc", own_pooled, film_text, preferred_element_type=jnp.float32)
-    film = total(film_term[0], "wide")
     text_term = jnp.einsum("mtx,pxd->pmtd", own_text, text_kv, preferred_element_type=jnp.float32)
     text_term = text_term.astype(jnp.bfloat16).reshape(2, TEXT, width_own)
 
-    (first,) = local_kernel(
+    row_pair = f32_like(2, width_own)
+    first, first_sums = local_kernel(
         functools.partial(first_norm_body, pixel_count),
-        [bf16_like(*flat)],
-        [spot, own_pixels, first_sums, affine[0]],
+        [bf16_like(*flat), row_pair],
+        [spot, own_pixels, affine[0], *first_parts],
         [],
         8,
         0,
     )
     pieces = channel_pieces(first)
+    packs = channel_pieces(after(pack, pieces))
     edges = piece_edges(pieces, col_count)
+    pieces[0] = after(pieces[0], film_term)
     inner, sums, *first_sends = convolve(
-        spot, pieces, edges, kernel_one, own_pixels, f32_like(2, width_own), row_count, col_count
-    )
-    inner_sums = total(sums, "wide")
-    kernel_two = gathered_blocks(after(conv_weights[1], inner_sums), 5)
-    (second,) = local_kernel(
+        spot,
+        pieces,
+        edges,
+        kernel_one,
+        own_pixels,
+        f32_like(2, width_own),
+        [],
+        row_count,
+        col_count,
+    )
+    inner_parts = part_totals(jnp.concatenate([film_term[0], sums]))
+    second, film, inner_sums = local_kernel(
         functools.partial(second_norm_body, pixel_count),
-        [bf16_like(*flat)],
-        [spot, inner, inner_sums, film, affine[1]],
+        [bf16_like(*flat), row_pair, row_pair],
+        [spot, inner, affine[1], *inner_parts],
         [],
         8,
         0,
     )
     pieces = channel_pieces(second)
     edges = piece_edges(pieces, col_count)
-    in_maps = gathered_blocks(after(attn_in, *kernel_two[:5], *edges), 2)
-    text_proj = total(after(text_term, *in_maps[:5]), "wide")
-    out_maps = gathered_blocks(after(jnp.stack([out_self, out_cross]), *in_maps[:5]), 1, 2)
-    middle, middle_low, *second_sends = convolve(
-        spot, pieces, edges, kernel_two, own_pixels, bf16_like(*flat), row_count, col_count
+    pieces[0] = after(pieces[0], packs)
+    middle, middle_low, *both_sends = convolve(
+        spot,
+        pieces,
+        edges,
+        kernel_two,
+        own_pixels,
+        bf16_like(*flat),
+        first_sends,
+        row_count,
+        col_count,
     )
 
     middle_pieces = channel_pieces(middle_low)
-    parts = len(in_maps)
+    text_proj = total(after(text_term, middle_low), "wide")
     column = f32_like(token_count, 1)
     square = 2 * token_count * C * width_own
     kept_query, kept_pair, sent, cross_query, normed, scaled, center, inverse = local_kernel(
-        functools.partial(project_body, groups, parts),
+        functools.partial(project_body, groups),
         [
             bf16_like(*half),
             bf16_like(*flat),
@@ -867,23 +980,23 @@
             column,
             column,
         ],
-        [spot, *middle_pieces, *norm_gains, middle, *in_maps],
+        [spot, *middle_pieces, *far(packs), middle, *far([maps])],
         [],
         24,
         4 * square,
     )
     got = flipped(sent, "wide", 1)
     kept_grad, sent_grad, grad_crossed = local_kernel(
-        functools.partial(out_grad_body, groups, len(out_maps)),
+        functools.partial(out_grad_body, groups),
         [bf16_like(*half), bf16_like(*half), bf16_like(*flat)],
-        [spot, *grad_pieces, *out_maps],
-        [pltpu.VMEM((groups, *flat), jnp.bfloat16)],
+        [spot, *far(packs), *far([maps])],
+        [],
         16,
         2 * square,
     )
     got_grad = flipped(sent_grad, "wide", 1)
     pair = jnp.concatenate([kept_pair, got[:, HEAD_DIM:]])
-    pairs = spread_chips(pair, token_count)
+    pairs = spread_chips(pair)
     query_grad = jnp.concatenate(
         [
             jnp.concatenate([kept_query, got[:, :HEAD_DIM]]),
@@ -891,7 +1004,7 @@
         ],
         axis=1,
     )
-    query_grads = spread_chips(after(query_grad, *pairs), token_count)
+    query_grads = spread_chips(after(query_grad, *pairs))
     scores = 2 * (2 * token_count) * HEAD_DIM * pixel_count
     kept_out, sent_out, stats = local_kernel(
         functools.partial(attend_body, len(pairs)),
@@ -902,7 +1015,6 @@
         2 * scores,
     )
     all_stats = spread_stats(stats)
-    got_out = flipped(sent_out, "wide", 1)
     crossed, grad_cross_query, text_grads = local_kernel(
         cross_body,
         [bf16_like(*flat), bf16_like(*flat), bf16_like(2, TEXT, width_own)],
@@ -919,51 +1031,80 @@
         24,
         3 * scores,
     )
-    got_dq = flipped(sent_dq, "wide", 1)
-    kept_dk, sent_dk = local_kernel(
+    kept_dk, sent_all = local_kernel(
         functools.partial(key_grad_body, len(query_grads)),
-        [bf16_like(*flat), bf16_like(*flat)],
-        [spot, pair, *query_grads, *all_stats],
+        [bf16_like(*flat), bf16_like(token_count, 4 * HEAD_DIM)],
+        [spot, pair, sent_dq, sent_out, *query_grads, *all_stats],
         [],
         24,
         4 * scores,
     )
-    got_dk = flipped(sent_dk, "wide", 1)
+    got_all = flipped(sent_all, "wide", 1)
+    if has_slots():
+        both_blocks = swapped_blocks(spot, after(both_sends[0], kept_pair), both_sends[1])
+        kept_dk = after(kept_dk, both_blocks)
+        both_blocks = traded_blocks(both_blocks)
     text_all = total(after(text_grads, *all_stats), "wide").astype(jnp.float32)
-    first_blocks = swapped_blocks([after(send, text_all) for send in first_sends])
-    second_blocks = swapped_blocks([after(send, text_all) for send in second_sends])
-    mixed = local_kernel(
-        functools.partial(mix_body, groups, len(out_maps)),
-        [bf16_like(*flat)] * groups,
-        [spot, kept_out, got_out, crossed, *out_maps],
-        [pltpu.VMEM((groups, *flat), jnp.bfloat16)],
+    (mixed,) = local_kernel(
+        functools.partial(mix_body, groups),
+        [bf16_like(groups * token_count, width_own)],
+        [spot, kept_out, got_all, crossed, *far([maps])],
+        [],
         16,
         2 * square,
     )
-    mixed = sent_parts(mixed)
-    result = middle
-    for part in mixed:
-        result = result + part.astype(jnp.float32)
-    projected_grads = [after(kept_dq, *mixed), got_dq, kept_dk, got_dk, grad_cross_query]
-    *norm_parts, sums = local_kernel(
-        functools.partial(project_back_body, groups, parts),
-        [bf16_like(*flat)] * groups + [f32_like(2, token_count)],
-        [spot, *projected_grads, center, inverse, *middle_pieces, *norm_gains, *in_maps],
-        [pltpu.VMEM((groups, *flat), jnp.float32)],
+    mixed = lax.psum_scatter(mixed, "tensor", scatter_dimension=0, tiled=True)
+    result = middle + mixed.astype(jnp.float32)
+    projected_grads = [kept_dq, kept_dk, got_all, grad_cross_query]
+    norm_parts = local_kernel(
+        functools.partial(project_back_body, groups),
+        [bf16_like(token_count + 16, width_own)] * groups,
+        [spot, *projected_grads, center, inverse, *far([maps]), *far(middle_pieces), *far(packs)],
+        [],
         24,
         4 * square,
     )
     norm_parts = sent_parts(norm_parts)
-    sums = total(sums, "tensor")
-    (weight_parts,) = local_kernel(
-        functools.partial(weight_grad_body, groups, has_slots()),
-        [bf16_like(C, 6 * width_own)],
-        [spot, *projected_grads, kept_out, got_out, crossed, normed, *grad_pieces],
-        [],
+    columns = 6 * width_own
+    width_block = C // lax.axis_size("wide")
+    if has_slots():
+        weight_shapes = [bf16_like(groups, width_block, columns)] * 2
+    else:
+        weight_shapes = [bf16_like(C, columns)]
+    weight_parts = local_kernel(
+        functools.partial(weight_grad_body, groups),
+        weight_shapes,
+        [spot, *projected_grads, kept_out, crossed, *far([normed]), *far(packs)],
+        [pltpu.VMEM((groups, *flat), jnp.bfloat16)],
         24,
         6 * square,
     )
-    weight_sums = lax.psum_scatter(weight_parts, "wide", scatter_dimension=0, tiled=True)
+    if has_slots():
+        weight_own, *weight_sends = local_kernel(
+            weight_sum_body,
+            [f32_like(width_block, columns)] + [bf16_like(width_block, columns)] * 3,
+            [spot, weight_parts[0], flipped(weight_parts[1], "wide", 1)],
+            [],
+            24,
+            0,
+        )
+        norm_parts[0] = after(norm_parts[0], weight_sends)
+        weight_got = [flipped(weight_sends[k], "wide", 2 * k + 2) for k in range(3)]
+        attn_in_grad, self_grad, cross_grad = local_kernel(
+            weight_out_body,
+            [f32_like(4, width_block, width_own)] + [f32_like(width_own, width_block)] * 2,
+            [spot, weight_own, *weight_got],
+            [],
+            16,
+            0,
+        )
+    else:
+        weight_sums = lax.psum_scatter(weight_parts[0], "wide", scatter_dimension=0, tiled=True)
+        weight_sums = weight_sums.astype(jnp.float32)
+        in_count = 4 * width_own
+        attn_in_grad = jnp.moveaxis(weight_sums[:, :in_count].reshape(-1, 4, width_own), 1, 0)
+        self_grad = weight_sums[:, in_count : in_count + width_own].T
+        cross_grad = weight_sums[:, in_count + width_own :].T
     grad_middle, grad_two, last, head, terms = local_kernel(
         functools.partial(norm_back_body, groups, col_count),
         [
@@ -976,7 +1117,6 @@
         [
             spot,
             *norm_parts,
-            after(sums, weight_parts, first_blocks, second_blocks),
             scaled,
             inverse,
             flat_cotangent,
@@ -988,10 +1128,10 @@
     )
 
     edges = edge_rows(last, head)
-    grads_two = gathered_grads(after(grad_two, *edges), col_count)
-    back_parts = sent_parts(
-        convolve_back(spot, grad_two, edges, kernel_two, row_count, col_count)
-    )
+    grads_two = gathered_grads(grad_two)
+    back_parts = convolve_back(spot, grad_two, edges, kernel_two, row_count, col_count)
+    back_parts = sent_parts(back_parts)
+    back_parts[0] = after(back_parts[0], text_all, attn_in_grad)
     back, rows = local_kernel(
         functools.partial(second_back_body, groups, pixel_count),
         [f32_like(*flat), f32_like(8, width_own)],
@@ -1000,23 +1140,19 @@
         16,
         0,
     )
-    second_rows = total(after(rows, *grads_two), "wide")
-    grad_one, last, head, film_rows = local_kernel(
+    grad_one, last, head, film_rows, second_rows = local_kernel(
         functools.partial(second_input_body, pixel_count, col_count),
-        [bf16_like(*flat), bf16_like(*edge), bf16_like(*edge), f32_like(2, width_own)],
-        [spot, back, inner, inner_sums, film, affine[1], second_rows],
+        [bf16_like(*flat), bf16_like(*edge), bf16_like(*edge), row_pair, f32_like(8, width_own)],
+        [spot, back, inner, inner_sums, film, affine[1], *part_totals(rows)],
         [],
         16,
         0,
     )
     edges = edge_rows(last, head)
-    grads_one = gathered_grads(after(grad_one, *edges), col_count)
+    grads_one = gathered_grads(grad_one)
     conv_grad = None
     if has_slots():
-        conv_grad = kernel_grad(
-            spot, second_blocks, grads_two, row_count, col_count, 1, conv_grad
-        )
-        second_rows = after(second_rows, conv_grad)
+        conv_grad = kernel_grad(spot, both_blocks, grads_two, row_count, col_count, 1, conv_grad)
     time_grad = own_features.astype(jnp.float32)[0][:, None, None] * film_rows[None]
     text_grad = own_pooled.astype(jnp.float32)[0][:, None, None] * film_rows[None]
     kv_grad = jnp.einsum(
@@ -1025,6 +1161,9 @@
     back_parts = sent_parts(
         convolve_back(spot, grad_one, edges, kernel_one, row_count, col_count)
     )
+    back_parts[0], conv_grad, time_grad, text_grad, kv_grad, result = lax.optimization_barrier(
+        (back_parts[0], conv_grad, time_grad, text_grad, kv_grad, result)
+    )
     back, rows = local_kernel(
         functools.partial(first_back_body, groups, pixel_count),
         [f32_like(*flat), f32_like(2, width_own)],
@@ -1033,29 +1172,25 @@
         16,
         0,
     )
-    first_rows = total(rows, "wide")
+    row_parts = part_totals(rows)
     if has_slots():
-        conv_grad = kernel_grad(
-            spot, first_blocks, grads_one, row_count, col_count, 0, conv_grad
-        )
+        conv_grad = kernel_grad(spot, both_blocks, grads_one, row_count, col_count, 0, conv_grad)
     else:
         conv_grad = jnp.stack(
             [
-                kernel_grad_whole(first_sends, grad_one, row_count, col_count),
-                kernel_grad_whole(second_sends, grad_two, row_count, col_count),
+                kernel_grad_whole(both_sends[0][:, 0], grads_one, row_count, col_count),
+                kernel_grad_whole(both_sends[0][:, 1], grads_two, row_count, col_count),
             ]
         )
-    (pixels_grad,) = local_kernel(
+    back, conv_grad = lax.optimization_barrier((back, conv_grad))
+    pixels_grad, first_rows = local_kernel(
         functools.partial(first_input_body, pixel_count),
-        [f32_like(*flat)],
-        [spot, back, own_pixels, first_sums, affine[0], first_rows, grad_middle],
+        [f32_like(*flat), row_pair],
+        [spot, back, own_pixels, first_sums, affine[0], grad_middle, *row_parts],
         [],
         16,
         0,
     )
-    weight_sums = weight_sums.astype(jnp.float32)
-    in_count = 4 * width_own
-    attn_in_grad = jnp.moveaxis(weight_sums[:, :in_count].reshape(-1, 4, width_own), 1, 0)
     return (
         result.reshape(own_shape),
         pixels_grad.reshape(own_shape),
@@ -1068,8 +1203,8 @@
         second_rows[4],
         attn_in_grad,
         kv_grad,
-        weight_sums[:, in_count : in_count + width_own].T,
-        weight_sums[:, in_count + width_own :].T,
+        self_grad,
+        cross_grad,
     )
 
 

time: 400 us -> 349 us (0.87); the launches traced: 394 us -> 348 us
  local copies, waits for them, and re-layouts: 57.4 us -> 18.3 us
  starting transfers between devices: 140 us -> 109 us
  Pallas kernels: 46 us -> 67.1 us
  waiting for transfers between devices: 117 us -> 124 us
    ppermute x134 -> x67, starting transfers between devices: 129 us -> 95.5 us  [flipped(): return lax.ppermute(values, axis, [(i, i ^ mask) for i in range(count)])]
    unnamed x401 -> x141, local copies, waits for them, and re-layouts: 48.7 us -> 15.4 us
    pallas_call x20 -> x24, Pallas kernels: 38.9 us -> 57.6 us  [local_kernel(): pl.pallas_call(body, grid=(1,), out_shape=outs, in_specs=[in_smem] + [in_...]
    ppermute x0 -> x3, waiting for transfers between devices: none -> 15.9 us  [over_chips(): return [values, over_x, over_y, lax.ppermute(relayed, 'wide', far_pairs)]]
    ppermute x134 -> x67, waiting for transfers between devices: 111 us -> 103 us  [flipped(): return lax.ppermute(values, axis, [(i, i ^ mask) for i in range(count)])]
  transfers between devices with their start and end apart: 143 -> 83, of which waited for: 43 -> 41; matrix products, arithmetic and copies ran while one was open for 6% -> 4% of each run, Pallas kernels for 10% -> 17%
where the time goes in v1:
time: 349 us; the launch traced here: 348 us
  waiting for transfers between devices  124 us (36%)
  starting transfers between devices  109 us (31%)
  Pallas kernels  67.1 us (19%)
  local copies, waits for them, and re-layouts  18.3 us (5%)
  between operations  16.2 us (5%)
  other arithmetic  10.5 us (3%)
    ppermute x67, waiting for transfers between devices, flipped(): return lax.ppermute(values, axis, [(i, i ^ mask) for i in range(count)])  103 us
    ppermute x67, starting transfers between devices, flipped(): return lax.ppermute(values, axis, [(i, i ^ mask) for i in range(count)])  95.5 us
    pallas_call x24, Pallas kernels, local_kernel(): pl.pallas_call(body, grid=(1,), out_shape=outs, in_specs=[in_smem] + [in_...  57.6 us
    ppermute x3, waiting for transfers between devices, over_chips(): return [values, over_x, over_y, lax.ppermute(relayed, 'wide', far_pairs)]  15.9 us
    unnamed x141, local copies, waits for them, and re-layouts  15.4 us
    pallas_call x2, Pallas kernels, kernel_grad(): pl.pallas_call(functools.partial(kernel_grad_body, width, layer), out_sha...  9.53 us
  transfers between devices with their start and end apart: 83, of which 41 were waited for; matrix products, arithmetic and copies ran while one was open for 4% of the time, Pallas kernels for 17%

profile of v1, /device:TPU:0, one launch (start us, length us, event | category | flops | bytes accessed | tf_op | source)
XLA Modules:
  0.0 348.4 jit_solution(13666735399706178832)
XLA Ops:
  13.6 3.7 %collective-permute-start.3 = (f32[2,256]{1,0:T(2,128)S(1)}, f32[2,256]{1,0:T(2,128)S(1)}, u32[]{:S(2)}, u32[]{:S(2)}) collective-permute-start(f32[2,256]{1,0:T(2,128)S(1)} %add.46.refs_0_), channel_id=1, source_target_pairs={{0,24},{4,28},{8,16},{12,20},{16,8},{20,12},{24,0},{28,4},{1,25},{... | collective-permute-start | bytes 6152 | tf_op jit(solution)/shard_map/ppermute | solution.py:157
  25.0 3.7 %collective-permute-start.6 = (bf16[256,256]{1,0:T(8,128)(2,1)S(1)}, bf16[256,256]{1,0:T(8,128)(2,1)S(1)}, u32[]{:S(2)}, u32[]{:S(2)}) collective-permute-start(bf16[256,256]{1,0:T(8,128)(2,1)S(1)} %get-tuple-element.108.refs_0_), channel_id=1, source_target_pairs={{0,3},{1,2},{2,1},{3,0},{4,7},{5,6},{6,5},{7,4},{8,11},{9,10},{10,... | collective-permute-start | bytes 393224 | tf_op jit(solution)/shard_map/ppermute | solution.py:157
  29.4 3.4 collective-permute-done.6.refs_3_
  32.8 8.8 %collective-permute-done.10.refs_8_.refs_2_ = bf16[9,128,256]{2,1,0:T(8,128)(2,1)} collective-permute-done((bf16[9,128,256]{2,1,0:T(8,128)(2,1)S(1)}, bf16[9,128,256]{2,1,0:T(8,128)(2,1)}, u32[]{:S(2)}, u32[]{:S(2)}) %collective-permute-start.10) | collective-permute-done | bytes 589856 | tf_op jit(solution)/shard_map/ppermute | solution.py:157
  48.9 14.4 %collective-permute-done.11.refs_9_.refs_3_ = bf16[9,128,256]{2,1,0:T(8,128)(2,1)} collective-permute-done((bf16[9,128,256]{2,1,0:T(8,128)(2,1)}, bf16[9,128,256]{2,1,0:T(8,128)(2,1)}, u32[]{:S(2)}, u32[]{:S(2)}) %collective-permute-start.11) | collective-permute-done | bytes 589856 | tf_op jit(solution)/shard_map/ppermute | solution.py:165
  69.4 4.5 %shard_map.257 = (f32[256,256]{1,0:T(8,128)S(1)}, f32[2,256]{1,0:T(2,128)S(1)}, bf16[4,256,128]{2,1,0:T(8,128)(2,1)S(1)}, bf16[4,256,128]{2,1,0:T(8,128)(2,1)S(1)}) custom-call(s32[3]{0:T(128)S(1)} %pad_add_fusion.spot, bf16[256,256]{1,0:T(8,128)(2,1)S(1)} %get-tuple-element.108.refs_0_, bf16[256,256]{1,0:T(8,128)(2,1)S(1)} %collective-permute-done.4.refs_1_, ...), custom_call_target="tpu_custom_call" | custom-call | flops 1207959552 | bytes 6686732 | tf_op jit(solution)/shard_map/pallas_call | solution.py:24
  73.9 5.2 %collective-permute-start.16 = (f32[4,256]{1,0:T(4,128)S(1)}, f32[4,256]{1,0:T(4,128)S(1)}, u32[]{:S(2)}, u32[]{:S(2)}) collective-permute-start(f32[4,256]{1,0:T(4,128)S(1)} %pad_maximum_fusion.6), channel_id=1, source_target_pairs={{0,4},{4,0},{8,12},{12,8},{16,20},{20,16},{24,28},{28,24},{1,5},{5... | collective-permute-start | bytes 12296 | tf_op jit(solution)/shard_map/ppermute | solution.py:157
  88.4 3.4 collective-permute-start.25
  92.9 3.9 %collective-permute-done.25.refs_3_ = bf16[256,256]{1,0:T(8,128)(2,1)S(1)} collective-permute-done((bf16[256,256]{1,0:T(8,128)(2,1)S(1)}, bf16[256,256]{1,0:T(8,128)(2,1)S(1)}, u32[]{:S(2)}, u32[]{:S(2)}) %collective-permute-start.25) | collective-permute-done | bytes 131104 | tf_op jit(solution)/shard_map/ppermute | solution.py:157
  96.8 5.1 %collective-permute-done.24.refs_2_ = bf16[256,256]{1,0:T(8,128)(2,1)S(1)} collective-permute-done((bf16[256,256]{1,0:T(8,128)(2,1)S(1)}, bf16[256,256]{1,0:T(8,128)(2,1)S(1)}, u32[]{:S(2)}, u32[]{:S(2)}) %collective-permute-start.24) | collective-permute-done | bytes 131104 | tf_op jit(solution)/shard_map/ppermute | solution.py:157
  112.5 6.9 %collective-permute-done.21.refs_6_.refs_2_ = bf16[272,256]{1,0:T(8,128)(2,1)S(1)} collective-permute-done((bf16[272,256]{1,0:T(8,128)(2,1)S(1)}, bf16[272,256]{1,0:T(8,128)(2,1)S(1)}, u32[]{:S(2)}, u32[]{:S(2)}) %collective-permute-start.21) | collective-permute-done | bytes 139296 | tf_op jit(solution)/shard_map/ppermute | solution.py:157
  120.1 4.7 %shard_map.259 = (f32[256,256]{1,0:T(8,128)S(1)}, bf16[256,256]{1,0:T(8,128)(2,1)S(1)}, bf16[4,2,256,128]{3,2,1,0:T(8,128)(2,1)S(1)}, bf16[4,2,256,128]{3,2,1,0:T(8,128)(2,1)S(1)}) custom-call(s32[3]{0:T(128)S(1)} %pad_add_fusion.spot, bf16[256,256]{1,0:T(8,128)(2,1)S(1)} %get-tuple-element.115.refs_0_, ...), custom_call_target="tpu_custom_call" | custom-call | flops 1207959552 | bytes 7864332 | tf_op jit(solution)/shard_map/pallas_call | solution.py:24
  130.8 3.9 %collective-permute-done.30.refs_3_ = bf16[256,256]{1,0:T(8,128)(2,1)S(1)} collective-permute-done((bf16[256,256]{1,0:T(8,128)(2,1)S(1)}, bf16[256,256]{1,0:T(8,128)(2,1)S(1)}, u32[]{:S(2)}, u32[]{:S(2)}) %collective-permute-start.30) | collective-permute-done | bytes 131104 | tf_op jit(solution)/shard_map/ppermute | solution.py:157
  134.7 5.2 %collective-permute-done.29.refs_2_ = bf16[256,256]{1,0:T(8,128)(2,1)S(1)} collective-permute-done((bf16[256,256]{1,0:T(8,128)(2,1)S(1)}, bf16[256,256]{1,0:T(8,128)(2,1)S(1)}, u32[]{:S(2)}, u32[]{:S(2)}) %collective-permute-start.29) | collective-permute-done | bytes 131104 | tf_op jit(solution)/shard_map/ppermute | solution.py:157
  139.9 3.3 shard_map.260
  146.9 6.4 %collective-permute-done.34.refs_2_ = bf16[512,256]{1,0:T(8,128)(2,1)S(1)} collective-permute-done((bf16[512,256]{1,0:T(8,128)(2,1)S(1)}, bf16[512,256]{1,0:T(8,128)(2,1)S(1)}, u32[]{:S(2)}, u32[]{:S(2)}) %collective-permute-start.34) | collective-permute-done | bytes 262176 | tf_op jit(solution)/shard_map/ppermute | solution.py:157
  163.4 4.4 %collective-permute-done.37.refs_2_ = bf16[512,256]{1,0:T(8,128)(2,1)S(1)} collective-permute-done((bf16[512,256]{1,0:T(8,128)(2,1)S(1)}, bf16[512,256]{1,0:T(8,128)(2,1)S(1)}, u32[]{:S(2)}, u32[]{:S(2)}) %collective-permute-start.37) | collective-permute-done | bytes 262176 | tf_op jit(solution)/shard_map/ppermute | solution.py:157
  185.1 4.9 %collective-permute-done.46 = bf16[2,128,256]{2,1,0:T(8,128)(2,1)S(1)} collective-permute-done((bf16[2,128,256]{2,1,0:T(8,128)(2,1)S(1)}, bf16[2,128,256]{2,1,0:T(8,128)(2,1)S(1)}, u32[]{:S(2)}, u32[]{:S(2)}) %collective-permute-start.46) | collective-permute-done | bytes 131104 | tf_op jit(solution)/shard_map/ppermute | solution.py:157
  195.6 3.7 %shard_map.268 = (bf16[4,128,1536]{2,1,0:T(8,128)(2,1)S(1)}, bf16[4,128,1536]{2,1,0:T(8,128)(2,1)}) custom-call(s32[3]{0:T(128)S(1)} %pad_add_fusion.spot, bf16[256,128]{1,0:T(8,128)(2,1)S(1)} %get-tuple-element.126.kq, bf16[256,256]{1,0:T(8,128)(2,1)S(1)} %get-tuple-element.137.kp, bf16[256,512]{1,0:T(8,128)(2,1)S(1)} %collective-permute-done.43.got.received, ...), custom_call_target="tpu_custom_call" | custom-call | flops 805306368 | bytes 5013516 | tf_op jit(solution)/shard_map/pallas_call | solution.py:24
  207.2 3.6 %shard_map.267 = (bf16[272,256]{1,0:T(8,128)(2,1)S(1)}, bf16[272,256]{1,0:T(8,128)(2,1)S(1)}, bf16[272,256]{1,0:T(8,128)(2,1)S(1)}, bf16[272,256]{1,0:T(8,128)(2,1)S(1)}) custom-call(s32[3]{0:T(128)S(1)} %pad_add_fusion.spot, bf16[256,128]{1,0:T(8,128)(2,1)S(1)} %copy-done.26, bf16[256,256]{1,0:T(8,128)(2,1)S(1)} %copy-done.22, ...), custom_call_target="tpu_custom_call" | custom-call | flops 536870912 | bytes 5376012 | tf_op jit(solution)/shard_map/pallas_call | solution.py:24
  218.6 6.3 %collective-permute-done.48.refs_1_ = bf16[272,256]{1,0:T(8,128)(2,1)S(1)} collective-permute-done((bf16[272,256]{1,0:T(8,128)(2,1)S(1)}, bf16[272,256]{1,0:T(8,128)(2,1)S(1)}, u32[]{:S(2)}, u32[]{:S(2)}) %collective-permute-start.48) | collective-permute-done | bytes 139296 | tf_op jit(solution)/shard_map/ppermute | solution.py:157
  225.3 3.8 %collective-permute-done.50.refs_3_ = bf16[272,256]{1,0:T(8,128)(2,1)S(1)} collective-permute-done((bf16[272,256]{1,0:T(8,128)(2,1)S(1)}, bf16[272,256]{1,0:T(8,128)(2,1)S(1)}, u32[]{:S(2)}, u32[]{:S(2)}) %collective-permute-start.50) | collective-permute-done | bytes 139296 | tf_op jit(solution)/shard_map/ppermute | solution.py:157
  236.9 3.5 %collective-permute-done.52.bottom = bf16[128,256]{1,0:T(8,128)(2,1)S(1)} collective-permute-done((bf16[128,256]{1,0:T(8,128)(2,1)S(1)}, bf16[128,256]{1,0:T(8,128)(2,1)S(1)}, u32[]{:S(2)}, u32[]{:S(2)}) %collective-permute-start.52) | collective-permute-done | bytes 65568 | tf_op jit(solution)/shard_map/ppermute | solution.py:218
  240.5 3.9 %shard_map.271 = (bf16[256,256]{1,0:T(8,128)(2,1)S(1)}, bf16[256,256]{1,0:T(8,128)(2,1)S(1)}, bf16[256,256]{1,0:T(8,128)(2,1)S(1)}, bf16[256,256]{1,0:T(8,128)(2,1)S(1)}) custom-call(s32[3]{0:T(128)S(1)} %pad_add_fusion.spot, bf16[256,256]{1,0:T(8,128)(2,1)} %get-tuple-element.159.grad, bf16[128,256]{1,0:T(8,128)(2,1)S(1)} %collective-permute-done.51.top, ...), custom_call_target="tpu_custom_call" | custom-call | flops 1207959552 | bytes 5505036 | tf_op jit(solution)/shard_map/pallas_call | solution.py:24
  244.4 3.5 %collective-permute-start.56 = (bf16[256,256]{1,0:T(8,128)(2,1)S(1)}, bf16[256,256]{1,0:T(8,128)(2,1)S(1)}, u32[]{:S(2)}, u32[]{:S(2)}) collective-permute-start(bf16[256,256]{1,0:T(8,128)(2,1)S(1)} %get-tuple-element.166), channel_id=1, source_target_pairs={{0,1},{1,0},{2,3},{3,2},{4,5},{5,4},{6,7},{7,6},{8,9},{9,8},{10,11... | collective-permute-start | bytes 393224 | tf_op jit(solution)/shard_map/ppermute | solution.py:157
  257.3 11.6 %collective-permute-start.59 = (f32[8,256]{1,0:T(8,128)S(1)}, f32[8,256]{1,0:T(8,128)S(1)}, u32[]{:S(2)}, u32[]{:S(2)}) collective-permute-start(f32[8,256]{1,0:T(8,128)S(1)} %get-tuple-element.173), channel_id=1, source_target_pairs={{0,4},{4,0},{8,12},{12,8},{16,20},{20,16},{24,28},{28,24},{1,5},{5... | collective-permute-start | bytes 24584 | tf_op jit(solution)/shard_map/ppermute | solution.py:157
  272.7 4.8 %collective-permute-start.61 = (f32[8,256]{1,0:T(8,128)S(1)}, f32[8,256]{1,0:T(8,128)S(1)}, u32[]{:S(2)}, u32[]{:S(2)}) collective-permute-start(f32[8,256]{1,0:T(8,128)S(1)} %add.54.refs_0_), channel_id=1, source_target_pairs={{0,16},{4,20},{8,24},{12,28},{16,0},{20,4},{24,8},{28,12},{1,17},{... | collective-permute-start | bytes 24584 | tf_op jit(solution)/shard_map/ppermute | solution.py:157
  284.5 5.3 %collective-permute-done.69 = bf16[2,128,256]{2,1,0:T(8,128)(2,1)S(1)} collective-permute-done((bf16[2,128,256]{2,1,0:T(8,128)(2,1)S(1)}, bf16[2,128,256]{2,1,0:T(8,128)(2,1)S(1)}, u32[]{:S(2)}, u32[]{:S(2)}) %collective-permute-start.69) | collective-permute-done | bytes 131104 | tf_op jit(solution)/shard_map/ppermute | solution.py:157
  305.5 3.8 %shard_map.275 = (bf16[256,256]{1,0:T(8,128)(2,1)S(1)}, bf16[256,256]{1,0:T(8,128)(2,1)S(1)}, bf16[256,256]{1,0:T(8,128)(2,1)S(1)}, bf16[256,256]{1,0:T(8,128)(2,1)S(1)}) custom-call(s32[3]{0:T(128)S(1)} %pad_add_fusion.spot, bf16[256,256]{1,0:T(8,128)(2,1)} %get-tuple-element.174.grad, bf16[128,256]{1,0:T(8,128)(2,1)S(1)} %collective-permute-done.63.top, ...), custom_call_target="tpu_custom_call" | custom-call | flops 1207959552 | bytes 5505036 | tf_op jit(solution)/shard_map/pallas_call | solution.py:24
  315.2 4.8 %shard_map.276.refs_4_ = f32[2,9,128,256]{3,2,1,0:T(8,128)} custom-call(s32[3]{0:T(128)S(1)} %pad_add_fusion.spot, bf16[4,2,256,128]{3,2,1,0:T(8,128)(2,1)} %copy-done.2, bf16[4,2,256,128]{3,2,1,0:T(8,128)(2,1)} %copy-done.50, bf16[2,2,256,128]{3,2,1,0:T(8,128)(2,1)} %copy-done.58, bf16[2,2,256,128]{3,2,1,0:T(8,128)(2,1)} %collective-permute-done.66.refs_1_, ...), custom_call_target="tpu_custom_call" | custom-call | flops 1207959552 | bytes 4194304 | tf_op jit(solution)/shard_map/pallas_call | solution.py:315
  320.0 4.4 %collective-permute-done.72.refs_2_ = bf16[256,256]{1,0:T(8,128)(2,1)S(1)} collective-permute-done((bf16[256,256]{1,0:T(8,128)(2,1)S(1)}, bf16[256,256]{1,0:T(8,128)(2,1)S(1)}, u32[]{:S(2)}, u32[]{:S(2)}) %collective-permute-start.72) | collective-permute-done | bytes 131104 | tf_op jit(solution)/shard_map/ppermute | solution.py:157
  334.2 4.8 %shard_map.279 = f32[2,9,128,256]{3,2,1,0:T(8,128)} custom-call(s32[3]{0:T(128)S(1)} %pad_add_fusion.spot, bf16[4,2,256,128]{3,2,1,0:T(8,128)(2,1)} %copy-done.2, bf16[4,2,256,128]{3,2,1,0:T(8,128)(2,1)} %copy-done.50, bf16[2,2,256,128]{3,2,1,0:T(8,128)(2,1)} %copy-done.58, ...), custom_call_target="tpu_custom_call", output_to_operand_aliasing={{}: (7, {})} | custom-call | flops 1207959552 | bytes 4194304 | tf_op jit(solution)/shard_map/pallas_call | solution.py:315
  (362 shorter events, 168.6 us)
Async XLA Ops:
  7.2 112.8 %all-gather.6.cloned.1.call-start = ((), (), s32[]{:S(2)}) async-start(), calls=%async_computation.1 | async-start | bytes 5308416 | tf_op jit(solution)/shard_map/all_gather | solution.py:186
  9.6 121.2 %all-gather.12.cloned.1.call-start = ((), (), s32[]{:S(2)}) async-start(), calls=%async_computation.5 | async-start | bytes 3538944 | tf_op jit(solution)/shard_map/all_gather | solution.py:186
  10.7 287.4 %reduce-scatter.2.cloned.1.call-start = ((), (), s32[]{:S(2)}) async-start(), calls=%async_computation.3 | async-start | bytes 655360 | tf_op jit(solution)/shard_map/reduce_scatter | solution.py:1056
  21.4 20.3 %collective-permute-start.10 = (bf16[9,128,256]{2,1,0:T(8,128)(2,1)S(1)}, bf16[9,128,256]{2,1,0:T(8,128)(2,1)}, u32[]{:S(2)}, u32[]{:S(2)}) collective-permute-start(bf16[9,128,256]{2,1,0:T(8,128)(2,1)S(1)} %get-tuple-element.109.refs_6_.refs_0_), channel_id=1, source_target_pairs={{0,16},{4,20},{8,24},{12,28},{16,0},{20,4},{24,8},{28,12},{1,17},{... | collective-permute-start | bytes 1769480 | tf_op jit(solution)/shard_map/ppermute | solution.py:157
  22.9 19.6 %collective-permute-start.9 = (bf16[9,128,256]{2,1,0:T(8,128)(2,1)S(1)}, bf16[9,128,256]{2,1,0:T(8,128)(2,1)}, u32[]{:S(2)}, u32[]{:S(2)}) collective-permute-start(bf16[9,128,256]{2,1,0:T(8,128)(2,1)S(1)} %get-tuple-element.109.refs_6_.refs_0_), channel_id=1, source_target_pairs={{0,8},{4,12},{8,0},{12,4},{16,24},{20,28},{24,16},{28,20},{1,9},{5... | collective-permute-start | bytes 1769480 | tf_op jit(solution)/shard_map/ppermute | solution.py:157
  28.6 16.9 %collective-permute-start.5 = (bf16[256,256]{1,0:T(8,128)(2,1)S(1)}, bf16[256,256]{1,0:T(8,128)(2,1)S(1)}, u32[]{:S(2)}, u32[]{:S(2)}) collective-permute-start(bf16[256,256]{1,0:T(8,128)(2,1)S(1)} %get-tuple-element.108.refs_0_), channel_id=1, source_target_pairs={{0,2},{1,3},{2,0},{3,1},{4,6},{5,7},{6,4},{7,5},{8,10},{9,11},{10,... | collective-permute-start | bytes 393224 | tf_op jit(solution)/shard_map/ppermute | solution.py:157
  28.6 16.9 %collective-permute-start.4 = (bf16[256,256]{1,0:T(8,128)(2,1)S(1)}, bf16[256,256]{1,0:T(8,128)(2,1)S(1)}, u32[]{:S(2)}, u32[]{:S(2)}) collective-permute-start(bf16[256,256]{1,0:T(8,128)(2,1)S(1)} %get-tuple-element.108.refs_0_), channel_id=1, source_target_pairs={{0,1},{1,0},{2,3},{3,2},{4,5},{5,4},{6,7},{7,6},{8,9},{9,8},{10,11... | collective-permute-start | bytes 393224 | tf_op jit(solution)/shard_map/ppermute | solution.py:157
  44.5 18.7 %collective-permute-start.11 = (bf16[9,128,256]{2,1,0:T(8,128)(2,1)}, bf16[9,128,256]{2,1,0:T(8,128)(2,1)}, u32[]{:S(2)}, u32[]{:S(2)}) collective-permute-start(bf16[9,128,256]{2,1,0:T(8,128)(2,1)} %broadcast_select_fusion), channel_id=1, source_target_pairs={{0,16},{4,12},{8,24},{12,4},{16,0},{20,28},{24,8},{28,20},{1,17},{... | collective-permute-start | bytes 1769480 | tf_op jit(solution)/shard_map/ppermute | solution.py:165
  45.6 18.3 %collective-permute-start.7 = (bf16[128,1024]{1,0:T(8,128)(2,1)S(1)}, bf16[128,1024]{1,0:T(8,128)(2,1)S(1)}, u32[]{:S(2)}, u32[]{:S(2)}) collective-permute-start(bf16[128,1024]{1,0:T(8,128)(2,1)S(1)} %pad_maximum_fusion.1), channel_id=1, source_target_pairs={{0,4},{4,8},{8,12},{12,16},{16,20},{20,24},{24,28},{1,5},{5,9},{9,... | collective-permute-start | bytes 786440 | tf_op jit(solution)/shard_map/ppermute | solution.py:217
  47.0 20.3 %collective-permute-start.12 = (bf16[9,128,256]{2,1,0:T(8,128)(2,1)S(1)}, bf16[9,128,256]{2,1,0:T(8,128)(2,1)S(1)}, u32[]{:S(2)}, u32[]{:S(2)}) collective-permute-start(bf16[9,128,256]{2,1,0:T(8,128)(2,1)S(1)} %get-tuple-element.109.refs_6_.refs_0_), channel_id=1, source_target_pairs={{0,4},{4,0},{8,12},{12,8},{16,20},{20,16},{24,28},{28,24},{1,5},{5... | collective-permute-start | bytes 1769480 | tf_op jit(solution)/shard_map/ppermute | solution.py:157
  48.4 19.0 %collective-permute-start.14 = (bf16[9,128,256]{2,1,0:T(8,128)(2,1)}, bf16[9,128,256]{2,1,0:T(8,128)(2,1)S(1)}, u32[]{:S(2)}, u32[]{:S(2)}) collective-permute-start(bf16[9,128,256]{2,1,0:T(8,128)(2,1)} %collective-permute-done.10.refs_8_.refs_2_), channel_id=1, source_target_pairs={{0,4},{4,0},{8,12},{12,8},{16,20},{20,16},{24,28},{28,24},{1,5},{5... | collective-permute-start | bytes 1769480 | tf_op jit(solution)/shard_map/ppermute | solution.py:157
  48.4 18.9 %collective-permute-start.13 = (bf16[9,128,256]{2,1,0:T(8,128)(2,1)}, bf16[9,128,256]{2,1,0:T(8,128)(2,1)S(1)}, u32[]{:S(2)}, u32[]{:S(2)}) collective-permute-start(bf16[9,128,256]{2,1,0:T(8,128)(2,1)} %collective-permute-done.9.refs_7_.refs_1_), channel_id=1, source_target_pairs={{0,4},{4,0},{8,12},{12,8},{16,20},{20,16},{24,28},{28,24},{1,5},{5... | collective-permute-start | bytes 1769480 | tf_op jit(solution)/shard_map/ppermute | solution.py:157
  102.0 17.4 %collective-permute-start.26 = (bf16[128,1024]{1,0:T(8,128)(2,1)S(1)}, bf16[128,1024]{1,0:T(8,128)(2,1)S(1)}, u32[]{:S(2)}, u32[]{:S(2)}) collective-permute-start(bf16[128,1024]{1,0:T(8,128)(2,1)S(1)} %pad_maximum_fusion.3), channel_id=1, source_target_pairs={{0,4},{4,8},{8,12},{12,16},{16,20},{20,24},{24,28},{1,5},{5,9},{9,... | collective-permute-start | bytes 786440 | tf_op jit(solution)/shard_map/ppermute | solution.py:217
  103.3 16.7 %collective-permute-start.27 = (bf16[128,1024]{1,0:T(8,128)(2,1)S(1)}, bf16[128,1024]{1,0:T(8,128)(2,1)S(1)}, u32[]{:S(2)}, u32[]{:S(2)}) collective-permute-start(bf16[128,1024]{1,0:T(8,128)(2,1)S(1)} %pad_maximum_fusion.4), channel_id=1, source_target_pairs={{4,0},{8,4},{12,8},{16,12},{20,16},{24,20},{28,24},{5,1},{9,5},{13... | collective-permute-start | bytes 786440 | tf_op jit(solution)/shard_map/ppermute | solution.py:218
  107.2 12.1 %collective-permute-start.21 = (bf16[272,256]{1,0:T(8,128)(2,1)S(1)}, bf16[272,256]{1,0:T(8,128)(2,1)S(1)}, u32[]{:S(2)}, u32[]{:S(2)}) collective-permute-start(bf16[272,256]{1,0:T(8,128)(2,1)S(1)} %get-tuple-element.114.refs_4_.refs_0_), channel_id=1, source_target_pairs={{0,2},{1,3},{2,0},{3,1},{4,6},{5,7},{6,4},{7,5},{8,10},{9,11},{10,... | collective-permute-start | bytes 417800 | tf_op jit(solution)/shard_map/ppermute | solution.py:157
  168.7 12.2 %collective-permute-start.38 = (bf16[512,256]{1,0:T(8,128)(2,1)S(1)}, bf16[512,256]{1,0:T(8,128)(2,1)S(1)}, u32[]{:S(2)}, u32[]{:S(2)}) collective-permute-start(bf16[512,256]{1,0:T(8,128)(2,1)S(1)} %broadcast_select_fusion.1), channel_id=1, source_target_pairs={{0,16},{4,12},{8,24},{12,4},{16,0},{20,28},{24,8},{28,20},{1,17},{... | collective-permute-start | bytes 786440 | tf_op jit(solution)/shard_map/ppermute | solution.py:165
  169.9 22.2 %collective-permute-start.42 = (bf16[4,2,256,128]{3,2,1,0:T(8,128)(2,1)S(1)}, bf16[4,2,256,128]{3,2,1,0:T(8,128)(2,1)S(1)}, u32[]{:S(2)}, u32[]{:S(2)}) collective-permute-start(bf16[4,2,256,128]{3,2,1,0:T(8,128)(2,1)S(1)} %copy-done.38), channel_id=1, source_target_pairs={{0,4},{4,0},{8,12},{12,8},{16,20},{20,16},{24,28},{28,24},{1,5},{5... | collective-permute-start | bytes 1572872 | tf_op jit(solution)/shard_map/ppermute | solution.py:157
  199.3 15.9 %collective-permute-start.47 = (bf16[4,128,1536]{2,1,0:T(8,128)(2,1)}, bf16[4,128,1536]{2,1,0:T(8,128)(2,1)}, u32[]{:S(2)}, u32[]{:S(2)}) collective-permute-start(bf16[4,128,1536]{2,1,0:T(8,128)(2,1)} %get-tuple-element.150), channel_id=1, source_target_pairs={{0,4},{4,0},{8,12},{12,8},{16,20},{20,16},{24,28},{28,24},{1,5},{5... | collective-permute-start | bytes 4718600 | tf_op jit(solution)/shard_map/ppermute | solution.py:157
  202.6 112.5 %all-gather.8.cloned.1.call-start = ((), (), s32[]{:S(2)}) async-start(), calls=%async_computation.2 | async-start | bytes 1179648 | tf_op jit(solution)/shard_map/all_gather | solution.py:182
  210.8 14.0 %collective-permute-start.48 = (bf16[272,256]{1,0:T(8,128)(2,1)S(1)}, bf16[272,256]{1,0:T(8,128)(2,1)S(1)}, u32[]{:S(2)}, u32[]{:S(2)}) collective-permute-start(bf16[272,256]{1,0:T(8,128)(2,1)S(1)} %get-tuple-element.155), channel_id=1, source_target_pairs={{0,1},{1,0},{2,3},{3,2},{4,5},{5,4},{6,7},{7,6},{8,9},{9,8},{10,11... | collective-permute-start | bytes 417800 | tf_op jit(solution)/shard_map/ppermute | solution.py:157
  211.0 14.3 %collective-permute-start.49 = (bf16[272,256]{1,0:T(8,128)(2,1)S(1)}, bf16[272,256]{1,0:T(8,128)(2,1)S(1)}, u32[]{:S(2)}, u32[]{:S(2)}) collective-permute-start(bf16[272,256]{1,0:T(8,128)(2,1)S(1)} %get-tuple-element.156), channel_id=1, source_target_pairs={{0,2},{1,3},{2,0},{3,1},{4,6},{5,7},{6,4},{7,5},{8,10},{9,11},{10,... | collective-permute-start | bytes 417800 | tf_op jit(solution)/shard_map/ppermute | solution.py:157
  213.4 15.7 %collective-permute-start.50 = (bf16[272,256]{1,0:T(8,128)(2,1)S(1)}, bf16[272,256]{1,0:T(8,128)(2,1)S(1)}, u32[]{:S(2)}, u32[]{:S(2)}) collective-permute-start(bf16[272,256]{1,0:T(8,128)(2,1)S(1)} %get-tuple-element.157), channel_id=1, source_target_pairs={{0,3},{1,2},{2,1},{3,0},{4,7},{5,6},{6,5},{7,4},{8,11},{9,10},{10,... | collective-permute-start | bytes 417800 | tf_op jit(solution)/shard_map/ppermute | solution.py:157
  230.6 103.6 %all-gather.10.cloned.1.call-start = ((), (), s32[]{:S(2)}) async-start(), calls=%async_computation.4 | async-start | bytes 1179648 | tf_op jit(solution)/shard_map/all_gather | solution.py:182
  230.6 17.3 %collective-permute-start.53 = (bf16[128,1536]{1,0:T(8,128)(2,1)}, bf16[128,1536]{1,0:T(8,128)(2,1)S(1)}, u32[]{:S(2)}, u32[]{:S(2)}) collective-permute-start(bf16[128,1536]{1,0:T(8,128)(2,1)} %copy-done.42), channel_id=1, source_target_pairs={{0,8},{4,12},{8,0},{12,4},{16,24},{20,28},{24,16},{28,20},{1,9},{5... | collective-permute-start | bytes 1179656 | tf_op jit(solution)/shard_map/ppermute | solution.py:157
  232.2 20.8 %collective-permute-start.54 = (bf16[128,1536]{1,0:T(8,128)(2,1)}, bf16[128,1536]{1,0:T(8,128)(2,1)S(1)}, u32[]{:S(2)}, u32[]{:S(2)}) collective-permute-start(bf16[128,1536]{1,0:T(8,128)(2,1)} %copy-done.41), channel_id=1, source_target_pairs={{0,16},{4,20},{8,24},{12,28},{16,0},{20,4},{24,8},{28,12},{1,17},{... | collective-permute-start | bytes 1179656 | tf_op jit(solution)/shard_map/ppermute | solution.py:157
  233.6 19.3 %collective-permute-start.55 = (bf16[128,1536]{1,0:T(8,128)(2,1)}, bf16[128,1536]{1,0:T(8,128)(2,1)S(1)}, u32[]{:S(2)}, u32[]{:S(2)}) collective-permute-start(bf16[128,1536]{1,0:T(8,128)(2,1)} %copy-done.40), channel_id=1, source_target_pairs={{0,24},{4,28},{8,16},{12,20},{16,8},{20,12},{24,0},{28,4},{1,25},{... | collective-permute-start | bytes 1179656 | tf_op jit(solution)/shard_map/ppermute | solution.py:157
  257.3 12.4 %collective-permute-start.59 = (f32[8,256]{1,0:T(8,128)S(1)}, f32[8,256]{1,0:T(8,128)S(1)}, u32[]{:S(2)}, u32[]{:S(2)}) collective-permute-start(f32[8,256]{1,0:T(8,128)S(1)} %get-tuple-element.173), channel_id=1, source_target_pairs={{0,4},{4,0},{8,12},{12,8},{16,20},{20,16},{24,28},{28,24},{1,5},{5... | collective-permute-start | bytes 24584 | tf_op jit(solution)/shard_map/ppermute | solution.py:157
  290.5 21.6 %collective-permute-start.65 = (bf16[2,2,256,128]{3,2,1,0:T(8,128)(2,1)S(1)}, bf16[2,2,256,128]{3,2,1,0:T(8,128)(2,1)S(1)}, u32[]{:S(2)}, u32[]{:S(2)}) collective-permute-start(bf16[2,2,256,128]{3,2,1,0:T(8,128)(2,1)S(1)} %copy-done.48), channel_id=1, source_target_pairs={{0,8},{4,12},{8,0},{12,4},{16,24},{20,28},{24,16},{28,20},{1,9},{5... | collective-permute-start | bytes 786440 | tf_op jit(solution)/shard_map/ppermute | solution.py:157
  292.2 22.9 %collective-permute-start.66 = (bf16[2,2,256,128]{3,2,1,0:T(8,128)(2,1)S(1)}, bf16[2,2,256,128]{3,2,1,0:T(8,128)(2,1)}, u32[]{:S(2)}, u32[]{:S(2)}) collective-permute-start(bf16[2,2,256,128]{3,2,1,0:T(8,128)(2,1)S(1)} %copy-done.46), channel_id=1, source_target_pairs={{0,16},{4,20},{8,24},{12,28},{16,0},{20,4},{24,8},{28,12},{1,17},{... | collective-permute-start | bytes 786440 | tf_op jit(solution)/shard_map/ppermute | solution.py:157
  292.3 22.8 %collective-permute-start.67 = (bf16[2,2,256,128]{3,2,1,0:T(8,128)(2,1)S(1)}, bf16[2,2,256,128]{3,2,1,0:T(8,128)(2,1)}, u32[]{:S(2)}, u32[]{:S(2)}) collective-permute-start(bf16[2,2,256,128]{3,2,1,0:T(8,128)(2,1)S(1)} %copy-done.44), channel_id=1, source_target_pairs={{0,24},{4,28},{8,16},{12,20},{16,8},{20,12},{24,0},{28,4},{1,25},{... | collective-permute-start | bytes 786440 | tf_op jit(solution)/shard_map/ppermute | solution.py:157
  311.8 12.6 %collective-permute-start.72 = (bf16[256,256]{1,0:T(8,128)(2,1)S(1)}, bf16[256,256]{1,0:T(8,128)(2,1)S(1)}, u32[]{:S(2)}, u32[]{:S(2)}) collective-permute-start(bf16[256,256]{1,0:T(8,128)(2,1)S(1)} %get-tuple-element.184), channel_id=1, source_target_pairs={{0,2},{1,3},{2,0},{3,1},{4,6},{5,7},{6,4},{7,5},{8,10},{9,11},{10,... | collective-permute-start | bytes 393224 | tf_op jit(solution)/shard_map/ppermute | solution.py:157
  312.1 12.3 %collective-permute-start.73 = (bf16[256,256]{1,0:T(8,128)(2,1)S(1)}, bf16[256,256]{1,0:T(8,128)(2,1)S(1)}, u32[]{:S(2)}, u32[]{:S(2)}) collective-permute-start(bf16[256,256]{1,0:T(8,128)(2,1)S(1)} %get-tuple-element.185), channel_id=1, source_target_pairs={{0,3},{1,2},{2,1},{3,0},{4,7},{5,6},{6,5},{7,4},{8,11},{9,10},{10,... | collective-permute-start | bytes 393224 | tf_op jit(solution)/shard_map/ppermute | solution.py:157
  (120 other events, 1211.9 us)
Sparse Core Ops, SparseCore 0:
  10.5 53.0 all-gather.5
  66.0 32.6 all-gather.11
  202.7 24.0 reduce-scatter.1
  230.7 32.3 all-gather.7
  282.9 28.7 all-gather.9

commit v2 on v1

--- a/solution.py
+++ b/solution.py
@@ -31,6 +31,7 @@
         input_output_aliases={} if aliases is None else aliases,
         compiler_params=pltpu.CompilerParams(vmem_limit_bytes=limit * MIB),
         cost_estimate=pl.CostEstimate(flops=flops, bytes_accessed=size, transcendentals=0),
+        name=getattr(body, "func", body).__name__,
     )(*operands)
 
 
@@ -157,17 +158,15 @@
     return lax.ppermute(values, axis, [(i, i ^ mask) for i in range(count)])
 
 
+def relayed_block(over_x, over_y):
+    odd = lax.rem(lax.axis_index("wide"), 2) == 1
+    far_pairs = [(i, i ^ (2 if i % 2 else 4)) for i in range(8)]
+    return lax.ppermute(jnp.where(odd, over_y, over_x), "wide", far_pairs)
+
+
 def over_chips(values):
     over_x, over_y = flipped(values, "wide", 2), flipped(values, "wide", 4)
-    odd = lax.rem(lax.axis_index("wide"), 2) == 1
-    relayed = jnp.where(odd, over_y, over_x)
-    far_pairs = [(i, i ^ (2 if i % 2 else 4)) for i in range(8)]
-    return [values, over_x, over_y, lax.ppermute(relayed, "wide", far_pairs)]
-
-
-def spread_slots(values):
-    mine = over_chips(values)
-    return mine + [flipped(part, "wide", 1) for part in mine]
+    return [values, over_x, over_y, relayed_block(over_x, over_y)]
 
 
 def has_slots():
@@ -176,10 +175,6 @@
 
 def after(value, *others):
     return lax.optimization_barrier((value, others))[0]
-
-
-def gathered_grads(grad):
-    return lax.all_gather(grad, "wide", tiled=True)
 
 
 def gathered_blocks(blocks):
@@ -196,14 +191,15 @@
     return [values]
 
 
-def spread_stats(values):
+def gathered_sums(parts):
     if has_slots():
-        over_x, over_y = flipped(values, "wide", 2), flipped(values, "wide", 4)
-        return [values, over_x, over_y, flipped(over_x, "wide", 4)]
-    mask = 2
-    while mask < lax.axis_size("wide"):
-        values = jnp.concatenate([values, flipped(values, "wide", mask)], axis=1)
-        mask *= 2
+        return [parts[0]] + [flipped(parts[k], "wide", 2 * k) for k in range(1, 4)]
+    values = parts[0]
+    mask = lax.axis_size("wide") // 2
+    while mask > 1:
+        half = values.shape[0] // 2
+        values = values[:half] + flipped(values[half:], "wide", mask)
+        mask //= 2
     return [values]
 
 
@@ -284,7 +280,7 @@
     for row in range(3):
         product = jnp.dot(
             turned_all[:, row * width : row * width + depth],
-            grads[...],
+            grads[layer],
             preferred_element_type=jnp.float32,
         )
         for column in range(3):
@@ -299,13 +295,9 @@
     return [kept, got, *pairs]
 
 
-def traded_blocks(blocks):
-    return blocks[:2] + [flipped(blocks[2 + k], "wide", 2 * k + 2) for k in range(3)]
-
-
 def kernel_grad(spot, pieces, grads, rows, width, layer, earlier):
-    area, span = pieces[0].shape[2:]
-    columns, depth = grads.shape[1], grads.shape[0]
+    span = pieces[0].shape[3]
+    depth, columns = grads.shape[1:]
     operands = [spot, *far(pieces), *far([grads])]
     specs = [in_smem] + [in_vmem] * (len(operands) - 1)
     shape = f32_like(2, 9, span, columns)
@@ -358,11 +350,18 @@
     return jnp.concatenate([jnp.cos(angles), jnp.sin(angles)], axis=1)
 
 
+def chip_parts(values):
+    if has_slots():
+        return [values] + [flipped(values, "wide", mask) for mask in (2, 4, 6)]
+    mask = 2
+    while mask < lax.axis_size("wide"):
+        values = values + flipped(values, "wide", mask)
+        mask *= 2
+    return [values]
+
+
 def part_totals(rows):
-    if not has_slots():
-        return [total(rows, "wide")]
-    rows = rows + flipped(rows, "wide", 1)
-    return [rows] + [flipped(rows, "wide", mask) for mask in (2, 4, 6)]
+    return chip_parts(rows + flipped(rows, "wide", 1))
 
 
 def sum_of_parts(refs):
@@ -371,8 +370,7 @@
     return (refs[0][...] + refs[1][...]) + (refs[2][...] + refs[3][...])
 
 
-def total(values, axis):
-    mask = 1
+def total(values, axis, mask=1):
     while mask < lax.axis_size(axis):
         values = values + flipped(values, axis, mask)
         mask *= 2
@@ -497,9 +495,11 @@
     rows[...] = stacked_rows([back * scaled, back])
 
 
-def first_input_body(pixel_count, spot, back, pixels, sums, affine, middle, *refs):
-    *parts, out, rows = refs
-    rows[...] = sum_of_parts(parts)
+def first_input_body(pixel_count, spot, back, pixels, sums, affine, middle, second, *refs):
+    *parts, out, gains, biases = refs
+    rows = sum_of_parts(parts)
+    gains[...] = jnp.concatenate([rows[0:1], second[0:1]], axis=0)
+    biases[...] = jnp.concatenate([rows[1:2], second[1:2]], axis=0)
     gain = affine[0:1]
     center, inverse = group_scale(sums[0:1], sums[1:2], pixel_count)
     dotted, plain = group_means(gain * rows[0:1], gain * rows[1:2], pixel_count)
@@ -552,16 +552,16 @@
     return rows[0:1] + rows[2:3] + rows[4:5], rows[1:2] + rows[3:4] + rows[5:6]
 
 
-def prepare_body(spot, pixels, cotangent, terms, pack, sums):
+def prepare_body(spot, pixels, cotangent, gain, bias, pack, sums):
     area = cotangent.shape[0]
     pack[:area] = cotangent[...].astype(jnp.bfloat16)
-    pack[area:] = packed_rows(terms[...])
+    pack[area:] = packed_rows(jnp.concatenate([gain[...], bias[...]], axis=0))
     sums[...] = channel_sums(pixels[...].astype(jnp.float32))
 
 
 def project_body(groups, spot, *refs):
     pieces, packs = refs[:groups], refs[groups : 2 * groups]
-    own, maps, keep_q, keep_kv, send, cross, normed, scaled, center, inverse = refs[2 * groups :]
+    own, maps, keep_query, keep, send, cross, normed, scaled, center, inverse = refs[2 * groups :]
     weights = Weights([maps], spot, groups)
     odd = lax.rem(spot[0], 2) == 1
     area = own.shape[0]
@@ -589,8 +589,9 @@
         projected.append(total_sum.astype(jnp.bfloat16))
     cross[...] = projected[3]
     chosen = [head_choice(values, odd) for values in projected[:3]]
-    keep_q[...] = chosen[0][0]
-    keep_kv[...] = jnp.concatenate([chosen[1][0], chosen[2][0]], axis=1)
+    chosen = chosen[1:] + chosen[:1]
+    keep_query[...] = chosen[2][0]
+    keep[...] = jnp.concatenate([pair[0] for pair in chosen[:2]], axis=1)
     send[...] = jnp.concatenate([pair[1] for pair in chosen], axis=1)
 
 
@@ -610,17 +611,28 @@
     cross[...] = sums[1]
 
 
-def mix_body(groups, spot, kept, received, crossed, maps, out):
+def text_out_body(spot, film, features, pooled, text, parts, time_grad, text_grad, kv_grad):
+    for rows, out in ((features, time_grad), (pooled, text_grad)):
+        column = jnp.transpose(jnp.broadcast_to(rows[...].astype(jnp.float32), (8, rows.shape[1])))
+        for part in range(2):
+            out[:, part, :] = column[:, 0:1] * film[part : part + 1, :]
+    summed = leading_sum(parts)
+    turned_text = flat_turn(text[...])
+    for part in range(2):
+        high = summed[part].astype(jnp.bfloat16)
+        low = (summed[part] - high.astype(jnp.float32)).astype(jnp.bfloat16)
+        kv_grad[part] = dot(turned_text, high) + dot(turned_text, low)
+
+
+def mix_body(groups, spot, kept, received, crossed, maps, *outs):
     weights = Weights([maps], spot, groups)
-    area = kept.shape[0]
     attended = heads_joined(
         kept[...], received[:, 3 * HEAD_DIM :], lax.rem(spot[0], 2) == 1
     )
     for mask in range(groups):
         total_sum = dot_last(attended, weights.tap(mask, 4))
         total_sum += dot_last(crossed[...], weights.tap(mask, 5))
-        start = pl.multiple_of(weights.block(mask) * area, area)
-        out[pl.ds(start, area), :] = total_sum.astype(jnp.bfloat16)
+        outs[mask][...] = total_sum.astype(jnp.bfloat16)
 
 
 def over_rows(refs, step, state):
@@ -643,25 +655,27 @@
 score_scale = HEAD_DIM ** (-0.5)
 
 
-def attend_body(count, spot, query_grad, *refs):
-    pairs = refs[:count]
-    keep, send, stats = refs[count:]
-    query, grad = query_grad[:, :HEAD_DIM], query_grad[:, HEAD_DIM:]
+def attend_body(count, spot, kept_query, got, kept_grad, got_grad, *refs):
+    blocks, parts = refs[:count], refs[count : 2 * count]
+    keep_out, send_out, keep_query, send_query = refs[2 * count :]
+    query = jnp.concatenate([kept_query[...], got[:, 2 * HEAD_DIM :]], axis=0)
+    grad = jnp.concatenate([kept_grad[...], got_grad[...]], axis=0)
     queries = query.shape[0]
 
-    def step(state, pair, index, start):
+    def forward(state, block, index, start):
         top, weight_sum, weighted = state
-        scores = dot_last(pair[:, :HEAD_DIM], query) * score_scale
+        scores = dot_last(block[:, :HEAD_DIM], query) * score_scale
         raised = jnp.maximum(top, jnp.max(scores, axis=0, keepdims=True))
         rescale = jnp.exp(top - raised)
         weights = jnp.exp(scores - raised)
         weight_sum = weight_sum * rescale + jnp.sum(weights, axis=0, keepdims=True)
-        weighted = weighted * rescale + dot_first(pair[:, HEAD_DIM:], weights.astype(jnp.bfloat16))
+        values = block[:, HEAD_DIM:]
+        weighted = weighted * rescale + dot_first(values, weights.astype(jnp.bfloat16))
         return raised, weight_sum, weighted
 
     top, weight_sum, weighted = over_rows(
-        pairs,
-        step,
+        blocks,
+        forward,
         (
             jnp.full((1, queries), -1e30, jnp.float32),
             jnp.zeros((1, queries), jnp.float32),
@@ -670,60 +684,49 @@
     )
     attended = weighted / weight_sum
     delta = jnp.sum(attended * jnp.transpose(grad.astype(jnp.float32)), axis=0, keepdims=True)
-    stats[...] = jnp.concatenate([top + jnp.log(weight_sum), delta], axis=0)
-    turned_back = jnp.transpose(attended).astype(jnp.bfloat16)
-    keep[...] = turned_back[: queries // 2]
-    send[...] = turned_back[queries // 2 :]
-
-
-def query_grad_body(count, spot, query_grad, stats, *refs):
-    pairs = refs[:count]
-    keep, send = refs[count:]
-    query, grad = query_grad[:, :HEAD_DIM], query_grad[:, HEAD_DIM:]
-    queries = query.shape[0]
-    log_sum, delta = stats[0:1, :], stats[1:2, :]
-
-    def step(state, pair, index, start):
-        scores = dot_last(pair[:, :HEAD_DIM], query) * score_scale
-        probs = jnp.exp(scores - log_sum)
-        grad_probs = dot_last(pair[:, HEAD_DIM:], grad)
-        grad_scores = (probs * (grad_probs - delta)).astype(jnp.bfloat16)
-        return state + dot_first(pair[:, :HEAD_DIM], grad_scores)
-
-    flat = over_rows(pairs, step, jnp.zeros((HEAD_DIM, queries), jnp.float32))
-    result = jnp.transpose(flat * score_scale).astype(jnp.bfloat16)
-    keep[...] = result[: queries // 2]
-    send[...] = result[queries // 2 :]
-
-
-def key_grad_body(count, spot, pair, sent_query, sent_out, *refs):
-    queries, stats = refs[:count], refs[count:-2]
-    keep, send = refs[-2:]
-    keys, values = pair[:, :HEAD_DIM], pair[:, HEAD_DIM:]
-    depth = keys.shape[0]
-
-    def step(state, block, index, start):
-        grad_keys, grad_values = state
-        rows = block.shape[0]
-        lanes = pl.ds(start if isinstance(start, int) else pl.multiple_of(start, 512), rows)
-        log_sum, delta = stats[index][0:1, lanes], stats[index][1:2, lanes]
-        query, grad = block[:, :HEAD_DIM], block[:, HEAD_DIM:]
+    log_sum = top + jnp.log(weight_sum)
+
+    def backward(state, block, index, start):
+        keys, values = block[:, :HEAD_DIM], block[:, HEAD_DIM:]
         probs = jnp.exp(dot_last(keys, query) * score_scale - log_sum)
-        grad_values += dot(probs.astype(jnp.bfloat16), grad)
-        grad_scores = probs * (dot_last(values, grad) - delta)
-        grad_keys += dot(grad_scores.astype(jnp.bfloat16), query)
-        return grad_keys, grad_values
-
-    zero = jnp.zeros((depth, HEAD_DIM), jnp.float32)
-    grad_keys, grad_values = over_rows(queries, step, (zero, zero))
-    both = jnp.concatenate([grad_keys * score_scale, grad_values], axis=1).astype(jnp.bfloat16)
-    keep[...] = both[: depth // 2]
-    send[:, : 2 * HEAD_DIM] = both[depth // 2 :]
+        grad_values = dot(probs.astype(jnp.bfloat16), grad)
+        grad_scores = (probs * (dot_last(values, grad) - delta)).astype(jnp.bfloat16)
+        grad_keys = dot(grad_scores, query) * score_scale
+        rows = pl.ds(start if isinstance(start, int) else pl.multiple_of(start, 512), block.shape[0])
+        parts[index][rows, :] = jnp.concatenate([grad_keys, grad_values], axis=1).astype(
+            jnp.bfloat16
+        )
+        return state + dot_first(keys, grad_scores)
+
+    flat = over_rows(blocks, backward, jnp.zeros((HEAD_DIM, queries), jnp.float32))
+    for values, keep, send in (
+        (attended, keep_out, send_out),
+        (flat * score_scale, keep_query, send_query),
+    ):
+        turned_back = jnp.transpose(values).astype(jnp.bfloat16)
+        keep[...] = turned_back[: queries // 2]
+        send[...] = turned_back[queries // 2 :]
+
+
+def key_sum_body(spot, sent_query, sent_out, *refs):
+    *parts, keep, send = refs
+    both = parts_sum(parts).astype(jnp.bfloat16)
+    half = keep.shape[0]
+    keep[...] = both[:half]
+    send[:, : 2 * HEAD_DIM] = both[half:]
     send[:, 2 * HEAD_DIM : 3 * HEAD_DIM] = sent_query[...]
     send[:, 3 * HEAD_DIM :] = sent_out[...]
 
 
-def cross_body(spot, query, text, grad, crossed, grad_query, text_grad):
+def leading_sum(ref):
+    summed = ref[0].astype(jnp.float32)
+    for index in range(1, ref.shape[0]):
+        summed += ref[index].astype(jnp.float32)
+    return summed
+
+
+def cross_body(spot, query, grad, parts, crossed, grad_query, text_grad):
+    text = leading_sum(parts).astype(jnp.bfloat16)
     live = lax.broadcasted_iota(jnp.int32, (query.shape[0], text.shape[1]), 1) < spot[2]
     for head in range(query.shape[1] // HEAD_DIM):
         lanes = slice(head * HEAD_DIM, (head + 1) * HEAD_DIM)
@@ -785,7 +788,7 @@
 
 
 def weight_grad_body(groups, spot, kq, kp, got, cross, kept, crossed, normed, *refs):
-    packs, outs, frame = refs[:groups], refs[groups:-1], refs[-1]
+    packs, (out, frame) = refs[:groups], refs[groups:]
     odd = lax.rem(spot[0], 2) == 1
     area, span = cross.shape
     right = jnp.concatenate(joined_grads(spot, kq, kp, got, cross), axis=1)
@@ -795,27 +798,13 @@
     for mask in range(groups):
         frame[lax.bitwise_xor(spot[1], mask)] = packs[mask][:area]
     for chunk in range(groups):
-        near = lax.bitwise_xor(lax.div(spot[0], 2), chunk) if len(outs) == 2 else chunk
-        product = jnp.concatenate(
-            [dot_first(normed[near], right), dot_first(frame[near], out_right)], axis=1
-        ).astype(jnp.bfloat16)
-        if len(outs) == 2:
-            low, high = product[: span // 2], product[span // 2 :]
-            outs[0][chunk] = jnp.where(odd, high, low)
-            outs[1][chunk] = jnp.where(odd, low, high)
-        else:
-            outs[0][chunk * span : (chunk + 1) * span, :] = product
-
-
-def weight_sum_body(spot, kept, got, own, *outs):
-    for index, out in enumerate((own,) + outs):
-        both = kept[index].astype(jnp.float32) + got[index].astype(jnp.float32)
-        out[...] = both.astype(out.dtype)
-
-
-def weight_out_body(spot, own, *refs):
-    *parts, in_grad, self_grad, cross_grad = refs
-    summed = own[...] + parts_sum(parts)
+        rows = slice(chunk * span, (chunk + 1) * span)
+        out[rows, : 4 * span] = dot_first(normed[chunk], right).astype(jnp.bfloat16)
+        out[rows, 4 * span :] = dot_first(frame[chunk], out_right).astype(jnp.bfloat16)
+
+
+def weight_out_body(spot, sums, in_grad, self_grad, cross_grad):
+    summed = sums[...].astype(jnp.float32)
     span = in_grad.shape[2]
     for position in range(4):
         in_grad[position] = summed[:, position * span : (position + 1) * span]
@@ -872,6 +861,7 @@
     own_shape = (map_count, row_count, col_count, width_own)
     flat = (token_count, width_own)
     half = (token_count, HEAD_DIM)
+    square = 2 * token_count * C * width_own
     edge = (col_count, width_own)
     spot = jnp.stack([lax.axis_index("wide"), lax.axis_index("tensor"), text_length[0]])
     spot = spot.astype(jnp.int32)
@@ -882,17 +872,13 @@
     pack, sums = local_kernel(
         prepare_body,
         [bf16_like(token_count + 16, width_own), f32_like(2, width_own)],
-        [spot, own_pixels, flat_cotangent, jnp.stack([layer_gain, layer_bias])],
+        [spot, *far([own_pixels, flat_cotangent, layer_gain[None], layer_bias[None]])],
         [],
         8,
         0,
     )
     first_parts = part_totals(sums)
-    if has_slots():
-        kernel_one = spread_slots(after(conv_weights[0], first_parts))
-    else:
-        kernel_one = gathered_blocks(conv_weights[0])
-    kernel_two = gathered_blocks(conv_weights[1])
+    kernel_one = gathered_blocks(conv_weights[0])
     maps = jnp.concatenate(
         [attn_in, jnp.transpose(jnp.stack([out_self, out_cross]), (0, 2, 1))], axis=0
     )
@@ -926,19 +912,17 @@
         0,
     )
     pieces = channel_pieces(first)
+    edges = piece_edges(pieces, col_count)
+    later = after(conv_weights, first)[1]
+    if has_slots():
+        kernel_two = over_chips(later)
+        kernel_two += [flipped(part, "wide", 1) for part in kernel_two]
+    else:
+        kernel_two = gathered_blocks(later)
     packs = channel_pieces(after(pack, pieces))
-    edges = piece_edges(pieces, col_count)
-    pieces[0] = after(pieces[0], film_term)
+    pieces[0] = after(pieces[0], film_term, packs, text_term)
     inner, sums, *first_sends = convolve(
-        spot,
-        pieces,
-        edges,
-        kernel_one,
-        own_pixels,
-        f32_like(2, width_own),
-        [],
-        row_count,
-        col_count,
+        spot, pieces, edges, kernel_one, own_pixels, row_pair, [], row_count, col_count
     )
     inner_parts = part_totals(jnp.concatenate([film_term[0], sums]))
     second, film, inner_sums = local_kernel(
@@ -949,9 +933,10 @@
         8,
         0,
     )
+    text_all = lax.all_gather(after(text_term, second), "wide")
+    second = after(second, kernel_two)
     pieces = channel_pieces(second)
     edges = piece_edges(pieces, col_count)
-    pieces[0] = after(pieces[0], packs)
     middle, middle_low, *both_sends = convolve(
         spot,
         pieces,
@@ -965,15 +950,24 @@
     )
 
     middle_pieces = channel_pieces(middle_low)
-    text_proj = total(after(text_term, middle_low), "wide")
+    kept_grad, sent_grad, grad_crossed = local_kernel(
+        functools.partial(out_grad_body, groups),
+        [bf16_like(*half), bf16_like(*half), bf16_like(*flat)],
+        [spot, *far([after(packs[0], middle_low)] + packs[1:]), *far([maps])],
+        [],
+        16,
+        2 * square,
+    )
+    got_grad = flipped(sent_grad, "wide", 1)
+    middle_pieces[0] = after(middle_pieces[0], got_grad)
     column = f32_like(token_count, 1)
-    square = 2 * token_count * C * width_own
+    triple = bf16_like(token_count, 3 * HEAD_DIM)
     kept_query, kept_pair, sent, cross_query, normed, scaled, center, inverse = local_kernel(
         functools.partial(project_body, groups),
         [
             bf16_like(*half),
             bf16_like(*flat),
-            bf16_like(token_count, 3 * HEAD_DIM),
+            triple,
             bf16_like(*flat),
             bf16_like(groups, *flat),
             f32_like(*flat),
@@ -986,75 +980,37 @@
         4 * square,
     )
     got = flipped(sent, "wide", 1)
-    kept_grad, sent_grad, grad_crossed = local_kernel(
-        functools.partial(out_grad_body, groups),
-        [bf16_like(*half), bf16_like(*half), bf16_like(*flat)],
-        [spot, *far(packs), *far([maps])],
-        [],
-        16,
-        2 * square,
-    )
-    got_grad = flipped(sent_grad, "wide", 1)
-    pair = jnp.concatenate([kept_pair, got[:, HEAD_DIM:]])
-    pairs = spread_chips(pair)
-    query_grad = jnp.concatenate(
-        [
-            jnp.concatenate([kept_query, got[:, :HEAD_DIM]]),
-            jnp.concatenate([kept_grad, got_grad]),
-        ],
-        axis=1,
-    )
-    query_grads = spread_chips(after(query_grad, *pairs))
-    scores = 2 * (2 * token_count) * HEAD_DIM * pixel_count
-    kept_out, sent_out, stats = local_kernel(
-        functools.partial(attend_body, len(pairs)),
-        [bf16_like(*half), bf16_like(*half), f32_like(2, 2 * token_count)],
-        [spot, query_grad, *pairs],
-        [],
-        24,
-        2 * scores,
-    )
-    all_stats = spread_stats(stats)
+    blocks = spread_chips(jnp.concatenate([kept_pair, got[:, : 2 * HEAD_DIM]]))
+    if has_slots():
+        both_blocks = swapped_blocks(spot, after(both_sends[0], blocks[:2][-1]), both_sends[1])
+        got_grad = after(got_grad, both_blocks)
     crossed, grad_cross_query, text_grads = local_kernel(
         cross_body,
         [bf16_like(*flat), bf16_like(*flat), bf16_like(2, TEXT, width_own)],
-        [spot, cross_query, text_proj, grad_crossed],
-        [],
-        8,
+        [spot, after(cross_query, blocks[:2][-1]), grad_crossed, *far([text_all])],
+        [],
+        24,
         12 * token_count * TEXT * width_own,
     )
-    kept_dq, sent_dq = local_kernel(
-        functools.partial(query_grad_body, len(pairs)),
-        [bf16_like(*half), bf16_like(*half)],
-        [spot, query_grad, stats, *pairs],
-        [],
-        24,
-        3 * scores,
+    got_grad = after(got_grad, crossed)
+    text_sums = lax.all_gather(text_grads, "wide")
+    *key_parts, kept_out, sent_out, kept_dq, sent_dq = local_kernel(
+        functools.partial(attend_body, len(blocks)),
+        [bf16_like(*block.shape) for block in blocks] + [bf16_like(*half)] * 4,
+        [spot, kept_query, got, kept_grad, got_grad, *blocks],
+        [],
+        40,
+        14 * (2 * token_count) * HEAD_DIM * pixel_count,
     )
     kept_dk, sent_all = local_kernel(
-        functools.partial(key_grad_body, len(query_grads)),
+        key_sum_body,
         [bf16_like(*flat), bf16_like(token_count, 4 * HEAD_DIM)],
-        [spot, pair, sent_dq, sent_out, *query_grads, *all_stats],
-        [],
-        24,
-        4 * scores,
+        [spot, sent_dq, sent_out, *gathered_sums(key_parts)],
+        [],
+        16,
+        0,
     )
     got_all = flipped(sent_all, "wide", 1)
-    if has_slots():
-        both_blocks = swapped_blocks(spot, after(both_sends[0], kept_pair), both_sends[1])
-        kept_dk = after(kept_dk, both_blocks)
-        both_blocks = traded_blocks(both_blocks)
-    text_all = total(after(text_grads, *all_stats), "wide").astype(jnp.float32)
-    (mixed,) = local_kernel(
-        functools.partial(mix_body, groups),
-        [bf16_like(groups * token_count, width_own)],
-        [spot, kept_out, got_all, crossed, *far([maps])],
-        [],
-        16,
-        2 * square,
-    )
-    mixed = lax.psum_scatter(mixed, "tensor", scatter_dimension=0, tiled=True)
-    result = middle + mixed.astype(jnp.float32)
     projected_grads = [kept_dq, kept_dk, got_all, grad_cross_query]
     norm_parts = local_kernel(
         functools.partial(project_back_body, groups),
@@ -1064,47 +1020,10 @@
         24,
         4 * square,
     )
-    norm_parts = sent_parts(norm_parts)
-    columns = 6 * width_own
-    width_block = C // lax.axis_size("wide")
+    received = sent_parts(norm_parts)
     if has_slots():
-        weight_shapes = [bf16_like(groups, width_block, columns)] * 2
-    else:
-        weight_shapes = [bf16_like(C, columns)]
-    weight_parts = local_kernel(
-        functools.partial(weight_grad_body, groups),
-        weight_shapes,
-        [spot, *projected_grads, kept_out, crossed, *far([normed]), *far(packs)],
-        [pltpu.VMEM((groups, *flat), jnp.bfloat16)],
-        24,
-        6 * square,
-    )
-    if has_slots():
-        weight_own, *weight_sends = local_kernel(
-            weight_sum_body,
-            [f32_like(width_block, columns)] + [bf16_like(width_block, columns)] * 3,
-            [spot, weight_parts[0], flipped(weight_parts[1], "wide", 1)],
-            [],
-            24,
-            0,
-        )
-        norm_parts[0] = after(norm_parts[0], weight_sends)
-        weight_got = [flipped(weight_sends[k], "wide", 2 * k + 2) for k in range(3)]
-        attn_in_grad, self_grad, cross_grad = local_kernel(
-            weight_out_body,
-            [f32_like(4, width_block, width_own)] + [f32_like(width_own, width_block)] * 2,
-            [spot, weight_own, *weight_got],
-            [],
-            16,
-            0,
-        )
-    else:
-        weight_sums = lax.psum_scatter(weight_parts[0], "wide", scatter_dimension=0, tiled=True)
-        weight_sums = weight_sums.astype(jnp.float32)
-        in_count = 4 * width_own
-        attn_in_grad = jnp.moveaxis(weight_sums[:, :in_count].reshape(-1, 4, width_own), 1, 0)
-        self_grad = weight_sums[:, in_count : in_count + width_own].T
-        cross_grad = weight_sums[:, in_count + width_own :].T
+        near = [flipped(after(both_blocks[2 + k], norm_parts[0]), "wide", 2 * k + 2) for k in range(2)]
+        received[0] = after(received[0], near)
     grad_middle, grad_two, last, head, terms = local_kernel(
         functools.partial(norm_back_body, groups, col_count),
         [
@@ -1116,7 +1035,7 @@
         ],
         [
             spot,
-            *norm_parts,
+            *received,
             scaled,
             inverse,
             flat_cotangent,
@@ -1128,10 +1047,27 @@
     )
 
     edges = edge_rows(last, head)
-    grads_two = gathered_grads(grad_two)
-    back_parts = convolve_back(spot, grad_two, edges, kernel_two, row_count, col_count)
+    weight_parts, = local_kernel(
+        functools.partial(weight_grad_body, groups),
+        [bf16_like(C, 6 * width_own)],
+        [
+            spot,
+            after(projected_grads[0], grad_two),
+            *projected_grads[1:],
+            kept_out,
+            crossed,
+            *far([normed]),
+            *far(packs),
+        ],
+        [pltpu.VMEM((groups, *flat), jnp.bfloat16)],
+        24,
+        6 * square,
+    )
+    weight_sums = lax.psum_scatter(weight_parts, "wide", scatter_dimension=0, tiled=True)
+    back_parts = convolve_back(
+        spot, after(grad_two, weight_parts), edges, kernel_two, row_count, col_count
+    )
     back_parts = sent_parts(back_parts)
-    back_parts[0] = after(back_parts[0], text_all, attn_in_grad)
     back, rows = local_kernel(
         functools.partial(second_back_body, groups, pixel_count),
         [f32_like(*flat), f32_like(8, width_own)],
@@ -1140,6 +1076,14 @@
         16,
         0,
     )
+    mixed = local_kernel(
+        functools.partial(mix_body, groups),
+        [bf16_like(*flat)] * groups,
+        [spot, after(kept_out, back), got_all, crossed, *far([maps])],
+        [],
+        16,
+        2 * square,
+    )
     grad_one, last, head, film_rows, second_rows = local_kernel(
         functools.partial(second_input_body, pixel_count, col_count),
         [bf16_like(*flat), bf16_like(*edge), bf16_like(*edge), row_pair, f32_like(8, width_own)],
@@ -1149,20 +1093,40 @@
         0,
     )
     edges = edge_rows(last, head)
-    grads_one = gathered_grads(grad_one)
-    conv_grad = None
+    mixed = sent_parts([after(part, grad_one) for part in mixed])
+    both_grads = lax.all_gather(jnp.stack([grad_one, grad_two]), "wide", axis=1, tiled=True)
+    back_parts = convolve_back(spot, grad_one, edges, kernel_one, row_count, col_count)
     if has_slots():
-        conv_grad = kernel_grad(spot, both_blocks, grads_two, row_count, col_count, 1, conv_grad)
-    time_grad = own_features.astype(jnp.float32)[0][:, None, None] * film_rows[None]
-    text_grad = own_pooled.astype(jnp.float32)[0][:, None, None] * film_rows[None]
-    kv_grad = jnp.einsum(
-        "tx,ptd->pxd", own_text[0].astype(jnp.float32), text_all, precision=highest
-    )
-    back_parts = sent_parts(
-        convolve_back(spot, grad_one, edges, kernel_one, row_count, col_count)
-    )
-    back_parts[0], conv_grad, time_grad, text_grad, kv_grad, result = lax.optimization_barrier(
-        (back_parts[0], conv_grad, time_grad, text_grad, kv_grad, result)
+        distant = flipped(after(both_blocks[4], back_parts[0]), "wide", 6)
+        both_blocks = both_blocks[:2] + near + [distant]
+    attn_in_grad, self_grad, cross_grad = local_kernel(
+        weight_out_body,
+        [f32_like(4, C // lax.axis_size("wide"), width_own)]
+        + [f32_like(width_own, C // lax.axis_size("wide"))] * 2,
+        [spot, after(weight_sums, back_parts[0])],
+        [],
+        16,
+        0,
+    )
+    back_parts = sent_parts(back_parts)
+    film_rows = after(film_rows, back_parts[1])
+    result = middle
+    for part in mixed:
+        result = result + part.astype(jnp.float32)
+    time_grad, text_grad, kv_grad = local_kernel(
+        text_out_body,
+        [
+            f32_like(time_rows, 2, width_own),
+            f32_like(text_rows, 2, width_own),
+            f32_like(2, text_rows, width_own),
+        ],
+        [spot, film_rows, own_features, own_pooled, own_text[0], *far([text_sums])],
+        [],
+        24,
+        4 * TEXT * text_rows * width_own,
+    )
+    back_parts[0], attn_in_grad, result, time_grad = lax.optimization_barrier(
+        (back_parts[0], attn_in_grad, result, time_grad)
     )
     back, rows = local_kernel(
         functools.partial(first_back_body, groups, pixel_count),
@@ -1174,19 +1138,19 @@
     )
     row_parts = part_totals(rows)
     if has_slots():
-        conv_grad = kernel_grad(spot, both_blocks, grads_one, row_count, col_count, 0, conv_grad)
+        conv_grad = kernel_grad(spot, both_blocks, both_grads, row_count, col_count, 1, None)
+        conv_grad = kernel_grad(spot, both_blocks, both_grads, row_count, col_count, 0, conv_grad)
     else:
         conv_grad = jnp.stack(
             [
-                kernel_grad_whole(both_sends[0][:, 0], grads_one, row_count, col_count),
-                kernel_grad_whole(both_sends[0][:, 1], grads_two, row_count, col_count),
+                kernel_grad_whole(both_sends[0][:, k], both_grads[k], row_count, col_count)
+                for k in range(2)
             ]
         )
-    back, conv_grad = lax.optimization_barrier((back, conv_grad))
-    pixels_grad, first_rows = local_kernel(
+    pixels_grad, gain_grad, bias_grad = local_kernel(
         functools.partial(first_input_body, pixel_count),
-        [f32_like(*flat), row_pair],
-        [spot, back, own_pixels, first_sums, affine[0], grad_middle, *row_parts],
+        [f32_like(*flat), row_pair, row_pair],
+        [spot, back, own_pixels, first_sums, affine[0], grad_middle, second_rows, *row_parts],
         [],
         16,
         0,
@@ -1197,8 +1161,8 @@
         conv_grad,
         time_grad,
         text_grad,
-        jnp.stack([first_rows[0], second_rows[0]]),
-        jnp.stack([first_rows[1], second_rows[1]]),
+        gain_grad,
+        bias_grad,
         second_rows[3],
         second_rows[4],
         attn_in_grad,

time: 349 us -> 312 us (0.89)
  waiting for transfers between devices: 124 us -> 94 us
  other arithmetic: 10.5 us -> 3.82 us
    ppermute x67 -> x58, waiting for transfers between devices: 103 us -> 79.4 us  [flipped(): return lax.ppermute(values, axis, [(i, i ^ mask) for i in range(count)])]
    ppermute x3 -> x2, waiting for transfers between devices: 15.9 us -> 2.27 us  [relayed_block(): return lax.ppermute(jnp.where(odd, over_y, over_x), 'wide', far_pairs)]
    all_gather x2 -> x3, waiting for transfers between devices: 0.02 us -> 8.64 us  [the longest x1 8.64 us: shards(): lax.all_gather(jnp.stack([grad_one, grad_two]), 'wide', axis=1, tiled=True)]
    mul x3 -> x0, other arithmetic: 3.73 us -> none  [the longest x1 2.31 us: shards(): own_pooled.astype(jnp.float32)[0][:, None, None] * film_rows[None]]
    ppermute x4, starting transfers between devices: 5.17 us -> 8.68 us  [edge_rows(): above = lax.ppermute(last, 'wide', [(i, i + 1) for i in range(count - 1)])]
    pallas_call x24 -> x23, Pallas kernels: 57.6 us -> 55.2 us  [local_kernel(): pl.pallas_call(body, grid=(1,), out_shape=outs, in_specs=[in_smem] + [in_...]
    unnamed x141 -> x94, local copies, waits for them, and re-layouts: 15.4 us -> 14 us
    ppermute x67 -> x58, starting transfers between devices: 95.5 us -> 95.5 us  [flipped(): return lax.ppermute(values, axis, [(i, i ^ mask) for i in range(count)])]
  transfers between devices with their start and end apart: 83 -> 74, of which waited for: 41 -> 36; matrix products, arithmetic and copies ran while one was open for 4% -> 3% of each run, Pallas kernels for 17% -> 20%
where the time goes in v2:
time: 312 us; the launch traced here: 311 us
  starting transfers between devices  112 us (36%)
  waiting for transfers between devices  94 us (30%)
  Pallas kernels  65.4 us (21%)
  local copies, waits for them, and re-layouts  17.8 us (6%)
  between operations  16.3 us (5%)
  other arithmetic  3.82 us (1%)
    ppermute x58, starting transfers between devices, flipped(): return lax.ppermute(values, axis, [(i, i ^ mask) for i in range(count)])  95.5 us
    ppermute x58, waiting for transfers between devices, flipped(): return lax.ppermute(values, axis, [(i, i ^ mask) for i in range(count)])  79.4 us
    pallas_call x23, Pallas kernels, local_kernel(): pl.pallas_call(body, grid=(1,), out_shape=outs, in_specs=[in_smem] + [in_...  55.2 us
    unnamed x94, local copies, waits for them, and re-layouts  14 us
    pallas_call x2, Pallas kernels, kernel_grad(): pl.pallas_call(functools.partial(kernel_grad_body, width, layer), out_sha...  10.3 us
    ppermute x4, starting transfers between devices, edge_rows(): above = lax.ppermute(last, 'wide', [(i, i + 1) for i in range(count - 1)])  8.68 us
    all_gather x1, waiting for transfers between devices, shards(): lax.all_gather(jnp.stack([grad_one, grad_two]), 'wide', axis=1, tiled=True)  8.64 us
  transfers between devices with their start and end apart: 74, of which 36 were waited for; matrix products, arithmetic and copies ran while one was open for 3% of the time, Pallas kernels for 20%

profile of v2, /device:TPU:0, one launch (start us, length us, event | category | flops | bytes accessed | tf_op | source)
XLA Modules:
  0.0 311.2 jit_solution(8520700230877503926)
XLA Ops:
  30.2 2.6 collective-permute-start.5
  34.2 7.1 %collective-permute-done.5.refs_2_ = bf16[256,256]{1,0:T(8,128)(2,1)S(1)} collective-permute-done((bf16[256,256]{1,0:T(8,128)(2,1)S(1)}, bf16[256,256]{1,0:T(8,128)(2,1)S(1)}, u32[]{:S(2)}, u32[]{:S(2)}) %collective-permute-start.5) | collective-permute-done | bytes 131104 | tf_op jit(solution)/shard_map/ppermute | solution.py:158
  51.1 3.0 collective-permute-start.10
  55.9 7.1 %collective-permute-start.21 = (bf16[9,128,256]{2,1,0:T(8,128)(2,1)}, bf16[9,128,256]{2,1,0:T(8,128)(2,1)}, u32[]{:S(2)}, u32[]{:S(2)}) collective-permute-start(bf16[9,128,256]{2,1,0:T(8,128)(2,1)} %collective-permute-done.17.refs_8_.refs_2_), channel_id=1, source_target_pairs={{0,4},{4,0},{8,12},{12,8},{16,20},{20,16},{24,28},{28,24},{1,5},{5... | collective-permute-start | bytes 1769480 | tf_op jit(solution)/shard_map/ppermute | solution.py:158
  64.2 4.6 %conv_body.2 = (f32[256,256]{1,0:T(8,128)S(1)}, f32[2,256]{1,0:T(2,128)S(1)}, bf16[4,256,128]{2,1,0:T(8,128)(2,1)S(1)}, bf16[4,256,128]{2,1,0:T(8,128)(2,1)S(1)}) custom-call(s32[3]{0:T(128)S(1)} %pad_add_fusion.spot, bf16[256,256]{1,0:T(8,128)(2,1)S(1)} %get-tuple-element.126.refs_0_, bf16[256,256]{1,0:T(8,128)(2,1)S(1)} %collective-permute-done.4.refs_1_, ...), custom_call_target="tpu_custom_call" | custom-call | flops 1207959552 | bytes 6686732 | tf_op jit(solution)/shard_map/conv_body/pallas_call | solution.py:24
  74.5 4.3 %collective-permute-start.14 = (f32[4,256]{1,0:T(4,128)S(1)}, f32[4,256]{1,0:T(4,128)S(1)}, u32[]{:S(2)}, u32[]{:S(2)}) collective-permute-start(f32[4,256]{1,0:T(4,128)S(1)} %fusion.17.refs_0_), channel_id=1, source_target_pairs={{0,16},{4,20},{8,24},{12,28},{16,0},{20,4},{24,8},{28,12},{1,17},{... | collective-permute-start | bytes 12296 | tf_op jit(solution)/shard_map/ppermute | solution.py:158
  91.8 6.5 %collective-permute-done.24.refs_2_ = bf16[256,256]{1,0:T(8,128)(2,1)S(1)} collective-permute-done((bf16[256,256]{1,0:T(8,128)(2,1)S(1)}, bf16[256,256]{1,0:T(8,128)(2,1)S(1)}, u32[]{:S(2)}, u32[]{:S(2)}) %collective-permute-start.24) | collective-permute-done | bytes 131104 | tf_op jit(solution)/shard_map/ppermute | solution.py:158
  99.7 3.0 collective-permute-start.26
  103.9 4.8 %conv_body.3 = (f32[256,256]{1,0:T(8,128)S(1)}, bf16[256,256]{1,0:T(8,128)(2,1)S(1)}, bf16[4,2,256,128]{3,2,1,0:T(8,128)(2,1)S(1)}, bf16[4,2,256,128]{3,2,1,0:T(8,128)(2,1)S(1)}) custom-call(s32[3]{0:T(128)S(1)} %pad_add_fusion.spot, bf16[256,256]{1,0:T(8,128)(2,1)S(1)} %get-tuple-element.131.refs_0_, bf16[256,256]{1,0:T(8,128)(2,1)S(1)} %collective-permute-done.23.refs_1_, ...), custom_call_target="tpu_custom_call" | custom-call | flops 1207959552 | bytes 7864332 | tf_op jit(solution)/shard_map/conv_body/pallas_call | solution.py:24
  114.7 2.7 out_grad_body.1
  117.4 3.1 %collective-permute-start.28 = (bf16[256,128]{1,0:T(8,128)(2,1)S(1)}, bf16[256,128]{1,0:T(8,128)(2,1)S(1)}, u32[]{:S(2)}, u32[]{:S(2)}) collective-permute-start(bf16[256,128]{1,0:T(8,128)(2,1)S(1)} %get-tuple-element.136), channel_id=1, source_target_pairs={{0,4},{4,0},{8,12},{12,8},{16,20},{20,16},{24,28},{28,24},{1,5},{5... | collective-permute-start | bytes 196616 | tf_op jit(solution)/shard_map/ppermute | solution.py:158
  122.0 3.3 %project_body.1 = (bf16[256,128]{1,0:T(8,128)(2,1)S(1)}, bf16[256,256]{1,0:T(8,128)(2,1)S(1)}, bf16[256,384]{1,0:T(8,128)(2,1)S(1)}, bf16[256,256]{1,0:T(8,128)(...) custom-call(s32[3]{0:T(128)S(1)} %pad_add_fusion.spot, ...), custom_call_target="tpu_custom_call" | custom-call | flops 536870912 | bytes 5801996 | tf_op jit(solution)/shard_map/project_body/pallas_call | solution.py:24
  126.7 4.2 %collective-permute-start.32 = (bf16[256,384]{1,0:T(8,128)(2,1)S(1)}, bf16[256,384]{1,0:T(8,128)(2,1)S(1)}, u32[]{:S(2)}, u32[]{:S(2)}) collective-permute-start(bf16[256,384]{1,0:T(8,128)(2,1)S(1)} %get-tuple-element.140), channel_id=1, source_target_pairs={{0,4},{4,0},{8,12},{12,8},{16,20},{20,16},{24,28},{28,24},{1,5},{5... | collective-permute-start | bytes 589832 | tf_op jit(solution)/shard_map/ppermute | solution.py:158
  132.7 5.6 %collective-permute-start.33 = (bf16[512,256]{1,0:T(8,128)(2,1)S(1)}, bf16[512,256]{1,0:T(8,128)(2,1)S(1)}, u32[]{:S(2)}, u32[]{:S(2)}) collective-permute-start(bf16[512,256]{1,0:T(8,128)(2,1)S(1)} %pad_maximum_fusion.5.refs_0_), channel_id=1, source_target_pairs={{0,8},{4,12},{8,0},{12,4},{16,24},{20,28},{24,16},{28,20},{1,9},{5... | collective-permute-start | bytes 786440 | tf_op jit(solution)/shard_map/ppermute | solution.py:158
  138.7 6.2 %collective-permute-done.33.refs_1_ = bf16[512,256]{1,0:T(8,128)(2,1)S(1)} collective-permute-done((bf16[512,256]{1,0:T(8,128)(2,1)S(1)}, bf16[512,256]{1,0:T(8,128)(2,1)S(1)}, u32[]{:S(2)}, u32[]{:S(2)}) %collective-permute-start.33) | collective-permute-done | bytes 262176 | tf_op jit(solution)/shard_map/ppermute | solution.py:158
  145.8 3.2 %cross_body.1 = (bf16[256,256]{1,0:T(8,128)(2,1)S(1)}, bf16[256,256]{1,0:T(8,128)(2,1)S(1)}, bf16[2,128,256]{2,1,0:T(8,128)(2,1)}) custom-call(s32[3]{0:T(128)S(1)} %pad_add_fusion.spot, bf16[256,256]{1,0:T(8,128)(2,1)S(1)} %copy-done.15, bf16[256,256]{1,0:T(8,128)(2,1)S(1)} %get-tuple-element.152.grad, bf16[8,2,128,256]{3,2,1,0:T(8,128)(2,1)} %bitcast.73), custom_call_target="tpu_custom_call" | custom-call | flops 100663296 | bytes 1703948 | tf_op jit(solution)/shard_map/cross_body/pallas_call | solution.py:24
  158.5 5.5 %attend_body.1 = (bf16[512,256]{1,0:T(8,128)(2,1)S(1)}, bf16[512,256]{1,0:T(8,128)(2,1)S(1)}, bf16[512,256]{1,0:T(8,128)(2,1)S(1)}, bf16[512,256]{1,0:T(8,128)(2...) custom-call(s32[3]{0:T(128)S(1)} %pad_add_fusion.spot, ...), custom_call_target="tpu_custom_call" | custom-call | flops 1879048192 | bytes 2752524 | tf_op jit(solution)/shard_map/attend_body/pallas_call | solution.py:24
  167.6 8.6 %collective-permute-done.37.refs_1_ = bf16[512,256]{1,0:T(8,128)(2,1)S(1)} collective-permute-done((bf16[512,256]{1,0:T(8,128)(2,1)S(1)}, bf16[512,256]{1,0:T(8,128)(2,1)S(1)}, u32[]{:S(2)}, u32[]{:S(2)}) %collective-permute-start.37) | collective-permute-done | bytes 262176 | tf_op jit(solution)/shard_map/ppermute | solution.py:158
  176.1 3.9 %collective-permute-done.38.refs_2_ = bf16[512,256]{1,0:T(8,128)(2,1)S(1)} collective-permute-done((bf16[512,256]{1,0:T(8,128)(2,1)S(1)}, bf16[512,256]{1,0:T(8,128)(2,1)S(1)}, u32[]{:S(2)}, u32[]{:S(2)}) %collective-permute-start.38) | collective-permute-done | bytes 262176 | tf_op jit(solution)/shard_map/ppermute | solution.py:158
  184.1 3.6 %project_back_body.1 = (bf16[272,256]{1,0:T(8,128)(2,1)S(1)}, bf16[272,256]{1,0:T(8,128)(2,1)S(1)}, bf16[272,256]{1,0:T(8,128)(2,1)S(1)}, bf16[272,256]{1,0:T(8,128)(2,1)S(1)}) custom-call(s32[3]{0:T(128)S(1)} %pad_add_fusion.spot, bf16[256,128]{1,0:T(8,128)(2,1)S(1)} %get-tuple-element.177.kq, bf16[256,256]{1,0:T(8,128)(2,1)S(1)} %get-tuple-element.163.kp, ...), custom_call_target="tpu_custom_call" | custom-call | flops 536870912 | bytes 5376012 | tf_op jit(solution)/shard_map/project_back_body/pallas_call | solution.py:24
  197.0 8.3 %collective-permute-done.44.refs_2_ = bf16[272,256]{1,0:T(8,128)(2,1)S(1)} collective-permute-done((bf16[272,256]{1,0:T(8,128)(2,1)S(1)}, bf16[272,256]{1,0:T(8,128)(2,1)S(1)}, u32[]{:S(2)}, u32[]{:S(2)}) %collective-permute-start.44) | collective-permute-done | bytes 139296 | tf_op jit(solution)/shard_map/ppermute | solution.py:158
  215.3 4.0 %back_body.2 = (bf16[256,256]{1,0:T(8,128)(2,1)S(1)}, bf16[256,256]{1,0:T(8,128)(2,1)S(1)}, bf16[256,256]{1,0:T(8,128)(2,1)S(1)}, bf16[256,256]{1,0:T(8,128)(2,1)S(1)}) custom-call(s32[3]{0:T(128)S(1)} %pad_add_fusion.spot, bf16[256,256]{1,0:T(8,128)(2,1)S(1)} %get-tuple-element.180.grad, bf16[128,256]{1,0:T(8,128)(2,1)S(1)} %collective-permute-done.46.top, ...), custom_call_target="tpu_custom_call" | custom-call | flops 1207959552 | bytes 5505036 | tf_op jit(solution)/shard_map/back_body/pallas_call | solution.py:24
  224.5 5.1 %collective-permute-done.49.refs_2_ = bf16[256,256]{1,0:T(8,128)(2,1)S(1)} collective-permute-done((bf16[256,256]{1,0:T(8,128)(2,1)S(1)}, bf16[256,256]{1,0:T(8,128)(2,1)S(1)}, u32[]{:S(2)}, u32[]{:S(2)}) %collective-permute-start.49) | collective-permute-done | bytes 131104 | tf_op jit(solution)/shard_map/ppermute | solution.py:158
  232.7 3.6 %collective-permute-start.51 = (f32[8,256]{1,0:T(8,128)S(1)}, f32[8,256]{1,0:T(8,128)S(1)}, u32[]{:S(2)}, u32[]{:S(2)}) collective-permute-start(f32[8,256]{1,0:T(8,128)S(1)} %get-tuple-element.191), channel_id=1, source_target_pairs={{0,4},{4,0},{8,12},{12,8},{16,20},{20,16},{24,28},{28,24},{1,5},{5... | collective-permute-start | bytes 24584 | tf_op jit(solution)/shard_map/ppermute | solution.py:158
  237.2 2.9 collective-permute-start.52
  251.9 3.1 %collective-permute-start.57 = (bf16[256,256]{1,0:T(8,128)(2,1)S(1)}, bf16[256,256]{1,0:T(8,128)(2,1)S(1)}, u32[]{:S(2)}, u32[]{:S(2)}) collective-permute-start(bf16[256,256]{1,0:T(8,128)(2,1)S(1)} %get-tuple-element.202), channel_id=1, source_target_pairs={{0,1},{1,0},{2,3},{3,2},{4,5},{5,4},{6,7},{7,6},{8,9},{9,8},{10,11... | collective-permute-start | bytes 393224 | tf_op jit(solution)/shard_map/ppermute | solution.py:158
  257.5 3.8 %back_body.3 = (bf16[256,256]{1,0:T(8,128)(2,1)S(1)}, bf16[256,256]{1,0:T(8,128)(2,1)S(1)}, bf16[256,256]{1,0:T(8,128)(2,1)S(1)}, bf16[256,256]{1,0:T(8,128)(2,1)S(1)}) custom-call(s32[3]{0:T(128)S(1)} %pad_add_fusion.spot, bf16[256,256]{1,0:T(8,128)(2,1)S(1)} %get-tuple-element.192.grad, bf16[128,256]{1,0:T(8,128)(2,1)S(1)} %collective-permute-done.55.top, ...), custom_call_target="tpu_custom_call" | custom-call | flops 1207959552 | bytes 5505036 | tf_op jit(solution)/shard_map/back_body/pallas_call | solution.py:24
  261.3 4.5 %collective-permute-start.67 = (bf16[2,2,256,128]{3,2,1,0:T(8,128)(2,1)S(1)}, bf16[2,2,256,128]{3,2,1,0:T(8,128)(2,1)}, u32[]{:S(2)}, u32[]{:S(2)}) collective-permute-start(bf16[2,2,256,128]{3,2,1,0:T(8,128)(2,1)S(1)} %get-tuple-element.222), channel_id=1, source_target_pairs={{0,24},{4,28},{8,16},{12,20},{16,8},{20,12},{24,0},{28,4},{1,25},{... | collective-permute-start | bytes 786440 | tf_op jit(solution)/shard_map/ppermute | solution.py:158
  271.6 3.4 %text_out_body.1 = (f32[128,2,256]{2,1,0:T(2,128)}, f32[512,2,256]{2,1,0:T(2,128)}, f32[2,512,256]{2,1,0:T(8,128)}) custom-call(s32[3]{0:T(128)S(1)} %pad_add_fusion.spot, f32[2,256]{1,0:T(2,128)S(1)} %get-tuple-element.209.film, bf16[1,128]{1,0:T(2,128)(2,1)S(1)} %copy-done.25, bf16[1,512]{1,0:T(2,128)(2,1)S(1)} %dynamic_slice.11.pooled, ...), custom_call_target="tpu_custom_call" | custom-call | flops 67108864 | bytes 3542284 | tf_op jit(solution)/shard_map/text_out_body/pallas_call | solution.py:24
  280.2 8.6 %all-gather.11.cloned.1.call-done.refs_3_ = bf16[2,2048,256]{2,1,0:T(8,128)(2,1)} async-done(((bf16[2,256,256]{2,1,0:T(8,128)(2,1)}), bf16[2,2048,256]{2,1,0:T(8,128)(2,1)}) %all-gather.11.cloned.1.call-update) | async-done | bytes 2097168 | tf_op jit(solution)/shard_map/all_gather | solution.py:1097
  288.8 5.1 %shard_map.255.refs_4_ = f32[2,9,128,256]{3,2,1,0:T(8,128)} custom-call(s32[3]{0:T(128)S(1)} %pad_add_fusion.spot, bf16[4,2,256,128]{3,2,1,0:T(8,128)(2,1)} %copy-done.2, bf16[4,2,256,128]{3,2,1,0:T(8,128)(2,1)} %copy-done.33, bf16[2,2,256,128]{3,2,1,0:T(8,128)(2,1)} %copy-done.37, bf16[2,2,256,128]{3,2,1,0:T(8,128)(2,1)} %copy-done.36, ...), custom_call_target="tpu_custom_call" | custom-call | flops 1207959552 | bytes 4194304 | tf_op jit(solution)/shard_map/pallas_call | solution.py:307
  297.5 5.1 %shard_map.256 = f32[2,9,128,256]{3,2,1,0:T(8,128)} custom-call(s32[3]{0:T(128)S(1)} %pad_add_fusion.spot, bf16[4,2,256,128]{3,2,1,0:T(8,128)(2,1)} %copy-done.2, bf16[4,2,256,128]{3,2,1,0:T(8,128)(2,1)} %copy-done.33, bf16[2,2,256,128]{3,2,1,0:T(8,128)(2,1)} %copy-done.37, bf16[2,2,256,128]{3,2,1,0:T(8,128)(2,1)} %copy-done.36, ...), custom_call_target="tpu_custom_call", output_to_operand_aliasing={{}: (7, {})} | custom-call | flops 1207959552 | bytes 4194304 | tf_op jit(solution)/shard_map/pallas_call | solution.py:307
  (286 shorter events, 144.4 us)
Async XLA Ops:
  7.2 57.0 %all-gather.9.cloned.1.call-start = ((), (), s32[]{:S(2)}) async-start(), calls=%async_computation.1 | async-start | bytes 5308416 | tf_op jit(solution)/shard_map/all_gather | solution.py:181
  9.4 105.4 %all-gather.13.cloned.1.call-start = ((), (), s32[]{:S(2)}) async-start(), calls=%async_computation.4 | async-start | bytes 3538944 | tf_op jit(solution)/shard_map/all_gather | solution.py:181
  12.2 132.7 %all-gather.15.cloned.1.call-start = ((), (), s32[]{:S(2)}) async-start(), calls=%async_computation.5 | async-start | bytes 1179648 | tf_op jit(solution)/shard_map/all_gather | solution.py:936
  27.5 20.0 %collective-permute-start.16 = (bf16[9,128,256]{2,1,0:T(8,128)(2,1)S(1)}, bf16[9,128,256]{2,1,0:T(8,128)(2,1)}, u32[]{:S(2)}, u32[]{:S(2)}) collective-permute-start(bf16[9,128,256]{2,1,0:T(8,128)(2,1)S(1)} %slice_bitcast_fusion.refs_6_.refs_0_), channel_id=1, source_target_pairs={{0,8},{4,12},{8,0},{12,4},{16,24},{20,28},{24,16},{28,20},{1,9},{5... | collective-permute-start | bytes 1769480 | tf_op jit(solution)/shard_map/ppermute | solution.py:158
  28.1 20.3 %collective-permute-start.17 = (bf16[9,128,256]{2,1,0:T(8,128)(2,1)S(1)}, bf16[9,128,256]{2,1,0:T(8,128)(2,1)}, u32[]{:S(2)}, u32[]{:S(2)}) collective-permute-start(bf16[9,128,256]{2,1,0:T(8,128)(2,1)S(1)} %slice_bitcast_fusion.refs_6_.refs_0_), channel_id=1, source_target_pairs={{0,16},{4,20},{8,24},{12,28},{16,0},{20,4},{24,8},{28,12},{1,17},{... | collective-permute-start | bytes 1769480 | tf_op jit(solution)/shard_map/ppermute | solution.py:158
  30.2 11.1 %collective-permute-start.5 = (bf16[256,256]{1,0:T(8,128)(2,1)S(1)}, bf16[256,256]{1,0:T(8,128)(2,1)S(1)}, u32[]{:S(2)}, u32[]{:S(2)}) collective-permute-start(bf16[256,256]{1,0:T(8,128)(2,1)S(1)} %get-tuple-element.126.refs_0_), channel_id=1, source_target_pairs={{0,2},{1,3},{2,0},{3,1},{4,6},{5,7},{6,4},{7,5},{8,10},{9,11},{10,... | collective-permute-start | bytes 393224 | tf_op jit(solution)/shard_map/ppermute | solution.py:158
  43.3 12.1 %collective-permute-start.8 = (bf16[272,256]{1,0:T(8,128)(2,1)S(1)}, bf16[272,256]{1,0:T(8,128)(2,1)S(1)}, u32[]{:S(2)}, u32[]{:S(2)}) collective-permute-start(bf16[272,256]{1,0:T(8,128)(2,1)S(1)} %get-tuple-element.135.refs_0_.refs_4_), channel_id=1, source_target_pairs={{0,2},{1,3},{2,0},{3,1},{4,6},{5,7},{6,4},{7,5},{8,10},{9,11},{10,... | collective-permute-start | bytes 417800 | tf_op jit(solution)/shard_map/ppermute | solution.py:158
  44.4 11.4 %collective-permute-start.9 = (bf16[272,256]{1,0:T(8,128)(2,1)S(1)}, bf16[272,256]{1,0:T(8,128)(2,1)S(1)}, u32[]{:S(2)}, u32[]{:S(2)}) collective-permute-start(bf16[272,256]{1,0:T(8,128)(2,1)S(1)} %get-tuple-element.135.refs_0_.refs_4_), channel_id=1, source_target_pairs={{0,3},{1,2},{2,1},{3,0},{4,7},{5,6},{6,5},{7,4},{8,11},{9,10},{10,... | collective-permute-start | bytes 417800 | tf_op jit(solution)/shard_map/ppermute | solution.py:158
  49.5 13.5 %collective-permute-start.18 = (bf16[9,128,256]{2,1,0:T(8,128)(2,1)S(1)}, bf16[9,128,256]{2,1,0:T(8,128)(2,1)}, u32[]{:S(2)}, u32[]{:S(2)}) collective-permute-start(bf16[9,128,256]{2,1,0:T(8,128)(2,1)S(1)} %broadcast_select_fusion), channel_id=1, source_target_pairs={{0,16},{4,12},{8,24},{12,4},{16,0},{20,28},{24,8},{28,20},{1,17},{... | collective-permute-start | bytes 1769480 | tf_op jit(solution)/shard_map/ppermute | solution.py:164
  51.1 13.1 %collective-permute-start.10 = (bf16[128,1024]{1,0:T(8,128)(2,1)S(1)}, bf16[128,1024]{1,0:T(8,128)(2,1)S(1)}, u32[]{:S(2)}, u32[]{:S(2)}) collective-permute-start(bf16[128,1024]{1,0:T(8,128)(2,1)S(1)} %pad_maximum_fusion.1), channel_id=1, source_target_pairs={{0,4},{4,8},{8,12},{12,16},{16,20},{20,24},{24,28},{1,5},{5,9},{9,... | collective-permute-start | bytes 786440 | tf_op jit(solution)/shard_map/ppermute | solution.py:213
  55.4 30.9 %collective-permute-start.19 = (bf16[9,128,256]{2,1,0:T(8,128)(2,1)S(1)}, bf16[9,128,256]{2,1,0:T(8,128)(2,1)}, u32[]{:S(2)}, u32[]{:S(2)}) collective-permute-start(bf16[9,128,256]{2,1,0:T(8,128)(2,1)S(1)} %slice_bitcast_fusion.refs_6_.refs_0_), channel_id=1, source_target_pairs={{0,4},{4,0},{8,12},{12,8},{16,20},{20,16},{24,28},{28,24},{1,5},{5... | collective-permute-start | bytes 1769480 | tf_op jit(solution)/shard_map/ppermute | solution.py:158
  55.8 30.6 %collective-permute-start.20 = (bf16[9,128,256]{2,1,0:T(8,128)(2,1)}, bf16[9,128,256]{2,1,0:T(8,128)(2,1)}, u32[]{:S(2)}, u32[]{:S(2)}) collective-permute-start(bf16[9,128,256]{2,1,0:T(8,128)(2,1)} %collective-permute-done.16.refs_7_.refs_1_), channel_id=1, source_target_pairs={{0,4},{4,0},{8,12},{12,8},{16,20},{20,16},{24,28},{28,24},{1,5},{5... | collective-permute-start | bytes 1769480 | tf_op jit(solution)/shard_map/ppermute | solution.py:158
  55.9 30.4 %collective-permute-start.21 = (bf16[9,128,256]{2,1,0:T(8,128)(2,1)}, bf16[9,128,256]{2,1,0:T(8,128)(2,1)}, u32[]{:S(2)}, u32[]{:S(2)}) collective-permute-start(bf16[9,128,256]{2,1,0:T(8,128)(2,1)} %collective-permute-done.17.refs_8_.refs_2_), channel_id=1, source_target_pairs={{0,4},{4,0},{8,12},{12,8},{16,20},{20,16},{24,28},{28,24},{1,5},{5... | collective-permute-start | bytes 1769480 | tf_op jit(solution)/shard_map/ppermute | solution.py:158
  63.0 23.3 %collective-permute-start.22 = (bf16[9,128,256]{2,1,0:T(8,128)(2,1)}, bf16[9,128,256]{2,1,0:T(8,128)(2,1)}, u32[]{:S(2)}, u32[]{:S(2)}) collective-permute-start(bf16[9,128,256]{2,1,0:T(8,128)(2,1)} %collective-permute-done.18.refs_9_.refs_3_), channel_id=1, source_target_pairs={{0,4},{4,0},{8,12},{12,8},{16,20},{20,16},{24,28},{28,24},{1,5},{5... | collective-permute-start | bytes 1769480 | tf_op jit(solution)/shard_map/ppermute | solution.py:158
  90.9 180.7 %all-gather.17.cloned.1.call-start = ((), (), s32[]{:S(2)}) async-start(), calls=%async_computation.6 | async-start | bytes 1179648 | tf_op jit(solution)/shard_map/all_gather | solution.py:996
  110.3 11.1 %collective-permute-start.29 = (bf16[256,256]{1,0:T(8,128)(2,1)S(1)}, bf16[256,256]{1,0:T(8,128)(2,1)S(1)}, u32[]{:S(2)}, u32[]{:S(2)}) collective-permute-start(bf16[256,256]{1,0:T(8,128)(2,1)S(1)} %get-tuple-element.137.refs_0_), channel_id=1, source_target_pairs={{0,1},{1,0},{2,3},{3,2},{4,5},{5,4},{6,7},{7,6},{8,9},{9,8},{10,11... | collective-permute-start | bytes 393224 | tf_op jit(solution)/shard_map/ppermute | solution.py:158
  132.7 12.2 %collective-permute-start.33 = (bf16[512,256]{1,0:T(8,128)(2,1)S(1)}, bf16[512,256]{1,0:T(8,128)(2,1)S(1)}, u32[]{:S(2)}, u32[]{:S(2)}) collective-permute-start(bf16[512,256]{1,0:T(8,128)(2,1)S(1)} %pad_maximum_fusion.5.refs_0_), channel_id=1, source_target_pairs={{0,8},{4,12},{8,0},{12,4},{16,24},{20,28},{24,16},{28,20},{1,9},{5... | collective-permute-start | bytes 786440 | tf_op jit(solution)/shard_map/ppermute | solution.py:158
  138.3 11.1 %collective-permute-start.35 = (bf16[512,256]{1,0:T(8,128)(2,1)S(1)}, bf16[512,256]{1,0:T(8,128)(2,1)S(1)}, u32[]{:S(2)}, u32[]{:S(2)}) collective-permute-start(bf16[512,256]{1,0:T(8,128)(2,1)S(1)} %pad_maximum_fusion.5.refs_0_), channel_id=1, source_target_pairs={{0,16},{4,20},{8,24},{12,28},{16,0},{20,4},{24,8},{28,12},{1,17},{... | collective-permute-start | bytes 786440 | tf_op jit(solution)/shard_map/ppermute | solution.py:158
  149.1 125.9 %reduce-scatter.2.cloned.1.call-start = ((), (), s32[]{:S(2)}) async-start(), calls=%async_computation.2 | async-start | bytes 3538944 | tf_op jit(solution)/shard_map/reduce_scatter | solution.py:1066
  164.0 12.1 %collective-permute-start.37 = (bf16[512,256]{1,0:T(8,128)(2,1)S(1)}, bf16[512,256]{1,0:T(8,128)(2,1)S(1)}, u32[]{:S(2)}, u32[]{:S(2)}) collective-permute-start(bf16[512,256]{1,0:T(8,128)(2,1)S(1)} %get-tuple-element.160), channel_id=1, source_target_pairs={{0,8},{4,12},{8,0},{12,4},{16,24},{20,28},{24,16},{28,20},{1,9},{5... | collective-permute-start | bytes 786440 | tf_op jit(solution)/shard_map/ppermute | solution.py:158
  165.8 14.2 %collective-permute-start.38 = (bf16[512,256]{1,0:T(8,128)(2,1)S(1)}, bf16[512,256]{1,0:T(8,128)(2,1)S(1)}, u32[]{:S(2)}, u32[]{:S(2)}) collective-permute-start(bf16[512,256]{1,0:T(8,128)(2,1)S(1)} %get-tuple-element.161), channel_id=1, source_target_pairs={{0,16},{4,20},{8,24},{12,28},{16,0},{20,4},{24,8},{28,12},{1,17},{... | collective-permute-start | bytes 786440 | tf_op jit(solution)/shard_map/ppermute | solution.py:158
  166.4 15.4 %collective-permute-start.39 = (bf16[512,256]{1,0:T(8,128)(2,1)S(1)}, bf16[512,256]{1,0:T(8,128)(2,1)S(1)}, u32[]{:S(2)}, u32[]{:S(2)}) collective-permute-start(bf16[512,256]{1,0:T(8,128)(2,1)S(1)} %get-tuple-element.162), channel_id=1, source_target_pairs={{0,24},{4,28},{8,16},{12,20},{16,8},{20,12},{24,0},{28,4},{1,25},{... | collective-permute-start | bytes 786440 | tf_op jit(solution)/shard_map/ppermute | solution.py:158
  192.0 13.3 %collective-permute-start.44 = (bf16[272,256]{1,0:T(8,128)(2,1)S(1)}, bf16[272,256]{1,0:T(8,128)(2,1)S(1)}, u32[]{:S(2)}, u32[]{:S(2)}) collective-permute-start(bf16[272,256]{1,0:T(8,128)(2,1)S(1)} %get-tuple-element.173), channel_id=1, source_target_pairs={{0,2},{1,3},{2,0},{3,1},{4,6},{5,7},{6,4},{7,5},{8,10},{9,11},{10,... | collective-permute-start | bytes 417800 | tf_op jit(solution)/shard_map/ppermute | solution.py:158
  193.0 12.3 %collective-permute-start.45 = (bf16[272,256]{1,0:T(8,128)(2,1)S(1)}, bf16[272,256]{1,0:T(8,128)(2,1)S(1)}, u32[]{:S(2)}, u32[]{:S(2)}) collective-permute-start(bf16[272,256]{1,0:T(8,128)(2,1)S(1)} %get-tuple-element.174), channel_id=1, source_target_pairs={{0,3},{1,2},{2,1},{3,0},{4,7},{5,6},{6,5},{7,4},{8,11},{9,10},{10,... | collective-permute-start | bytes 417800 | tf_op jit(solution)/shard_map/ppermute | solution.py:158
  210.1 78.7 %all-gather.11.cloned.1.call-start = ((), (), s32[]{:S(2)}) async-start(), calls=%async_computation.3 | async-start | bytes 2359296 | tf_op jit(solution)/shard_map/all_gather | solution.py:1097
  246.6 10.8 %collective-permute-start.55 = (bf16[128,256]{1,0:T(8,128)(2,1)S(1)}, bf16[128,256]{1,0:T(8,128)(2,1)S(1)}, u32[]{:S(2)}, u32[]{:S(2)}) collective-permute-start(bf16[128,256]{1,0:T(8,128)(2,1)S(1)} %get-tuple-element.193), channel_id=1, source_target_pairs={{0,4},{4,8},{8,12},{12,16},{16,20},{20,24},{24,28},{1,5},{5,9},{9,... | collective-permute-start | bytes 196616 | tf_op jit(solution)/shard_map/ppermute | solution.py:213
  251.9 15.6 %collective-permute-start.57 = (bf16[256,256]{1,0:T(8,128)(2,1)S(1)}, bf16[256,256]{1,0:T(8,128)(2,1)S(1)}, u32[]{:S(2)}, u32[]{:S(2)}) collective-permute-start(bf16[256,256]{1,0:T(8,128)(2,1)S(1)} %get-tuple-element.202), channel_id=1, source_target_pairs={{0,1},{1,0},{2,3},{3,2},{4,5},{5,4},{6,7},{7,6},{8,9},{9,8},{10,11... | collective-permute-start | bytes 393224 | tf_op jit(solution)/shard_map/ppermute | solution.py:158
  255.0 14.3 %collective-permute-start.58 = (bf16[256,256]{1,0:T(8,128)(2,1)S(1)}, bf16[256,256]{1,0:T(8,128)(2,1)S(1)}, u32[]{:S(2)}, u32[]{:S(2)}) collective-permute-start(bf16[256,256]{1,0:T(8,128)(2,1)S(1)} %get-tuple-element.204), channel_id=1, source_target_pairs={{0,2},{1,3},{2,0},{3,1},{4,6},{5,7},{6,4},{7,5},{8,10},{9,11},{10,... | collective-permute-start | bytes 393224 | tf_op jit(solution)/shard_map/ppermute | solution.py:158
  256.0 14.8 %collective-permute-start.59 = (bf16[256,256]{1,0:T(8,128)(2,1)S(1)}, bf16[256,256]{1,0:T(8,128)(2,1)S(1)}, u32[]{:S(2)}, u32[]{:S(2)}) collective-permute-start(bf16[256,256]{1,0:T(8,128)(2,1)S(1)} %get-tuple-element.206), channel_id=1, source_target_pairs={{0,3},{1,2},{2,1},{3,0},{4,7},{5,6},{6,5},{7,4},{8,11},{9,10},{10,... | collective-permute-start | bytes 393224 | tf_op jit(solution)/shard_map/ppermute | solution.py:158
  261.3 18.9 %collective-permute-start.67 = (bf16[2,2,256,128]{3,2,1,0:T(8,128)(2,1)S(1)}, bf16[2,2,256,128]{3,2,1,0:T(8,128)(2,1)}, u32[]{:S(2)}, u32[]{:S(2)}) collective-permute-start(bf16[2,2,256,128]{3,2,1,0:T(8,128)(2,1)S(1)} %get-tuple-element.222), channel_id=1, source_target_pairs={{0,24},{4,28},{8,16},{12,20},{16,8},{20,12},{24,0},{28,4},{1,25},{... | collective-permute-start | bytes 786440 | tf_op jit(solution)/shard_map/ppermute | solution.py:158
  267.4 11.5 %collective-permute-start.61 = (bf16[256,256]{1,0:T(8,128)(2,1)S(1)}, bf16[256,256]{1,0:T(8,128)(2,1)S(1)}, u32[]{:S(2)}, u32[]{:S(2)}) collective-permute-start(bf16[256,256]{1,0:T(8,128)(2,1)S(1)} %get-tuple-element.214), channel_id=1, source_target_pairs={{0,2},{1,3},{2,0},{3,1},{4,6},{5,7},{6,4},{7,5},{8,10},{9,11},{10,... | collective-permute-start | bytes 393224 | tf_op jit(solution)/shard_map/ppermute | solution.py:158
  280.0 14.0 %collective-permute-start.63 = (f32[2,256]{1,0:T(2,128)S(1)}, f32[2,256]{1,0:T(2,128)S(1)}, u32[]{:S(2)}, u32[]{:S(2)}) collective-permute-start(f32[2,256]{1,0:T(2,128)S(1)} %get-tuple-element.220), channel_id=1, source_target_pairs={{0,4},{4,0},{8,12},{12,8},{16,20},{20,16},{24,28},{28,24},{1,5},{5... | collective-permute-start | bytes 6152 | tf_op jit(solution)/shard_map/ppermute | solution.py:158
  (88 other events, 772.8 us)
Sparse Core Ops, SparseCore 0:
  10.5 51.1 all-gather.8
  64.1 31.6 all-gather.12
  98.3 23.4 all-gather.14
  149.2 26.4 all-gather.16
  210.3 46.8 reduce-scatter.1
  259.6 29.1 all-gather.10

commit v3 on v2

--- a/solution.py
+++ b/solution.py
@@ -80,7 +80,7 @@
 
 def conv_body(groups, parts, count, rows, width, spot, *refs):
     pieces = refs[:groups]
-    top, bottom = refs[groups : groups + 2]
+    near, far_row = refs[groups : groups + 2]
     weights = Weights(refs[groups + 2 : groups + 2 + parts], spot, groups)
     source, *rest = refs[groups + 2 + parts :]
     earlier, rest = rest[:count], rest[count:]
@@ -94,7 +94,7 @@
         block = lax.bitwise_xor(spot[1], mask)
         own = pieces[mask][...]
         lanes = slice(mask * span, (mask + 1) * span)
-        framed = jnp.concatenate([top[:, lanes], own, bottom[:, lanes]], axis=0)
+        framed = framed_rows(near[:, lanes], far_row[:, lanes], own, weights.odd)
         for column, values in enumerate(turned(weights.ordered(framed), width)):
             frame[block, column] = values
     total_sum = jnp.zeros(first_out.shape, jnp.float32)
@@ -123,11 +123,11 @@
         second_out[...] = middle.astype(jnp.bfloat16)
 
 
-def back_body(groups, rows, width, spot, grad, top, bottom, *refs):
+def back_body(groups, rows, width, spot, grad, near, far_row, *refs):
     frame, held = refs[-2:]
     outs = refs[-2 - groups : -2]
     weights = Weights(refs[: -2 - groups], spot, groups)
-    framed = jnp.concatenate([top[...], grad[...], bottom[...]], axis=0)
+    framed = framed_rows(near[...], far_row[...], grad[...], weights.odd)
     for column, values in enumerate(turned(framed, width)):
         frame[column] = values
     for chunk in range(groups):
@@ -149,6 +149,10 @@
     return jax.ShapeDtypeStruct(shape, jnp.bfloat16)
 
 
+def far_like(shape):
+    return pltpu.HBM(shape.shape, shape.dtype)
+
+
 def f32_like(*shape):
     return jax.ShapeDtypeStruct(shape, jnp.float32)
 
@@ -208,11 +212,18 @@
     return [values] + [flipped(values, "tensor", mask) for mask in range(1, count)]
 
 
-def edge_rows(last, first):
+def edge_rows(near, far_row):
     count = lax.axis_size("wide")
-    above = lax.ppermute(last, "wide", [(i, i + 1) for i in range(count - 1)])
-    below = lax.ppermute(first, "wide", [(i + 1, i) for i in range(count - 1)])
-    return above, below
+    beyond = [(i, i + 1) for i in range(1, count - 1, 2)]
+    beyond += [(i + 1, i) for i in range(1, count - 1, 2)]
+    from_far = lax.ppermute(far_row, "wide", beyond)
+    return flipped(after(near, far_row), "wide", 1), from_far
+
+
+def framed_rows(near, far_row, own, odd):
+    top = jnp.where(odd, near, far_row)
+    bottom = jnp.where(odd, far_row, near)
+    return jnp.concatenate([top, own, bottom], axis=0)
 
 
 def convolve(spot, pieces, edges, kernel, source, second_shape, earlier, rows, width):
@@ -231,10 +242,10 @@
 
 
 def piece_edges(pieces, width):
-    return edge_rows(
-        jnp.concatenate([piece[-width:] for piece in pieces], axis=1),
-        jnp.concatenate([piece[:width] for piece in pieces], axis=1),
-    )
+    odd = lax.rem(lax.axis_index("wide"), 2) == 1
+    last = jnp.concatenate([piece[-width:] for piece in pieces], axis=1)
+    first = jnp.concatenate([piece[:width] for piece in pieces], axis=1)
+    return edge_rows(jnp.where(odd, first, last), jnp.where(odd, last, first))
 
 
 def convolve_back(spot, grad, edges, kernel, rows, width):
@@ -256,69 +267,50 @@
     return [parts[0]] + [flipped(parts[mask], "tensor", mask) for mask in range(1, len(parts))]
 
 
-def pair_blocks_body(spot, kept, got, *outs):
-    for index, out in enumerate(outs):
-        out[0] = kept[index + 1]
-        out[1] = got[index + 1]
-
-
-def kernel_grad_body(width, layer, spot, kept, got, *refs):
-    *pairs, grads = refs[:4]
-    out, turned_all = refs[-2:]
+def kernel_grad_body(width, spot, kept, got, *refs):
+    *pairs, grads, out, turned_all = refs
+    layer = pl.program_id(0)
     area, span = kept.shape[2:]
     depth = 8 * area
     turned_all[:, :width] = jnp.zeros((3 * span, width), jnp.bfloat16)
     turned_all[:, depth + width :] = jnp.zeros((3 * span, width), jnp.bfloat16)
     pieces = [kept[0, layer], got[0, layer]]
     pieces += [pair[core, layer] for pair in pairs for core in range(2)]
+    lane = lax.broadcasted_iota(jnp.int32, (span, width), 1)
     for mask, piece in enumerate(pieces):
         start = pl.multiple_of(lax.bitwise_xor(spot[0], mask) * area, area)
-        for column, values in enumerate(turned(piece, width)):
-            turned_all[column * span : (column + 1) * span, pl.ds(start + width, area)] = flat_turn(
-                values
-            )
+        flat = jnp.transpose(piece.astype(jnp.float32))
+        for row in range(area // width):
+            center = flat[:, row * width : (row + 1) * width]
+            before = jnp.where(lane == 0, 0.0, pltpu.roll(center, 1, 1))
+            behind = jnp.where(lane == width - 1, 0.0, pltpu.roll(center, width - 1, 1))
+            lanes = pl.ds(start + (row + 1) * width, width)
+            for column, values in enumerate((before, center, behind)):
+                turned_all[column * span : (column + 1) * span, lanes] = values.astype(jnp.bfloat16)
     for row in range(3):
-        product = jnp.dot(
-            turned_all[:, row * width : row * width + depth],
-            grads[layer],
-            preferred_element_type=jnp.float32,
-        )
+        product = dot(turned_all[:, row * width : row * width + depth], grads[0])
         for column in range(3):
             out[0, 3 * row + column] = product[column * span : (column + 1) * span, :]
 
 
-def swapped_blocks(spot, kept, sent):
-    got = flipped(sent, "wide", 1)
-    pairs = local_kernel(
-        pair_blocks_body, [bf16_like(2, *kept.shape[1:])] * 3, [spot, *far([kept, got])], [], 16, 0
-    )
-    return [kept, got, *pairs]
-
-
-def kernel_grad(spot, pieces, grads, rows, width, layer, earlier):
+def kernel_grad(spot, pieces, grads, width):
     span = pieces[0].shape[3]
     depth, columns = grads.shape[1:]
-    operands = [spot, *far(pieces), *far([grads])]
-    specs = [in_smem] + [in_vmem] * (len(operands) - 1)
-    shape = f32_like(2, 9, span, columns)
-    if earlier is not None:
-        operands.append(earlier)
-        specs.append(pl.BlockSpec(memory_space=pl.ANY))
     return pl.pallas_call(
-        functools.partial(kernel_grad_body, width, layer),
-        out_shape=shape,
-        in_specs=specs,
-        grid=(1,),
-        out_specs=pl.BlockSpec((1, 9, span, columns), lambda i: (layer, 0, 0, 0)),
-        scratch_shapes=[
-            pltpu.VMEM((3 * span, depth + 2 * width), jnp.bfloat16),
-        ],
-        input_output_aliases={} if earlier is None else {len(operands) - 1: 0},
+        functools.partial(kernel_grad_body, width),
+        out_shape=f32_like(2, 9, span, columns),
+        grid=(2,),
+        in_specs=[in_smem]
+        + [in_vmem] * len(pieces)
+        + [pl.BlockSpec((1, depth, columns), lambda i: (i, 0, 0))],
+        out_specs=pl.BlockSpec((1, 9, span, columns), lambda i: (i, 0, 0, 0)),
+        scratch_shapes=[pltpu.VMEM((3 * span, depth + 2 * width), jnp.bfloat16)],
         compiler_params=pltpu.CompilerParams(vmem_limit_bytes=24 * MIB),
         cost_estimate=pl.CostEstimate(
-            flops=2 * 9 * depth * span * columns, bytes_accessed=4 * MIB, transcendentals=0
+            flops=4 * 9 * depth * span * columns, bytes_accessed=6 * MIB, transcendentals=0
         ),
-    )(*operands)
+        name="kernel_grad_body",
+    )(spot, *far(pieces), *far([grads]))
 
 
 def kernel_grad_whole(send, grads, rows, width):
@@ -463,7 +455,7 @@
 
 
 def second_input_body(pixel_count, width, spot, back, inner, sums, film, affine, *refs):
-    *parts, low, last, first, film_rows, rows = refs
+    *parts, low, near, far_row, film_rows, rows = refs
     rows[...] = sum_of_parts(parts)
     slope, shift, gain = 1.0 + film[0:1], film[1:2], affine[0:1]
     plain_sum, square_sum = sums[0:1], sums[1:2]
@@ -474,8 +466,9 @@
     grad = inverse * (back[...] * gain - plain - scaled * dotted)
     grad_low = (grad * slope).astype(jnp.bfloat16)
     low[...] = grad_low
-    last[...] = grad_low[-width:]
-    first[...] = grad_low[:width]
+    odd = lax.rem(spot[0], 2) == 1
+    near[...] = jnp.where(odd, grad_low[:width], grad_low[-width:])
+    far_row[...] = jnp.where(odd, grad_low[-width:], grad_low[:width])
     scaled_sum = inverse * (lifted_sum - pixel_count * center)
     scaled_inner = inverse * (slope * square_sum + (shift - center) * plain_sum)
     film_rows[0:1, :] = inverse * (
@@ -624,11 +617,9 @@
         kv_grad[part] = dot(turned_text, high) + dot(turned_text, low)
 
 
-def mix_body(groups, spot, kept, received, crossed, maps, *outs):
+def mix_body(groups, spot, kept, other, crossed, maps, *outs):
     weights = Weights([maps], spot, groups)
-    attended = heads_joined(
-        kept[...], received[:, 3 * HEAD_DIM :], lax.rem(spot[0], 2) == 1
-    )
+    attended = heads_joined(kept[...], other[...], lax.rem(spot[0], 2) == 1)
     for mask in range(groups):
         total_sum = dot_last(attended, weights.tap(mask, 4))
         total_sum += dot_last(crossed[...], weights.tap(mask, 5))
@@ -655,77 +646,13 @@
 score_scale = HEAD_DIM ** (-0.5)
 
 
-def attend_body(count, spot, kept_query, got, kept_grad, got_grad, *refs):
-    blocks, parts = refs[:count], refs[count : 2 * count]
-    keep_out, send_out, keep_query, send_query = refs[2 * count :]
-    query = jnp.concatenate([kept_query[...], got[:, 2 * HEAD_DIM :]], axis=0)
-    grad = jnp.concatenate([kept_grad[...], got_grad[...]], axis=0)
-    queries = query.shape[0]
-
-    def forward(state, block, index, start):
-        top, weight_sum, weighted = state
-        scores = dot_last(block[:, :HEAD_DIM], query) * score_scale
-        raised = jnp.maximum(top, jnp.max(scores, axis=0, keepdims=True))
-        rescale = jnp.exp(top - raised)
-        weights = jnp.exp(scores - raised)
-        weight_sum = weight_sum * rescale + jnp.sum(weights, axis=0, keepdims=True)
-        values = block[:, HEAD_DIM:]
-        weighted = weighted * rescale + dot_first(values, weights.astype(jnp.bfloat16))
-        return raised, weight_sum, weighted
-
-    top, weight_sum, weighted = over_rows(
-        blocks,
-        forward,
-        (
-            jnp.full((1, queries), -1e30, jnp.float32),
-            jnp.zeros((1, queries), jnp.float32),
-            jnp.zeros((HEAD_DIM, queries), jnp.float32),
-        ),
-    )
-    attended = weighted / weight_sum
-    delta = jnp.sum(attended * jnp.transpose(grad.astype(jnp.float32)), axis=0, keepdims=True)
-    log_sum = top + jnp.log(weight_sum)
-
-    def backward(state, block, index, start):
-        keys, values = block[:, :HEAD_DIM], block[:, HEAD_DIM:]
-        probs = jnp.exp(dot_last(keys, query) * score_scale - log_sum)
-        grad_values = dot(probs.astype(jnp.bfloat16), grad)
-        grad_scores = (probs * (dot_last(values, grad) - delta)).astype(jnp.bfloat16)
-        grad_keys = dot(grad_scores, query) * score_scale
-        rows = pl.ds(start if isinstance(start, int) else pl.multiple_of(start, 512), block.shape[0])
-        parts[index][rows, :] = jnp.concatenate([grad_keys, grad_values], axis=1).astype(
-            jnp.bfloat16
-        )
-        return state + dot_first(keys, grad_scores)
-
-    flat = over_rows(blocks, backward, jnp.zeros((HEAD_DIM, queries), jnp.float32))
-    for values, keep, send in (
-        (attended, keep_out, send_out),
-        (flat * score_scale, keep_query, send_query),
-    ):
-        turned_back = jnp.transpose(values).astype(jnp.bfloat16)
-        keep[...] = turned_back[: queries // 2]
-        send[...] = turned_back[queries // 2 :]
-
-
-def key_sum_body(spot, sent_query, sent_out, *refs):
-    *parts, keep, send = refs
-    both = parts_sum(parts).astype(jnp.bfloat16)
-    half = keep.shape[0]
-    keep[...] = both[:half]
-    send[:, : 2 * HEAD_DIM] = both[half:]
-    send[:, 2 * HEAD_DIM : 3 * HEAD_DIM] = sent_query[...]
-    send[:, 3 * HEAD_DIM :] = sent_out[...]
-
-
-def leading_sum(ref):
-    summed = ref[0].astype(jnp.float32)
-    for index in range(1, ref.shape[0]):
-        summed += ref[index].astype(jnp.float32)
-    return summed
-
-
-def cross_body(spot, query, grad, parts, crossed, grad_query, text_grad):
+def cross_body(spot, query, grad, parts, *refs):
+    *blocks, crossed, grad_query, text_grad = refs
+    if blocks:
+        kept_block, got_block, *pairs = blocks
+        for index, pair in enumerate(pairs):
+            pair[0] = kept_block[index + 1]
+            pair[1] = got_block[index + 1]
     text = leading_sum(parts).astype(jnp.bfloat16)
     live = lax.broadcasted_iota(jnp.int32, (query.shape[0], text.shape[1]), 1) < spot[2]
     for head in range(query.shape[1] // HEAD_DIM):
@@ -744,6 +671,78 @@
         text_grad[1, :, lanes] = dot_first(low, back).astype(jnp.bfloat16)
 
 
+def attend_body(count, extra, spot, kept_query, got, kept_grad, got_grad, *refs):
+    blocks, refs = refs[:count], refs[count:]
+    cross_in, refs = refs[: 3 + extra], refs[3 + extra :]
+    parts, refs = refs[:count], refs[count:]
+    keep_out, send_out, keep_query, send_query, *cross_out = refs
+    cross_body(spot, *cross_in, *cross_out)
+    query = jnp.concatenate([kept_query[...], got[:, 2 * HEAD_DIM :]], axis=0)
+    grad = jnp.concatenate([kept_grad[...], got_grad[...]], axis=0)
+    queries = query.shape[0]
+
+    def forward(state, block, index, start):
+        top, weight_sum, weighted = state
+        scores = dot_last(block[:, :HEAD_DIM], query) * score_scale
+        raised = jnp.maximum(top, jnp.max(scores, axis=0, keepdims=True))
+        rescale = jnp.exp(top - raised)
+        weights = jnp.exp(scores - raised)
+        weight_sum = weight_sum * rescale + jnp.sum(weights, axis=0, keepdims=True)
+        values = block[:, HEAD_DIM:]
+        weighted = weighted * rescale + dot_first(values, weights.astype(jnp.bfloat16))
+        return raised, weight_sum, weighted
+
+    top, weight_sum, weighted = over_rows(
+        blocks,
+        forward,
+        (
+            jnp.full((1, queries), -1e30, jnp.float32),
+            jnp.zeros((1, queries), jnp.float32),
+            jnp.zeros((HEAD_DIM, queries), jnp.float32),
+        ),
+    )
+    attended = weighted / weight_sum
+    delta = jnp.sum(attended * jnp.transpose(grad.astype(jnp.float32)), axis=0, keepdims=True)
+    log_sum = top + jnp.log(weight_sum)
+
+    def backward(state, block, index, start):
+        keys, values = block[:, :HEAD_DIM], block[:, HEAD_DIM:]
+        probs = jnp.exp(dot_last(keys, query) * score_scale - log_sum)
+        grad_values = dot(probs.astype(jnp.bfloat16), grad)
+        grad_scores = (probs * (dot_last(values, grad) - delta)).astype(jnp.bfloat16)
+        grad_keys = dot(grad_scores, query) * score_scale
+        rows = pl.ds(start if isinstance(start, int) else pl.multiple_of(start, 512), block.shape[0])
+        parts[index][rows, :] = jnp.concatenate([grad_keys, grad_values], axis=1).astype(
+            jnp.bfloat16
+        )
+        return state + dot_first(keys, grad_scores)
+
+    flat = over_rows(blocks, backward, jnp.zeros((HEAD_DIM, queries), jnp.float32))
+    for values, keep, send in (
+        (attended, keep_out, send_out),
+        (flat * score_scale, keep_query, send_query),
+    ):
+        turned_back = jnp.transpose(values).astype(jnp.bfloat16)
+        keep[...] = turned_back[: queries // 2]
+        send[...] = turned_back[queries // 2 :]
+
+
+def key_sum_body(spot, sent_query, *refs):
+    *parts, keep, send = refs
+    both = parts_sum(parts).astype(jnp.bfloat16)
+    half = keep.shape[0]
+    keep[...] = both[:half]
+    send[:, : 2 * HEAD_DIM] = both[half:]
+    send[:, 2 * HEAD_DIM :] = sent_query[...]
+
+
+def leading_sum(ref):
+    summed = ref[0].astype(jnp.float32)
+    for index in range(1, ref.shape[0]):
+        summed += ref[index].astype(jnp.float32)
+    return summed
+
+
 def joined_grads(spot, kept_query, kept_pair, got, cross):
     odd = lax.rem(spot[0], 2) == 1
     parts = [got[:, i * HEAD_DIM : (i + 1) * HEAD_DIM] for i in range(3)]
@@ -755,19 +754,21 @@
     ]
 
 
-def project_back_body(groups, spot, kq, kp, got, cross, center, inverse, maps, *refs):
+def project_back_body(groups, spot, kq, kp, got, cross, center, inverse, kept, other, *refs):
+    crossed, normed, maps, *refs = refs
     pieces, packs = refs[:groups], refs[groups : 2 * groups]
-    outs = refs[2 * groups :]
+    *outs, out, frame = refs[2 * groups :]
+    odd = lax.rem(spot[0], 2) == 1
     weights = Weights([maps], spot, groups)
     grads = joined_grads(spot, kq, kp, got, cross)
-    area = cross.shape[0]
+    area, span = cross.shape
     plain = dotted = 0.0
     for mask in range(groups):
         part = 0.0
         for position in range(4):
             part += dot_last(grads[position], weights.tap(mask, position))
         outs[mask][:area] = part.astype(jnp.bfloat16)
-        eased = part * unpacked_rows(packs[mask], part.shape[0])[0]
+        eased = part * unpacked_rows(packs[mask], area)[0]
         unit = (pieces[mask][...].astype(jnp.float32) - center[...]) * inverse[...]
         plain += eased
         dotted += eased * unit
@@ -783,18 +784,10 @@
         for values in (plain, dotted)
     ]
     packed = packed_rows(jnp.concatenate(sums, axis=0))
-    for out in outs:
-        out[area:] = packed
-
-
-def weight_grad_body(groups, spot, kq, kp, got, cross, kept, crossed, normed, *refs):
-    packs, (out, frame) = refs[:groups], refs[groups:]
-    odd = lax.rem(spot[0], 2) == 1
-    area, span = cross.shape
-    right = jnp.concatenate(joined_grads(spot, kq, kp, got, cross), axis=1)
-    out_right = jnp.concatenate(
-        [heads_joined(kept[...], got[:, 3 * HEAD_DIM :], odd), crossed[...]], axis=1
-    )
+    for part in outs:
+        part[area:] = packed
+    right = jnp.concatenate(grads, axis=1)
+    out_right = jnp.concatenate([heads_joined(kept[...], other[...], odd), crossed[...]], axis=1)
     for mask in range(groups):
         frame[lax.bitwise_xor(spot[1], mask)] = packs[mask][:area]
     for chunk in range(groups):
@@ -813,7 +806,7 @@
 
 
 def norm_back_body(groups, width, spot, *refs):
-    scaled, inverse, cotangent, gain, middle, low, last, first, terms = refs[groups:]
+    scaled, inverse, cotangent, gain, middle, low, near, far_row, terms = refs[groups:]
     area = scaled.shape[0]
     grad = plain = dotted = 0.0
     for ref in refs[:groups]:
@@ -832,8 +825,9 @@
     middle[...] = back
     grad_low = (back * root_half).astype(jnp.bfloat16)
     low[...] = grad_low
-    last[...] = grad_low[-width:]
-    first[...] = grad_low[:width]
+    odd = lax.rem(spot[0], 2) == 1
+    near[...] = jnp.where(odd, grad_low[:width], grad_low[-width:])
+    far_row[...] = jnp.where(odd, grad_low[-width:], grad_low[:width])
 
 
 def shards(
@@ -924,6 +918,7 @@
     inner, sums, *first_sends = convolve(
         spot, pieces, edges, kernel_one, own_pixels, row_pair, [], row_count, col_count
     )
+    sums = after(sums, kernel_two)
     inner_parts = part_totals(jnp.concatenate([film_term[0], sums]))
     second, film, inner_sums = local_kernel(
         functools.partial(second_norm_body, pixel_count),
@@ -934,7 +929,6 @@
         0,
     )
     text_all = lax.all_gather(after(text_term, second), "wide")
-    second = after(second, kernel_two)
     pieces = channel_pieces(second)
     edges = piece_edges(pieces, col_count)
     middle, middle_low, *both_sends = convolve(
@@ -950,6 +944,7 @@
     )
 
     middle_pieces = channel_pieces(middle_low)
+    block_pair = [both_sends[0], flipped(both_sends[1], "wide", 1)] if has_slots() else []
     kept_grad, sent_grad, grad_crossed = local_kernel(
         functools.partial(out_grad_body, groups),
         [bf16_like(*half), bf16_like(*half), bf16_like(*flat)],
@@ -959,7 +954,7 @@
         2 * square,
     )
     got_grad = flipped(sent_grad, "wide", 1)
-    middle_pieces[0] = after(middle_pieces[0], got_grad)
+    middle_pieces[0] = after(middle_pieces[0], got_grad, block_pair)
     column = f32_like(token_count, 1)
     triple = bf16_like(token_count, 3 * HEAD_DIM)
     kept_query, kept_pair, sent, cross_query, normed, scaled, center, inverse = local_kernel(
@@ -969,10 +964,10 @@
             bf16_like(*flat),
             triple,
             bf16_like(*flat),
-            bf16_like(groups, *flat),
-            f32_like(*flat),
-            column,
-            column,
+            far_like(bf16_like(groups, *flat)),
+            far_like(f32_like(*flat)),
+            far_like(column),
+            far_like(column),
         ],
         [spot, *middle_pieces, *far(packs), middle, *far([maps])],
         [],
@@ -981,49 +976,62 @@
     )
     got = flipped(sent, "wide", 1)
     blocks = spread_chips(jnp.concatenate([kept_pair, got[:, : 2 * HEAD_DIM]]))
-    if has_slots():
-        both_blocks = swapped_blocks(spot, after(both_sends[0], blocks[:2][-1]), both_sends[1])
-        got_grad = after(got_grad, both_blocks)
-    crossed, grad_cross_query, text_grads = local_kernel(
-        cross_body,
-        [bf16_like(*flat), bf16_like(*flat), bf16_like(2, TEXT, width_own)],
-        [spot, after(cross_query, blocks[:2][-1]), grad_crossed, *far([text_all])],
-        [],
-        24,
-        12 * token_count * TEXT * width_own,
-    )
-    got_grad = after(got_grad, crossed)
+    pair_shapes = [bf16_like(2, *block.shape[1:]) for block in block_pair[:1] * 3]
+    attend_shapes = [bf16_like(*block.shape) for block in blocks] + [bf16_like(*half)] * 4
+    cross_shapes = [bf16_like(*flat), bf16_like(*flat), bf16_like(2, TEXT, width_own)]
+    outs = local_kernel(
+        functools.partial(attend_body, len(blocks), len(block_pair)),
+        [far_like(shape) for shape in attend_shapes + pair_shapes + cross_shapes],
+        [
+            spot,
+            kept_query,
+            got,
+            *far([kept_grad, got_grad]),
+            *blocks,
+            cross_query,
+            *far([grad_crossed, text_all]),
+            *far(block_pair),
+        ],
+        [],
+        48,
+        14 * (2 * token_count) * HEAD_DIM * pixel_count,
+    )
+    key_parts, outs = outs[: len(blocks)], outs[len(blocks) :]
+    kept_out, sent_out, kept_dq, sent_dq, *block_pairs = outs
+    *block_pairs, crossed, grad_cross_query, text_grads = block_pairs
     text_sums = lax.all_gather(text_grads, "wide")
-    *key_parts, kept_out, sent_out, kept_dq, sent_dq = local_kernel(
-        functools.partial(attend_body, len(blocks)),
-        [bf16_like(*block.shape) for block in blocks] + [bf16_like(*half)] * 4,
-        [spot, kept_query, got, kept_grad, got_grad, *blocks],
-        [],
-        40,
-        14 * (2 * token_count) * HEAD_DIM * pixel_count,
-    )
+    key_sums = gathered_sums(key_parts)
     kept_dk, sent_all = local_kernel(
         key_sum_body,
-        [bf16_like(*flat), bf16_like(token_count, 4 * HEAD_DIM)],
-        [spot, sent_dq, sent_out, *gathered_sums(key_parts)],
+        [bf16_like(*flat), bf16_like(token_count, 3 * HEAD_DIM)],
+        [spot, *far([sent_dq, key_sums[0]]), *key_sums[1:]],
         [],
         16,
         0,
     )
     got_all = flipped(sent_all, "wide", 1)
+    got_out = flipped(sent_out, "wide", 1)
+    kept_dq, grad_cross_query = far([kept_dq, grad_cross_query])
     projected_grads = [kept_dq, kept_dk, got_all, grad_cross_query]
-    norm_parts = local_kernel(
+    *norm_parts, weight_parts = local_kernel(
         functools.partial(project_back_body, groups),
-        [bf16_like(token_count + 16, width_own)] * groups,
-        [spot, *projected_grads, center, inverse, *far([maps]), *far(middle_pieces), *far(packs)],
-        [],
-        24,
-        4 * square,
-    )
+        [bf16_like(token_count + 16, width_own)] * groups + [far_like(bf16_like(C, 6 * width_own))],
+        [
+            spot,
+            *projected_grads,
+            *far([center, inverse, kept_out, got_out, crossed, normed, maps]),
+            *far(middle_pieces),
+            *far(packs),
+        ],
+        [pltpu.VMEM((groups, *flat), jnp.bfloat16)],
+        32,
+        10 * square,
+    )
+    weight_sums = lax.psum_scatter(weight_parts, "wide", scatter_dimension=0, tiled=True)
     received = sent_parts(norm_parts)
     if has_slots():
-        near = [flipped(after(both_blocks[2 + k], norm_parts[0]), "wide", 2 * k + 2) for k in range(2)]
-        received[0] = after(received[0], near)
+        close = [flipped(after(block_pairs[k], norm_parts[0]), "wide", 2 * k + 2) for k in range(2)]
+        received[0] = after(received[0], close)
     grad_middle, grad_two, last, head, terms = local_kernel(
         functools.partial(norm_back_body, groups, col_count),
         [
@@ -1047,25 +1055,16 @@
     )
 
     edges = edge_rows(last, head)
-    weight_parts, = local_kernel(
-        functools.partial(weight_grad_body, groups),
-        [bf16_like(C, 6 * width_own)],
-        [
-            spot,
-            after(projected_grads[0], grad_two),
-            *projected_grads[1:],
-            kept_out,
-            crossed,
-            *far([normed]),
-            *far(packs),
-        ],
-        [pltpu.VMEM((groups, *flat), jnp.bfloat16)],
-        24,
-        6 * square,
-    )
-    weight_sums = lax.psum_scatter(weight_parts, "wide", scatter_dimension=0, tiled=True)
+    mixed = local_kernel(
+        functools.partial(mix_body, groups),
+        [bf16_like(*flat)] * groups,
+        [spot, after(kept_out, grad_two), got_out, *far([crossed, maps])],
+        [],
+        16,
+        2 * square,
+    )
     back_parts = convolve_back(
-        spot, after(grad_two, weight_parts), edges, kernel_two, row_count, col_count
+        spot, after(grad_two, mixed), edges, kernel_two, row_count, col_count
     )
     back_parts = sent_parts(back_parts)
     back, rows = local_kernel(
@@ -1076,14 +1075,6 @@
         16,
         0,
     )
-    mixed = local_kernel(
-        functools.partial(mix_body, groups),
-        [bf16_like(*flat)] * groups,
-        [spot, after(kept_out, back), got_all, crossed, *far([maps])],
-        [],
-        16,
-        2 * square,
-    )
     grad_one, last, head, film_rows, second_rows = local_kernel(
         functools.partial(second_input_body, pixel_count, col_count),
         [bf16_like(*flat), bf16_like(*edge), bf16_like(*edge), row_pair, f32_like(8, width_own)],
@@ -1093,12 +1084,10 @@
         0,
     )
     edges = edge_rows(last, head)
-    mixed = sent_parts([after(part, grad_one) for part in mixed])
     both_grads = lax.all_gather(jnp.stack([grad_one, grad_two]), "wide", axis=1, tiled=True)
     back_parts = convolve_back(spot, grad_one, edges, kernel_one, row_count, col_count)
     if has_slots():
-        distant = flipped(after(both_blocks[4], back_parts[0]), "wide", 6)
-        both_blocks = both_blocks[:2] + near + [distant]
+        block_pair += [*close, flipped(after(block_pairs[2], back_parts[0]), "wide", 6)]
     attn_in_grad, self_grad, cross_grad = local_kernel(
         weight_out_body,
         [f32_like(4, C // lax.axis_size("wide"), width_own)]
@@ -1110,9 +1099,6 @@
     )
     back_parts = sent_parts(back_parts)
     film_rows = after(film_rows, back_parts[1])
-    result = middle
-    for part in mixed:
-        result = result + part.astype(jnp.float32)
     time_grad, text_grad, kv_grad = local_kernel(
         text_out_body,
         [
@@ -1125,9 +1111,13 @@
         24,
         4 * TEXT * text_rows * width_own,
     )
-    back_parts[0], attn_in_grad, result, time_grad = lax.optimization_barrier(
-        (back_parts[0], attn_in_grad, result, time_grad)
-    )
+    back_parts[0], attn_in_grad, time_grad = lax.optimization_barrier(
+        (back_parts[0], attn_in_grad, time_grad)
+    )
+    mixed = sent_parts([after(part, *back_parts) for part in mixed])
+    result = middle
+    for part in mixed:
+        result = result + part.astype(jnp.float32)
     back, rows = local_kernel(
         functools.partial(first_back_body, groups, pixel_count),
         [f32_like(*flat), f32_like(2, width_own)],
@@ -1138,8 +1128,7 @@
     )
     row_parts = part_totals(rows)
     if has_slots():
-        conv_grad = kernel_grad(spot, both_blocks, both_grads, row_count, col_count, 1, None)
-        conv_grad = kernel_grad(spot, both_blocks, both_grads, row_count, col_count, 0, conv_grad)
+        conv_grad = kernel_grad(spot, block_pair, both_grads, col_count)
     else:
         conv_grad = jnp.stack(
             [

time: 312 us -> 295 us (0.946)
  starting transfers between devices: 112 us -> 103 us
  local copies, waits for them, and re-layouts: 17.8 us -> 9.31 us
  waiting for transfers between devices: 94 us -> 97.5 us
    ppermute x8 -> x4, starting transfers between devices: 14.1 us -> 2.68 us  [edge_rows(): from_far = lax.ppermute(far_row, 'wide', beyond)]
    ppermute x2, waiting for transfers between devices: 2.27 us -> 12.1 us  [relayed_block(): return lax.ppermute(jnp.where(odd, over_y, over_x), 'wide', far_pairs)]
    unnamed x94 -> x80, local copies, waits for them, and re-layouts: 14 us -> 5.13 us
    all_gather x1, waiting for transfers between devices: 8.64 us -> 0.01 us  [shards(): lax.all_gather(jnp.stack([grad_one, grad_two]), 'wide', axis=1, tiled=True)]
    ppermute x58 -> x63, waiting for transfers between devices: 79.4 us -> 85.3 us  [flipped(): return lax.ppermute(values, axis, [(i, i ^ mask) for i in range(count)])]
    pallas_call x2 -> x1, Pallas kernels: 10.3 us -> 6.56 us  [kernel_grad(): pl.pallas_call(functools.partial(kernel_grad_body, width), out_shape=f32_...]
    ppermute x8 -> x4, waiting for transfers between devices: 3.57 us -> 0.01 us  [edge_rows(): from_far = lax.ppermute(far_row, 'wide', beyond)]
    ppermute x58 -> x63, starting transfers between devices: 95.5 us -> 97.8 us  [flipped(): return lax.ppermute(values, axis, [(i, i ^ mask) for i in range(count)])]
  transfers between devices with their start and end apart: 74 -> 75, of which waited for: 36 -> 37; matrix products, arithmetic and copies ran while one was open for 3% -> 3% of each run, Pallas kernels for 20% -> 19%
where the time goes in v3:
time: 295 us
  starting transfers between devices  103 us (35%)
  waiting for transfers between devices  97.5 us (33%)
  Pallas kernels  63.3 us (21%)
  between operations  16.3 us (6%)
  local copies, waits for them, and re-layouts  9.31 us (3%)
  other arithmetic  3.95 us (1%)
    ppermute x63, starting transfers between devices, flipped(): return lax.ppermute(values, axis, [(i, i ^ mask) for i in range(count)])  97.8 us
    ppermute x63, waiting for transfers between devices, flipped(): return lax.ppermute(values, axis, [(i, i ^ mask) for i in range(count)])  85.3 us
    pallas_call x20, Pallas kernels, local_kernel(): pl.pallas_call(body, grid=(1,), out_shape=outs, in_specs=[in_smem] + [in_...  56.8 us
    ppermute x2, waiting for transfers between devices, relayed_block(): return lax.ppermute(jnp.where(odd, over_y, over_x), 'wide', far_pairs)  12.1 us
    pallas_call x1, Pallas kernels, kernel_grad(): pl.pallas_call(functools.partial(kernel_grad_body, width), out_shape=f32_...  6.56 us
  transfers between devices with their start and end apart: 75, of which 37 were waited for; matrix products, arithmetic and copies ran while one was open for 3% of the time, Pallas kernels for 19%

profile of v3, /device:TPU:0, one launch (start us, length us, event | category | flops | bytes accessed | tf_op | source)
XLA Modules:
  0.0 294.8 jit_solution(9977188846871895719)
XLA Ops:
  16.2 2.6 collective-permute-start.1
  22.3 2.5 collective-permute-done.3.refs_3_
  29.4 2.6 collective-permute-start.5
  33.4 7.1 %collective-permute-done.5.refs_2_ = bf16[256,256]{1,0:T(8,128)(2,1)S(1)} collective-permute-done((bf16[256,256]{1,0:T(8,128)(2,1)S(1)}, bf16[256,256]{1,0:T(8,128)(2,1)S(1)}, u32[]{:S(2)}, u32[]{:S(2)}) %collective-permute-start.5) | collective-permute-done | bytes 131104 | tf_op jit(solution)/shard_map/ppermute | solution.py:162
  49.6 5.0 %collective-permute-done.8.refs_2_.refs_6_.refs_9_ = bf16[272,256]{1,0:T(8,128)(2,1)S(1)} collective-permute-done((bf16[272,256]{1,0:T(8,128)(2,1)S(1)}, bf16[272,256]{1,0:T(8,128)(2,1)S(1)}, u32[]{:S(2)}, u32[]{:S(2)}) %collective-permute-start.8) | collective-permute-done | bytes 139296 | tf_op jit(solution)/shard_map/ppermute | solution.py:162
  55.1 6.7 %collective-permute-done.14.refs_9_.refs_3_ = bf16[9,128,256]{2,1,0:T(8,128)(2,1)} collective-permute-done((bf16[9,128,256]{2,1,0:T(8,128)(2,1)S(1)}, bf16[9,128,256]{2,1,0:T(8,128)(2,1)}, u32[]{:S(2)}, u32[]{:S(2)}) %collective-permute-start.14) | collective-permute-done | bytes 589856 | tf_op jit(solution)/shard_map/ppermute | solution.py:168
  63.6 4.6 %conv_body.2 = (f32[256,256]{1,0:T(8,128)S(1)}, f32[2,256]{1,0:T(2,128)S(1)}, bf16[4,256,128]{2,1,0:T(8,128)(2,1)S(1)}, bf16[4,256,128]{2,1,0:T(8,128)(2,1)S(1)}) custom-call(s32[3]{0:T(128)S(1)} %pad_add_fusion.spot, bf16[256,256]{1,0:T(8,128)(2,1)S(1)} %get-tuple-element.125.refs_0_, bf16[256,256]{1,0:T(8,128)(2,1)S(1)} %collective-permute-done.4.refs_1_, ...), custom_call_target="tpu_custom_call" | custom-call | flops 1207959552 | bytes 6686732 | tf_op jit(solution)/shard_map/conv_body/pallas_call | solution.py:24
  68.3 9.2 %collective-permute-start.19 = (f32[4,256]{1,0:T(4,128)S(1)}, f32[4,256]{1,0:T(4,128)S(1)}, u32[]{:S(2)}, u32[]{:S(2)}) collective-permute-start(f32[4,256]{1,0:T(4,128)S(1)} %pad_maximum_fusion.7), channel_id=1, source_target_pairs={{0,4},{4,0},{8,12},{12,8},{16,20},{20,16},{24,28},{28,24},{1,5},{5... | collective-permute-start | bytes 12296 | tf_op jit(solution)/shard_map/ppermute | solution.py:162
  91.9 7.0 %collective-permute-done.24.refs_2_ = bf16[256,256]{1,0:T(8,128)(2,1)S(1)} collective-permute-done((bf16[256,256]{1,0:T(8,128)(2,1)S(1)}, bf16[256,256]{1,0:T(8,128)(2,1)S(1)}, u32[]{:S(2)}, u32[]{:S(2)}) %collective-permute-start.24) | collective-permute-done | bytes 131104 | tf_op jit(solution)/shard_map/ppermute | solution.py:162
  100.6 5.5 %conv_body.3 = (f32[256,256]{1,0:T(8,128)S(1)}, bf16[256,256]{1,0:T(8,128)(2,1)S(1)}, bf16[4,2,256,128]{3,2,1,0:T(8,128)(2,1)S(1)}, bf16[4,2,256,128]{3,2,1,0:T(8,128)(2,1)}) custom-call(s32[3]{0:T(128)S(1)} %pad_add_fusion.spot, bf16[256,256]{1,0:T(8,128)(2,1)S(1)} %get-tuple-element.131.refs_0_, bf16[256,256]{1,0:T(8,128)(2,1)S(1)} %collective-permute-done.23.refs_1_, ...), custom_call_target="tpu_custom_call" | custom-call | flops 1207959552 | bytes 7864332 | tf_op jit(solution)/shard_map/conv_body/pallas_call | solution.py:24
  106.9 9.5 %collective-permute-start.29 = (bf16[4,2,256,128]{3,2,1,0:T(8,128)(2,1)}, bf16[4,2,256,128]{3,2,1,0:T(8,128)(2,1)S(1)}, u32[]{:S(2)}, u32[]{:S(2)}) collective-permute-start(bf16[4,2,256,128]{3,2,1,0:T(8,128)(2,1)} %get-tuple-element.140), channel_id=1, source_target_pairs={{0,4},{4,0},{8,12},{12,8},{16,20},{20,16},{24,28},{28,24},{1,5},{5... | collective-permute-start | bytes 1572872 | tf_op jit(solution)/shard_map/ppermute | solution.py:162
  120.8 2.6 out_grad_body.1
  125.3 5.9 %collective-permute-done.31.refs_2_.refs_5_ = bf16[256,256]{1,0:T(8,128)(2,1)S(1)} collective-permute-done((bf16[256,256]{1,0:T(8,128)(2,1)S(1)}, bf16[256,256]{1,0:T(8,128)(2,1)S(1)}, u32[]{:S(2)}, u32[]{:S(2)}) %collective-permute-start.31) | collective-permute-done | bytes 131104 | tf_op jit(solution)/shard_map/ppermute | solution.py:162
  131.2 3.9 %project_body.1 = (bf16[256,128]{1,0:T(8,128)(2,1)S(1)}, bf16[256,256]{1,0:T(8,128)(2,1)S(1)}, bf16[256,384]{1,0:T(8,128)(2,1)S(1)}, bf16[256,256]{1,0:T(8,128)(...) custom-call(s32[3]{0:T(128)S(1)} %pad_add_fusion.spot, ...), custom_call_target="tpu_custom_call" | custom-call | flops 536870912 | bytes 5801996 | tf_op jit(solution)/shard_map/project_body/pallas_call | solution.py:24
  138.5 6.6 %collective-permute-done.34.refs_1_ = bf16[512,256]{1,0:T(8,128)(2,1)S(1)} collective-permute-done((bf16[512,256]{1,0:T(8,128)(2,1)S(1)}, bf16[512,256]{1,0:T(8,128)(2,1)S(1)}, u32[]{:S(2)}, u32[]{:S(2)}) %collective-permute-start.34) | collective-permute-done | bytes 262176 | tf_op jit(solution)/shard_map/ppermute | solution.py:162
  146.9 5.4 %collective-permute-done.36.refs_3_ = bf16[512,256]{1,0:T(8,128)(2,1)S(1)} collective-permute-done((bf16[512,256]{1,0:T(8,128)(2,1)S(1)}, bf16[512,256]{1,0:T(8,128)(2,1)S(1)}, u32[]{:S(2)}, u32[]{:S(2)}) %collective-permute-start.36) | collective-permute-done | bytes 262176 | tf_op jit(solution)/shard_map/ppermute | solution.py:168
  152.3 8.8 %attend_body.1 = (bf16[512,256]{1,0:T(8,128)(2,1)}, bf16[512,256]{1,0:T(8,128)(2,1)}, bf16[512,256]{1,0:T(8,128)(2,1)}, bf16[512,256]{1,0:T(8,128)(2,1)}, bf16[2...) custom-call(s32[3]{0:T(128)S(1)} %pad_add_fusion.spot, ...), custom_call_target="tpu_custom_call" | custom-call | flops 1879048192 | bytes 6291468 | tf_op jit(solution)/shard_map/attend_body/pallas_call | solution.py:24
  164.9 5.9 %collective-permute-done.37.refs_1_ = bf16[512,256]{1,0:T(8,128)(2,1)S(1)} collective-permute-done((bf16[512,256]{1,0:T(8,128)(2,1)}, bf16[512,256]{1,0:T(8,128)(2,1)S(1)}, u32[]{:S(2)}, u32[]{:S(2)}) %collective-permute-start.37) | collective-permute-done | bytes 262176 | tf_op jit(solution)/shard_map/ppermute | solution.py:162
  170.8 4.2 %collective-permute-done.38.refs_2_ = bf16[512,256]{1,0:T(8,128)(2,1)S(1)} collective-permute-done((bf16[512,256]{1,0:T(8,128)(2,1)}, bf16[512,256]{1,0:T(8,128)(2,1)S(1)}, u32[]{:S(2)}, u32[]{:S(2)}) %collective-permute-start.38) | collective-permute-done | bytes 262176 | tf_op jit(solution)/shard_map/ppermute | solution.py:162
  179.4 6.5 %project_back_body.1 = (bf16[272,256]{1,0:T(8,128)(2,1)S(1)}, bf16[272,256]{1,0:T(8,128)(2,1)S(1)}, bf16[272,256]{1,0:T(8,128)(2,1)S(1)}, bf16[272,256]{1,0:T(8,128)(2,1)S(1)}, bf16[1024,1536]{1,0:T(8,128)(2,1)}) custom-call(s32[3]{0:T(128)S(1)} %pad_add_fusion.spot, bf16[256,128]{1,0:T(8,128)(2,1)} %get-tuple-element.150.kq, ...), custom_call_target="tpu_custom_call" | custom-call | flops 1342177280 | bytes 9242636 | tf_op jit(solution)/shard_map/project_back_body/pallas_call | solution.py:24
  187.7 2.8 collective-permute-start.44
  195.9 8.1 %collective-permute-done.45.refs_2_ = bf16[272,256]{1,0:T(8,128)(2,1)S(1)} collective-permute-done((bf16[272,256]{1,0:T(8,128)(2,1)S(1)}, bf16[272,256]{1,0:T(8,128)(2,1)S(1)}, u32[]{:S(2)}, u32[]{:S(2)}) %collective-permute-start.45) | collective-permute-done | bytes 139296 | tf_op jit(solution)/shard_map/ppermute | solution.py:162
  208.1 3.8 %back_body.2 = (bf16[256,256]{1,0:T(8,128)(2,1)S(1)}, bf16[256,256]{1,0:T(8,128)(2,1)S(1)}, bf16[256,256]{1,0:T(8,128)(2,1)S(1)}, bf16[256,256]{1,0:T(8,128)(2,1)S(1)}) custom-call(s32[3]{0:T(128)S(1)} %pad_add_fusion.spot, bf16[256,256]{1,0:T(8,128)(2,1)S(1)} %get-tuple-element.180.grad, bf16[128,256]{1,0:T(8,128)(2,1)S(1)} %collective-permute-done.47.near, ...), custom_call_target="tpu_custom_call" | custom-call | flops 1207959552 | bytes 5505036 | tf_op jit(solution)/shard_map/back_body/pallas_call | solution.py:24
  217.0 5.7 %collective-permute-done.50.refs_2_ = bf16[256,256]{1,0:T(8,128)(2,1)S(1)} collective-permute-done((bf16[256,256]{1,0:T(8,128)(2,1)S(1)}, bf16[256,256]{1,0:T(8,128)(2,1)S(1)}, u32[]{:S(2)}, u32[]{:S(2)}) %collective-permute-start.50) | collective-permute-done | bytes 131104 | tf_op jit(solution)/shard_map/ppermute | solution.py:162
  224.4 4.4 %collective-permute-start.52 = (f32[8,256]{1,0:T(8,128)S(1)}, f32[8,256]{1,0:T(8,128)S(1)}, u32[]{:S(2)}, u32[]{:S(2)}) collective-permute-start(f32[8,256]{1,0:T(8,128)S(1)} %get-tuple-element.192), channel_id=1, source_target_pairs={{0,4},{4,0},{8,12},{12,8},{16,20},{20,16},{24,28},{28,24},{1,5},{5... | collective-permute-start | bytes 24584 | tf_op jit(solution)/shard_map/ppermute | solution.py:162
  229.6 3.7 %collective-permute-start.53 = (f32[8,256]{1,0:T(8,128)S(1)}, f32[8,256]{1,0:T(8,128)S(1)}, u32[]{:S(2)}, u32[]{:S(2)}) collective-permute-start(f32[8,256]{1,0:T(8,128)S(1)} %add.42.refs_0_), channel_id=1, source_target_pairs={{0,8},{4,12},{8,0},{12,4},{16,24},{20,28},{24,16},{28,20},{1,9},{5... | collective-permute-start | bytes 24584 | tf_op jit(solution)/shard_map/ppermute | solution.py:162
  241.9 4.5 %back_body.3 = (bf16[256,256]{1,0:T(8,128)(2,1)S(1)}, bf16[256,256]{1,0:T(8,128)(2,1)S(1)}, bf16[256,256]{1,0:T(8,128)(2,1)}, bf16[256,256]{1,0:T(8,128)(2,1)S(1)}) custom-call(s32[3]{0:T(128)S(1)} %pad_add_fusion.spot, bf16[256,256]{1,0:T(8,128)(2,1)S(1)} %get-tuple-element.193.grad, bf16[128,256]{1,0:T(8,128)(2,1)S(1)} %collective-permute-done.56.near, ...), custom_call_target="tpu_custom_call" | custom-call | flops 1207959552 | bytes 5505036 | tf_op jit(solution)/shard_map/back_body/pallas_call | solution.py:24
  250.8 6.3 %collective-permute-start.68 = (bf16[2,2,256,128]{3,2,1,0:T(8,128)(2,1)S(1)}, bf16[2,2,256,128]{3,2,1,0:T(8,128)(2,1)}, u32[]{:S(2)}, u32[]{:S(2)}) collective-permute-start(bf16[2,2,256,128]{3,2,1,0:T(8,128)(2,1)S(1)} %copy-done.35), channel_id=1, source_target_pairs={{0,24},{4,28},{8,16},{12,20},{16,8},{20,12},{24,0},{28,4},{1,25},{... | collective-permute-start | bytes 786440 | tf_op jit(solution)/shard_map/ppermute | solution.py:162
  257.2 3.4 %text_out_body.1 = (f32[128,2,256]{2,1,0:T(2,128)}, f32[512,2,256]{2,1,0:T(2,128)}, f32[2,512,256]{2,1,0:T(8,128)}) custom-call(s32[3]{0:T(128)S(1)} %pad_add_fusion.spot, f32[2,256]{1,0:T(2,128)S(1)} %get-tuple-element.203.film, bf16[1,128]{1,0:T(2,128)(2,1)S(1)} %fusion.13.features, bf16[1,512]{1,0:T(2,128)(2,1)S(1)} %dynamic_slice.11.pooled, ...), custom_call_target="tpu_custom_call" | custom-call | flops 67108864 | bytes 3542284 | tf_op jit(solution)/shard_map/text_out_body/pallas_call | solution.py:24
  266.2 4.1 %collective-permute-start.65 = (f32[2,256]{1,0:T(2,128)S(1)}, f32[2,256]{1,0:T(2,128)S(1)}, u32[]{:S(2)}, u32[]{:S(2)}) collective-permute-start(f32[2,256]{1,0:T(2,128)S(1)} %add.47.refs_0_), channel_id=1, source_target_pairs={{0,8},{4,12},{8,0},{12,4},{16,24},{20,28},{24,16},{28,20},{1,9},{5... | collective-permute-start | bytes 6152 | tf_op jit(solution)/shard_map/ppermute | solution.py:162
  270.9 3.4 %collective-permute-start.61 = (bf16[256,256]{1,0:T(8,128)(2,1)S(1)}, bf16[256,256]{1,0:T(8,128)(2,1)S(1)}, u32[]{:S(2)}, u32[]{:S(2)}) collective-permute-start(bf16[256,256]{1,0:T(8,128)(2,1)S(1)} %get-tuple-element.210), channel_id=1, source_target_pairs={{0,1},{1,0},{2,3},{3,2},{4,5},{5,4},{6,7},{7,6},{8,9},{9,8},{10,11... | collective-permute-start | bytes 393224 | tf_op jit(solution)/shard_map/ppermute | solution.py:162
  278.1 6.6 %kernel_grad_body.1 = f32[2,9,128,256]{3,2,1,0:T(8,128)} custom-call(s32[3]{0:T(128)S(1)} %pad_add_fusion.spot, bf16[4,2,256,128]{3,2,1,0:T(8,128)(2,1)} %copy-done.17, bf16[4,2,256,128]{3,2,1,0:T(8,128)(2,1)} %copy-done.34, bf16[2,2,256,128]{3,2,1,0:T(8,128)(2,1)} %copy-done.37, bf16[2,2,256,128]{3,2,1,0:T(8,128)(2,1)} %copy-done.36, ...), custom_call_target="tpu_custom_call" | custom-call | flops 2415919104 | bytes 6291456 | tf_op jit(solution)/shard_map/kernel_grad_body/pallas_call | solution.py:299
  (268 shorter events, 109.9 us)
Async XLA Ops:
  7.2 56.4 %all-gather.9.cloned.1.call-start = ((), (), s32[]{:S(2)}) async-start(), calls=%async_computation.1 | async-start | bytes 5308416 | tf_op jit(solution)/shard_map/all_gather | solution.py:185
  9.4 111.4 %all-gather.13.cloned.1.call-start = ((), (), s32[]{:S(2)}) async-start(), calls=%async_computation.4 | async-start | bytes 3538944 | tf_op jit(solution)/shard_map/all_gather | solution.py:185
  12.2 140.1 %all-gather.15.cloned.1.call-start = ((), (), s32[]{:S(2)}) async-start(), calls=%async_computation.5 | async-start | bytes 1179648 | tf_op jit(solution)/shard_map/all_gather | solution.py:931
  26.6 19.6 %collective-permute-start.12 = (bf16[9,128,256]{2,1,0:T(8,128)(2,1)}, bf16[9,128,256]{2,1,0:T(8,128)(2,1)}, u32[]{:S(2)}, u32[]{:S(2)}) collective-permute-start(bf16[9,128,256]{2,1,0:T(8,128)(2,1)} %slice_bitcast_fusion.refs_6_.refs_0_), channel_id=1, source_target_pairs={{0,8},{4,12},{8,0},{12,4},{16,24},{20,28},{24,16},{28,20},{1,9},{5... | collective-permute-start | bytes 1769480 | tf_op jit(solution)/shard_map/ppermute | solution.py:162
  27.0 19.9 %collective-permute-start.13 = (bf16[9,128,256]{2,1,0:T(8,128)(2,1)}, bf16[9,128,256]{2,1,0:T(8,128)(2,1)}, u32[]{:S(2)}, u32[]{:S(2)}) collective-permute-start(bf16[9,128,256]{2,1,0:T(8,128)(2,1)} %slice_bitcast_fusion.refs_6_.refs_0_), channel_id=1, source_target_pairs={{0,16},{4,20},{8,24},{12,28},{16,0},{20,4},{24,8},{28,12},{1,17},{... | collective-permute-start | bytes 1769480 | tf_op jit(solution)/shard_map/ppermute | solution.py:162
  29.4 11.2 %collective-permute-start.5 = (bf16[256,256]{1,0:T(8,128)(2,1)S(1)}, bf16[256,256]{1,0:T(8,128)(2,1)S(1)}, u32[]{:S(2)}, u32[]{:S(2)}) collective-permute-start(bf16[256,256]{1,0:T(8,128)(2,1)S(1)} %get-tuple-element.125.refs_0_), channel_id=1, source_target_pairs={{0,2},{1,3},{2,0},{3,1},{4,6},{5,7},{6,4},{7,5},{8,10},{9,11},{10,... | collective-permute-start | bytes 393224 | tf_op jit(solution)/shard_map/ppermute | solution.py:162
  42.5 12.1 %collective-permute-start.8 = (bf16[272,256]{1,0:T(8,128)(2,1)S(1)}, bf16[272,256]{1,0:T(8,128)(2,1)S(1)}, u32[]{:S(2)}, u32[]{:S(2)}) collective-permute-start(bf16[272,256]{1,0:T(8,128)(2,1)S(1)} %get-tuple-element.137.refs_0_.refs_4_.refs_7_), channel_id=1, source_target_pairs={{0,2},{1,3},{2,0},{3,1},{4,6},{5,7},{6,4},{7,5},{8,10},{9,11},{10,... | collective-permute-start | bytes 417800 | tf_op jit(solution)/shard_map/ppermute | solution.py:162
  43.6 11.0 %collective-permute-start.9 = (bf16[272,256]{1,0:T(8,128)(2,1)S(1)}, bf16[272,256]{1,0:T(8,128)(2,1)S(1)}, u32[]{:S(2)}, u32[]{:S(2)}) collective-permute-start(bf16[272,256]{1,0:T(8,128)(2,1)S(1)} %get-tuple-element.137.refs_0_.refs_4_.refs_7_), channel_id=1, source_target_pairs={{0,3},{1,2},{2,1},{3,0},{4,7},{5,6},{6,5},{7,4},{8,11},{9,10},{10,... | collective-permute-start | bytes 417800 | tf_op jit(solution)/shard_map/ppermute | solution.py:162
  48.0 13.8 %collective-permute-start.14 = (bf16[9,128,256]{2,1,0:T(8,128)(2,1)S(1)}, bf16[9,128,256]{2,1,0:T(8,128)(2,1)}, u32[]{:S(2)}, u32[]{:S(2)}) collective-permute-start(bf16[9,128,256]{2,1,0:T(8,128)(2,1)S(1)} %broadcast_select_fusion), channel_id=1, source_target_pairs={{0,16},{4,12},{8,24},{12,4},{16,0},{20,28},{24,8},{28,20},{1,17},{... | collective-permute-start | bytes 1769480 | tf_op jit(solution)/shard_map/ppermute | solution.py:168
  48.9 13.1 %collective-permute-start.10 = (bf16[128,1024]{1,0:T(8,128)(2,1)S(1)}, bf16[128,1024]{1,0:T(8,128)(2,1)S(1)}, u32[]{:S(2)}, u32[]{:S(2)}) collective-permute-start(bf16[128,1024]{1,0:T(8,128)(2,1)S(1)} %get-tuple-element.126), channel_id=1, source_target_pairs={{0,4},{4,0},{8,12},{12,8},{16,20},{20,16},{24,28},{28,24},{1,5},{5... | collective-permute-start | bytes 786440 | tf_op jit(solution)/shard_map/ppermute | solution.py:162
  49.1 19.2 %collective-permute-start.15 = (bf16[9,128,256]{2,1,0:T(8,128)(2,1)}, bf16[9,128,256]{2,1,0:T(8,128)(2,1)}, u32[]{:S(2)}, u32[]{:S(2)}) collective-permute-start(bf16[9,128,256]{2,1,0:T(8,128)(2,1)} %slice_bitcast_fusion.refs_6_.refs_0_), channel_id=1, source_target_pairs={{0,4},{4,0},{8,12},{12,8},{16,20},{20,16},{24,28},{28,24},{1,5},{5... | collective-permute-start | bytes 1769480 | tf_op jit(solution)/shard_map/ppermute | solution.py:162
  54.6 13.7 %collective-permute-start.16 = (bf16[9,128,256]{2,1,0:T(8,128)(2,1)}, bf16[9,128,256]{2,1,0:T(8,128)(2,1)}, u32[]{:S(2)}, u32[]{:S(2)}) collective-permute-start(bf16[9,128,256]{2,1,0:T(8,128)(2,1)} %collective-permute-done.12.refs_7_.refs_1_), channel_id=1, source_target_pairs={{0,4},{4,0},{8,12},{12,8},{16,20},{20,16},{24,28},{28,24},{1,5},{5... | collective-permute-start | bytes 1769480 | tf_op jit(solution)/shard_map/ppermute | solution.py:162
  54.7 13.7 %collective-permute-start.17 = (bf16[9,128,256]{2,1,0:T(8,128)(2,1)}, bf16[9,128,256]{2,1,0:T(8,128)(2,1)}, u32[]{:S(2)}, u32[]{:S(2)}) collective-permute-start(bf16[9,128,256]{2,1,0:T(8,128)(2,1)} %collective-permute-done.13.refs_8_.refs_2_), channel_id=1, source_target_pairs={{0,4},{4,0},{8,12},{12,8},{16,20},{20,16},{24,28},{28,24},{1,5},{5... | collective-permute-start | bytes 1769480 | tf_op jit(solution)/shard_map/ppermute | solution.py:162
  87.1 11.7 %collective-permute-start.24 = (bf16[256,256]{1,0:T(8,128)(2,1)S(1)}, bf16[256,256]{1,0:T(8,128)(2,1)S(1)}, u32[]{:S(2)}, u32[]{:S(2)}) collective-permute-start(bf16[256,256]{1,0:T(8,128)(2,1)S(1)} %get-tuple-element.131.refs_0_), channel_id=1, source_target_pairs={{0,2},{1,3},{2,0},{3,1},{4,6},{5,7},{6,4},{7,5},{8,10},{9,11},{10,... | collective-permute-start | bytes 393224 | tf_op jit(solution)/shard_map/ppermute | solution.py:162
  99.8 157.4 %all-gather.17.cloned.1.call-start = ((), (), s32[]{:S(2)}) async-start(), calls=%async_computation.6 | async-start | bytes 1179648 | tf_op jit(solution)/shard_map/all_gather | solution.py:1002
  106.9 18.4 %collective-permute-start.29 = (bf16[4,2,256,128]{3,2,1,0:T(8,128)(2,1)}, bf16[4,2,256,128]{3,2,1,0:T(8,128)(2,1)S(1)}, u32[]{:S(2)}, u32[]{:S(2)}) collective-permute-start(bf16[4,2,256,128]{3,2,1,0:T(8,128)(2,1)} %get-tuple-element.140), channel_id=1, source_target_pairs={{0,4},{4,0},{8,12},{12,8},{16,20},{20,16},{24,28},{28,24},{1,5},{5... | collective-permute-start | bytes 1572872 | tf_op jit(solution)/shard_map/ppermute | solution.py:162
  118.3 12.9 %collective-permute-start.31 = (bf16[256,256]{1,0:T(8,128)(2,1)S(1)}, bf16[256,256]{1,0:T(8,128)(2,1)S(1)}, u32[]{:S(2)}, u32[]{:S(2)}) collective-permute-start(bf16[256,256]{1,0:T(8,128)(2,1)S(1)} %get-tuple-element.141.refs_0_.refs_3_), channel_id=1, source_target_pairs={{0,2},{1,3},{2,0},{3,1},{4,6},{5,7},{6,4},{7,5},{8,10},{9,11},{10,... | collective-permute-start | bytes 393224 | tf_op jit(solution)/shard_map/ppermute | solution.py:162
  119.3 11.9 %collective-permute-start.32 = (bf16[256,256]{1,0:T(8,128)(2,1)S(1)}, bf16[256,256]{1,0:T(8,128)(2,1)S(1)}, u32[]{:S(2)}, u32[]{:S(2)}) collective-permute-start(bf16[256,256]{1,0:T(8,128)(2,1)S(1)} %get-tuple-element.141.refs_0_.refs_3_), channel_id=1, source_target_pairs={{0,3},{1,2},{2,1},{3,0},{4,7},{5,6},{6,5},{7,4},{8,11},{9,10},{10,... | collective-permute-start | bytes 393224 | tf_op jit(solution)/shard_map/ppermute | solution.py:162
  161.1 99.5 %reduce-scatter.2.cloned.1.call-start = ((), (), s32[]{:S(2)}) async-start(), calls=%async_computation.2 | async-start | bytes 3538944 | tf_op jit(solution)/shard_map/reduce_scatter | solution.py:1030
  162.4 12.5 %collective-permute-start.38 = (bf16[512,256]{1,0:T(8,128)(2,1)}, bf16[512,256]{1,0:T(8,128)(2,1)S(1)}, u32[]{:S(2)}, u32[]{:S(2)}) collective-permute-start(bf16[512,256]{1,0:T(8,128)(2,1)} %get-tuple-element.154), channel_id=1, source_target_pairs={{0,16},{4,20},{8,24},{12,28},{16,0},{20,4},{24,8},{28,12},{1,17},{... | collective-permute-start | bytes 786440 | tf_op jit(solution)/shard_map/ppermute | solution.py:162
  164.1 11.8 %collective-permute-start.39 = (bf16[512,256]{1,0:T(8,128)(2,1)}, bf16[512,256]{1,0:T(8,128)(2,1)S(1)}, u32[]{:S(2)}, u32[]{:S(2)}) collective-permute-start(bf16[512,256]{1,0:T(8,128)(2,1)} %get-tuple-element.155), channel_id=1, source_target_pairs={{0,24},{4,28},{8,16},{12,20},{16,8},{20,12},{24,0},{28,4},{1,25},{... | collective-permute-start | bytes 786440 | tf_op jit(solution)/shard_map/ppermute | solution.py:162
  186.0 92.1 %all-gather.11.cloned.1.call-start = ((), (), s32[]{:S(2)}) async-start(), calls=%async_computation.3 | async-start | bytes 2359296 | tf_op jit(solution)/shard_map/all_gather | solution.py:1087
  190.5 13.5 %collective-permute-start.45 = (bf16[272,256]{1,0:T(8,128)(2,1)S(1)}, bf16[272,256]{1,0:T(8,128)(2,1)S(1)}, u32[]{:S(2)}, u32[]{:S(2)}) collective-permute-start(bf16[272,256]{1,0:T(8,128)(2,1)S(1)} %get-tuple-element.171), channel_id=1, source_target_pairs={{0,2},{1,3},{2,0},{3,1},{4,6},{5,7},{6,4},{7,5},{8,10},{9,11},{10,... | collective-permute-start | bytes 417800 | tf_op jit(solution)/shard_map/ppermute | solution.py:162
  191.4 12.5 %collective-permute-start.46 = (bf16[272,256]{1,0:T(8,128)(2,1)S(1)}, bf16[272,256]{1,0:T(8,128)(2,1)S(1)}, u32[]{:S(2)}, u32[]{:S(2)}) collective-permute-start(bf16[272,256]{1,0:T(8,128)(2,1)S(1)} %get-tuple-element.172), channel_id=1, source_target_pairs={{0,3},{1,2},{2,1},{3,0},{4,7},{5,6},{6,5},{7,4},{8,11},{9,10},{10,... | collective-permute-start | bytes 417800 | tf_op jit(solution)/shard_map/ppermute | solution.py:162
  246.4 10.8 %collective-permute-start.58 = (bf16[256,256]{1,0:T(8,128)(2,1)S(1)}, bf16[256,256]{1,0:T(8,128)(2,1)S(1)}, u32[]{:S(2)}, u32[]{:S(2)}) collective-permute-start(bf16[256,256]{1,0:T(8,128)(2,1)S(1)} %get-tuple-element.202), channel_id=1, source_target_pairs={{0,1},{1,0},{2,3},{3,2},{4,5},{5,4},{6,7},{7,6},{8,9},{9,8},{10,11... | collective-permute-start | bytes 393224 | tf_op jit(solution)/shard_map/ppermute | solution.py:162
  248.4 14.6 %collective-permute-start.59 = (bf16[256,256]{1,0:T(8,128)(2,1)}, bf16[256,256]{1,0:T(8,128)(2,1)S(1)}, u32[]{:S(2)}, u32[]{:S(2)}) collective-permute-start(bf16[256,256]{1,0:T(8,128)(2,1)} %get-tuple-element.207), channel_id=1, source_target_pairs={{0,2},{1,3},{2,0},{3,1},{4,6},{5,7},{6,4},{7,5},{8,10},{9,11},{10,... | collective-permute-start | bytes 393224 | tf_op jit(solution)/shard_map/ppermute | solution.py:162
  249.2 13.9 %collective-permute-start.60 = (bf16[256,256]{1,0:T(8,128)(2,1)S(1)}, bf16[256,256]{1,0:T(8,128)(2,1)S(1)}, u32[]{:S(2)}, u32[]{:S(2)}) collective-permute-start(bf16[256,256]{1,0:T(8,128)(2,1)S(1)} %get-tuple-element.208), channel_id=1, source_target_pairs={{0,3},{1,2},{2,1},{3,0},{4,7},{5,6},{6,5},{7,4},{8,11},{9,10},{10,... | collective-permute-start | bytes 393224 | tf_op jit(solution)/shard_map/ppermute | solution.py:162
  250.8 25.8 %collective-permute-start.68 = (bf16[2,2,256,128]{3,2,1,0:T(8,128)(2,1)S(1)}, bf16[2,2,256,128]{3,2,1,0:T(8,128)(2,1)}, u32[]{:S(2)}, u32[]{:S(2)}) collective-permute-start(bf16[2,2,256,128]{3,2,1,0:T(8,128)(2,1)S(1)} %copy-done.35), channel_id=1, source_target_pairs={{0,24},{4,28},{8,16},{12,20},{16,8},{20,12},{24,0},{28,4},{1,25},{... | collective-permute-start | bytes 786440 | tf_op jit(solution)/shard_map/ppermute | solution.py:162
  266.2 10.4 %collective-permute-start.65 = (f32[2,256]{1,0:T(2,128)S(1)}, f32[2,256]{1,0:T(2,128)S(1)}, u32[]{:S(2)}, u32[]{:S(2)}) collective-permute-start(f32[2,256]{1,0:T(2,128)S(1)} %add.47.refs_0_), channel_id=1, source_target_pairs={{0,8},{4,12},{8,0},{12,4},{16,24},{20,28},{24,16},{28,20},{1,9},{5... | collective-permute-start | bytes 6152 | tf_op jit(solution)/shard_map/ppermute | solution.py:162
  270.9 15.5 %collective-permute-start.61 = (bf16[256,256]{1,0:T(8,128)(2,1)S(1)}, bf16[256,256]{1,0:T(8,128)(2,1)S(1)}, u32[]{:S(2)}, u32[]{:S(2)}) collective-permute-start(bf16[256,256]{1,0:T(8,128)(2,1)S(1)} %get-tuple-element.210), channel_id=1, source_target_pairs={{0,1},{1,0},{2,3},{3,2},{4,5},{5,4},{6,7},{7,6},{8,9},{9,8},{10,11... | collective-permute-start | bytes 393224 | tf_op jit(solution)/shard_map/ppermute | solution.py:162
  274.2 12.9 %collective-permute-start.62 = (bf16[256,256]{1,0:T(8,128)(2,1)S(1)}, bf16[256,256]{1,0:T(8,128)(2,1)S(1)}, u32[]{:S(2)}, u32[]{:S(2)}) collective-permute-start(bf16[256,256]{1,0:T(8,128)(2,1)S(1)} %get-tuple-element.211), channel_id=1, source_target_pairs={{0,2},{1,3},{2,0},{3,1},{4,6},{5,7},{6,4},{7,5},{8,10},{9,11},{10,... | collective-permute-start | bytes 393224 | tf_op jit(solution)/shard_map/ppermute | solution.py:162
  275.0 12.2 %collective-permute-start.63 = (bf16[256,256]{1,0:T(8,128)(2,1)S(1)}, bf16[256,256]{1,0:T(8,128)(2,1)S(1)}, u32[]{:S(2)}, u32[]{:S(2)}) collective-permute-start(bf16[256,256]{1,0:T(8,128)(2,1)S(1)} %get-tuple-element.212), channel_id=1, source_target_pairs={{0,3},{1,2},{2,1},{3,0},{4,7},{5,6},{6,5},{7,4},{8,11},{9,10},{10,... | collective-permute-start | bytes 393224 | tf_op jit(solution)/shard_map/ppermute | solution.py:162
  (82 other events, 806.8 us)
Sparse Core Ops, SparseCore 0:
  10.5 49.5 all-gather.8
  62.6 32.5 all-gather.12
  99.9 25.9 all-gather.14
  161.2 26.9 all-gather.16
  191.4 46.3 reduce-scatter.1
  240.7 31.5 all-gather.10

commit v4 on v3

--- a/solution.py
+++ b/solution.py
@@ -873,11 +873,6 @@
     )
     first_parts = part_totals(sums)
     kernel_one = gathered_blocks(conv_weights[0])
-    maps = jnp.concatenate(
-        [attn_in, jnp.transpose(jnp.stack([out_self, out_cross]), (0, 2, 1))], axis=0
-    )
-    maps = gathered_blocks(maps)[0]
-
     features = sinusoid(timestep).astype(jnp.bfloat16)
     present = jnp.arange(TEXT)[None, :] < text_length[:, None]
     pooled = jnp.einsum(
@@ -905,16 +900,21 @@
         8,
         0,
     )
-    pieces = channel_pieces(first)
+    maps = jnp.concatenate(
+        [after(attn_in, first), jnp.transpose(after(jnp.stack([out_self, out_cross]), first), (0, 2, 1))], axis=0
+    )
+    maps = gathered_blocks(maps)[0]
+    packs = channel_pieces(pack)
+    pieces = channel_pieces(after(first, packs))
     edges = piece_edges(pieces, col_count)
     later = after(conv_weights, first)[1]
     if has_slots():
         kernel_two = over_chips(later)
-        kernel_two += [flipped(part, "wide", 1) for part in kernel_two]
+        last = after(kernel_two[3], *edges)
+        kernel_two += [flipped(part, "wide", 1) for part in [*kernel_two[:3], last]]
     else:
         kernel_two = gathered_blocks(later)
-    packs = channel_pieces(after(pack, pieces))
-    pieces[0] = after(pieces[0], film_term, packs, text_term)
+    pieces[0] = after(pieces[0], film_term, text_term)
     inner, sums, *first_sends = convolve(
         spot, pieces, edges, kernel_one, own_pixels, row_pair, [], row_count, col_count
     )
@@ -1066,6 +1066,10 @@
     back_parts = convolve_back(
         spot, after(grad_two, mixed), edges, kernel_two, row_count, col_count
     )
+    mixed = sent_parts([after(part, back_parts[0]) for part in mixed])
+    result = middle
+    for part in mixed:
+        result = result + part.astype(jnp.float32)
     back_parts = sent_parts(back_parts)
     back, rows = local_kernel(
         functools.partial(second_back_body, groups, pixel_count),
@@ -1078,7 +1082,7 @@
     grad_one, last, head, film_rows, second_rows = local_kernel(
         functools.partial(second_input_body, pixel_count, col_count),
         [bf16_like(*flat), bf16_like(*edge), bf16_like(*edge), row_pair, f32_like(8, width_own)],
-        [spot, back, inner, inner_sums, film, affine[1], *part_totals(rows)],
+        [spot, after(back, mixed), inner, inner_sums, film, affine[1], *part_totals(rows)],
         [],
         16,
         0,
@@ -1114,10 +1118,6 @@
     back_parts[0], attn_in_grad, time_grad = lax.optimization_barrier(
         (back_parts[0], attn_in_grad, time_grad)
     )
-    mixed = sent_parts([after(part, *back_parts) for part in mixed])
-    result = middle
-    for part in mixed:
-        result = result + part.astype(jnp.float32)
     back, rows = local_kernel(
         functools.partial(first_back_body, groups, pixel_count),
         [f32_like(*flat), f32_like(2, width_own)],

time: 295 us -> 290 us (0.983)
  transfers between devices with their start and end apart: 75 -> 75, of which waited for: 37 -> 37; matrix products, arithmetic and copies ran while one was open for 3% -> 3% of each run, Pallas kernels for 19% -> 18%
where the time goes in v4:
time: 290 us
  starting transfers between devices  101 us (35%)
  waiting for transfers between devices  96 us (33%)
  Pallas kernels  62.7 us (22%)
  between operations  16.2 us (6%)
  local copies, waits for them, and re-layouts  7.85 us (3%)
  other arithmetic  3.97 us (1%)
    ppermute x63, starting transfers between devices, flipped(): return lax.ppermute(values, axis, [(i, i ^ mask) for i in range(count)])  97.3 us
    ppermute x63, waiting for transfers between devices, flipped(): return lax.ppermute(values, axis, [(i, i ^ mask) for i in range(count)])  85.4 us
    pallas_call x20, Pallas kernels, local_kernel(): pl.pallas_call(body, grid=(1,), out_shape=outs, in_specs=[in_smem] + [in_...  56.1 us
    ppermute x2, waiting for transfers between devices, relayed_block(): return lax.ppermute(jnp.where(odd, over_y, over_x), 'wide', far_pairs)  10.4 us
    pallas_call x1, Pallas kernels, kernel_grad(): pl.pallas_call(functools.partial(kernel_grad_body, width), out_shape=f32_...  6.57 us
  transfers between devices with their start and end apart: 75, of which 37 were waited for; matrix products, arithmetic and copies ran while one was open for 3% of the time, Pallas kernels for 18%

profile of v4, /device:TPU:0, one launch (start us, length us, event | category | flops | bytes accessed | tf_op | source)
XLA Modules:
  0.0 289.6 jit_solution(12098102375766686855)
XLA Ops:
  12.9 2.6 collective-permute-start.1
  24.8 2.6 collective-permute-start.5
  30.4 6.9 %collective-permute-done.5.refs_2_.refs_6_.refs_9_ = bf16[272,256]{1,0:T(8,128)(2,1)S(1)} collective-permute-done((bf16[272,256]{1,0:T(8,128)(2,1)S(1)}, bf16[272,256]{1,0:T(8,128)(2,1)S(1)}, u32[]{:S(2)}, u32[]{:S(2)}) %collective-permute-start.5) | collective-permute-done | bytes 139296 | tf_op jit(solution)/shard_map/ppermute | solution.py:162
  43.4 7.6 %collective-permute-done.8.refs_2_ = bf16[256,256]{1,0:T(8,128)(2,1)S(1)} collective-permute-done((bf16[256,256]{1,0:T(8,128)(2,1)S(1)}, bf16[256,256]{1,0:T(8,128)(2,1)S(1)}, u32[]{:S(2)}, u32[]{:S(2)}) %collective-permute-start.8) | collective-permute-done | bytes 131104 | tf_op jit(solution)/shard_map/ppermute | solution.py:162
  54.6 2.9 %collective-permute-start.10 = (bf16[128,1024]{1,0:T(8,128)(2,1)S(1)}, bf16[128,1024]{1,0:T(8,128)(2,1)S(1)}, u32[]{:S(2)}, u32[]{:S(2)}) collective-permute-start(bf16[128,1024]{1,0:T(8,128)(2,1)S(1)} %get-tuple-element.130), channel_id=1, source_target_pairs={{0,4},{4,0},{8,12},{12,8},{16,20},{20,16},{24,28},{28,24},{1,5},{5... | collective-permute-start | bytes 786440 | tf_op jit(solution)/shard_map/ppermute | solution.py:162
  59.0 4.3 %collective-permute-done.14.refs_9_.refs_3_ = bf16[9,128,256]{2,1,0:T(8,128)(2,1)} collective-permute-done((bf16[9,128,256]{2,1,0:T(8,128)(2,1)S(1)}, bf16[9,128,256]{2,1,0:T(8,128)(2,1)}, u32[]{:S(2)}, u32[]{:S(2)}) %collective-permute-start.14) | collective-permute-done | bytes 589856 | tf_op jit(solution)/shard_map/ppermute | solution.py:168
  65.8 4.6 %conv_body.2 = (f32[256,256]{1,0:T(8,128)S(1)}, f32[2,256]{1,0:T(2,128)S(1)}, bf16[4,256,128]{2,1,0:T(8,128)(2,1)S(1)}, bf16[4,256,128]{2,1,0:T(8,128)(2,1)S(1)}) custom-call(s32[3]{0:T(128)S(1)} %pad_add_fusion.spot, bf16[256,256]{1,0:T(8,128)(2,1)S(1)} %get-tuple-element.129.refs_0_, bf16[256,256]{1,0:T(8,128)(2,1)S(1)} %collective-permute-done.7.refs_1_, ...), custom_call_target="tpu_custom_call" | custom-call | flops 1207959552 | bytes 6686732 | tf_op jit(solution)/shard_map/conv_body/pallas_call | solution.py:24
  71.7 3.1 %collective-permute-start.20 = (f32[4,256]{1,0:T(4,128)S(1)}, f32[4,256]{1,0:T(4,128)S(1)}, u32[]{:S(2)}, u32[]{:S(2)}) collective-permute-start(f32[4,256]{1,0:T(4,128)S(1)} %fusion.17.refs_0_), channel_id=1, source_target_pairs={{0,8},{4,12},{8,0},{12,4},{16,24},{20,28},{24,16},{28,20},{1,9},{5... | collective-permute-start | bytes 12296 | tf_op jit(solution)/shard_map/ppermute | solution.py:162
  78.4 2.7 collective-permute-done.22.refs_3_
  83.2 2.9 %collective-permute-start.24 = (bf16[256,256]{1,0:T(8,128)(2,1)S(1)}, bf16[256,256]{1,0:T(8,128)(2,1)S(1)}, u32[]{:S(2)}, u32[]{:S(2)}) collective-permute-start(bf16[256,256]{1,0:T(8,128)(2,1)S(1)} %get-tuple-element.136.refs_0_), channel_id=1, source_target_pairs={{0,2},{1,3},{2,0},{3,1},{4,6},{5,7},{6,4},{7,5},{8,10},{9,11},{10,... | collective-permute-start | bytes 393224 | tf_op jit(solution)/shard_map/ppermute | solution.py:162
  88.6 6.9 %collective-permute-done.24.refs_2_ = bf16[256,256]{1,0:T(8,128)(2,1)S(1)} collective-permute-done((bf16[256,256]{1,0:T(8,128)(2,1)S(1)}, bf16[256,256]{1,0:T(8,128)(2,1)S(1)}, u32[]{:S(2)}, u32[]{:S(2)}) %collective-permute-start.24) | collective-permute-done | bytes 131104 | tf_op jit(solution)/shard_map/ppermute | solution.py:162
  97.3 5.5 %conv_body.3 = (f32[256,256]{1,0:T(8,128)S(1)}, bf16[256,256]{1,0:T(8,128)(2,1)S(1)}, bf16[4,2,256,128]{3,2,1,0:T(8,128)(2,1)S(1)}, bf16[4,2,256,128]{3,2,1,0:T(8,128)(2,1)}) custom-call(s32[3]{0:T(128)S(1)} %pad_add_fusion.spot, bf16[256,256]{1,0:T(8,128)(2,1)S(1)} %get-tuple-element.136.refs_0_, bf16[256,256]{1,0:T(8,128)(2,1)S(1)} %collective-permute-done.23.refs_1_, ...), custom_call_target="tpu_custom_call" | custom-call | flops 1207959552 | bytes 7864332 | tf_op jit(solution)/shard_map/conv_body/pallas_call | solution.py:24
  103.5 8.9 %collective-permute-start.29 = (bf16[4,2,256,128]{3,2,1,0:T(8,128)(2,1)}, bf16[4,2,256,128]{3,2,1,0:T(8,128)(2,1)S(1)}, u32[]{:S(2)}, u32[]{:S(2)}) collective-permute-start(bf16[4,2,256,128]{3,2,1,0:T(8,128)(2,1)} %get-tuple-element.147), channel_id=1, source_target_pairs={{0,4},{4,0},{8,12},{12,8},{16,20},{20,16},{24,28},{28,24},{1,5},{5... | collective-permute-start | bytes 1572872 | tf_op jit(solution)/shard_map/ppermute | solution.py:162
  116.8 2.6 out_grad_body.1
  121.4 5.9 %collective-permute-done.31.refs_2_.refs_5_ = bf16[256,256]{1,0:T(8,128)(2,1)S(1)} collective-permute-done((bf16[256,256]{1,0:T(8,128)(2,1)S(1)}, bf16[256,256]{1,0:T(8,128)(2,1)S(1)}, u32[]{:S(2)}, u32[]{:S(2)}) %collective-permute-start.31) | collective-permute-done | bytes 131104 | tf_op jit(solution)/shard_map/ppermute | solution.py:162
  127.3 3.9 %project_body.1 = (bf16[256,128]{1,0:T(8,128)(2,1)S(1)}, bf16[256,256]{1,0:T(8,128)(2,1)S(1)}, bf16[256,384]{1,0:T(8,128)(2,1)S(1)}, bf16[256,256]{1,0:T(8,128)(...) custom-call(s32[3]{0:T(128)S(1)} %pad_add_fusion.spot, ...), custom_call_target="tpu_custom_call" | custom-call | flops 536870912 | bytes 5801996 | tf_op jit(solution)/shard_map/project_body/pallas_call | solution.py:24
  134.2 6.9 %collective-permute-done.34.refs_1_ = bf16[512,256]{1,0:T(8,128)(2,1)S(1)} collective-permute-done((bf16[512,256]{1,0:T(8,128)(2,1)S(1)}, bf16[512,256]{1,0:T(8,128)(2,1)S(1)}, u32[]{:S(2)}, u32[]{:S(2)}) %collective-permute-start.34) | collective-permute-done | bytes 262176 | tf_op jit(solution)/shard_map/ppermute | solution.py:162
  142.7 6.1 %collective-permute-done.36.refs_3_ = bf16[512,256]{1,0:T(8,128)(2,1)S(1)} collective-permute-done((bf16[512,256]{1,0:T(8,128)(2,1)S(1)}, bf16[512,256]{1,0:T(8,128)(2,1)S(1)}, u32[]{:S(2)}, u32[]{:S(2)}) %collective-permute-start.36) | collective-permute-done | bytes 262176 | tf_op jit(solution)/shard_map/ppermute | solution.py:168
  148.7 8.7 %attend_body.1 = (bf16[512,256]{1,0:T(8,128)(2,1)}, bf16[512,256]{1,0:T(8,128)(2,1)}, bf16[512,256]{1,0:T(8,128)(2,1)}, bf16[512,256]{1,0:T(8,128)(2,1)}, bf16[2...) custom-call(s32[3]{0:T(128)S(1)} %pad_add_fusion.spot, ...), custom_call_target="tpu_custom_call" | custom-call | flops 1879048192 | bytes 6291468 | tf_op jit(solution)/shard_map/attend_body/pallas_call | solution.py:24
  161.3 5.9 %collective-permute-done.37.refs_1_ = bf16[512,256]{1,0:T(8,128)(2,1)S(1)} collective-permute-done((bf16[512,256]{1,0:T(8,128)(2,1)}, bf16[512,256]{1,0:T(8,128)(2,1)S(1)}, u32[]{:S(2)}, u32[]{:S(2)}) %collective-permute-start.37) | collective-permute-done | bytes 262176 | tf_op jit(solution)/shard_map/ppermute | solution.py:162
  167.2 2.5 collective-permute-done.38.refs_2_
  175.2 6.6 %project_back_body.1 = (bf16[272,256]{1,0:T(8,128)(2,1)S(1)}, bf16[272,256]{1,0:T(8,128)(2,1)S(1)}, bf16[272,256]{1,0:T(8,128)(2,1)S(1)}, bf16[272,256]{1,0:T(8,128)(2,1)S(1)}, bf16[1024,1536]{1,0:T(8,128)(2,1)}) custom-call(s32[3]{0:T(128)S(1)} %pad_add_fusion.spot, bf16[256,128]{1,0:T(8,128)(2,1)} %get-tuple-element.157.kq, ...), custom_call_target="tpu_custom_call" | custom-call | flops 1342177280 | bytes 9242636 | tf_op jit(solution)/shard_map/project_back_body/pallas_call | solution.py:24
  191.5 7.8 %collective-permute-done.45.refs_2_ = bf16[272,256]{1,0:T(8,128)(2,1)S(1)} collective-permute-done((bf16[272,256]{1,0:T(8,128)(2,1)S(1)}, bf16[272,256]{1,0:T(8,128)(2,1)S(1)}, u32[]{:S(2)}, u32[]{:S(2)}) %collective-permute-start.45) | collective-permute-done | bytes 139296 | tf_op jit(solution)/shard_map/ppermute | solution.py:162
  200.9 2.5 mix_body.1
  203.4 3.8 %back_body.2 = (bf16[256,256]{1,0:T(8,128)(2,1)S(1)}, bf16[256,256]{1,0:T(8,128)(2,1)S(1)}, bf16[256,256]{1,0:T(8,128)(2,1)S(1)}, bf16[256,256]{1,0:T(8,128)(2,1)S(1)}) custom-call(s32[3]{0:T(128)S(1)} %pad_add_fusion.spot, bf16[256,256]{1,0:T(8,128)(2,1)S(1)} %get-tuple-element.187.grad, bf16[128,256]{1,0:T(8,128)(2,1)S(1)} %collective-permute-done.47.near, ...), custom_call_target="tpu_custom_call" | custom-call | flops 1207959552 | bytes 5505036 | tf_op jit(solution)/shard_map/back_body/pallas_call | solution.py:24
  220.0 6.7 %collective-permute-start.55 = (f32[8,256]{1,0:T(8,128)S(1)}, f32[8,256]{1,0:T(8,128)S(1)}, u32[]{:S(2)}, u32[]{:S(2)}) collective-permute-start(f32[8,256]{1,0:T(8,128)S(1)} %get-tuple-element.204), channel_id=1, source_target_pairs={{0,4},{4,0},{8,12},{12,8},{16,20},{20,16},{24,28},{28,24},{1,5},{5... | collective-permute-start | bytes 24584 | tf_op jit(solution)/shard_map/ppermute | solution.py:162
  232.4 2.6 collective-permute-done.58.refs_3_
  237.4 3.6 %collective-permute-start.59 = (bf16[128,256]{1,0:T(8,128)(2,1)S(1)}, bf16[128,256]{1,0:T(8,128)(2,1)S(1)}, u32[]{:S(2)}, u32[]{:S(2)}) collective-permute-start(bf16[128,256]{1,0:T(8,128)(2,1)S(1)} %get-tuple-element.208), channel_id=1, source_target_pairs={{0,4},{4,0},{8,12},{12,8},{16,20},{20,16},{24,28},{28,24},{1,5},{5... | collective-permute-start | bytes 196616 | tf_op jit(solution)/shard_map/ppermute | solution.py:162
  241.9 3.8 %back_body.3 = (bf16[256,256]{1,0:T(8,128)(2,1)S(1)}, bf16[256,256]{1,0:T(8,128)(2,1)S(1)}, bf16[256,256]{1,0:T(8,128)(2,1)S(1)}, bf16[256,256]{1,0:T(8,128)(2,1)S(1)}) custom-call(s32[3]{0:T(128)S(1)} %pad_add_fusion.spot, bf16[256,256]{1,0:T(8,128)(2,1)S(1)} %get-tuple-element.205.grad, bf16[128,256]{1,0:T(8,128)(2,1)S(1)} %collective-permute-done.59.near, ...), custom_call_target="tpu_custom_call" | custom-call | flops 1207959552 | bytes 5505036 | tf_op jit(solution)/shard_map/back_body/pallas_call | solution.py:24
  247.7 9.1 %collective-permute-start.61 = (bf16[256,256]{1,0:T(8,128)(2,1)S(1)}, bf16[256,256]{1,0:T(8,128)(2,1)S(1)}, u32[]{:S(2)}, u32[]{:S(2)}) collective-permute-start(bf16[256,256]{1,0:T(8,128)(2,1)S(1)} %get-tuple-element.214), channel_id=1, source_target_pairs={{0,1},{1,0},{2,3},{3,2},{4,5},{5,4},{6,7},{7,6},{8,9},{9,8},{10,11... | collective-permute-start | bytes 393224 | tf_op jit(solution)/shard_map/ppermute | solution.py:162
  260.8 3.4 %text_out_body.1 = (f32[128,2,256]{2,1,0:T(2,128)}, f32[512,2,256]{2,1,0:T(2,128)}, f32[2,512,256]{2,1,0:T(8,128)}) custom-call(s32[3]{0:T(128)S(1)} %pad_add_fusion.spot, f32[2,256]{1,0:T(2,128)S(1)} %get-tuple-element.215.film, bf16[1,128]{1,0:T(2,128)(2,1)S(1)} %fusion.13.features, bf16[1,512]{1,0:T(2,128)(2,1)S(1)} %dynamic_slice.11.pooled, ...), custom_call_target="tpu_custom_call" | custom-call | flops 67108864 | bytes 3542284 | tf_op jit(solution)/shard_map/text_out_body/pallas_call | solution.py:24
  274.5 6.6 %kernel_grad_body.1 = f32[2,9,128,256]{3,2,1,0:T(8,128)} custom-call(s32[3]{0:T(128)S(1)} %pad_add_fusion.spot, bf16[4,2,256,128]{3,2,1,0:T(8,128)(2,1)} %copy-done.17, bf16[4,2,256,128]{3,2,1,0:T(8,128)(2,1)} %copy-done.31, bf16[2,2,256,128]{3,2,1,0:T(8,128)(2,1)} %copy-done.34, bf16[2,2,256,128]{3,2,1,0:T(8,128)(2,1)} %copy-done.33, ...), custom_call_target="tpu_custom_call" | custom-call | flops 2415919104 | bytes 6291456 | tf_op jit(solution)/shard_map/kernel_grad_body/pallas_call | solution.py:299
  (262 shorter events, 113.0 us)
Async XLA Ops:
  7.3 58.5 %all-gather.9.cloned.1.call-start = ((), (), s32[]{:S(2)}) async-start(), calls=%async_computation.1 | async-start | bytes 5308416 | tf_op jit(solution)/shard_map/all_gather | solution.py:185
  9.4 107.4 %all-gather.13.cloned.1.call-start = ((), (), s32[]{:S(2)}) async-start(), calls=%async_computation.4 | async-start | bytes 3538944 | tf_op jit(solution)/shard_map/all_gather | solution.py:185
  23.1 125.6 %all-gather.15.cloned.1.call-start = ((), (), s32[]{:S(2)}) async-start(), calls=%async_computation.5 | async-start | bytes 1179648 | tf_op jit(solution)/shard_map/all_gather | solution.py:931
  24.8 12.5 %collective-permute-start.5 = (bf16[272,256]{1,0:T(8,128)(2,1)S(1)}, bf16[272,256]{1,0:T(8,128)(2,1)S(1)}, u32[]{:S(2)}, u32[]{:S(2)}) collective-permute-start(bf16[272,256]{1,0:T(8,128)(2,1)S(1)} %get-tuple-element.142.refs_0_.refs_4_.refs_7_), channel_id=1, source_target_pairs={{0,2},{1,3},{2,0},{3,1},{4,6},{5,7},{6,4},{7,5},{8,10},{9,11},{10,... | collective-permute-start | bytes 417800 | tf_op jit(solution)/shard_map/ppermute | solution.py:162
  27.4 9.9 %collective-permute-start.6 = (bf16[272,256]{1,0:T(8,128)(2,1)S(1)}, bf16[272,256]{1,0:T(8,128)(2,1)S(1)}, u32[]{:S(2)}, u32[]{:S(2)}) collective-permute-start(bf16[272,256]{1,0:T(8,128)(2,1)S(1)} %get-tuple-element.142.refs_0_.refs_4_.refs_7_), channel_id=1, source_target_pairs={{0,3},{1,2},{2,1},{3,0},{4,7},{5,6},{6,5},{7,4},{8,11},{9,10},{10,... | collective-permute-start | bytes 417800 | tf_op jit(solution)/shard_map/ppermute | solution.py:162
  29.6 22.6 %collective-permute-start.12 = (bf16[9,128,256]{2,1,0:T(8,128)(2,1)}, bf16[9,128,256]{2,1,0:T(8,128)(2,1)}, u32[]{:S(2)}, u32[]{:S(2)}) collective-permute-start(bf16[9,128,256]{2,1,0:T(8,128)(2,1)} %slice_bitcast_fusion.refs_6_.refs_0_), channel_id=1, source_target_pairs={{0,8},{4,12},{8,0},{12,4},{16,24},{20,28},{24,16},{28,20},{1,9},{5... | collective-permute-start | bytes 1769480 | tf_op jit(solution)/shard_map/ppermute | solution.py:162
  30.1 22.1 %collective-permute-start.13 = (bf16[9,128,256]{2,1,0:T(8,128)(2,1)}, bf16[9,128,256]{2,1,0:T(8,128)(2,1)}, u32[]{:S(2)}, u32[]{:S(2)}) collective-permute-start(bf16[9,128,256]{2,1,0:T(8,128)(2,1)} %slice_bitcast_fusion.refs_6_.refs_0_), channel_id=1, source_target_pairs={{0,16},{4,20},{8,24},{12,28},{16,0},{20,4},{24,8},{28,12},{1,17},{... | collective-permute-start | bytes 1769480 | tf_op jit(solution)/shard_map/ppermute | solution.py:162
  39.4 11.6 %collective-permute-start.8 = (bf16[256,256]{1,0:T(8,128)(2,1)S(1)}, bf16[256,256]{1,0:T(8,128)(2,1)S(1)}, u32[]{:S(2)}, u32[]{:S(2)}) collective-permute-start(bf16[256,256]{1,0:T(8,128)(2,1)S(1)} %get-tuple-element.129.refs_0_), channel_id=1, source_target_pairs={{0,2},{1,3},{2,0},{3,1},{4,6},{5,7},{6,4},{7,5},{8,10},{9,11},{10,... | collective-permute-start | bytes 393224 | tf_op jit(solution)/shard_map/ppermute | solution.py:162
  40.4 13.3 %collective-permute-start.9 = (bf16[256,256]{1,0:T(8,128)(2,1)S(1)}, bf16[256,256]{1,0:T(8,128)(2,1)S(1)}, u32[]{:S(2)}, u32[]{:S(2)}) collective-permute-start(bf16[256,256]{1,0:T(8,128)(2,1)S(1)} %get-tuple-element.129.refs_0_), channel_id=1, source_target_pairs={{0,3},{1,2},{2,1},{3,0},{4,7},{5,6},{6,5},{7,4},{8,11},{9,10},{10,... | collective-permute-start | bytes 393224 | tf_op jit(solution)/shard_map/ppermute | solution.py:162
  53.3 10.1 %collective-permute-start.14 = (bf16[9,128,256]{2,1,0:T(8,128)(2,1)S(1)}, bf16[9,128,256]{2,1,0:T(8,128)(2,1)}, u32[]{:S(2)}, u32[]{:S(2)}) collective-permute-start(bf16[9,128,256]{2,1,0:T(8,128)(2,1)S(1)} %broadcast_select_fusion), channel_id=1, source_target_pairs={{0,16},{4,12},{8,24},{12,4},{16,0},{20,28},{24,8},{28,20},{1,17},{... | collective-permute-start | bytes 1769480 | tf_op jit(solution)/shard_map/ppermute | solution.py:168
  57.7 12.7 %collective-permute-start.15 = (bf16[9,128,256]{2,1,0:T(8,128)(2,1)}, bf16[9,128,256]{2,1,0:T(8,128)(2,1)}, u32[]{:S(2)}, u32[]{:S(2)}) collective-permute-start(bf16[9,128,256]{2,1,0:T(8,128)(2,1)} %slice_bitcast_fusion.refs_6_.refs_0_), channel_id=1, source_target_pairs={{0,4},{4,0},{8,12},{12,8},{16,20},{20,16},{24,28},{28,24},{1,5},{5... | collective-permute-start | bytes 1769480 | tf_op jit(solution)/shard_map/ppermute | solution.py:162
  57.7 12.7 %collective-permute-start.16 = (bf16[9,128,256]{2,1,0:T(8,128)(2,1)}, bf16[9,128,256]{2,1,0:T(8,128)(2,1)}, u32[]{:S(2)}, u32[]{:S(2)}) collective-permute-start(bf16[9,128,256]{2,1,0:T(8,128)(2,1)} %collective-permute-done.12.refs_7_.refs_1_), channel_id=1, source_target_pairs={{0,4},{4,0},{8,12},{12,8},{16,20},{20,16},{24,28},{28,24},{1,5},{5... | collective-permute-start | bytes 1769480 | tf_op jit(solution)/shard_map/ppermute | solution.py:162
  58.6 11.8 %collective-permute-start.17 = (bf16[9,128,256]{2,1,0:T(8,128)(2,1)}, bf16[9,128,256]{2,1,0:T(8,128)(2,1)}, u32[]{:S(2)}, u32[]{:S(2)}) collective-permute-start(bf16[9,128,256]{2,1,0:T(8,128)(2,1)} %collective-permute-done.13.refs_8_.refs_2_), channel_id=1, source_target_pairs={{0,4},{4,0},{8,12},{12,8},{16,20},{20,16},{24,28},{28,24},{1,5},{5... | collective-permute-start | bytes 1769480 | tf_op jit(solution)/shard_map/ppermute | solution.py:162
  83.2 12.3 %collective-permute-start.24 = (bf16[256,256]{1,0:T(8,128)(2,1)S(1)}, bf16[256,256]{1,0:T(8,128)(2,1)S(1)}, u32[]{:S(2)}, u32[]{:S(2)}) collective-permute-start(bf16[256,256]{1,0:T(8,128)(2,1)S(1)} %get-tuple-element.136.refs_0_), channel_id=1, source_target_pairs={{0,2},{1,3},{2,0},{3,1},{4,6},{5,7},{6,4},{7,5},{8,10},{9,11},{10,... | collective-permute-start | bytes 393224 | tf_op jit(solution)/shard_map/ppermute | solution.py:162
  96.5 164.4 %all-gather.17.cloned.1.call-start = ((), (), s32[]{:S(2)}) async-start(), calls=%async_computation.6 | async-start | bytes 1179648 | tf_op jit(solution)/shard_map/all_gather | solution.py:1002
  103.5 17.8 %collective-permute-start.29 = (bf16[4,2,256,128]{3,2,1,0:T(8,128)(2,1)}, bf16[4,2,256,128]{3,2,1,0:T(8,128)(2,1)S(1)}, u32[]{:S(2)}, u32[]{:S(2)}) collective-permute-start(bf16[4,2,256,128]{3,2,1,0:T(8,128)(2,1)} %get-tuple-element.147), channel_id=1, source_target_pairs={{0,4},{4,0},{8,12},{12,8},{16,20},{20,16},{24,28},{28,24},{1,5},{5... | collective-permute-start | bytes 1572872 | tf_op jit(solution)/shard_map/ppermute | solution.py:162
  114.3 12.9 %collective-permute-start.31 = (bf16[256,256]{1,0:T(8,128)(2,1)S(1)}, bf16[256,256]{1,0:T(8,128)(2,1)S(1)}, u32[]{:S(2)}, u32[]{:S(2)}) collective-permute-start(bf16[256,256]{1,0:T(8,128)(2,1)S(1)} %get-tuple-element.148.refs_0_.refs_3_), channel_id=1, source_target_pairs={{0,2},{1,3},{2,0},{3,1},{4,6},{5,7},{6,4},{7,5},{8,10},{9,11},{10,... | collective-permute-start | bytes 393224 | tf_op jit(solution)/shard_map/ppermute | solution.py:162
  115.5 11.8 %collective-permute-start.32 = (bf16[256,256]{1,0:T(8,128)(2,1)S(1)}, bf16[256,256]{1,0:T(8,128)(2,1)S(1)}, u32[]{:S(2)}, u32[]{:S(2)}) collective-permute-start(bf16[256,256]{1,0:T(8,128)(2,1)S(1)} %get-tuple-element.148.refs_0_.refs_3_), channel_id=1, source_target_pairs={{0,3},{1,2},{2,1},{3,0},{4,7},{5,6},{6,5},{7,4},{8,11},{9,10},{10,... | collective-permute-start | bytes 393224 | tf_op jit(solution)/shard_map/ppermute | solution.py:162
  157.5 106.7 %reduce-scatter.2.cloned.1.call-start = ((), (), s32[]{:S(2)}) async-start(), calls=%async_computation.2 | async-start | bytes 3538944 | tf_op jit(solution)/shard_map/reduce_scatter | solution.py:1030
  158.4 11.3 %collective-permute-start.38 = (bf16[512,256]{1,0:T(8,128)(2,1)}, bf16[512,256]{1,0:T(8,128)(2,1)S(1)}, u32[]{:S(2)}, u32[]{:S(2)}) collective-permute-start(bf16[512,256]{1,0:T(8,128)(2,1)} %get-tuple-element.161), channel_id=1, source_target_pairs={{0,16},{4,20},{8,24},{12,28},{16,0},{20,4},{24,8},{28,12},{1,17},{... | collective-permute-start | bytes 786440 | tf_op jit(solution)/shard_map/ppermute | solution.py:162
  159.4 12.1 %collective-permute-start.39 = (bf16[512,256]{1,0:T(8,128)(2,1)}, bf16[512,256]{1,0:T(8,128)(2,1)S(1)}, u32[]{:S(2)}, u32[]{:S(2)}) collective-permute-start(bf16[512,256]{1,0:T(8,128)(2,1)} %get-tuple-element.162), channel_id=1, source_target_pairs={{0,24},{4,28},{8,16},{12,20},{16,8},{20,12},{24,0},{28,4},{1,25},{... | collective-permute-start | bytes 786440 | tf_op jit(solution)/shard_map/ppermute | solution.py:162
  181.8 92.7 %all-gather.11.cloned.1.call-start = ((), (), s32[]{:S(2)}) async-start(), calls=%async_computation.3 | async-start | bytes 2359296 | tf_op jit(solution)/shard_map/all_gather | solution.py:1091
  185.9 13.4 %collective-permute-start.45 = (bf16[272,256]{1,0:T(8,128)(2,1)S(1)}, bf16[272,256]{1,0:T(8,128)(2,1)S(1)}, u32[]{:S(2)}, u32[]{:S(2)}) collective-permute-start(bf16[272,256]{1,0:T(8,128)(2,1)S(1)} %get-tuple-element.178), channel_id=1, source_target_pairs={{0,2},{1,3},{2,0},{3,1},{4,6},{5,7},{6,4},{7,5},{8,10},{9,11},{10,... | collective-permute-start | bytes 417800 | tf_op jit(solution)/shard_map/ppermute | solution.py:162
  187.3 12.0 %collective-permute-start.46 = (bf16[272,256]{1,0:T(8,128)(2,1)S(1)}, bf16[272,256]{1,0:T(8,128)(2,1)S(1)}, u32[]{:S(2)}, u32[]{:S(2)}) collective-permute-start(bf16[272,256]{1,0:T(8,128)(2,1)S(1)} %get-tuple-element.179), channel_id=1, source_target_pairs={{0,3},{1,2},{2,1},{3,0},{4,7},{5,6},{6,5},{7,4},{8,11},{9,10},{10,... | collective-permute-start | bytes 417800 | tf_op jit(solution)/shard_map/ppermute | solution.py:162
  212.1 18.3 %collective-permute-start.49 = (bf16[256,256]{1,0:T(8,128)(2,1)S(1)}, bf16[256,256]{1,0:T(8,128)(2,1)S(1)}, u32[]{:S(2)}, u32[]{:S(2)}) collective-permute-start(bf16[256,256]{1,0:T(8,128)(2,1)S(1)} %get-tuple-element.193), channel_id=1, source_target_pairs={{0,1},{1,0},{2,3},{3,2},{4,5},{5,4},{6,7},{7,6},{8,9},{9,8},{10,11... | collective-permute-start | bytes 393224 | tf_op jit(solution)/shard_map/ppermute | solution.py:162
  212.9 19.2 %collective-permute-start.50 = (bf16[256,256]{1,0:T(8,128)(2,1)S(1)}, bf16[256,256]{1,0:T(8,128)(2,1)S(1)}, u32[]{:S(2)}, u32[]{:S(2)}) collective-permute-start(bf16[256,256]{1,0:T(8,128)(2,1)S(1)} %get-tuple-element.194), channel_id=1, source_target_pairs={{0,2},{1,3},{2,0},{3,1},{4,6},{5,7},{6,4},{7,5},{8,10},{9,11},{10,... | collective-permute-start | bytes 393224 | tf_op jit(solution)/shard_map/ppermute | solution.py:162
  215.1 17.0 %collective-permute-start.51 = (bf16[256,256]{1,0:T(8,128)(2,1)S(1)}, bf16[256,256]{1,0:T(8,128)(2,1)S(1)}, u32[]{:S(2)}, u32[]{:S(2)}) collective-permute-start(bf16[256,256]{1,0:T(8,128)(2,1)S(1)} %get-tuple-element.195), channel_id=1, source_target_pairs={{0,3},{1,2},{2,1},{3,0},{4,7},{5,6},{6,5},{7,4},{8,11},{9,10},{10,... | collective-permute-start | bytes 393224 | tf_op jit(solution)/shard_map/ppermute | solution.py:162
  245.7 28.8 %collective-permute-start.68 = (bf16[2,2,256,128]{3,2,1,0:T(8,128)(2,1)S(1)}, bf16[2,2,256,128]{3,2,1,0:T(8,128)(2,1)}, u32[]{:S(2)}, u32[]{:S(2)}) collective-permute-start(bf16[2,2,256,128]{3,2,1,0:T(8,128)(2,1)S(1)} %copy-done.32), channel_id=1, source_target_pairs={{0,24},{4,28},{8,16},{12,20},{16,8},{20,12},{24,0},{28,4},{1,25},{... | collective-permute-start | bytes 786440 | tf_op jit(solution)/shard_map/ppermute | solution.py:162
  247.7 13.2 %collective-permute-start.61 = (bf16[256,256]{1,0:T(8,128)(2,1)S(1)}, bf16[256,256]{1,0:T(8,128)(2,1)S(1)}, u32[]{:S(2)}, u32[]{:S(2)}) collective-permute-start(bf16[256,256]{1,0:T(8,128)(2,1)S(1)} %get-tuple-element.214), channel_id=1, source_target_pairs={{0,1},{1,0},{2,3},{3,2},{4,5},{5,4},{6,7},{7,6},{8,9},{9,8},{10,11... | collective-permute-start | bytes 393224 | tf_op jit(solution)/shard_map/ppermute | solution.py:162
  256.8 11.9 %collective-permute-start.62 = (bf16[256,256]{1,0:T(8,128)(2,1)S(1)}, bf16[256,256]{1,0:T(8,128)(2,1)S(1)}, u32[]{:S(2)}, u32[]{:S(2)}) collective-permute-start(bf16[256,256]{1,0:T(8,128)(2,1)S(1)} %get-tuple-element.219), channel_id=1, source_target_pairs={{0,2},{1,3},{2,0},{3,1},{4,6},{5,7},{6,4},{7,5},{8,10},{9,11},{10,... | collective-permute-start | bytes 393224 | tf_op jit(solution)/shard_map/ppermute | solution.py:162
  257.4 11.4 %collective-permute-start.63 = (bf16[256,256]{1,0:T(8,128)(2,1)S(1)}, bf16[256,256]{1,0:T(8,128)(2,1)S(1)}, u32[]{:S(2)}, u32[]{:S(2)}) collective-permute-start(bf16[256,256]{1,0:T(8,128)(2,1)S(1)} %get-tuple-element.220), channel_id=1, source_target_pairs={{0,3},{1,2},{2,1},{3,0},{4,7},{5,6},{6,5},{7,4},{8,11},{9,10},{10,... | collective-permute-start | bytes 393224 | tf_op jit(solution)/shard_map/ppermute | solution.py:162
  270.9 10.1 %collective-permute-start.65 = (f32[2,256]{1,0:T(2,128)S(1)}, f32[2,256]{1,0:T(2,128)S(1)}, u32[]{:S(2)}, u32[]{:S(2)}) collective-permute-start(f32[2,256]{1,0:T(2,128)S(1)} %add.47.refs_0_), channel_id=1, source_target_pairs={{0,8},{4,12},{8,0},{12,4},{16,24},{20,28},{24,16},{28,20},{1,9},{5... | collective-permute-start | bytes 6152 | tf_op jit(solution)/shard_map/ppermute | solution.py:162
  (79 other events, 817.8 us)
Sparse Core Ops, SparseCore 0:
  10.5 50.2 all-gather.8
  63.3 32.4 all-gather.12
  98.3 24.3 all-gather.14
  157.6 26.0 all-gather.16
  187.0 46.3 reduce-scatter.1
  236.8 36.8 all-gather.10

commit v5 on v4

--- a/solution.py
+++ b/solution.py
@@ -233,7 +233,8 @@
     sends = [bf16_like(groups, *layers, area, block)] * count
     return local_kernel(
         functools.partial(conv_body, groups, len(kernel), len(earlier), rows, width),
-        [f32_like(area, span), second_shape] + sends,
+        [f32_like(area, span), second_shape]
+        + [far_like(shape) if earlier else shape for shape in sends],
         [spot, *pieces, *edges, *far(kernel), source, *far(earlier)],
         [pltpu.VMEM((groups, 3, (rows + 2) * width, span), jnp.bfloat16)],
         32,
@@ -554,7 +555,8 @@
 
 def project_body(groups, spot, *refs):
     pieces, packs = refs[:groups], refs[groups : 2 * groups]
-    own, maps, keep_query, keep, send, cross, normed, scaled, center, inverse = refs[2 * groups :]
+    own, maps, keep_query, keep, send, *rest = refs[2 * groups :]
+    cross, normed, scaled, center, inverse = rest
     weights = Weights([maps], spot, groups)
     odd = lax.rem(spot[0], 2) == 1
     area = own.shape[0]
@@ -619,7 +621,7 @@
 
 def mix_body(groups, spot, kept, other, crossed, maps, *outs):
     weights = Weights([maps], spot, groups)
-    attended = heads_joined(kept[...], other[...], lax.rem(spot[0], 2) == 1)
+    attended = heads_joined(kept[...], other[:, :HEAD_DIM], lax.rem(spot[0], 2) == 1)
     for mask in range(groups):
         total_sum = dot_last(attended, weights.tap(mask, 4))
         total_sum += dot_last(crossed[...], weights.tap(mask, 5))
@@ -671,11 +673,11 @@
         text_grad[1, :, lanes] = dot_first(low, back).astype(jnp.bfloat16)
 
 
-def attend_body(count, extra, spot, kept_query, got, kept_grad, got_grad, *refs):
+def attend_body(count, extra, halves, spot, kept_query, got, kept_grad, got_grad, *refs):
     blocks, refs = refs[:count], refs[count:]
     cross_in, refs = refs[: 3 + extra], refs[3 + extra :]
-    parts, refs = refs[:count], refs[count:]
-    keep_out, send_out, keep_query, send_query, *cross_out = refs
+    parts, refs = refs[: count * halves], refs[count * halves :]
+    keep_out, keep_query, send, *cross_out = refs
     cross_body(spot, *cross_in, *cross_out)
     query = jnp.concatenate([kept_query[...], got[:, 2 * HEAD_DIM :]], axis=0)
     grad = jnp.concatenate([kept_grad[...], got_grad[...]], axis=0)
@@ -688,7 +690,7 @@
         rescale = jnp.exp(top - raised)
         weights = jnp.exp(scores - raised)
         weight_sum = weight_sum * rescale + jnp.sum(weights, axis=0, keepdims=True)
-        values = block[:, HEAD_DIM:]
+        values = block[:, HEAD_DIM : 2 * HEAD_DIM]
         weighted = weighted * rescale + dot_first(values, weights.astype(jnp.bfloat16))
         return raised, weight_sum, weighted
 
@@ -706,34 +708,23 @@
     log_sum = top + jnp.log(weight_sum)
 
     def backward(state, block, index, start):
-        keys, values = block[:, :HEAD_DIM], block[:, HEAD_DIM:]
+        keys, values = block[:, :HEAD_DIM], block[:, HEAD_DIM : 2 * HEAD_DIM]
         probs = jnp.exp(dot_last(keys, query) * score_scale - log_sum)
         grad_values = dot(probs.astype(jnp.bfloat16), grad)
         grad_scores = (probs * (dot_last(values, grad) - delta)).astype(jnp.bfloat16)
         grad_keys = dot(grad_scores, query) * score_scale
-        rows = pl.ds(start if isinstance(start, int) else pl.multiple_of(start, 512), block.shape[0])
-        parts[index][rows, :] = jnp.concatenate([grad_keys, grad_values], axis=1).astype(
-            jnp.bfloat16
-        )
+        both = jnp.concatenate([grad_keys, grad_values], axis=1).astype(jnp.bfloat16)
+        rows = block.shape[0] // halves
+        first = start if isinstance(start, int) else pl.multiple_of(start, 512)
+        for half in range(halves):
+            parts[halves * index + half][pl.ds(first, rows), :] = both[half * rows : (half + 1) * rows]
         return state + dot_first(keys, grad_scores)
 
     flat = over_rows(blocks, backward, jnp.zeros((HEAD_DIM, queries), jnp.float32))
-    for values, keep, send in (
-        (attended, keep_out, send_out),
-        (flat * score_scale, keep_query, send_query),
-    ):
+    for index, (values, keep) in enumerate(((attended, keep_out), (flat * score_scale, keep_query))):
         turned_back = jnp.transpose(values).astype(jnp.bfloat16)
         keep[...] = turned_back[: queries // 2]
-        send[...] = turned_back[queries // 2 :]
-
-
-def key_sum_body(spot, sent_query, *refs):
-    *parts, keep, send = refs
-    both = parts_sum(parts).astype(jnp.bfloat16)
-    half = keep.shape[0]
-    keep[...] = both[:half]
-    send[:, : 2 * HEAD_DIM] = both[half:]
-    send[:, 2 * HEAD_DIM :] = sent_query[...]
+        send[:, index * HEAD_DIM : (index + 1) * HEAD_DIM] = turned_back[queries // 2 :]
 
 
 def leading_sum(ref):
@@ -743,24 +734,25 @@
     return summed
 
 
-def joined_grads(spot, kept_query, kept_pair, got, cross):
+def joined_grads(spot, kept_query, got, cross, kept_pairs, got_pairs):
     odd = lax.rem(spot[0], 2) == 1
-    parts = [got[:, i * HEAD_DIM : (i + 1) * HEAD_DIM] for i in range(3)]
+    own, other = [parts_sum(pairs).astype(jnp.bfloat16) for pairs in (kept_pairs, got_pairs)]
     return [
-        heads_joined(kept_query[...], parts[2], odd),
-        heads_joined(kept_pair[:, :HEAD_DIM], parts[0], odd),
-        heads_joined(kept_pair[:, HEAD_DIM:], parts[1], odd),
+        heads_joined(kept_query[...], got[:, HEAD_DIM:], odd),
+        heads_joined(own[:, :HEAD_DIM], other[:, :HEAD_DIM], odd),
+        heads_joined(own[:, HEAD_DIM:], other[:, HEAD_DIM:], odd),
         cross[...],
     ]
 
 
-def project_back_body(groups, spot, kq, kp, got, cross, center, inverse, kept, other, *refs):
+def project_back_body(groups, count, spot, kq, got, cross, center, inverse, kept, *refs):
     crossed, normed, maps, *refs = refs
+    kept_pairs, got_pairs, refs = refs[:count], refs[count : 2 * count], refs[2 * count :]
     pieces, packs = refs[:groups], refs[groups : 2 * groups]
     *outs, out, frame = refs[2 * groups :]
     odd = lax.rem(spot[0], 2) == 1
     weights = Weights([maps], spot, groups)
-    grads = joined_grads(spot, kq, kp, got, cross)
+    grads = joined_grads(spot, kq, got, cross, kept_pairs, got_pairs)
     area, span = cross.shape
     plain = dotted = 0.0
     for mask in range(groups):
@@ -787,7 +779,8 @@
     for part in outs:
         part[area:] = packed
     right = jnp.concatenate(grads, axis=1)
-    out_right = jnp.concatenate([heads_joined(kept[...], other[...], odd), crossed[...]], axis=1)
+    attended = heads_joined(kept[...], got[:, :HEAD_DIM], odd)
+    out_right = jnp.concatenate([attended, crossed[...]], axis=1)
     for mask in range(groups):
         frame[lax.bitwise_xor(spot[1], mask)] = packs[mask][:area]
     for chunk in range(groups):
@@ -947,7 +940,7 @@
     block_pair = [both_sends[0], flipped(both_sends[1], "wide", 1)] if has_slots() else []
     kept_grad, sent_grad, grad_crossed = local_kernel(
         functools.partial(out_grad_body, groups),
-        [bf16_like(*half), bf16_like(*half), bf16_like(*flat)],
+        [far_like(bf16_like(*half)), bf16_like(*half), far_like(bf16_like(*flat))],
         [spot, *far([after(packs[0], middle_low)] + packs[1:]), *far([maps])],
         [],
         16,
@@ -957,7 +950,7 @@
     middle_pieces[0] = after(middle_pieces[0], got_grad, block_pair)
     column = f32_like(token_count, 1)
     triple = bf16_like(token_count, 3 * HEAD_DIM)
-    kept_query, kept_pair, sent, cross_query, normed, scaled, center, inverse = local_kernel(
+    kept_query, kept_pair, sent, *outs = local_kernel(
         functools.partial(project_body, groups),
         [
             bf16_like(*half),
@@ -974,13 +967,16 @@
         24,
         4 * square,
     )
+    cross_query, normed, scaled, center, inverse = outs
     got = flipped(sent, "wide", 1)
     blocks = spread_chips(jnp.concatenate([kept_pair, got[:, : 2 * HEAD_DIM]]))
     pair_shapes = [bf16_like(2, *block.shape[1:]) for block in block_pair[:1] * 3]
-    attend_shapes = [bf16_like(*block.shape) for block in blocks] + [bf16_like(*half)] * 4
+    halves = 2 if has_slots() else 1
+    attend_shapes = [bf16_like(block.shape[0] // halves, 2 * HEAD_DIM) for block in blocks * halves]
+    attend_shapes += [bf16_like(*half), bf16_like(*half), bf16_like(*flat)]
     cross_shapes = [bf16_like(*flat), bf16_like(*flat), bf16_like(2, TEXT, width_own)]
     outs = local_kernel(
-        functools.partial(attend_body, len(blocks), len(block_pair)),
+        functools.partial(attend_body, len(blocks), len(block_pair), halves),
         [far_like(shape) for shape in attend_shapes + pair_shapes + cross_shapes],
         [
             spot,
@@ -996,30 +992,29 @@
         48,
         14 * (2 * token_count) * HEAD_DIM * pixel_count,
     )
-    key_parts, outs = outs[: len(blocks)], outs[len(blocks) :]
-    kept_out, sent_out, kept_dq, sent_dq, *block_pairs = outs
+    key_parts, outs = outs[: len(blocks) * halves], outs[len(blocks) * halves :]
+    kept_out, kept_dq, sent_both, *block_pairs = outs
     *block_pairs, crossed, grad_cross_query, text_grads = block_pairs
     text_sums = lax.all_gather(text_grads, "wide")
-    key_sums = gathered_sums(key_parts)
-    kept_dk, sent_all = local_kernel(
-        key_sum_body,
-        [bf16_like(*flat), bf16_like(token_count, 3 * HEAD_DIM)],
-        [spot, *far([sent_dq, key_sums[0]]), *key_sums[1:]],
-        [],
-        16,
-        0,
-    )
-    got_all = flipped(sent_all, "wide", 1)
-    got_out = flipped(sent_out, "wide", 1)
-    kept_dq, grad_cross_query = far([kept_dq, grad_cross_query])
-    projected_grads = [kept_dq, kept_dk, got_all, grad_cross_query]
+    if has_slots():
+        key_parts = [key_parts[0]] + [flipped(key_parts[mask], "wide", mask) for mask in range(1, 8)]
+        kept_pairs, got_pairs = key_parts[0::2], key_parts[1::2]
+        kept_pairs[0] = far(kept_pairs[:1])[0]
+    else:
+        (summed,) = gathered_sums(key_parts)
+        kept_pairs = [summed[:token_count]]
+        got_pairs = [flipped(summed[token_count:], "wide", 1)]
+    got_both = flipped(sent_both, "wide", 1)
     *norm_parts, weight_parts = local_kernel(
-        functools.partial(project_back_body, groups),
+        functools.partial(project_back_body, groups, len(kept_pairs)),
         [bf16_like(token_count + 16, width_own)] * groups + [far_like(bf16_like(C, 6 * width_own))],
         [
             spot,
-            *projected_grads,
-            *far([center, inverse, kept_out, got_out, crossed, normed, maps]),
+            *far([kept_dq]),
+            got_both,
+            *far([grad_cross_query, center, inverse, kept_out, crossed, normed, maps]),
+            *kept_pairs,
+            *got_pairs,
             *far(middle_pieces),
             *far(packs),
         ],
@@ -1058,7 +1053,7 @@
     mixed = local_kernel(
         functools.partial(mix_body, groups),
         [bf16_like(*flat)] * groups,
-        [spot, after(kept_out, grad_two), got_out, *far([crossed, maps])],
+        [spot, after(kept_out, grad_two), got_both, *far([crossed, maps])],
         [],
         16,
         2 * square,
@@ -1096,7 +1091,7 @@
         weight_out_body,
         [f32_like(4, C // lax.axis_size("wide"), width_own)]
         + [f32_like(width_own, C // lax.axis_size("wide"))] * 2,
-        [spot, after(weight_sums, back_parts[0])],
+        [spot, *far([after(weight_sums, back_parts[0])])],
         [],
         16,
         0,

time: 290 us -> 289 us (level)
  local copies, waits for them, and re-layouts: 7.85 us -> 4.8 us
  waiting for transfers between devices: 96 us -> 98.9 us
    unnamed x74 -> x62, local copies, waits for them, and re-layouts: 4.23 us -> 1.18 us
    ppermute x63 -> x66, waiting for transfers between devices: 85.4 us -> 87.3 us  [flipped(): return lax.ppermute(values, axis, [(i, i ^ mask) for i in range(count)])]
    ppermute x63 -> x66, starting transfers between devices: 97.3 us -> 95.7 us  [flipped(): return lax.ppermute(values, axis, [(i, i ^ mask) for i in range(count)])]
    pallas_call x20 -> x19, Pallas kernels: 56.1 us -> 56.6 us  [local_kernel(): pl.pallas_call(body, grid=(1,), out_shape=outs, in_specs=[in_smem] + [in_...]
  transfers between devices with their start and end apart: 75 -> 78, of which waited for: 37 -> 39; matrix products, arithmetic and copies ran while one was open for 3% -> 3% of each run, Pallas kernels for 18% -> 18%
where the time goes in v5:
time: 289 us; the launch traced here: 288 us
  starting transfers between devices  99.8 us (35%)
  waiting for transfers between devices  98.9 us (34%)
  Pallas kernels  63.2 us (22%)
  between operations  16.2 us (6%)
  local copies, waits for them, and re-layouts  4.8 us (2%)
  other arithmetic  3.97 us (1%)
    ppermute x66, starting transfers between devices, flipped(): return lax.ppermute(values, axis, [(i, i ^ mask) for i in range(count)])  95.7 us
    ppermute x66, waiting for transfers between devices, flipped(): return lax.ppermute(values, axis, [(i, i ^ mask) for i in range(count)])  87.3 us
    pallas_call x19, Pallas kernels, local_kernel(): pl.pallas_call(body, grid=(1,), out_shape=outs, in_specs=[in_smem] + [in_...  56.6 us
    ppermute x2, waiting for transfers between devices, relayed_block(): return lax.ppermute(jnp.where(odd, over_y, over_x), 'wide', far_pairs)  10.4 us
    pallas_call x1, Pallas kernels, kernel_grad(): pl.pallas_call(functools.partial(kernel_grad_body, width), out_shape=f32_...  6.56 us
  transfers between devices with their start and end apart: 78, of which 39 were waited for; matrix products, arithmetic and copies ran while one was open for 3% of the time, Pallas kernels for 18%

profile of v5, /device:TPU:0, one launch (start us, length us, event | category | flops | bytes accessed | tf_op | source)
XLA Modules:
  0.0 288.3 jit_solution(10799139837997767425)
XLA Ops:
  12.9 2.6 collective-permute-start.1
  24.8 2.6 collective-permute-start.5
  30.4 6.9 %collective-permute-done.5.refs_2_.refs_6_.refs_17_ = bf16[272,256]{1,0:T(8,128)(2,1)S(1)} collective-permute-done((bf16[272,256]{1,0:T(8,128)(2,1)S(1)}, bf16[272,256]{1,0:T(8,128)(2,1)S(1)}, u32[]{:S(2)}, u32[]{:S(2)}) %collective-permute-start.5) | collective-permute-done | bytes 139296 | tf_op jit(solution)/shard_map/ppermute | solution.py:162
  43.4 7.6 %collective-permute-done.8.refs_2_ = bf16[256,256]{1,0:T(8,128)(2,1)S(1)} collective-permute-done((bf16[256,256]{1,0:T(8,128)(2,1)S(1)}, bf16[256,256]{1,0:T(8,128)(2,1)S(1)}, u32[]{:S(2)}, u32[]{:S(2)}) %collective-permute-start.8) | collective-permute-done | bytes 131104 | tf_op jit(solution)/shard_map/ppermute | solution.py:162
  54.6 2.9 %collective-permute-start.10 = (bf16[128,1024]{1,0:T(8,128)(2,1)S(1)}, bf16[128,1024]{1,0:T(8,128)(2,1)S(1)}, u32[]{:S(2)}, u32[]{:S(2)}) collective-permute-start(bf16[128,1024]{1,0:T(8,128)(2,1)S(1)} %get-tuple-element.131), channel_id=1, source_target_pairs={{0,4},{4,0},{8,12},{12,8},{16,20},{20,16},{24,28},{28,24},{1,5},{5... | collective-permute-start | bytes 786440 | tf_op jit(solution)/shard_map/ppermute | solution.py:162
  59.0 4.3 %collective-permute-done.14.refs_9_.refs_3_ = bf16[9,128,256]{2,1,0:T(8,128)(2,1)} collective-permute-done((bf16[9,128,256]{2,1,0:T(8,128)(2,1)S(1)}, bf16[9,128,256]{2,1,0:T(8,128)(2,1)}, u32[]{:S(2)}, u32[]{:S(2)}) %collective-permute-start.14) | collective-permute-done | bytes 589856 | tf_op jit(solution)/shard_map/ppermute | solution.py:168
  65.8 4.6 %conv_body.2 = (f32[256,256]{1,0:T(8,128)S(1)}, f32[2,256]{1,0:T(2,128)S(1)}, bf16[4,256,128]{2,1,0:T(8,128)(2,1)S(1)}, bf16[4,256,128]{2,1,0:T(8,128)(2,1)S(1)}) custom-call(s32[3]{0:T(128)S(1)} %pad_add_fusion.spot, bf16[256,256]{1,0:T(8,128)(2,1)S(1)} %get-tuple-element.130.refs_0_, bf16[256,256]{1,0:T(8,128)(2,1)S(1)} %collective-permute-done.7.refs_1_, ...), custom_call_target="tpu_custom_call" | custom-call | flops 1207959552 | bytes 6686732 | tf_op jit(solution)/shard_map/conv_body/pallas_call | solution.py:24
  71.7 3.1 %collective-permute-start.20 = (f32[4,256]{1,0:T(4,128)S(1)}, f32[4,256]{1,0:T(4,128)S(1)}, u32[]{:S(2)}, u32[]{:S(2)}) collective-permute-start(f32[4,256]{1,0:T(4,128)S(1)} %fusion.17.refs_0_), channel_id=1, source_target_pairs={{0,8},{4,12},{8,0},{12,4},{16,24},{20,28},{24,16},{28,20},{1,9},{5... | collective-permute-start | bytes 12296 | tf_op jit(solution)/shard_map/ppermute | solution.py:162
  78.4 2.7 collective-permute-done.22.refs_3_
  83.2 2.9 %collective-permute-start.24 = (bf16[256,256]{1,0:T(8,128)(2,1)S(1)}, bf16[256,256]{1,0:T(8,128)(2,1)S(1)}, u32[]{:S(2)}, u32[]{:S(2)}) collective-permute-start(bf16[256,256]{1,0:T(8,128)(2,1)S(1)} %get-tuple-element.137.refs_0_), channel_id=1, source_target_pairs={{0,2},{1,3},{2,0},{3,1},{4,6},{5,7},{6,4},{7,5},{8,10},{9,11},{10,... | collective-permute-start | bytes 393224 | tf_op jit(solution)/shard_map/ppermute | solution.py:162
  88.6 6.9 %collective-permute-done.24.refs_2_ = bf16[256,256]{1,0:T(8,128)(2,1)S(1)} collective-permute-done((bf16[256,256]{1,0:T(8,128)(2,1)S(1)}, bf16[256,256]{1,0:T(8,128)(2,1)S(1)}, u32[]{:S(2)}, u32[]{:S(2)}) %collective-permute-start.24) | collective-permute-done | bytes 131104 | tf_op jit(solution)/shard_map/ppermute | solution.py:162
  97.3 5.6 %conv_body.3 = (f32[256,256]{1,0:T(8,128)S(1)}, bf16[256,256]{1,0:T(8,128)(2,1)S(1)}, bf16[4,2,256,128]{3,2,1,0:T(8,128)(2,1)}, bf16[4,2,256,128]{3,2,1,0:T(8,128)(2,1)}) custom-call(s32[3]{0:T(128)S(1)} %pad_add_fusion.spot, bf16[256,256]{1,0:T(8,128)(2,1)S(1)} %get-tuple-element.137.refs_0_, bf16[256,256]{1,0:T(8,128)(2,1)S(1)} %collective-permute-done.23.refs_1_, ...), custom_call_target="tpu_custom_call" | custom-call | flops 1207959552 | bytes 7864332 | tf_op jit(solution)/shard_map/conv_body/pallas_call | solution.py:24
  102.9 8.9 %collective-permute-start.29 = (bf16[4,2,256,128]{3,2,1,0:T(8,128)(2,1)}, bf16[4,2,256,128]{3,2,1,0:T(8,128)(2,1)S(1)}, u32[]{:S(2)}, u32[]{:S(2)}) collective-permute-start(bf16[4,2,256,128]{3,2,1,0:T(8,128)(2,1)} %get-tuple-element.148), channel_id=1, source_target_pairs={{0,4},{4,0},{8,12},{12,8},{16,20},{20,16},{24,28},{28,24},{1,5},{5... | collective-permute-start | bytes 1572872 | tf_op jit(solution)/shard_map/ppermute | solution.py:162
  116.2 3.3 %out_grad_body.1 = (bf16[256,128]{1,0:T(8,128)(2,1)}, bf16[256,128]{1,0:T(8,128)(2,1)S(1)}, bf16[256,256]{1,0:T(8,128)(2,1)}) custom-call(s32[3]{0:T(128)S(1)} %pad_add_fusion.spot, bf16[272,256]{1,0:T(8,128)(2,1)} %copy-done.2, bf16[272,256]{1,0:T(8,128)(2,1)} %copy-done.14, bf16[272,256]{1,0:T(8,128)(2,1)} %copy-done.15, bf16[272,256]{1,0:T(8,128)(2,1)} %copy-done.16, ...), custom_call_target="tpu_custom_call" | custom-call | flops 268435456 | bytes 3964940 | tf_op jit(solution)/shard_map/out_grad_body/pallas_call | solution.py:24
  120.7 5.8 %collective-permute-done.31.refs_2_.refs_13_ = bf16[256,256]{1,0:T(8,128)(2,1)S(1)} collective-permute-done((bf16[256,256]{1,0:T(8,128)(2,1)S(1)}, bf16[256,256]{1,0:T(8,128)(2,1)S(1)}, u32[]{:S(2)}, u32[]{:S(2)}) %collective-permute-start.31) | collective-permute-done | bytes 131104 | tf_op jit(solution)/shard_map/ppermute | solution.py:162
  126.6 3.9 %project_body.1 = (bf16[256,128]{1,0:T(8,128)(2,1)S(1)}, bf16[256,256]{1,0:T(8,128)(2,1)S(1)}, bf16[256,384]{1,0:T(8,128)(2,1)S(1)}, bf16[256,256]{1,0:T(8,128)(...) custom-call(s32[3]{0:T(128)S(1)} %pad_add_fusion.spot, ...), custom_call_target="tpu_custom_call" | custom-call | flops 536870912 | bytes 5801996 | tf_op jit(solution)/shard_map/project_body/pallas_call | solution.py:24
  133.5 6.9 %collective-permute-done.34.refs_1_ = bf16[512,256]{1,0:T(8,128)(2,1)S(1)} collective-permute-done((bf16[512,256]{1,0:T(8,128)(2,1)S(1)}, bf16[512,256]{1,0:T(8,128)(2,1)S(1)}, u32[]{:S(2)}, u32[]{:S(2)}) %collective-permute-start.34) | collective-permute-done | bytes 262176 | tf_op jit(solution)/shard_map/ppermute | solution.py:162
  142.0 6.1 %collective-permute-done.36.refs_3_ = bf16[512,256]{1,0:T(8,128)(2,1)S(1)} collective-permute-done((bf16[512,256]{1,0:T(8,128)(2,1)S(1)}, bf16[512,256]{1,0:T(8,128)(2,1)S(1)}, u32[]{:S(2)}, u32[]{:S(2)}) %collective-permute-start.36) | collective-permute-done | bytes 262176 | tf_op jit(solution)/shard_map/ppermute | solution.py:168
  148.1 8.8 %attend_body.1 = (bf16[256,256]{1,0:T(8,128)(2,1)}, bf16[256,256]{1,0:T(8,128)(2,1)}, bf16[256,256]{1,0:T(8,128)(2,1)}, bf16[256,256]{1,0:T(8,128)(2,1)}, bf16[2...) custom-call(s32[3]{0:T(128)S(1)} %pad_add_fusion.spot, ...), custom_call_target="tpu_custom_call" | custom-call | flops 1879048192 | bytes 6291468 | tf_op jit(solution)/shard_map/attend_body/pallas_call | solution.py:24
  163.8 2.6 collective-permute-done.39.refs_5_
  166.6 3.4 %collective-permute-done.42.refs_8_ = bf16[256,256]{1,0:T(8,128)(2,1)S(1)} collective-permute-done((bf16[256,256]{1,0:T(8,128)(2,1)}, bf16[256,256]{1,0:T(8,128)(2,1)S(1)}, u32[]{:S(2)}, u32[]{:S(2)}) %collective-permute-start.42) | collective-permute-done | bytes 131104 | tf_op jit(solution)/shard_map/ppermute | solution.py:162
  169.9 3.6 %collective-permute-done.43.refs_9_ = bf16[256,256]{1,0:T(8,128)(2,1)S(1)} collective-permute-done((bf16[256,256]{1,0:T(8,128)(2,1)}, bf16[256,256]{1,0:T(8,128)(2,1)S(1)}, u32[]{:S(2)}, u32[]{:S(2)}) %collective-permute-start.43) | collective-permute-done | bytes 131104 | tf_op jit(solution)/shard_map/ppermute | solution.py:162
  173.5 6.6 %project_back_body.1 = (bf16[272,256]{1,0:T(8,128)(2,1)S(1)}, bf16[272,256]{1,0:T(8,128)(2,1)S(1)}, bf16[272,256]{1,0:T(8,128)(2,1)S(1)}, bf16[272,256]{1,0:T(8,128)(2,1)S(1)}, bf16[1024,1536]{1,0:T(8,128)(2,1)}) custom-call(s32[3]{0:T(128)S(1)} %pad_add_fusion.spot, bf16[256,128]{1,0:T(8,128)(2,1)} %get-tuple-element.158.kq, ...), custom_call_target="tpu_custom_call" | custom-call | flops 1342177280 | bytes 10029068 | tf_op jit(solution)/shard_map/project_back_body/pallas_call | solution.py:24
  189.6 8.3 %collective-permute-done.48.refs_2_ = bf16[272,256]{1,0:T(8,128)(2,1)S(1)} collective-permute-done((bf16[272,256]{1,0:T(8,128)(2,1)S(1)}, bf16[272,256]{1,0:T(8,128)(2,1)S(1)}, u32[]{:S(2)}, u32[]{:S(2)}) %collective-permute-start.48) | collective-permute-done | bytes 139296 | tf_op jit(solution)/shard_map/ppermute | solution.py:162
  199.5 2.7 mix_body.1
  202.2 3.8 %back_body.2 = (bf16[256,256]{1,0:T(8,128)(2,1)S(1)}, bf16[256,256]{1,0:T(8,128)(2,1)S(1)}, bf16[256,256]{1,0:T(8,128)(2,1)S(1)}, bf16[256,256]{1,0:T(8,128)(2,1)S(1)}) custom-call(s32[3]{0:T(128)S(1)} %pad_add_fusion.spot, bf16[256,256]{1,0:T(8,128)(2,1)S(1)} %get-tuple-element.189.grad, bf16[128,256]{1,0:T(8,128)(2,1)S(1)} %collective-permute-done.50.near, ...), custom_call_target="tpu_custom_call" | custom-call | flops 1207959552 | bytes 5505036 | tf_op jit(solution)/shard_map/back_body/pallas_call | solution.py:24
  219.2 4.9 %collective-permute-start.58 = (f32[8,256]{1,0:T(8,128)S(1)}, f32[8,256]{1,0:T(8,128)S(1)}, u32[]{:S(2)}, u32[]{:S(2)}) collective-permute-start(f32[8,256]{1,0:T(8,128)S(1)} %get-tuple-element.206), channel_id=1, source_target_pairs={{0,4},{4,0},{8,12},{12,8},{16,20},{20,16},{24,28},{28,24},{1,5},{5... | collective-permute-start | bytes 24584 | tf_op jit(solution)/shard_map/ppermute | solution.py:162
  235.5 3.9 %collective-permute-start.62 = (bf16[128,256]{1,0:T(8,128)(2,1)S(1)}, bf16[128,256]{1,0:T(8,128)(2,1)S(1)}, u32[]{:S(2)}, u32[]{:S(2)}) collective-permute-start(bf16[128,256]{1,0:T(8,128)(2,1)S(1)} %get-tuple-element.210), channel_id=1, source_target_pairs={{0,4},{4,0},{8,12},{12,8},{16,20},{20,16},{24,28},{28,24},{1,5},{5... | collective-permute-start | bytes 196616 | tf_op jit(solution)/shard_map/ppermute | solution.py:162
  240.2 3.8 %back_body.3 = (bf16[256,256]{1,0:T(8,128)(2,1)S(1)}, bf16[256,256]{1,0:T(8,128)(2,1)S(1)}, bf16[256,256]{1,0:T(8,128)(2,1)S(1)}, bf16[256,256]{1,0:T(8,128)(2,1)S(1)}) custom-call(s32[3]{0:T(128)S(1)} %pad_add_fusion.spot, bf16[256,256]{1,0:T(8,128)(2,1)S(1)} %get-tuple-element.207.grad, bf16[128,256]{1,0:T(8,128)(2,1)S(1)} %collective-permute-done.62.near, ...), custom_call_target="tpu_custom_call" | custom-call | flops 1207959552 | bytes 5505036 | tf_op jit(solution)/shard_map/back_body/pallas_call | solution.py:24
  245.8 8.8 %collective-permute-start.64 = (bf16[256,256]{1,0:T(8,128)(2,1)S(1)}, bf16[256,256]{1,0:T(8,128)(2,1)S(1)}, u32[]{:S(2)}, u32[]{:S(2)}) collective-permute-start(bf16[256,256]{1,0:T(8,128)(2,1)S(1)} %get-tuple-element.216), channel_id=1, source_target_pairs={{0,1},{1,0},{2,3},{3,2},{4,5},{5,4},{6,7},{7,6},{8,9},{9,8},{10,11... | collective-permute-start | bytes 393224 | tf_op jit(solution)/shard_map/ppermute | solution.py:162
  258.5 3.4 %text_out_body.1 = (f32[128,2,256]{2,1,0:T(2,128)}, f32[512,2,256]{2,1,0:T(2,128)}, f32[2,512,256]{2,1,0:T(8,128)}) custom-call(s32[3]{0:T(128)S(1)} %pad_add_fusion.spot, f32[2,256]{1,0:T(2,128)S(1)} %get-tuple-element.217.film, bf16[1,128]{1,0:T(2,128)(2,1)S(1)} %fusion.13.features, bf16[1,512]{1,0:T(2,128)(2,1)S(1)} %dynamic_slice.11.pooled, ...), custom_call_target="tpu_custom_call" | custom-call | flops 67108864 | bytes 3542284 | tf_op jit(solution)/shard_map/text_out_body/pallas_call | solution.py:24
  273.2 6.6 %kernel_grad_body.1 = f32[2,9,128,256]{3,2,1,0:T(8,128)} custom-call(s32[3]{0:T(128)S(1)} %pad_add_fusion.spot, bf16[4,2,256,128]{3,2,1,0:T(8,128)(2,1)} %get-tuple-element.147.refs_7_.kept, bf16[4,2,256,128]{3,2,1,0:T(8,128)(2,1)} %copy-done.25, bf16[2,2,256,128]{3,2,1,0:T(8,128)(2,1)} %copy-done.28, bf16[2,2,256,128]{3,2,1,0:T(8,128)(2,1)} %copy-done.27, ...), custom_call_target="tpu_custom_call" | custom-call | flops 2415919104 | bytes 6291456 | tf_op jit(solution)/shard_map/kernel_grad_body/pallas_call | solution.py:300
  (255 shorter events, 113.5 us)
Async XLA Ops:
  7.3 58.5 %all-gather.9.cloned.1.call-start = ((), (), s32[]{:S(2)}) async-start(), calls=%async_computation.1 | async-start | bytes 5308416 | tf_op jit(solution)/shard_map/all_gather | solution.py:185
  9.4 106.8 %all-gather.13.cloned.1.call-start = ((), (), s32[]{:S(2)}) async-start(), calls=%async_computation.4 | async-start | bytes 3538944 | tf_op jit(solution)/shard_map/all_gather | solution.py:185
  23.1 124.9 %all-gather.15.cloned.1.call-start = ((), (), s32[]{:S(2)}) async-start(), calls=%async_computation.5 | async-start | bytes 1179648 | tf_op jit(solution)/shard_map/all_gather | solution.py:924
  24.8 12.5 %collective-permute-start.5 = (bf16[272,256]{1,0:T(8,128)(2,1)S(1)}, bf16[272,256]{1,0:T(8,128)(2,1)S(1)}, u32[]{:S(2)}, u32[]{:S(2)}) collective-permute-start(bf16[272,256]{1,0:T(8,128)(2,1)S(1)} %get-tuple-element.143.refs_0_.refs_4_.refs_15_), channel_id=1, source_target_pairs={{0,2},{1,3},{2,0},{3,1},{4,6},{5,7},{6,4},{7,5},{8,10},{9,11},{10,... | collective-permute-start | bytes 417800 | tf_op jit(solution)/shard_map/ppermute | solution.py:162
  27.4 9.9 %collective-permute-start.6 = (bf16[272,256]{1,0:T(8,128)(2,1)S(1)}, bf16[272,256]{1,0:T(8,128)(2,1)S(1)}, u32[]{:S(2)}, u32[]{:S(2)}) collective-permute-start(bf16[272,256]{1,0:T(8,128)(2,1)S(1)} %get-tuple-element.143.refs_0_.refs_4_.refs_15_), channel_id=1, source_target_pairs={{0,3},{1,2},{2,1},{3,0},{4,7},{5,6},{6,5},{7,4},{8,11},{9,10},{10,... | collective-permute-start | bytes 417800 | tf_op jit(solution)/shard_map/ppermute | solution.py:162
  29.6 22.6 %collective-permute-start.12 = (bf16[9,128,256]{2,1,0:T(8,128)(2,1)}, bf16[9,128,256]{2,1,0:T(8,128)(2,1)}, u32[]{:S(2)}, u32[]{:S(2)}) collective-permute-start(bf16[9,128,256]{2,1,0:T(8,128)(2,1)} %slice_bitcast_fusion.refs_6_.refs_0_), channel_id=1, source_target_pairs={{0,8},{4,12},{8,0},{12,4},{16,24},{20,28},{24,16},{28,20},{1,9},{5... | collective-permute-start | bytes 1769480 | tf_op jit(solution)/shard_map/ppermute | solution.py:162
  30.1 22.1 %collective-permute-start.13 = (bf16[9,128,256]{2,1,0:T(8,128)(2,1)}, bf16[9,128,256]{2,1,0:T(8,128)(2,1)}, u32[]{:S(2)}, u32[]{:S(2)}) collective-permute-start(bf16[9,128,256]{2,1,0:T(8,128)(2,1)} %slice_bitcast_fusion.refs_6_.refs_0_), channel_id=1, source_target_pairs={{0,16},{4,20},{8,24},{12,28},{16,0},{20,4},{24,8},{28,12},{1,17},{... | collective-permute-start | bytes 1769480 | tf_op jit(solution)/shard_map/ppermute | solution.py:162
  39.4 11.6 %collective-permute-start.8 = (bf16[256,256]{1,0:T(8,128)(2,1)S(1)}, bf16[256,256]{1,0:T(8,128)(2,1)S(1)}, u32[]{:S(2)}, u32[]{:S(2)}) collective-permute-start(bf16[256,256]{1,0:T(8,128)(2,1)S(1)} %get-tuple-element.130.refs_0_), channel_id=1, source_target_pairs={{0,2},{1,3},{2,0},{3,1},{4,6},{5,7},{6,4},{7,5},{8,10},{9,11},{10,... | collective-permute-start | bytes 393224 | tf_op jit(solution)/shard_map/ppermute | solution.py:162
  40.4 13.3 %collective-permute-start.9 = (bf16[256,256]{1,0:T(8,128)(2,1)S(1)}, bf16[256,256]{1,0:T(8,128)(2,1)S(1)}, u32[]{:S(2)}, u32[]{:S(2)}) collective-permute-start(bf16[256,256]{1,0:T(8,128)(2,1)S(1)} %get-tuple-element.130.refs_0_), channel_id=1, source_target_pairs={{0,3},{1,2},{2,1},{3,0},{4,7},{5,6},{6,5},{7,4},{8,11},{9,10},{10,... | collective-permute-start | bytes 393224 | tf_op jit(solution)/shard_map/ppermute | solution.py:162
  53.3 10.1 %collective-permute-start.14 = (bf16[9,128,256]{2,1,0:T(8,128)(2,1)S(1)}, bf16[9,128,256]{2,1,0:T(8,128)(2,1)}, u32[]{:S(2)}, u32[]{:S(2)}) collective-permute-start(bf16[9,128,256]{2,1,0:T(8,128)(2,1)S(1)} %broadcast_select_fusion), channel_id=1, source_target_pairs={{0,16},{4,12},{8,24},{12,4},{16,0},{20,28},{24,8},{28,20},{1,17},{... | collective-permute-start | bytes 1769480 | tf_op jit(solution)/shard_map/ppermute | solution.py:168
  57.7 12.7 %collective-permute-start.15 = (bf16[9,128,256]{2,1,0:T(8,128)(2,1)}, bf16[9,128,256]{2,1,0:T(8,128)(2,1)}, u32[]{:S(2)}, u32[]{:S(2)}) collective-permute-start(bf16[9,128,256]{2,1,0:T(8,128)(2,1)} %slice_bitcast_fusion.refs_6_.refs_0_), channel_id=1, source_target_pairs={{0,4},{4,0},{8,12},{12,8},{16,20},{20,16},{24,28},{28,24},{1,5},{5... | collective-permute-start | bytes 1769480 | tf_op jit(solution)/shard_map/ppermute | solution.py:162
  57.7 12.7 %collective-permute-start.16 = (bf16[9,128,256]{2,1,0:T(8,128)(2,1)}, bf16[9,128,256]{2,1,0:T(8,128)(2,1)}, u32[]{:S(2)}, u32[]{:S(2)}) collective-permute-start(bf16[9,128,256]{2,1,0:T(8,128)(2,1)} %collective-permute-done.12.refs_7_.refs_1_), channel_id=1, source_target_pairs={{0,4},{4,0},{8,12},{12,8},{16,20},{20,16},{24,28},{28,24},{1,5},{5... | collective-permute-start | bytes 1769480 | tf_op jit(solution)/shard_map/ppermute | solution.py:162
  58.6 11.8 %collective-permute-start.17 = (bf16[9,128,256]{2,1,0:T(8,128)(2,1)}, bf16[9,128,256]{2,1,0:T(8,128)(2,1)}, u32[]{:S(2)}, u32[]{:S(2)}) collective-permute-start(bf16[9,128,256]{2,1,0:T(8,128)(2,1)} %collective-permute-done.13.refs_8_.refs_2_), channel_id=1, source_target_pairs={{0,4},{4,0},{8,12},{12,8},{16,20},{20,16},{24,28},{28,24},{1,5},{5... | collective-permute-start | bytes 1769480 | tf_op jit(solution)/shard_map/ppermute | solution.py:162
  83.2 12.3 %collective-permute-start.24 = (bf16[256,256]{1,0:T(8,128)(2,1)S(1)}, bf16[256,256]{1,0:T(8,128)(2,1)S(1)}, u32[]{:S(2)}, u32[]{:S(2)}) collective-permute-start(bf16[256,256]{1,0:T(8,128)(2,1)S(1)} %get-tuple-element.137.refs_0_), channel_id=1, source_target_pairs={{0,2},{1,3},{2,0},{3,1},{4,6},{5,7},{6,4},{7,5},{8,10},{9,11},{10,... | collective-permute-start | bytes 393224 | tf_op jit(solution)/shard_map/ppermute | solution.py:162
  96.5 162.1 %all-gather.17.cloned.1.call-start = ((), (), s32[]{:S(2)}) async-start(), calls=%async_computation.6 | async-start | bytes 1179648 | tf_op jit(solution)/shard_map/all_gather | solution.py:998
  102.9 17.8 %collective-permute-start.29 = (bf16[4,2,256,128]{3,2,1,0:T(8,128)(2,1)}, bf16[4,2,256,128]{3,2,1,0:T(8,128)(2,1)S(1)}, u32[]{:S(2)}, u32[]{:S(2)}) collective-permute-start(bf16[4,2,256,128]{3,2,1,0:T(8,128)(2,1)} %get-tuple-element.148), channel_id=1, source_target_pairs={{0,4},{4,0},{8,12},{12,8},{16,20},{20,16},{24,28},{28,24},{1,5},{5... | collective-permute-start | bytes 1572872 | tf_op jit(solution)/shard_map/ppermute | solution.py:162
  113.7 12.9 %collective-permute-start.31 = (bf16[256,256]{1,0:T(8,128)(2,1)S(1)}, bf16[256,256]{1,0:T(8,128)(2,1)S(1)}, u32[]{:S(2)}, u32[]{:S(2)}) collective-permute-start(bf16[256,256]{1,0:T(8,128)(2,1)S(1)} %get-tuple-element.149.refs_0_.refs_11_), channel_id=1, source_target_pairs={{0,2},{1,3},{2,0},{3,1},{4,6},{5,7},{6,4},{7,5},{8,10},{9,11},{10,... | collective-permute-start | bytes 393224 | tf_op jit(solution)/shard_map/ppermute | solution.py:162
  114.8 11.8 %collective-permute-start.32 = (bf16[256,256]{1,0:T(8,128)(2,1)S(1)}, bf16[256,256]{1,0:T(8,128)(2,1)S(1)}, u32[]{:S(2)}, u32[]{:S(2)}) collective-permute-start(bf16[256,256]{1,0:T(8,128)(2,1)S(1)} %get-tuple-element.149.refs_0_.refs_11_), channel_id=1, source_target_pairs={{0,3},{1,2},{2,1},{3,0},{4,7},{5,6},{6,5},{7,4},{8,11},{9,10},{10,... | collective-permute-start | bytes 393224 | tf_op jit(solution)/shard_map/ppermute | solution.py:162
  156.9 105.1 %reduce-scatter.2.cloned.1.call-start = ((), (), s32[]{:S(2)}) async-start(), calls=%async_computation.2 | async-start | bytes 3538944 | tf_op jit(solution)/shard_map/reduce_scatter | solution.py:1025
  163.8 9.7 %collective-permute-start.43 = (bf16[256,256]{1,0:T(8,128)(2,1)}, bf16[256,256]{1,0:T(8,128)(2,1)S(1)}, u32[]{:S(2)}, u32[]{:S(2)}) collective-permute-start(bf16[256,256]{1,0:T(8,128)(2,1)} %get-tuple-element.171), channel_id=1, source_target_pairs={{0,20},{4,16},{8,28},{12,24},{16,4},{20,0},{24,12},{28,8},{1,21},{... | collective-permute-start | bytes 393224 | tf_op jit(solution)/shard_map/ppermute | solution.py:162
  180.2 93.0 %all-gather.11.cloned.1.call-start = ((), (), s32[]{:S(2)}) async-start(), calls=%async_computation.3 | async-start | bytes 2359296 | tf_op jit(solution)/shard_map/all_gather | solution.py:1086
  184.6 13.2 %collective-permute-start.48 = (bf16[272,256]{1,0:T(8,128)(2,1)S(1)}, bf16[272,256]{1,0:T(8,128)(2,1)S(1)}, u32[]{:S(2)}, u32[]{:S(2)}) collective-permute-start(bf16[272,256]{1,0:T(8,128)(2,1)S(1)} %get-tuple-element.180), channel_id=1, source_target_pairs={{0,2},{1,3},{2,0},{3,1},{4,6},{5,7},{6,4},{7,5},{8,10},{9,11},{10,... | collective-permute-start | bytes 417800 | tf_op jit(solution)/shard_map/ppermute | solution.py:162
  185.5 12.3 %collective-permute-start.49 = (bf16[272,256]{1,0:T(8,128)(2,1)S(1)}, bf16[272,256]{1,0:T(8,128)(2,1)S(1)}, u32[]{:S(2)}, u32[]{:S(2)}) collective-permute-start(bf16[272,256]{1,0:T(8,128)(2,1)S(1)} %get-tuple-element.181), channel_id=1, source_target_pairs={{0,3},{1,2},{2,1},{3,0},{4,7},{5,6},{6,5},{7,4},{8,11},{9,10},{10,... | collective-permute-start | bytes 417800 | tf_op jit(solution)/shard_map/ppermute | solution.py:162
  210.6 17.8 %collective-permute-start.52 = (bf16[256,256]{1,0:T(8,128)(2,1)S(1)}, bf16[256,256]{1,0:T(8,128)(2,1)S(1)}, u32[]{:S(2)}, u32[]{:S(2)}) collective-permute-start(bf16[256,256]{1,0:T(8,128)(2,1)S(1)} %get-tuple-element.195), channel_id=1, source_target_pairs={{0,1},{1,0},{2,3},{3,2},{4,5},{5,4},{6,7},{7,6},{8,9},{9,8},{10,11... | collective-permute-start | bytes 393224 | tf_op jit(solution)/shard_map/ppermute | solution.py:162
  211.6 19.6 %collective-permute-start.53 = (bf16[256,256]{1,0:T(8,128)(2,1)S(1)}, bf16[256,256]{1,0:T(8,128)(2,1)S(1)}, u32[]{:S(2)}, u32[]{:S(2)}) collective-permute-start(bf16[256,256]{1,0:T(8,128)(2,1)S(1)} %get-tuple-element.196), channel_id=1, source_target_pairs={{0,2},{1,3},{2,0},{3,1},{4,6},{5,7},{6,4},{7,5},{8,10},{9,11},{10,... | collective-permute-start | bytes 393224 | tf_op jit(solution)/shard_map/ppermute | solution.py:162
  213.5 17.7 %collective-permute-start.54 = (bf16[256,256]{1,0:T(8,128)(2,1)S(1)}, bf16[256,256]{1,0:T(8,128)(2,1)S(1)}, u32[]{:S(2)}, u32[]{:S(2)}) collective-permute-start(bf16[256,256]{1,0:T(8,128)(2,1)S(1)} %get-tuple-element.197), channel_id=1, source_target_pairs={{0,3},{1,2},{2,1},{3,0},{4,7},{5,6},{6,5},{7,4},{8,11},{9,10},{10,... | collective-permute-start | bytes 393224 | tf_op jit(solution)/shard_map/ppermute | solution.py:162
  244.1 28.1 %collective-permute-start.71 = (bf16[2,2,256,128]{3,2,1,0:T(8,128)(2,1)S(1)}, bf16[2,2,256,128]{3,2,1,0:T(8,128)(2,1)}, u32[]{:S(2)}, u32[]{:S(2)}) collective-permute-start(bf16[2,2,256,128]{3,2,1,0:T(8,128)(2,1)S(1)} %copy-done.26), channel_id=1, source_target_pairs={{0,24},{4,28},{8,16},{12,20},{16,8},{20,12},{24,0},{28,4},{1,25},{... | collective-permute-start | bytes 786440 | tf_op jit(solution)/shard_map/ppermute | solution.py:162
  245.8 12.8 %collective-permute-start.64 = (bf16[256,256]{1,0:T(8,128)(2,1)S(1)}, bf16[256,256]{1,0:T(8,128)(2,1)S(1)}, u32[]{:S(2)}, u32[]{:S(2)}) collective-permute-start(bf16[256,256]{1,0:T(8,128)(2,1)S(1)} %get-tuple-element.216), channel_id=1, source_target_pairs={{0,1},{1,0},{2,3},{3,2},{4,5},{5,4},{6,7},{7,6},{8,9},{9,8},{10,11... | collective-permute-start | bytes 393224 | tf_op jit(solution)/shard_map/ppermute | solution.py:162
  254.6 11.6 %collective-permute-start.65 = (bf16[256,256]{1,0:T(8,128)(2,1)S(1)}, bf16[256,256]{1,0:T(8,128)(2,1)S(1)}, u32[]{:S(2)}, u32[]{:S(2)}) collective-permute-start(bf16[256,256]{1,0:T(8,128)(2,1)S(1)} %get-tuple-element.221), channel_id=1, source_target_pairs={{0,2},{1,3},{2,0},{3,1},{4,6},{5,7},{6,4},{7,5},{8,10},{9,11},{10,... | collective-permute-start | bytes 393224 | tf_op jit(solution)/shard_map/ppermute | solution.py:162
  254.8 11.3 %collective-permute-start.66 = (bf16[256,256]{1,0:T(8,128)(2,1)S(1)}, bf16[256,256]{1,0:T(8,128)(2,1)S(1)}, u32[]{:S(2)}, u32[]{:S(2)}) collective-permute-start(bf16[256,256]{1,0:T(8,128)(2,1)S(1)} %get-tuple-element.222), channel_id=1, source_target_pairs={{0,3},{1,2},{2,1},{3,0},{4,7},{5,6},{6,5},{7,4},{8,11},{9,10},{10,... | collective-permute-start | bytes 393224 | tf_op jit(solution)/shard_map/ppermute | solution.py:162
  268.4 11.4 %collective-permute-start.68 = (f32[2,256]{1,0:T(2,128)S(1)}, f32[2,256]{1,0:T(2,128)S(1)}, u32[]{:S(2)}, u32[]{:S(2)}) collective-permute-start(f32[2,256]{1,0:T(2,128)S(1)} %add.47.refs_0_), channel_id=1, source_target_pairs={{0,8},{4,12},{8,0},{12,4},{16,24},{20,28},{24,16},{28,20},{1,9},{5... | collective-permute-start | bytes 6152 | tf_op jit(solution)/shard_map/ppermute | solution.py:162
  269.5 10.2 %collective-permute-start.69 = (f32[2,256]{1,0:T(2,128)S(1)}, f32[2,256]{1,0:T(2,128)S(1)}, u32[]{:S(2)}, u32[]{:S(2)}) collective-permute-start(f32[2,256]{1,0:T(2,128)S(1)} %add.47.refs_0_), channel_id=1, source_target_pairs={{0,16},{4,20},{8,24},{12,28},{16,0},{20,4},{24,8},{28,12},{1,17},{... | collective-permute-start | bytes 6152 | tf_op jit(solution)/shard_map/ppermute | solution.py:162
  (76 other events, 813.8 us)
Sparse Core Ops, SparseCore 0:
  10.5 50.2 all-gather.8
  63.3 32.4 all-gather.12
  98.3 24.3 all-gather.14
  157.0 27.7 all-gather.16
  188.0 47.1 reduce-scatter.1
  237.8 35.3 all-gather.10

commit v6 on v5

--- a/solution.py
+++ b/solution.py
@@ -455,8 +455,8 @@
     rows[5:8, :] = jnp.zeros((3, own.shape[1]), jnp.float32)
 
 
-def second_input_body(pixel_count, width, spot, back, inner, sums, film, affine, *refs):
-    *parts, low, near, far_row, film_rows, rows = refs
+def second_input_body(pixel_count, width, spot, back, inner, sums, film, affine, other, *refs):
+    *parts, low, both, near, far_row, film_rows, rows = refs
     rows[...] = sum_of_parts(parts)
     slope, shift, gain = 1.0 + film[0:1], film[1:2], affine[0:1]
     plain_sum, square_sum = sums[0:1], sums[1:2]
@@ -467,6 +467,8 @@
     grad = inverse * (back[...] * gain - plain - scaled * dotted)
     grad_low = (grad * slope).astype(jnp.bfloat16)
     low[...] = grad_low
+    both[0] = grad_low
+    both[1] = other[...]
     odd = lax.rem(spot[0], 2) == 1
     near[...] = jnp.where(odd, grad_low[:width], grad_low[-width:])
     far_row[...] = jnp.where(odd, grad_low[-width:], grad_low[:width])
@@ -1074,16 +1076,19 @@
         16,
         0,
     )
-    grad_one, last, head, film_rows, second_rows = local_kernel(
+    grad_one, both_low, last, head, film_rows, second_rows = local_kernel(
         functools.partial(second_input_body, pixel_count, col_count),
-        [bf16_like(*flat), bf16_like(*edge), bf16_like(*edge), row_pair, f32_like(8, width_own)],
-        [spot, after(back, mixed), inner, inner_sums, film, affine[1], *part_totals(rows)],
+        [
+            bf16_like(*flat),
+            far_like(bf16_like(2, *flat)),
+            bf16_like(*edge), bf16_like(*edge), row_pair, f32_like(8, width_own)],
+        [spot, after(back, mixed), inner, inner_sums, film, affine[1], *far([grad_two]), *part_totals(rows)],
         [],
         16,
         0,
     )
     edges = edge_rows(last, head)
-    both_grads = lax.all_gather(jnp.stack([grad_one, grad_two]), "wide", axis=1, tiled=True)
+    both_grads = lax.all_gather(both_low, "wide", axis=1, tiled=True)
     back_parts = convolve_back(spot, grad_one, edges, kernel_one, row_count, col_count)
     if has_slots():
         block_pair += [*close, flipped(after(block_pairs[2], back_parts[0]), "wide", 6)]

time: 289 us -> 288 us (level)
  transfers between devices with their start and end apart: 78 -> 78, of which waited for: 39 -> 38; matrix products, arithmetic and copies ran while one was open for 3% -> 3% of each run, Pallas kernels for 18% -> 19%
where the time goes in v6:
time: 288 us
  starting transfers between devices  99.9 us (35%)
  waiting for transfers between devices  97.8 us (34%)
  Pallas kernels  64.3 us (22%)
  between operations  16.2 us (6%)
  local copies, waits for them, and re-layouts  4.8 us (2%)
  other arithmetic  3.24 us (1%)
    ppermute x66, starting transfers between devices, flipped(): return lax.ppermute(values, axis, [(i, i ^ mask) for i in range(count)])  95.8 us
    ppermute x66, waiting for transfers between devices, flipped(): return lax.ppermute(values, axis, [(i, i ^ mask) for i in range(count)])  87.2 us
    pallas_call x19, Pallas kernels, local_kernel(): pl.pallas_call(body, grid=(1,), out_shape=outs, in_specs=[in_smem] + [in_...  57.8 us
    ppermute x2, waiting for transfers between devices, relayed_block(): return lax.ppermute(jnp.where(odd, over_y, over_x), 'wide', far_pairs)  10.4 us
    pallas_call x1, Pallas kernels, kernel_grad(): pl.pallas_call(functools.partial(kernel_grad_body, width), out_shape=f32_...  6.57 us
  transfers between devices with their start and end apart: 78, of which 38 were waited for; matrix products, arithmetic and copies ran while one was open for 3% of the time, Pallas kernels for 19%

profile of v6, /device:TPU:0, one launch (start us, length us, event | category | flops | bytes accessed | tf_op | source)
XLA Modules:
  0.0 287.7 jit_solution(10243599956945692794)
XLA Ops:
  12.9 2.6 collective-permute-start.1
  24.8 2.6 collective-permute-start.5
  30.4 6.9 %collective-permute-done.5.refs_2_.refs_6_.refs_17_ = bf16[272,256]{1,0:T(8,128)(2,1)S(1)} collective-permute-done((bf16[272,256]{1,0:T(8,128)(2,1)S(1)}, bf16[272,256]{1,0:T(8,128)(2,1)S(1)}, u32[]{:S(2)}, u32[]{:S(2)}) %collective-permute-start.5) | collective-permute-done | bytes 139296 | tf_op jit(solution)/shard_map/ppermute | solution.py:162
  43.4 7.6 %collective-permute-done.8.refs_2_ = bf16[256,256]{1,0:T(8,128)(2,1)S(1)} collective-permute-done((bf16[256,256]{1,0:T(8,128)(2,1)S(1)}, bf16[256,256]{1,0:T(8,128)(2,1)S(1)}, u32[]{:S(2)}, u32[]{:S(2)}) %collective-permute-start.8) | collective-permute-done | bytes 131104 | tf_op jit(solution)/shard_map/ppermute | solution.py:162
  54.6 2.9 %collective-permute-start.10 = (bf16[128,1024]{1,0:T(8,128)(2,1)S(1)}, bf16[128,1024]{1,0:T(8,128)(2,1)S(1)}, u32[]{:S(2)}, u32[]{:S(2)}) collective-permute-start(bf16[128,1024]{1,0:T(8,128)(2,1)S(1)} %get-tuple-element.132), channel_id=1, source_target_pairs={{0,4},{4,0},{8,12},{12,8},{16,20},{20,16},{24,28},{28,24},{1,5},{5... | collective-permute-start | bytes 786440 | tf_op jit(solution)/shard_map/ppermute | solution.py:162
  59.0 4.3 %collective-permute-done.14.refs_9_.refs_3_ = bf16[9,128,256]{2,1,0:T(8,128)(2,1)} collective-permute-done((bf16[9,128,256]{2,1,0:T(8,128)(2,1)S(1)}, bf16[9,128,256]{2,1,0:T(8,128)(2,1)}, u32[]{:S(2)}, u32[]{:S(2)}) %collective-permute-start.14) | collective-permute-done | bytes 589856 | tf_op jit(solution)/shard_map/ppermute | solution.py:168
  65.8 4.6 %conv_body.2 = (f32[256,256]{1,0:T(8,128)S(1)}, f32[2,256]{1,0:T(2,128)S(1)}, bf16[4,256,128]{2,1,0:T(8,128)(2,1)S(1)}, bf16[4,256,128]{2,1,0:T(8,128)(2,1)S(1)}) custom-call(s32[3]{0:T(128)S(1)} %pad_add_fusion.spot, bf16[256,256]{1,0:T(8,128)(2,1)S(1)} %get-tuple-element.131.refs_0_, bf16[256,256]{1,0:T(8,128)(2,1)S(1)} %collective-permute-done.7.refs_1_, ...), custom_call_target="tpu_custom_call" | custom-call | flops 1207959552 | bytes 6686732 | tf_op jit(solution)/shard_map/conv_body/pallas_call | solution.py:24
  71.7 3.1 %collective-permute-start.20 = (f32[4,256]{1,0:T(4,128)S(1)}, f32[4,256]{1,0:T(4,128)S(1)}, u32[]{:S(2)}, u32[]{:S(2)}) collective-permute-start(f32[4,256]{1,0:T(4,128)S(1)} %fusion.17.refs_0_), channel_id=1, source_target_pairs={{0,8},{4,12},{8,0},{12,4},{16,24},{20,28},{24,16},{28,20},{1,9},{5... | collective-permute-start | bytes 12296 | tf_op jit(solution)/shard_map/ppermute | solution.py:162
  78.4 2.7 collective-permute-done.22.refs_3_
  83.2 2.9 %collective-permute-start.24 = (bf16[256,256]{1,0:T(8,128)(2,1)S(1)}, bf16[256,256]{1,0:T(8,128)(2,1)S(1)}, u32[]{:S(2)}, u32[]{:S(2)}) collective-permute-start(bf16[256,256]{1,0:T(8,128)(2,1)S(1)} %get-tuple-element.138.refs_0_), channel_id=1, source_target_pairs={{0,2},{1,3},{2,0},{3,1},{4,6},{5,7},{6,4},{7,5},{8,10},{9,11},{10,... | collective-permute-start | bytes 393224 | tf_op jit(solution)/shard_map/ppermute | solution.py:162
  88.6 6.9 %collective-permute-done.24.refs_2_ = bf16[256,256]{1,0:T(8,128)(2,1)S(1)} collective-permute-done((bf16[256,256]{1,0:T(8,128)(2,1)S(1)}, bf16[256,256]{1,0:T(8,128)(2,1)S(1)}, u32[]{:S(2)}, u32[]{:S(2)}) %collective-permute-start.24) | collective-permute-done | bytes 131104 | tf_op jit(solution)/shard_map/ppermute | solution.py:162
  97.3 5.6 %conv_body.3 = (f32[256,256]{1,0:T(8,128)S(1)}, bf16[256,256]{1,0:T(8,128)(2,1)S(1)}, bf16[4,2,256,128]{3,2,1,0:T(8,128)(2,1)}, bf16[4,2,256,128]{3,2,1,0:T(8,128)(2,1)}) custom-call(s32[3]{0:T(128)S(1)} %pad_add_fusion.spot, bf16[256,256]{1,0:T(8,128)(2,1)S(1)} %get-tuple-element.138.refs_0_, bf16[256,256]{1,0:T(8,128)(2,1)S(1)} %collective-permute-done.23.refs_1_, ...), custom_call_target="tpu_custom_call" | custom-call | flops 1207959552 | bytes 7864332 | tf_op jit(solution)/shard_map/conv_body/pallas_call | solution.py:24
  102.9 8.9 %collective-permute-start.29 = (bf16[4,2,256,128]{3,2,1,0:T(8,128)(2,1)}, bf16[4,2,256,128]{3,2,1,0:T(8,128)(2,1)S(1)}, u32[]{:S(2)}, u32[]{:S(2)}) collective-permute-start(bf16[4,2,256,128]{3,2,1,0:T(8,128)(2,1)} %get-tuple-element.149), channel_id=1, source_target_pairs={{0,4},{4,0},{8,12},{12,8},{16,20},{20,16},{24,28},{28,24},{1,5},{5... | collective-permute-start | bytes 1572872 | tf_op jit(solution)/shard_map/ppermute | solution.py:162
  116.2 3.3 %out_grad_body.1 = (bf16[256,128]{1,0:T(8,128)(2,1)}, bf16[256,128]{1,0:T(8,128)(2,1)S(1)}, bf16[256,256]{1,0:T(8,128)(2,1)}) custom-call(s32[3]{0:T(128)S(1)} %pad_add_fusion.spot, bf16[272,256]{1,0:T(8,128)(2,1)} %copy-done.2, bf16[272,256]{1,0:T(8,128)(2,1)} %copy-done.15, bf16[272,256]{1,0:T(8,128)(2,1)} %copy-done.16, bf16[272,256]{1,0:T(8,128)(2,1)} %copy-done.17, ...), custom_call_target="tpu_custom_call" | custom-call | flops 268435456 | bytes 3964940 | tf_op jit(solution)/shard_map/out_grad_body/pallas_call | solution.py:24
  120.8 5.8 %collective-permute-done.31.refs_2_.refs_13_ = bf16[256,256]{1,0:T(8,128)(2,1)S(1)} collective-permute-done((bf16[256,256]{1,0:T(8,128)(2,1)S(1)}, bf16[256,256]{1,0:T(8,128)(2,1)S(1)}, u32[]{:S(2)}, u32[]{:S(2)}) %collective-permute-start.31) | collective-permute-done | bytes 131104 | tf_op jit(solution)/shard_map/ppermute | solution.py:162
  126.6 3.9 %project_body.1 = (bf16[256,128]{1,0:T(8,128)(2,1)S(1)}, bf16[256,256]{1,0:T(8,128)(2,1)S(1)}, bf16[256,384]{1,0:T(8,128)(2,1)S(1)}, bf16[256,256]{1,0:T(8,128)(...) custom-call(s32[3]{0:T(128)S(1)} %pad_add_fusion.spot, ...), custom_call_target="tpu_custom_call" | custom-call | flops 536870912 | bytes 5801996 | tf_op jit(solution)/shard_map/project_body/pallas_call | solution.py:24
  133.5 6.9 %collective-permute-done.34.refs_1_ = bf16[512,256]{1,0:T(8,128)(2,1)S(1)} collective-permute-done((bf16[512,256]{1,0:T(8,128)(2,1)S(1)}, bf16[512,256]{1,0:T(8,128)(2,1)S(1)}, u32[]{:S(2)}, u32[]{:S(2)}) %collective-permute-start.34) | collective-permute-done | bytes 262176 | tf_op jit(solution)/shard_map/ppermute | solution.py:162
  142.0 6.1 %collective-permute-done.36.refs_3_ = bf16[512,256]{1,0:T(8,128)(2,1)S(1)} collective-permute-done((bf16[512,256]{1,0:T(8,128)(2,1)S(1)}, bf16[512,256]{1,0:T(8,128)(2,1)S(1)}, u32[]{:S(2)}, u32[]{:S(2)}) %collective-permute-start.36) | collective-permute-done | bytes 262176 | tf_op jit(solution)/shard_map/ppermute | solution.py:168
  148.1 8.8 %attend_body.1 = (bf16[256,256]{1,0:T(8,128)(2,1)}, bf16[256,256]{1,0:T(8,128)(2,1)}, bf16[256,256]{1,0:T(8,128)(2,1)}, bf16[256,256]{1,0:T(8,128)(2,1)}, bf16[2...) custom-call(s32[3]{0:T(128)S(1)} %pad_add_fusion.spot, ...), custom_call_target="tpu_custom_call" | custom-call | flops 1879048192 | bytes 6291468 | tf_op jit(solution)/shard_map/attend_body/pallas_call | solution.py:24
  163.8 2.6 collective-permute-done.39.refs_5_
  166.6 3.4 %collective-permute-done.42.refs_8_ = bf16[256,256]{1,0:T(8,128)(2,1)S(1)} collective-permute-done((bf16[256,256]{1,0:T(8,128)(2,1)}, bf16[256,256]{1,0:T(8,128)(2,1)S(1)}, u32[]{:S(2)}, u32[]{:S(2)}) %collective-permute-start.42) | collective-permute-done | bytes 131104 | tf_op jit(solution)/shard_map/ppermute | solution.py:162
  169.9 3.6 %collective-permute-done.43.refs_9_ = bf16[256,256]{1,0:T(8,128)(2,1)S(1)} collective-permute-done((bf16[256,256]{1,0:T(8,128)(2,1)}, bf16[256,256]{1,0:T(8,128)(2,1)S(1)}, u32[]{:S(2)}, u32[]{:S(2)}) %collective-permute-start.43) | collective-permute-done | bytes 131104 | tf_op jit(solution)/shard_map/ppermute | solution.py:162
  173.5 6.6 %project_back_body.1 = (bf16[272,256]{1,0:T(8,128)(2,1)S(1)}, bf16[272,256]{1,0:T(8,128)(2,1)S(1)}, bf16[272,256]{1,0:T(8,128)(2,1)S(1)}, bf16[272,256]{1,0:T(8,128)(2,1)S(1)}, bf16[1024,1536]{1,0:T(8,128)(2,1)}) custom-call(s32[3]{0:T(128)S(1)} %pad_add_fusion.spot, bf16[256,128]{1,0:T(8,128)(2,1)} %get-tuple-element.159.kq, ...), custom_call_target="tpu_custom_call" | custom-call | flops 1342177280 | bytes 10029068 | tf_op jit(solution)/shard_map/project_back_body/pallas_call | solution.py:24
  189.6 8.2 %collective-permute-done.48.refs_2_ = bf16[272,256]{1,0:T(8,128)(2,1)S(1)} collective-permute-done((bf16[272,256]{1,0:T(8,128)(2,1)S(1)}, bf16[272,256]{1,0:T(8,128)(2,1)S(1)}, u32[]{:S(2)}, u32[]{:S(2)}) %collective-permute-start.48) | collective-permute-done | bytes 139296 | tf_op jit(solution)/shard_map/ppermute | solution.py:162
  199.5 2.7 mix_body.1
  202.2 3.8 %back_body.2 = (bf16[256,256]{1,0:T(8,128)(2,1)S(1)}, bf16[256,256]{1,0:T(8,128)(2,1)S(1)}, bf16[256,256]{1,0:T(8,128)(2,1)S(1)}, bf16[256,256]{1,0:T(8,128)(2,1)S(1)}) custom-call(s32[3]{0:T(128)S(1)} %pad_add_fusion.spot, bf16[256,256]{1,0:T(8,128)(2,1)S(1)} %get-tuple-element.190.grad.other, bf16[128,256]{1,0:T(8,128)(2,1)S(1)} %collective-permute-done.50.near, ...), custom_call_target="tpu_custom_call" | custom-call | flops 1207959552 | bytes 5505036 | tf_op jit(solution)/shard_map/back_body/pallas_call | solution.py:24
  219.1 5.0 %collective-permute-start.58 = (f32[8,256]{1,0:T(8,128)S(1)}, f32[8,256]{1,0:T(8,128)S(1)}, u32[]{:S(2)}, u32[]{:S(2)}) collective-permute-start(f32[8,256]{1,0:T(8,128)S(1)} %get-tuple-element.207), channel_id=1, source_target_pairs={{0,4},{4,0},{8,12},{12,8},{16,20},{20,16},{24,28},{28,24},{1,5},{5... | collective-permute-start | bytes 24584 | tf_op jit(solution)/shard_map/ppermute | solution.py:162
  235.9 3.8 %collective-permute-start.62 = (bf16[128,256]{1,0:T(8,128)(2,1)S(1)}, bf16[128,256]{1,0:T(8,128)(2,1)S(1)}, u32[]{:S(2)}, u32[]{:S(2)}) collective-permute-start(bf16[128,256]{1,0:T(8,128)(2,1)S(1)} %get-tuple-element.211), channel_id=1, source_target_pairs={{0,4},{4,0},{8,12},{12,8},{16,20},{20,16},{24,28},{28,24},{1,5},{5... | collective-permute-start | bytes 196616 | tf_op jit(solution)/shard_map/ppermute | solution.py:162
  240.6 3.9 %back_body.3 = (bf16[256,256]{1,0:T(8,128)(2,1)S(1)}, bf16[256,256]{1,0:T(8,128)(2,1)S(1)}, bf16[256,256]{1,0:T(8,128)(2,1)S(1)}, bf16[256,256]{1,0:T(8,128)(2,1)S(1)}) custom-call(s32[3]{0:T(128)S(1)} %pad_add_fusion.spot, bf16[256,256]{1,0:T(8,128)(2,1)S(1)} %get-tuple-element.208.grad, bf16[128,256]{1,0:T(8,128)(2,1)S(1)} %collective-permute-done.62.near, ...), custom_call_target="tpu_custom_call" | custom-call | flops 1207959552 | bytes 5505036 | tf_op jit(solution)/shard_map/back_body/pallas_call | solution.py:24
  246.2 8.8 %collective-permute-start.64 = (bf16[256,256]{1,0:T(8,128)(2,1)S(1)}, bf16[256,256]{1,0:T(8,128)(2,1)S(1)}, u32[]{:S(2)}, u32[]{:S(2)}) collective-permute-start(bf16[256,256]{1,0:T(8,128)(2,1)S(1)} %get-tuple-element.217), channel_id=1, source_target_pairs={{0,1},{1,0},{2,3},{3,2},{4,5},{5,4},{6,7},{7,6},{8,9},{9,8},{10,11... | collective-permute-start | bytes 393224 | tf_op jit(solution)/shard_map/ppermute | solution.py:162
  259.0 3.4 %text_out_body.1 = (f32[128,2,256]{2,1,0:T(2,128)}, f32[512,2,256]{2,1,0:T(2,128)}, f32[2,512,256]{2,1,0:T(8,128)}) custom-call(s32[3]{0:T(128)S(1)} %pad_add_fusion.spot, f32[2,256]{1,0:T(2,128)S(1)} %get-tuple-element.218.film, bf16[1,128]{1,0:T(2,128)(2,1)S(1)} %fusion.13.features, bf16[1,512]{1,0:T(2,128)(2,1)S(1)} %dynamic_slice.11.pooled, ...), custom_call_target="tpu_custom_call" | custom-call | flops 67108864 | bytes 3542284 | tf_op jit(solution)/shard_map/text_out_body/pallas_call | solution.py:24
  272.6 6.6 %kernel_grad_body.1 = f32[2,9,128,256]{3,2,1,0:T(8,128)} custom-call(s32[3]{0:T(128)S(1)} %pad_add_fusion.spot, bf16[4,2,256,128]{3,2,1,0:T(8,128)(2,1)} %get-tuple-element.148.refs_7_.kept, bf16[4,2,256,128]{3,2,1,0:T(8,128)(2,1)} %copy-done.26, bf16[2,2,256,128]{3,2,1,0:T(8,128)(2,1)} %copy-done.29, bf16[2,2,256,128]{3,2,1,0:T(8,128)(2,1)} %copy-done.28, ...), custom_call_target="tpu_custom_call" | custom-call | flops 2415919104 | bytes 6291456 | tf_op jit(solution)/shard_map/kernel_grad_body/pallas_call | solution.py:300
  (256 shorter events, 112.9 us)
Async XLA Ops:
  7.3 58.5 %all-gather.9.cloned.1.call-start = ((), (), s32[]{:S(2)}) async-start(), calls=%async_computation.1 | async-start | bytes 5308416 | tf_op jit(solution)/shard_map/all_gather | solution.py:185
  9.4 106.8 %all-gather.13.cloned.1.call-start = ((), (), s32[]{:S(2)}) async-start(), calls=%async_computation.4 | async-start | bytes 3538944 | tf_op jit(solution)/shard_map/all_gather | solution.py:185
  23.1 124.9 %all-gather.15.cloned.1.call-start = ((), (), s32[]{:S(2)}) async-start(), calls=%async_computation.5 | async-start | bytes 1179648 | tf_op jit(solution)/shard_map/all_gather | solution.py:926
  24.8 12.5 %collective-permute-start.5 = (bf16[272,256]{1,0:T(8,128)(2,1)S(1)}, bf16[272,256]{1,0:T(8,128)(2,1)S(1)}, u32[]{:S(2)}, u32[]{:S(2)}) collective-permute-start(bf16[272,256]{1,0:T(8,128)(2,1)S(1)} %get-tuple-element.144.refs_0_.refs_4_.refs_15_), channel_id=1, source_target_pairs={{0,2},{1,3},{2,0},{3,1},{4,6},{5,7},{6,4},{7,5},{8,10},{9,11},{10,... | collective-permute-start | bytes 417800 | tf_op jit(solution)/shard_map/ppermute | solution.py:162
  27.4 9.9 %collective-permute-start.6 = (bf16[272,256]{1,0:T(8,128)(2,1)S(1)}, bf16[272,256]{1,0:T(8,128)(2,1)S(1)}, u32[]{:S(2)}, u32[]{:S(2)}) collective-permute-start(bf16[272,256]{1,0:T(8,128)(2,1)S(1)} %get-tuple-element.144.refs_0_.refs_4_.refs_15_), channel_id=1, source_target_pairs={{0,3},{1,2},{2,1},{3,0},{4,7},{5,6},{6,5},{7,4},{8,11},{9,10},{10,... | collective-permute-start | bytes 417800 | tf_op jit(solution)/shard_map/ppermute | solution.py:162
  29.6 22.6 %collective-permute-start.12 = (bf16[9,128,256]{2,1,0:T(8,128)(2,1)}, bf16[9,128,256]{2,1,0:T(8,128)(2,1)}, u32[]{:S(2)}, u32[]{:S(2)}) collective-permute-start(bf16[9,128,256]{2,1,0:T(8,128)(2,1)} %slice_bitcast_fusion.refs_6_.refs_0_), channel_id=1, source_target_pairs={{0,8},{4,12},{8,0},{12,4},{16,24},{20,28},{24,16},{28,20},{1,9},{5... | collective-permute-start | bytes 1769480 | tf_op jit(solution)/shard_map/ppermute | solution.py:162
  30.1 22.1 %collective-permute-start.13 = (bf16[9,128,256]{2,1,0:T(8,128)(2,1)}, bf16[9,128,256]{2,1,0:T(8,128)(2,1)}, u32[]{:S(2)}, u32[]{:S(2)}) collective-permute-start(bf16[9,128,256]{2,1,0:T(8,128)(2,1)} %slice_bitcast_fusion.refs_6_.refs_0_), channel_id=1, source_target_pairs={{0,16},{4,20},{8,24},{12,28},{16,0},{20,4},{24,8},{28,12},{1,17},{... | collective-permute-start | bytes 1769480 | tf_op jit(solution)/shard_map/ppermute | solution.py:162
  39.4 11.6 %collective-permute-start.8 = (bf16[256,256]{1,0:T(8,128)(2,1)S(1)}, bf16[256,256]{1,0:T(8,128)(2,1)S(1)}, u32[]{:S(2)}, u32[]{:S(2)}) collective-permute-start(bf16[256,256]{1,0:T(8,128)(2,1)S(1)} %get-tuple-element.131.refs_0_), channel_id=1, source_target_pairs={{0,2},{1,3},{2,0},{3,1},{4,6},{5,7},{6,4},{7,5},{8,10},{9,11},{10,... | collective-permute-start | bytes 393224 | tf_op jit(solution)/shard_map/ppermute | solution.py:162
  40.4 13.3 %collective-permute-start.9 = (bf16[256,256]{1,0:T(8,128)(2,1)S(1)}, bf16[256,256]{1,0:T(8,128)(2,1)S(1)}, u32[]{:S(2)}, u32[]{:S(2)}) collective-permute-start(bf16[256,256]{1,0:T(8,128)(2,1)S(1)} %get-tuple-element.131.refs_0_), channel_id=1, source_target_pairs={{0,3},{1,2},{2,1},{3,0},{4,7},{5,6},{6,5},{7,4},{8,11},{9,10},{10,... | collective-permute-start | bytes 393224 | tf_op jit(solution)/shard_map/ppermute | solution.py:162
  53.3 10.1 %collective-permute-start.14 = (bf16[9,128,256]{2,1,0:T(8,128)(2,1)S(1)}, bf16[9,128,256]{2,1,0:T(8,128)(2,1)}, u32[]{:S(2)}, u32[]{:S(2)}) collective-permute-start(bf16[9,128,256]{2,1,0:T(8,128)(2,1)S(1)} %broadcast_select_fusion), channel_id=1, source_target_pairs={{0,16},{4,12},{8,24},{12,4},{16,0},{20,28},{24,8},{28,20},{1,17},{... | collective-permute-start | bytes 1769480 | tf_op jit(solution)/shard_map/ppermute | solution.py:168
  57.7 12.7 %collective-permute-start.15 = (bf16[9,128,256]{2,1,0:T(8,128)(2,1)}, bf16[9,128,256]{2,1,0:T(8,128)(2,1)}, u32[]{:S(2)}, u32[]{:S(2)}) collective-permute-start(bf16[9,128,256]{2,1,0:T(8,128)(2,1)} %slice_bitcast_fusion.refs_6_.refs_0_), channel_id=1, source_target_pairs={{0,4},{4,0},{8,12},{12,8},{16,20},{20,16},{24,28},{28,24},{1,5},{5... | collective-permute-start | bytes 1769480 | tf_op jit(solution)/shard_map/ppermute | solution.py:162
  57.7 12.7 %collective-permute-start.16 = (bf16[9,128,256]{2,1,0:T(8,128)(2,1)}, bf16[9,128,256]{2,1,0:T(8,128)(2,1)}, u32[]{:S(2)}, u32[]{:S(2)}) collective-permute-start(bf16[9,128,256]{2,1,0:T(8,128)(2,1)} %collective-permute-done.12.refs_7_.refs_1_), channel_id=1, source_target_pairs={{0,4},{4,0},{8,12},{12,8},{16,20},{20,16},{24,28},{28,24},{1,5},{5... | collective-permute-start | bytes 1769480 | tf_op jit(solution)/shard_map/ppermute | solution.py:162
  58.6 11.8 %collective-permute-start.17 = (bf16[9,128,256]{2,1,0:T(8,128)(2,1)}, bf16[9,128,256]{2,1,0:T(8,128)(2,1)}, u32[]{:S(2)}, u32[]{:S(2)}) collective-permute-start(bf16[9,128,256]{2,1,0:T(8,128)(2,1)} %collective-permute-done.13.refs_8_.refs_2_), channel_id=1, source_target_pairs={{0,4},{4,0},{8,12},{12,8},{16,20},{20,16},{24,28},{28,24},{1,5},{5... | collective-permute-start | bytes 1769480 | tf_op jit(solution)/shard_map/ppermute | solution.py:162
  83.2 12.3 %collective-permute-start.24 = (bf16[256,256]{1,0:T(8,128)(2,1)S(1)}, bf16[256,256]{1,0:T(8,128)(2,1)S(1)}, u32[]{:S(2)}, u32[]{:S(2)}) collective-permute-start(bf16[256,256]{1,0:T(8,128)(2,1)S(1)} %get-tuple-element.138.refs_0_), channel_id=1, source_target_pairs={{0,2},{1,3},{2,0},{3,1},{4,6},{5,7},{6,4},{7,5},{8,10},{9,11},{10,... | collective-permute-start | bytes 393224 | tf_op jit(solution)/shard_map/ppermute | solution.py:162
  86.1 9.4 %collective-permute-start.25 = (bf16[256,256]{1,0:T(8,128)(2,1)S(1)}, bf16[256,256]{1,0:T(8,128)(2,1)S(1)}, u32[]{:S(2)}, u32[]{:S(2)}) collective-permute-start(bf16[256,256]{1,0:T(8,128)(2,1)S(1)} %get-tuple-element.138.refs_0_), channel_id=1, source_target_pairs={{0,3},{1,2},{2,1},{3,0},{4,7},{5,6},{6,5},{7,4},{8,11},{9,10},{10,... | collective-permute-start | bytes 393224 | tf_op jit(solution)/shard_map/ppermute | solution.py:162
  96.5 162.5 %all-gather.17.cloned.1.call-start = ((), (), s32[]{:S(2)}) async-start(), calls=%async_computation.6 | async-start | bytes 1179648 | tf_op jit(solution)/shard_map/all_gather | solution.py:1000
  102.9 17.9 %collective-permute-start.29 = (bf16[4,2,256,128]{3,2,1,0:T(8,128)(2,1)}, bf16[4,2,256,128]{3,2,1,0:T(8,128)(2,1)S(1)}, u32[]{:S(2)}, u32[]{:S(2)}) collective-permute-start(bf16[4,2,256,128]{3,2,1,0:T(8,128)(2,1)} %get-tuple-element.149), channel_id=1, source_target_pairs={{0,4},{4,0},{8,12},{12,8},{16,20},{20,16},{24,28},{28,24},{1,5},{5... | collective-permute-start | bytes 1572872 | tf_op jit(solution)/shard_map/ppermute | solution.py:162
  113.7 12.9 %collective-permute-start.31 = (bf16[256,256]{1,0:T(8,128)(2,1)S(1)}, bf16[256,256]{1,0:T(8,128)(2,1)S(1)}, u32[]{:S(2)}, u32[]{:S(2)}) collective-permute-start(bf16[256,256]{1,0:T(8,128)(2,1)S(1)} %get-tuple-element.150.refs_0_.refs_11_), channel_id=1, source_target_pairs={{0,2},{1,3},{2,0},{3,1},{4,6},{5,7},{6,4},{7,5},{8,10},{9,11},{10,... | collective-permute-start | bytes 393224 | tf_op jit(solution)/shard_map/ppermute | solution.py:162
  114.8 11.8 %collective-permute-start.32 = (bf16[256,256]{1,0:T(8,128)(2,1)S(1)}, bf16[256,256]{1,0:T(8,128)(2,1)S(1)}, u32[]{:S(2)}, u32[]{:S(2)}) collective-permute-start(bf16[256,256]{1,0:T(8,128)(2,1)S(1)} %get-tuple-element.150.refs_0_.refs_11_), channel_id=1, source_target_pairs={{0,3},{1,2},{2,1},{3,0},{4,7},{5,6},{6,5},{7,4},{8,11},{9,10},{10,... | collective-permute-start | bytes 393224 | tf_op jit(solution)/shard_map/ppermute | solution.py:162
  156.9 105.5 %reduce-scatter.2.cloned.1.call-start = ((), (), s32[]{:S(2)}) async-start(), calls=%async_computation.2 | async-start | bytes 3538944 | tf_op jit(solution)/shard_map/reduce_scatter | solution.py:1027
  163.8 9.7 %collective-permute-start.43 = (bf16[256,256]{1,0:T(8,128)(2,1)}, bf16[256,256]{1,0:T(8,128)(2,1)S(1)}, u32[]{:S(2)}, u32[]{:S(2)}) collective-permute-start(bf16[256,256]{1,0:T(8,128)(2,1)} %get-tuple-element.172), channel_id=1, source_target_pairs={{0,20},{4,16},{8,28},{12,24},{16,4},{20,0},{24,12},{28,8},{1,21},{... | collective-permute-start | bytes 393224 | tf_op jit(solution)/shard_map/ppermute | solution.py:162
  180.2 92.4 %all-gather.11.cloned.1.call-start = ((), (), s32[]{:S(2)}) async-start(), calls=%async_computation.3 | async-start | bytes 2359296 | tf_op jit(solution)/shard_map/all_gather | solution.py:1091
  184.6 13.2 %collective-permute-start.48 = (bf16[272,256]{1,0:T(8,128)(2,1)S(1)}, bf16[272,256]{1,0:T(8,128)(2,1)S(1)}, u32[]{:S(2)}, u32[]{:S(2)}) collective-permute-start(bf16[272,256]{1,0:T(8,128)(2,1)S(1)} %get-tuple-element.181), channel_id=1, source_target_pairs={{0,2},{1,3},{2,0},{3,1},{4,6},{5,7},{6,4},{7,5},{8,10},{9,11},{10,... | collective-permute-start | bytes 417800 | tf_op jit(solution)/shard_map/ppermute | solution.py:162
  185.6 12.3 %collective-permute-start.49 = (bf16[272,256]{1,0:T(8,128)(2,1)S(1)}, bf16[272,256]{1,0:T(8,128)(2,1)S(1)}, u32[]{:S(2)}, u32[]{:S(2)}) collective-permute-start(bf16[272,256]{1,0:T(8,128)(2,1)S(1)} %get-tuple-element.182), channel_id=1, source_target_pairs={{0,3},{1,2},{2,1},{3,0},{4,7},{5,6},{6,5},{7,4},{8,11},{9,10},{10,... | collective-permute-start | bytes 417800 | tf_op jit(solution)/shard_map/ppermute | solution.py:162
  210.6 17.8 %collective-permute-start.52 = (bf16[256,256]{1,0:T(8,128)(2,1)S(1)}, bf16[256,256]{1,0:T(8,128)(2,1)S(1)}, u32[]{:S(2)}, u32[]{:S(2)}) collective-permute-start(bf16[256,256]{1,0:T(8,128)(2,1)S(1)} %get-tuple-element.196), channel_id=1, source_target_pairs={{0,1},{1,0},{2,3},{3,2},{4,5},{5,4},{6,7},{7,6},{8,9},{9,8},{10,11... | collective-permute-start | bytes 393224 | tf_op jit(solution)/shard_map/ppermute | solution.py:162
  211.6 19.6 %collective-permute-start.53 = (bf16[256,256]{1,0:T(8,128)(2,1)S(1)}, bf16[256,256]{1,0:T(8,128)(2,1)S(1)}, u32[]{:S(2)}, u32[]{:S(2)}) collective-permute-start(bf16[256,256]{1,0:T(8,128)(2,1)S(1)} %get-tuple-element.197), channel_id=1, source_target_pairs={{0,2},{1,3},{2,0},{3,1},{4,6},{5,7},{6,4},{7,5},{8,10},{9,11},{10,... | collective-permute-start | bytes 393224 | tf_op jit(solution)/shard_map/ppermute | solution.py:162
  213.5 17.8 %collective-permute-start.54 = (bf16[256,256]{1,0:T(8,128)(2,1)S(1)}, bf16[256,256]{1,0:T(8,128)(2,1)S(1)}, u32[]{:S(2)}, u32[]{:S(2)}) collective-permute-start(bf16[256,256]{1,0:T(8,128)(2,1)S(1)} %get-tuple-element.198), channel_id=1, source_target_pairs={{0,3},{1,2},{2,1},{3,0},{4,7},{5,6},{6,5},{7,4},{8,11},{9,10},{10,... | collective-permute-start | bytes 393224 | tf_op jit(solution)/shard_map/ppermute | solution.py:162
  244.5 28.1 %collective-permute-start.71 = (bf16[2,2,256,128]{3,2,1,0:T(8,128)(2,1)S(1)}, bf16[2,2,256,128]{3,2,1,0:T(8,128)(2,1)}, u32[]{:S(2)}, u32[]{:S(2)}) collective-permute-start(bf16[2,2,256,128]{3,2,1,0:T(8,128)(2,1)S(1)} %copy-done.27), channel_id=1, source_target_pairs={{0,24},{4,28},{8,16},{12,20},{16,8},{20,12},{24,0},{28,4},{1,25},{... | collective-permute-start | bytes 786440 | tf_op jit(solution)/shard_map/ppermute | solution.py:162
  246.2 12.8 %collective-permute-start.64 = (bf16[256,256]{1,0:T(8,128)(2,1)S(1)}, bf16[256,256]{1,0:T(8,128)(2,1)S(1)}, u32[]{:S(2)}, u32[]{:S(2)}) collective-permute-start(bf16[256,256]{1,0:T(8,128)(2,1)S(1)} %get-tuple-element.217), channel_id=1, source_target_pairs={{0,1},{1,0},{2,3},{3,2},{4,5},{5,4},{6,7},{7,6},{8,9},{9,8},{10,11... | collective-permute-start | bytes 393224 | tf_op jit(solution)/shard_map/ppermute | solution.py:162
  255.0 11.6 %collective-permute-start.65 = (bf16[256,256]{1,0:T(8,128)(2,1)S(1)}, bf16[256,256]{1,0:T(8,128)(2,1)S(1)}, u32[]{:S(2)}, u32[]{:S(2)}) collective-permute-start(bf16[256,256]{1,0:T(8,128)(2,1)S(1)} %get-tuple-element.222), channel_id=1, source_target_pairs={{0,2},{1,3},{2,0},{3,1},{4,6},{5,7},{6,4},{7,5},{8,10},{9,11},{10,... | collective-permute-start | bytes 393224 | tf_op jit(solution)/shard_map/ppermute | solution.py:162
  255.3 11.3 %collective-permute-start.66 = (bf16[256,256]{1,0:T(8,128)(2,1)S(1)}, bf16[256,256]{1,0:T(8,128)(2,1)S(1)}, u32[]{:S(2)}, u32[]{:S(2)}) collective-permute-start(bf16[256,256]{1,0:T(8,128)(2,1)S(1)} %get-tuple-element.223), channel_id=1, source_target_pairs={{0,3},{1,2},{2,1},{3,0},{4,7},{5,6},{6,5},{7,4},{8,11},{9,10},{10,... | collective-permute-start | bytes 393224 | tf_op jit(solution)/shard_map/ppermute | solution.py:162
  268.8 10.4 %collective-permute-start.68 = (f32[2,256]{1,0:T(2,128)S(1)}, f32[2,256]{1,0:T(2,128)S(1)}, u32[]{:S(2)}, u32[]{:S(2)}) collective-permute-start(f32[2,256]{1,0:T(2,128)S(1)} %add.47.refs_0_), channel_id=1, source_target_pairs={{0,8},{4,12},{8,0},{12,4},{16,24},{20,28},{24,16},{28,20},{1,9},{5... | collective-permute-start | bytes 6152 | tf_op jit(solution)/shard_map/ppermute | solution.py:162
  (77 other events, 819.1 us)
Sparse Core Ops, SparseCore 0:
  10.5 50.2 all-gather.8
  63.3 32.4 all-gather.12
  98.3 24.3 all-gather.14
  157.0 27.7 all-gather.16
  188.0 47.2 reduce-scatter.1
  237.8 33.8 all-gather.10
